TPU v7x, 32 devices: a whole 2x2x4 slice. The times are simulated.
32 devices in a mesh: gz: 4 (over y, core), xy: 8 (over z, x).
Axes of the slice: x: 2, y: 2, z: 4, core: 2. Of those that a mesh axis runs over, the one named last changes fastest.
Arguments:
- density: float32 [32, 1024, 128], P('gz', 'xy'), may hold values from -96 to 96
- live_slices: int32 [4, 8], replicated, may hold values from 1 to 8, as said below
- shear_slopes: float32 [2], replicated, may hold values from -0.12 to 0.12
- palette: float32 [3], replicated, may hold values from 0.5 to 2
- depth_order: int32 [2, 4], replicated, may hold values from 0 to 3, each once within a row
- tile_owner: int32 [2, 4], replicated, may hold values from 0 to 3, each once within a row
Outputs:
- owned_tiles: float32 [2, 4, 4, 256, 128], P(None, None, 'gz', 'xy')
Inputs may be any that keep to these rules, and one draw needn't show every extreme that they name: `live_slices`: some brick has all 8 slices live. `depth_order`: each row lists every slab once. `tile_owner`: each row names every index of gz once.
All inputs are finite; a program needn't handle non-finite values.
Results may differ from a plain program's by a relative error of at most 0.00042.
Values may be sent and summed in bfloat16 or wider, within the bound.
No kernel may reach another device: no remote copies, remote signals or barrier semaphores. Data moves between devices by JAX's collectives and lax.ppermute only.
A program may use at most 64 MiB of HBM per device.

v0:
```python
import jax
import jax.numpy as jnp
from jax import lax
from jax.sharding import PartitionSpec as P

TAPS = (1.0 / 9,) * 9
LIGHT = (0.48, 0.6, 0.64)


def extended(block, sides, width):
    for axis, dim in sides:
        count = lax.axis_size(axis)
        forward = [(i, i + 1) for i in range(count - 1)]
        backward = [(target, source) for source, target in forward]
        low = lax.ppermute(
            lax.slice_in_dim(block, block.shape[dim] - width, None, axis=dim), axis, forward
        )
        high = lax.ppermute(lax.slice_in_dim(block, 0, width, axis=dim), axis, backward)
        block = jnp.concatenate([low, block, high], axis=dim)
    return block


def smooth_along(volume, along):
    extent = volume.shape[along] - 8
    total = TAPS[0] * lax.slice_in_dim(volume, 0, extent, axis=along)
    for offset in range(1, 9):
        total = total + TAPS[offset] * lax.slice_in_dim(volume, offset, offset + extent, axis=along)
    return total


def smooth_all(volume):
    return smooth_along(smooth_along(smooth_along(volume, 0), 1), 2)


def shade(padded, live_mask, palette, extinct, stack_axis):
    center = padded[1:-1, 1:-1, 1:-1]
    diff_depth = 0.5 * (padded[2:, 1:-1, 1:-1] - padded[:-2, 1:-1, 1:-1])
    diff_rows = 0.5 * (padded[1:-1, 2:, 1:-1] - padded[1:-1, :-2, 1:-1])
    diff_cols = 0.5 * (padded[1:-1, 1:-1, 2:] - padded[1:-1, 1:-1, :-2])
    magnitude = jnp.sqrt(
        diff_depth * diff_depth + diff_rows * diff_rows + diff_cols * diff_cols + 0.01
    )
    facing = (
        jnp.maximum(0.0, LIGHT[0] * diff_depth + LIGHT[1] * diff_rows + LIGHT[2] * diff_cols)
        / magnitude
    )
    opacity = jnp.where(live_mask, 1.0 - jnp.exp(-extinct * jax.nn.softplus(2.0 * center)), 0.0)
    bright = opacity * (0.25 + 0.75 * facing)
    stacked = jnp.stack(
        [bright * palette[0], bright * palette[1], bright * palette[2], opacity], axis=stack_axis
    )
    return stacked.astype(jnp.bfloat16)


def shear_matrix(shear_slope, slice_depth, columns, total_depth):
    shift = shear_slope * (slice_depth + 0.5 - 0.5 * total_depth)
    shift = shift[..., None, None]
    source = lax.broadcasted_iota(jnp.float32, (columns, columns), 0)
    target = lax.broadcasted_iota(jnp.float32, (columns, columns), 1)
    return jnp.maximum(0.0, 1.0 - jnp.abs(source - target + shift)).astype(jnp.bfloat16)


def composite(fragments, order_row):
    ordered = jnp.take(fragments, order_row, axis=0)

    def blend(carry, fragment):
        shaded, transmit = carry
        return ((shaded + transmit * fragment[:3], transmit * (1.0 - fragment[3])), None)

    plane = fragments.shape[2:]
    init = (jnp.zeros((3,) + plane, jnp.float32), jnp.ones(plane, jnp.float32))
    (shaded, transmit), _ = lax.scan(blend, init, ordered)
    return jnp.concatenate([shaded, (1.0 - transmit)[None]], axis=0)


def march_range(slabs, first, count, offset, slope, slab_start, total_depth, backward):
    planes, height, columns = (slabs.shape[1], slabs.shape[2], slabs.shape[3])

    def advance(step, carry):
        shaded, transmit = carry
        if backward:
            position = first + count - 1 - step
        else:
            position = first + step
        layer = lax.dynamic_index_in_dim(slabs, position, 0, keepdims=False)
        matrix = shear_matrix(
            slope, slab_start + (offset + position).astype(jnp.float32), columns, total_depth
        )
        sheared = jnp.dot(
            layer.reshape(planes * height, columns), matrix, preferred_element_type=jnp.float32
        )
        sheared = sheared.reshape(planes, height, columns)
        return (shaded + transmit * sheared[:3], transmit * (1.0 - sheared[3]))

    init = (jnp.zeros((3, height, columns), jnp.float32), jnp.ones((height, columns), jnp.float32))
    return lax.fori_loop(jnp.int32(0), count, advance, init)


def body(density, live_slices, shear_slopes, palette, depth_order, tile_owner):
    depth_cells, row_cells, columns = density.shape
    n_depth = lax.axis_size("gz")
    n_rows = lax.axis_size("xy")
    depth_index = lax.axis_index("gz")
    row_index = lax.axis_index("xy")
    total_depth = depth_cells * n_depth
    extinct = 3.0 / total_depth
    widened = extended(density, (("gz", 0), ("xy", 1)), 5)
    widened = jnp.pad(widened, ((0, 0), (0, 0), (5, 5)))
    smoothed = smooth_all(widened)
    depth_pos = lax.broadcasted_iota(jnp.int32, (depth_cells + 2, 1, 1), 0)
    row_pos = lax.broadcasted_iota(jnp.int32, (1, row_cells + 2, 1), 1)
    col_pos = lax.broadcasted_iota(jnp.int32, (1, 1, columns + 2), 2)
    keep_depth = ((depth_pos > 0) | (depth_index > 0)) & (
        (depth_pos < depth_cells + 1) | (depth_index < n_depth - 1)
    )
    keep_rows = ((row_pos > 0) | (row_index > 0)) & (
        (row_pos < row_cells + 1) | (row_index < n_rows - 1)
    )
    keep_cols = (col_pos > 0) & (col_pos < columns + 1)
    padded = jnp.where(keep_depth & keep_rows & keep_cols, smoothed, 0.0)
    own_live = lax.dynamic_slice(live_slices, (depth_index, row_index), (1, 1))[0, 0]
    local_depth = lax.broadcasted_iota(jnp.int32, (depth_cells, 1, 1), 0)
    live_mask = local_depth < own_live
    layers = shade(padded, live_mask, palette, extinct, 1)
    slab_start = (depth_index * depth_cells).astype(jnp.float32)
    fragments = []
    for view_index in range(2):
        shaded, transmit = march_range(
            layers,
            0,
            own_live,
            0,
            shear_slopes[view_index],
            slab_start,
            total_depth,
            view_index == 1,
        )
        fragments.append(jnp.concatenate([shaded, (1.0 - transmit)[None]], axis=0))
    stacked = jnp.stack(fragments)
    tile_rows = row_cells // n_depth
    tiles = stacked.reshape(2, 4, n_depth, tile_rows, columns).transpose(0, 2, 1, 3, 4)
    ranks = lax.broadcasted_iota(jnp.int32, (n_depth,), 0)
    inverse = jnp.sum(
        ranks[None, None, :] * (tile_owner[:, None, :] == ranks[None, :, None]).astype(jnp.int32),
        axis=2,
    )
    outgoing = jnp.stack(
        [jnp.take(tiles[view_index], inverse[view_index], axis=0) for view_index in range(2)]
    )
    incoming = lax.all_to_all(outgoing, "gz", split_axis=1, concat_axis=1, tiled=True)
    images = [composite(incoming[view_index], depth_order[view_index]) for view_index in range(2)]
    return jnp.stack(images)[:, :, None]


def solution(mesh):
    placed = (P("gz", "xy", None), P(), P(), P(), P(), P())
    return jax.shard_map(
        body, mesh=mesh, in_specs=placed, out_specs=P(None, None, "gz", "xy", None), check_vma=False
    )
```

profile of v0, /device:TPU:2, one launch (start us, length us, event | category | flops | bytes accessed | tf_op | source)
XLA Modules:
  0.0 75.3 jit_solution(8740080986341516086)
XLA Ops:
  0.0 1.2 %fusion.36 = (f32[5,128,128]{2,1,0:T(8,128)S(1)}, f32[5,128,128]{2,1,0:T(8,128)S(1)}) fusion(f32[8,128,128]{2,1,0:T(8,128)} %param.16), kind=kLoop, calls=%fused_computation.133 | loop fusion | bytes 1310720 | tf_op jit(solution)/shard_map/slice | solution.py:18
  1.2 1.8 %collective-permute-start = (f32[5,128,128]{2,1,0:T(8,128)S(1)}, f32[5,128,128]{2,1,0:T(8,128)S(1)}, u32[]{:S(2)}, u32[]{:S(2)}) collective-permute-start(f32[5,128,128]{2,1,0:T(8,128)S(1)} %get-tuple-element.468), channel_id=1, source_target_pairs={{0,8},{8,16},{16,24},{1,9},{9,17},{17,25},{2,10},{10,18},{18,26},{... | collective-permute-start | bytes 983048 | tf_op jit(solution)/shard_map/ppermute | solution.py:15
  3.0 1.3 %collective-permute-start.1 = (f32[5,128,128]{2,1,0:T(8,128)S(1)}, f32[5,128,128]{2,1,0:T(8,128)S(1)}, u32[]{:S(2)}, u32[]{:S(2)}) collective-permute-start(f32[5,128,128]{2,1,0:T(8,128)S(1)} %get-tuple-element.467), channel_id=1, source_target_pairs={{8,0},{16,8},{24,16},{9,1},{17,9},{25,17},{10,2},{18,10},{26,18},{... | collective-permute-start | bytes 983048 | tf_op jit(solution)/shard_map/ppermute | solution.py:18
  4.3 1.4 %fusion.38 = (f32[1]{0:T(128)}, f32[1]{0:T(128)}, f32[1]{0:T(128)}) fusion(f32[3]{0:T(128)} %param.19), kind=kLoop, calls=%fused_computation.135 | loop fusion | bytes 24 | tf_op jit(solution)/shard_map/slice | solution.py:50
  5.7 1.3 %fusion.37 = (f32[1]{0:T(128)}, f32[1]{0:T(128)}) fusion(f32[2]{0:T(128)} %param.18), kind=kLoop, calls=%fused_computation.134 | loop fusion | bytes 16 | tf_op jit(solution)/shard_map/slice | solution.py:133
  7.0 0.8 %select_reduce_fusion = s32[2,4]{1,0:T(2,128)S(1)} fusion(s32[2,4]{1,0:T(2,128)} %param.21), kind=kLoop, calls=%fused_computation.116 | loop fusion | flops 88 | bytes 64 | tf_op jit(solution)/shard_map/reduce_sum | solution.py:143
  7.9 1.3 %dynamic_slice.29 = s32[1,1]{1,0:T(1,128)} dynamic-slice(s32[4,8]{1,0:T(4,128)} %param.17, s32[]{:T(128)S(6)} %select_n.44, s32[]{:T(128)S(6)} %select_n.45), dynamic_slice_sizes={1,1} | dynamic-slice | bytes 12 | tf_op jit(solution)/shard_map/dynamic_slice | solution.py:121
  9.5 3.5 %collective-permute-start.2 = (f32[18,5,128]{2,1,0:T(8,128)S(1)}, f32[18,5,128]{2,1,0:T(8,128)S(1)}, u32[]{:S(2)}, u32[]{:S(2)}) collective-permute-start(f32[18,5,128]{2,1,0:T(8,128)S(1)} %get-tuple-element.459), channel_id=1, source_target_pairs={{0,1},{1,2},{2,3},{3,4},{4,5},{5,6},{6,7},{8,9},{9,10},{10,11},{11... | collective-permute-start | bytes 138248 | tf_op jit(solution)/shard_map/ppermute | solution.py:15
  13.0 2.4 %collective-permute-start.3 = (f32[18,5,128]{2,1,0:T(8,128)S(1)}, f32[18,5,128]{2,1,0:T(8,128)S(1)}, u32[]{:S(2)}, u32[]{:S(2)}) collective-permute-start(f32[18,5,128]{2,1,0:T(8,128)S(1)} %get-tuple-element.460), channel_id=1, source_target_pairs={{1,0},{2,1},{3,2},{4,3},{5,4},{6,5},{7,6},{9,8},{10,9},{11,10},{12... | collective-permute-start | bytes 138248 | tf_op jit(solution)/shard_map/ppermute | solution.py:18
  15.3 0.6 iota_compare_fusion.5
  16.6 3.5 %collective-permute-done.3 = f32[18,5,128]{2,1,0:T(8,128)S(1)} collective-permute-done((f32[18,5,128]{2,1,0:T(8,128)S(1)}, f32[18,5,128]{2,1,0:T(8,128)S(1)}, u32[]{:S(2)}, u32[]{:S(2)}) %collective-permute-start.3) | collective-permute-done | bytes 46112 | tf_op jit(solution)/shard_map/ppermute | solution.py:18
  20.1 0.8 %select_maximum_fusion = f32[18,138,138]{2,1,0:T(8,128)S(1)} fusion(f32[18,5,128]{2,1,0:T(8,128)S(1)} %collective-permute-done.3, f32[18,128,128]{2,1,0:T(8,128)S(1)} %constant_dynamic-update-slice_fusion, f32[18,5,128]{2,1,0:T(8,128)S(1)} %collective-permute-done.2), kind=kLoop, calls=%fused_computation.42 | loop fusion | flops 2742336 | bytes 2642976 | tf_op jit(solution)/shard_map/concatenate | solution.py:19
  21.4 1.0 %fusion.26 = f32[10,130,138]{2,1,0:T(8,128)S(1)} fusion(f32[10,138,138]{2,1,0:T(8,128)S(1)} %fusion.23), kind=kLoop, calls=%fused_computation.66 | loop fusion | flops 1614600 | bytes 7176000 | tf_op jit(solution)/shard_map/add | solution.py:27
  22.4 3.2 %fusion.25 = f32[10,130,130]{2,1,0:T(8,128)S(1)} fusion(f32[10,130,138]{2,1,0:T(8,128)S(1)} %fusion.26, pred[130]{0:T(512)(128)(4,1)S(1)} %fusion.34, pred[10,130]{1,0:T(8,128)(4,1)S(1)} %broadcast_and_fusion), kind=kLoop, calls=%fused_computation.57 | loop fusion | flops 1859000 | bytes 6761430 | tf_op jit(solution)/shard_map/jit(_where)/select_n | solution.py:120
  25.7 1.8 %fusion.31 = (bf16[8,1,128,128]{3,2,1,0:T(8,128)(2,1)S(1)}, f32[8,128,128]{2,1,0:T(8,128)S(1)}, bf16[8,1,128,128]{3,2,1,0:T(8,128)(2,1)S(1)}) fusion(f32[]{:T(128)} %bitcast.7, f32[10,130,130]{2,1,0:T(8,128)S(1)} %fusion.25, pred[8]{0:T(512)(128)(4,1)S(1)} %iota_compare_fusion.5), kind=kLoop, calls=%fused_computation.89 | loop fusion | flops 4587520 | bytes 4718604 | tf_op jit(solution)/shard_map/stack | solution.py:49
  27.4 1.4 %fusion.32 = (bf16[8,1,128,128]{3,2,1,0:T(8,128)(2,1)S(1)}, bf16[8,1,128,128]{3,2,1,0:T(8,128)(2,1)S(1)}) fusion(f32[8,128,128]{2,1,0:T(8,128)S(1)} %get-tuple-element.457, f32[]{:T(128)} %bitcast.10, f32[]{:T(128)} %bitcast.13), kind=kLoop, calls=%fused_computation.90 | loop fusion | flops 524288 | bytes 1048584 | tf_op jit(solution)/shard_map/stack | solution.py:49
  29.0 3.9 %while.58 = (s32[]{:T(128)}, f32[3,128,128]{2,1,0:T(8,128)S(1)}, f32[128,128]{1,0:T(8,128)S(1)}, s32[]{:T(128)}, bf16[8,4,128,128]{3,2,1,0:T(8,128)(2,1)S(1)}, /...) while((s32[]{:T(128)}, f32[3,128,128]{2,1,0:T(8,128)S(1)}, ...), condition=%wide.region_1.2_spmd, body=%wide.region_0.1_spmd.sunk | while | flops 17006600 | bytes 1900739 | solution.py:96
  33.0 3.8 %while.59 = (s32[]{:T(128)}, f32[3,128,128]{2,1,0:T(8,128)S(1)}, f32[128,128]{1,0:T(8,128)S(1)}, s32[]{:T(128)}, s32[]{:T(128)}, /*index=5*/bf16[8,4,128,128]{3,...) while((s32[]{:T(128)}, f32[3,128,128]{2,1,0:T(8,128)S(1)}, ...), condition=%wide.region_3.4_spmd, body=%wide.region_2.3_spmd.sunk | while | flops 17006600 | bytes 1900759 | solution.py:96
  38.2 0.8 %pad_maximum_fusion.1 = f32[2,4,4,32,128]{4,3,2,0,1:T(8,128)} fusion(f32[1,4,4,32,128]{4,3,2,0,1:T(8,128)S(1)} %get-tuple-element.478, f32[1,4,4,32,128]{4,3,2,0,1:T(8,128)S(1)} %get-tuple-element.479), kind=kLoop, calls=%fused_computation.84 | loop fusion | flops 131072 | bytes 1048576 | tf_op jit(solution)/shard_map/stack | solution.py:147
  39.1 24.8 %all-to-all-start = ((f32[2,4,4,32,128]{4,3,2,0,1:T(8,128)}), f32[2,4,4,32,128]{4,3,2,0,1:T(8,128)S(1)}, u32[]{:S(2)}, u32[]{:S(2)}) async-start(f32[2,4,4,32,128]{4,3,2,0,1:T(8,128)} %pad_maximum_fusion.1), calls=%async_computation | async-start | bytes 1048576 | tf_op jit(solution)/shard_map/all_to_all | solution.py:150
  63.9 8.8 %all-to-all-done = f32[2,4,4,32,128]{4,3,2,0,1:T(8,128)S(1)} async-done(((f32[2,4,4,32,128]{4,3,2,0,1:T(8,128)}), f32[2,4,4,32,128]{4,3,2,0,1:T(8,128)S(1)}, u32[]{:S(2)}, u32[]{:S(2)}) %all-to-all-start) | async-done | bytes 524320 | tf_op jit(solution)/shard_map/all_to_all | solution.py:150
  72.7 0.6 gather_fusion.2
  73.7 0.6 gather_fusion.3
  74.6 0.7 maximum_bitcast_fusion.1
  (82 shorter events, 4.3 us)
Async XLA Ops:
  0.0 9.4 %copy-start = (f32[8,128,128]{2,1,0:T(8,128)S(1)}, f32[8,128,128]{2,1,0:T(8,128)}, u32[]{:S(2)}) copy-start(f32[8,128,128]{2,1,0:T(8,128)} %param.16) | copy-start | bytes 1572868
  1.2 8.2 %collective-permute-start = (f32[5,128,128]{2,1,0:T(8,128)S(1)}, f32[5,128,128]{2,1,0:T(8,128)S(1)}, u32[]{:S(2)}, u32[]{:S(2)}) collective-permute-start(f32[5,128,128]{2,1,0:T(8,128)S(1)} %get-tuple-element.468), channel_id=1, source_target_pairs={{0,8},{8,16},{16,24},{1,9},{9,17},{17,25},{2,10},{10,18},{18,26},{... | collective-permute-start | bytes 983048 | tf_op jit(solution)/shard_map/ppermute | solution.py:15
  3.0 6.5 %collective-permute-start.1 = (f32[5,128,128]{2,1,0:T(8,128)S(1)}, f32[5,128,128]{2,1,0:T(8,128)S(1)}, u32[]{:S(2)}, u32[]{:S(2)}) collective-permute-start(f32[5,128,128]{2,1,0:T(8,128)S(1)} %get-tuple-element.467), channel_id=1, source_target_pairs={{8,0},{16,8},{24,16},{9,1},{17,9},{25,17},{10,2},{18,10},{26,18},{... | collective-permute-start | bytes 983048 | tf_op jit(solution)/shard_map/ppermute | solution.py:18
  9.5 7.1 %collective-permute-start.2 = (f32[18,5,128]{2,1,0:T(8,128)S(1)}, f32[18,5,128]{2,1,0:T(8,128)S(1)}, u32[]{:S(2)}, u32[]{:S(2)}) collective-permute-start(f32[18,5,128]{2,1,0:T(8,128)S(1)} %get-tuple-element.459), channel_id=1, source_target_pairs={{0,1},{1,2},{2,3},{3,4},{4,5},{5,6},{6,7},{8,9},{9,10},{10,11},{11... | collective-permute-start | bytes 138248 | tf_op jit(solution)/shard_map/ppermute | solution.py:15
  13.0 7.1 %collective-permute-start.3 = (f32[18,5,128]{2,1,0:T(8,128)S(1)}, f32[18,5,128]{2,1,0:T(8,128)S(1)}, u32[]{:S(2)}, u32[]{:S(2)}) collective-permute-start(f32[18,5,128]{2,1,0:T(8,128)S(1)} %get-tuple-element.460), channel_id=1, source_target_pairs={{1,0},{2,1},{3,2},{4,3},{5,4},{6,5},{7,6},{9,8},{10,9},{11,10},{12... | collective-permute-start | bytes 138248 | tf_op jit(solution)/shard_map/ppermute | solution.py:18
  38.1 25.8 %copy-start.1 = (s32[2,4]{1,0:T(2,128)S(1)}, s32[2,4]{1,0:T(2,128)}, u32[]{:S(2)}) copy-start(s32[2,4]{1,0:T(2,128)} %param.20) | copy-start | bytes 100
  39.1 33.6 %all-to-all-start = ((f32[2,4,4,32,128]{4,3,2,0,1:T(8,128)}), f32[2,4,4,32,128]{4,3,2,0,1:T(8,128)S(1)}, u32[]{:S(2)}, u32[]{:S(2)}) async-start(f32[2,4,4,32,128]{4,3,2,0,1:T(8,128)} %pad_maximum_fusion.1), calls=%async_computation | async-start | bytes 1048576 | tf_op jit(solution)/shard_map/all_to_all | solution.py:150
where the time goes:
time: 76.2 us; the launch traced here: 75.3 us
  starting transfers between devices  33.7 us (44%)
  other arithmetic  12.8 us (17%)
  waiting for transfers between devices  12.3 us (16%)
  local copies, waits for them, and re-layouts  7.86 us (10%)
  loops' own time  6.85 us (9%)
  between operations  1.04 us (1%)
    all_to_all x1, starting transfers between devices, body(): lax.all_to_all(outgoing, 'gz', split_axis=1, concat_axis=1, tiled=True)  24.8 us
    all_to_all x1, waiting for transfers between devices, body(): lax.all_to_all(outgoing, 'gz', split_axis=1, concat_axis=1, tiled=True)  8.81 us
    another operation x2, loops' own time, march_range(): return lax.fori_loop(jnp.int32(0), count, advance, init)  6.59 us
    ppermute x2, starting transfers between devices, extended(): lax.ppermute(lax.slice_in_dim(block, block.shape[dim] - width, None, axis...  5.22 us
    ppermute x2, starting transfers between devices, extended(): lax.ppermute(lax.slice_in_dim(block, 0, width, axis=dim), axis, backward)  3.68 us
    ppermute x2, waiting for transfers between devices, extended(): lax.ppermute(lax.slice_in_dim(block, 0, width, axis=dim), axis, backward)  3.48 us
    another operation x3, other arithmetic, shade(): jnp.stack([bright * palette[0], bright * palette[1], bright * palette[2],...  3.31 us
    select_n x1, other arithmetic, body(): padded = jnp.where(keep_depth & keep_rows & keep_cols, smoothed, 0.0)  3.23 us
  transfers between devices with their start and end apart: 5, of which 2 were waited for; matrix products, arithmetic and copies ran while one was open for 8% of the time, Pallas kernels for 0%

commit v1 on v0

v1 whole, which is shorter than its diff:
```python
import jax
import jax.numpy as jnp
from jax import lax
from jax.experimental import pallas as pl
from jax.experimental.pallas import tpu as pltpu
from jax.sharding import PartitionSpec as P

LIGHT = (0.48, 0.6, 0.64)
REACH = 4
HALO = REACH + 1
TAPS = 2 * REACH + 1
ROW_TILE = 8
VIEWS = 2
VMEM_BYTES = 40 * 1024 * 1024


def column_matrix(columns):
    source = lax.broadcasted_iota(jnp.int32, (columns, columns), 0)
    target = lax.broadcasted_iota(jnp.int32, (columns, columns), 1)

    def band(shift):
        at = target + shift
        inside = (jnp.abs(source - at) <= REACH) & (at >= 0) & (at < columns)
        return jnp.where(inside, 1.0, 0.0).astype(jnp.float32)

    return jnp.concatenate([band(0), band(1) - band(-1)], axis=1).astype(jnp.bfloat16)


def shear_matrices(slopes_ref, slice_depth, columns, total_depth):
    source = lax.broadcasted_iota(jnp.int32, (columns, columns), 0)
    target = lax.broadcasted_iota(jnp.int32, (columns, columns), 1)
    distance = (source - target).astype(jnp.float32)
    parts = []
    for view in range(VIEWS):
        shift = slopes_ref[view] * (slice_depth + 0.5 - 0.5 * total_depth)
        parts.append(jnp.maximum(0.0, 1.0 - jnp.abs(distance + shift)))
    return jnp.concatenate(parts, axis=1).astype(jnp.bfloat16)


def window_sums(layers, taps):
    sums, width = layers, 1
    while 2 * width < taps:
        sums = [sums[i] + sums[i + width] for i in range(len(sums) - width)]
        width *= 2
    return [sums[i] + layers[i + width] for i in range(len(layers) - width)]


def make_render(n_depth, n_rows, depth_cells, row_cells, columns):
    total_depth = depth_cells * n_depth
    extinct = 3.0 / total_depth
    padded_rows = row_cells + 2 * ROW_TILE
    first, last = ROW_TILE, ROW_TILE + row_cells
    tile_rows = row_cells // n_depth
    cells = TAPS**3
    floor = 0.01 * (2.0 * cells) ** 2

    def kernel(
        live_ref, slopes_ref, palette_ref, owner_ref,
        own_ref, dlo_ref, dhi_ref, rlo_ref, rhi_ref, clo_ref, chi_ref,
        out_ref,
        deep, triple, smooth, across, sheared,
    ):
        depth_index = lax.axis_index("gz")
        row_index = lax.axis_index("xy")

        for chunk in range(padded_rows // ROW_TILE):
            if chunk == 0:
                low = [clo_ref[i] for i in range(HALO)]
                mid = [rlo_ref[i] for i in range(depth_cells)]
                high = [chi_ref[i] for i in range(HALO)]
            elif chunk == padded_rows // ROW_TILE - 1:
                low = [clo_ref[HALO + i] for i in range(HALO)]
                mid = [rhi_ref[i] for i in range(depth_cells)]
                high = [chi_ref[HALO + i] for i in range(HALO)]
            else:
                rows = pl.ds((chunk - 1) * ROW_TILE, ROW_TILE)
                low = [dlo_ref[i, rows] for i in range(HALO)]
                mid = [own_ref[i, rows] for i in range(depth_cells)]
                high = [dhi_ref[i, rows] for i in range(HALO)]
            for z, total in enumerate(window_sums(low + mid + high, TAPS)):
                deep[z, pl.ds(chunk * ROW_TILE, ROW_TILE)] = total

        band = column_matrix(columns)
        weights = jnp.concatenate([band, band, band], axis=0)
        for z in range(depth_cells + 2):
            lead = first - REACH
            span = row_cells + 2 * REACH
            triple[pl.ds(ROW_TILE, span)] = (
                deep[z, pl.ds(lead - 1, span)]
                + deep[z, pl.ds(lead, span)]
                + deep[z, pl.ds(lead + 1, span)]
            )
            base = ROW_TILE - lead
            total = (
                triple[pl.ds(base - 3, padded_rows)]
                + triple[pl.ds(base, padded_rows)]
                + triple[pl.ds(base + 3, padded_rows)]
            )
            hi = total.astype(jnp.bfloat16)
            rest = total - hi.astype(jnp.float32)
            mid = rest.astype(jnp.bfloat16)
            lo = (rest - mid.astype(jnp.float32)).astype(jnp.bfloat16)
            split = jnp.concatenate([hi, mid, lo], axis=1)
            if 1 <= z <= depth_cells:
                both = jnp.dot(split, weights, preferred_element_type=jnp.float32)
                smooth[z] = both[:, :columns]
                across[z - 1] = both[first:last, columns:]
            else:
                smooth[z] = jnp.dot(
                    split, weights[:, :columns], preferred_element_type=jnp.float32
                )

        @pl.when(row_index == 0)
        def _():
            smooth[:, first - 1 : first, :] = jnp.zeros(
                (depth_cells + 2, 1, columns), jnp.float32
            )

        @pl.when(row_index == n_rows - 1)
        def _():
            smooth[:, last : last + 1, :] = jnp.zeros((depth_cells + 2, 1, columns), jnp.float32)

        @pl.when(depth_index == 0)
        def _():
            smooth[0] = jnp.zeros((padded_rows, columns), jnp.float32)

        @pl.when(depth_index == n_depth - 1)
        def _():
            smooth[depth_cells + 1] = jnp.zeros((padded_rows, columns), jnp.float32)

        own_live = live_ref[depth_index, row_index]
        slab_start = (depth_index * depth_cells).astype(jnp.float32)
        for z in range(depth_cells):
            center = smooth[z + 1, pl.ds(first, row_cells)]
            diff_depth = (
                smooth[z + 2, pl.ds(first, row_cells)] - smooth[z, pl.ds(first, row_cells)]
            )
            diff_rows = (
                smooth[z + 1, pl.ds(first + 1, row_cells)]
                - smooth[z + 1, pl.ds(first - 1, row_cells)]
            )
            diff_cols = across[z]
            square = diff_depth * diff_depth + diff_rows * diff_rows + diff_cols * diff_cols
            toward = LIGHT[0] * diff_depth + LIGHT[1] * diff_rows + LIGHT[2] * diff_cols
            facing = jnp.maximum(0.0, toward) * lax.rsqrt(square + floor)
            twice = center * (2.0 / cells)
            small = jnp.exp(-jnp.abs(twice))
            log1p = jnp.where(small < 1e-4, small * (1.0 - 0.5 * small), jnp.log(1.0 + small))
            softplus = jnp.maximum(twice, 0.0) + log1p
            opacity = jnp.where(z < own_live, 1.0 - jnp.exp(-extinct * softplus), 0.0)
            bright = opacity * (0.25 + 0.75 * facing)
            rgba = jnp.concatenate(
                [(bright * palette_ref[c]).astype(jnp.bfloat16) for c in range(3)]
                + [opacity.astype(jnp.bfloat16)],
                axis=0,
            )
            matrix = shear_matrices(slopes_ref, slab_start + float(z), columns, total_depth)
            sheared[z] = jnp.dot(rgba, matrix, preferred_element_type=jnp.float32)

        for chunk in range(row_cells // ROW_TILE):
            tile = chunk * ROW_TILE // tile_rows
            inside = chunk * ROW_TILE - tile * tile_rows
            for view in range(VIEWS):
                lanes = pl.ds(view * columns, columns)
                colour, transmit = None, None
                for z in range(depth_cells):
                    part = [
                        sheared[z, pl.ds(c * row_cells + chunk * ROW_TILE, ROW_TILE), lanes]
                        for c in range(4)
                    ]
                    clear = 1.0 - part[3]
                    if z == 0:
                        colour, transmit = part[:3], clear
                    elif view == 0:
                        colour = [colour[c] + transmit * part[c] for c in range(3)]
                        transmit = transmit * clear
                    else:
                        colour = [part[c] + clear * colour[c] for c in range(3)]
                        transmit = transmit * clear
                place = owner_ref[view, tile]
                for c, value in enumerate(colour + [1.0 - transmit]):
                    out_ref[place, view, c, pl.ds(inside, ROW_TILE)] = value

    smem = pl.BlockSpec(memory_space=pltpu.SMEM)
    vmem = pl.BlockSpec(memory_space=pltpu.VMEM)
    return pl.pallas_call(
        kernel,
        out_shape=jax.ShapeDtypeStruct((n_depth, VIEWS, 4, tile_rows, columns), jnp.float32),
        in_specs=[smem] * 4 + [vmem] * 7,
        out_specs=vmem,
        scratch_shapes=[
            pltpu.VMEM((depth_cells + 2, padded_rows, columns), jnp.float32),
            pltpu.VMEM((padded_rows + 2 * ROW_TILE, columns), jnp.float32),
            pltpu.VMEM((depth_cells + 2, padded_rows, columns), jnp.float32),
            pltpu.VMEM((depth_cells, row_cells, columns), jnp.float32),
            pltpu.VMEM((depth_cells, 4 * row_cells, VIEWS * columns), jnp.float32),
        ],
        compiler_params=pltpu.CompilerParams(vmem_limit_bytes=VMEM_BYTES),
        name="render",
    )


def composite_kernel(order_ref, in_ref, out_ref):
    count = in_ref.shape[0]
    for view in range(VIEWS):
        colour, transmit = None, None
        for k in range(count):
            source = order_ref[view, k]
            part = [in_ref[source, view, c] for c in range(4)]
            clear = 1.0 - part[3]
            if k == 0:
                colour, transmit = part[:3], clear
            else:
                colour = [colour[c] + transmit * part[c] for c in range(3)]
                transmit = transmit * clear
        for c, value in enumerate(colour + [1.0 - transmit]):
            out_ref[view, c, 0] = value


def body(density, live_slices, shear_slopes, palette, depth_order, tile_owner):
    depth_cells, row_cells, columns = density.shape
    n_depth = lax.axis_size("gz")
    n_rows = lax.axis_size("xy")

    def both_ways(axis, to_next, to_previous):
        count = lax.axis_size(axis)
        forward = [(i, i + 1) for i in range(count - 1)]
        backward = [(target, source) for source, target in forward]
        return lax.ppermute(to_next, axis, forward), lax.ppermute(to_previous, axis, backward)

    dlo, dhi = both_ways("gz", density[depth_cells - HALO :], density[:HALO])
    rlo, rhi = both_ways("xy", density[:, row_cells - ROW_TILE :], density[:, :ROW_TILE])
    clo, chi = both_ways(
        "gz",
        jnp.concatenate([rlo[depth_cells - HALO :], rhi[depth_cells - HALO :]], axis=0),
        jnp.concatenate([rlo[:HALO], rhi[:HALO]], axis=0),
    )
    render = make_render(n_depth, n_rows, depth_cells, row_cells, columns)
    outgoing = render(
        live_slices, shear_slopes, palette, tile_owner,
        density, dlo, dhi, rlo, rhi, clo, chi,
    )
    incoming = lax.all_to_all(outgoing, "gz", split_axis=0, concat_axis=0, tiled=True)
    tile_rows = row_cells // n_depth
    return pl.pallas_call(
        composite_kernel,
        out_shape=jax.ShapeDtypeStruct((VIEWS, 4, 1, tile_rows, columns), jnp.float32),
        in_specs=[pl.BlockSpec(memory_space=pltpu.SMEM), pl.BlockSpec(memory_space=pltpu.VMEM)],
        out_specs=pl.BlockSpec(memory_space=pltpu.VMEM),
        compiler_params=pltpu.CompilerParams(vmem_limit_bytes=VMEM_BYTES),
        name="composite",
    )(depth_order, incoming)


def solution(mesh):
    placed = (P("gz", "xy", None), P(), P(), P(), P(), P())
    return jax.shard_map(
        body, mesh=mesh, in_specs=placed, out_specs=P(None, None, "gz", "xy", None), check_vma=False
    )
```

time: 76.2 us -> 37.1 us (0.49)
  the two profiles are of different devices: /device:TPU:2 before, /device:TPU:0 now
where the time goes in v1:
time: 37.1 us; the launch traced here: 36.7 us
  starting transfers between devices  16.1 us (43%)
  blocking collectives  12.6 us (34%)
  Pallas kernels  4.05 us (11%)
  local copies, waits for them, and re-layouts  1.95 us (5%)
  waiting for transfers between devices  1.83 us (5%)
    all_to_all x1, blocking collectives, body(): lax.all_to_all(outgoing, 'gz', split_axis=0, concat_axis=0, tiled=True)  12.6 us
    ppermute x3, starting transfers between devices, both_ways(): lax.ppermute(to_next, axis, forward)  12.2 us
    ppermute x3, starting transfers between devices, both_ways(): lax.ppermute(to_previous, axis, backward)  3.86 us
    pallas_call x1, Pallas kernels, body(): render(live_slices, shear_slopes, palette, tile_owner, density, dlo, dhi,...  2.81 us
    ppermute x3, waiting for transfers between devices, both_ways(): lax.ppermute(to_previous, axis, backward)  1.83 us
    pallas_call x1, Pallas kernels, body(): pl.pallas_call(composite_kernel, out_shape=jax.ShapeDtypeStruct((VIEWS, 4...  1.24 us
    slice x1, local copies, waits for them, and re-layouts, body(): dlo, dhi = both_ways('gz', density[depth_cells - HALO:], density[:HALO])  1.12 us
    slice x1, local copies, waits for them, and re-layouts, body(): density[:, :ROW_TILE]  0.78 us
  transfers between devices with their start and end apart: 6, of which 1 were waited for; matrix products, arithmetic and copies ran while one was open for 3% of the time, Pallas kernels for 0%

profile of v1, /device:TPU:0, one launch (start us, length us, event | category | flops | bytes accessed | tf_op | source)
XLA Modules:
  0.0 36.7 jit_solution(1456721130909530731)
XLA Ops:
  0.0 0.8 %fusion = (f32[8,8,128]{2,1,0:T(8,128)S(1)}, f32[8,8,128]{2,1,0:T(8,128)S(1)}) fusion(f32[8,128,128]{2,1,0:T(8,128)} %own_ref.1), kind=kLoop, calls=%fused_computation.2 | loop fusion | bytes 131072 | tf_op jit(solution)/shard_map/slice | solution.py:232
  0.8 1.3 %collective-permute-start.3 = (f32[8,8,128]{2,1,0:T(8,128)S(1)}, f32[8,8,128]{2,1,0:T(8,128)S(1)}, u32[]{:S(2)}, u32[]{:S(2)}) collective-permute-start(f32[8,8,128]{2,1,0:T(8,128)S(1)} %get-tuple-element.5), channel_id=1, source_target_pairs={{1,0},{2,1},{3,2},{4,3},{5,4},{6,5},{7,6},{9,8},{10,9},{11,10},{12... | collective-permute-start | bytes 98312 | tf_op jit(solution)/shard_map/ppermute | solution.py:229
  2.1 0.0 copy-start
  2.1 5.6 %collective-permute-start.2 = (f32[8,8,128]{2,1,0:T(8,128)S(1)}, f32[8,8,128]{2,1,0:T(8,128)S(1)}, u32[]{:S(2)}, u32[]{:S(2)}) collective-permute-start(f32[8,8,128]{2,1,0:T(8,128)S(1)} %get-tuple-element.6), channel_id=1, source_target_pairs={{0,1},{1,2},{2,3},{3,4},{4,5},{5,6},{6,7},{8,9},{9,10},{10,11},{11... | collective-permute-start | bytes 98312 | tf_op jit(solution)/shard_map/ppermute | solution.py:229
  7.7 1.1 %fusion.1 = (f32[5,128,128]{2,1,0:T(8,128)S(1)}, f32[5,128,128]{2,1,0:T(8,128)S(1)}) fusion(f32[8,128,128]{2,1,0:T(8,128)} %own_ref.1), kind=kLoop, calls=%fused_computation.3 | loop fusion | bytes 1310720 | tf_op jit(solution)/shard_map/slice | solution.py:231
  8.8 1.3 %collective-permute-start.1 = (f32[5,128,128]{2,1,0:T(8,128)S(1)}, f32[5,128,128]{2,1,0:T(8,128)S(1)}, u32[]{:S(2)}, u32[]{:S(2)}) collective-permute-start(f32[5,128,128]{2,1,0:T(8,128)S(1)} %get-tuple-element.7), channel_id=1, source_target_pairs={{8,0},{16,8},{24,16},{9,1},{17,9},{25,17},{10,2},{18,10},{26,18},{... | collective-permute-start | bytes 983048 | tf_op jit(solution)/shard_map/ppermute | solution.py:229
  10.1 3.1 %collective-permute-start = (f32[5,128,128]{2,1,0:T(8,128)S(1)}, f32[5,128,128]{2,1,0:T(8,128)S(1)}, u32[]{:S(2)}, u32[]{:S(2)}) collective-permute-start(f32[5,128,128]{2,1,0:T(8,128)S(1)} %get-tuple-element.8), channel_id=1, source_target_pairs={{0,8},{8,16},{16,24},{1,9},{9,17},{17,25},{2,10},{10,18},{18,26},{... | collective-permute-start | bytes 983048 | tf_op jit(solution)/shard_map/ppermute | solution.py:229
  13.2 0.0 collective-permute-done.3.rhi_ref
  13.2 0.0 collective-permute-done.2.rlo_ref
  13.2 3.5 %collective-permute-start.4 = (f32[10,8,128]{2,1,0:T(8,128)S(1)}, f32[10,8,128]{2,1,0:T(8,128)S(1)}, u32[]{:S(2)}, u32[]{:S(2)}) collective-permute-start(f32[10,8,128]{2,1,0:T(8,128)S(1)} %pad_maximum_fusion), channel_id=1, source_target_pairs={{0,8},{8,16},{16,24},{1,9},{9,17},{17,25},{2,10},{10,18},{18,26},{... | collective-permute-start | bytes 122888 | tf_op jit(solution)/shard_map/ppermute | solution.py:229
  16.8 0.0 copy-start.1
  16.8 0.0 copy-start.2
  16.8 0.0 copy-start.4
  16.8 0.0 copy-start.5
  16.9 1.3 %collective-permute-start.5 = (f32[10,8,128]{2,1,0:T(8,128)S(1)}, f32[10,8,128]{2,1,0:T(8,128)S(1)}, u32[]{:S(2)}, u32[]{:S(2)}) collective-permute-start(f32[10,8,128]{2,1,0:T(8,128)S(1)} %pad_maximum_fusion.1), channel_id=1, source_target_pairs={{8,0},{16,8},{24,16},{9,1},{17,9},{25,17},{10,2},{18,10},{26,18},{... | collective-permute-start | bytes 122888 | tf_op jit(solution)/shard_map/ppermute | solution.py:229
  18.2 0.0 collective-permute-done.4.clo_ref
  18.2 1.8 %collective-permute-done.5.chi_ref = f32[10,8,128]{2,1,0:T(8,128)S(1)} collective-permute-done((f32[10,8,128]{2,1,0:T(8,128)S(1)}, f32[10,8,128]{2,1,0:T(8,128)S(1)}, u32[]{:S(2)}, u32[]{:S(2)}) %collective-permute-start.5) | collective-permute-done | bytes 40992 | tf_op jit(solution)/shard_map/ppermute | solution.py:229
  20.0 0.0 collective-permute-done.1.dhi_ref
  20.0 0.0 collective-permute-done.dlo_ref
  20.0 0.0 copy-done
  20.0 2.8 %render.1 = f32[4,2,4,32,128]{4,3,2,1,0:T(8,128)S(1)} custom-call(s32[4,8]{1,0:T(4,128)S(1)} %copy-done.1, f32[2]{0:T(128)S(1)} %copy-done.4, f32[3]{0:T(128)S(1)} %copy-done.5, s32[2,4]{1,0:T(2,128)S(1)} %copy-done.2, f32[8,128,128]{2,1,0:T(8,128)S(1)} %copy-done, f32[5,128,128]{2,1,0:T(8,128)S(1)} %collective-permute-done.dlo_ref, ...), custom_call_target="tpu_custom_call" | custom-call | tf_op jit(solution)/shard_map/render/pallas_call | solution.py:239
  22.9 0.0 copy-start.3
  22.9 12.6 %all_to_all.5.in_ref = f32[4,2,4,32,128]{4,3,2,1,0:T(8,128)S(1)} all-to-all(f32[4,2,4,32,128]{4,3,2,1,0:T(8,128)S(1)} %render.1), channel_id=1, replica_groups=mesh['gz'=4,'xy'=8] {'gz'}, dimensions={0} | all-to-all | bytes 1048576 | tf_op jit(solution)/shard_map/all_to_all | solution.py:243
  35.5 1.2 %composite.1 = f32[2,4,1,32,128]{4,3,2,1,0:T(8,128)} custom-call(s32[2,4]{1,0:T(2,128)S(1)} %copy-done.3, f32[4,2,4,32,128]{4,3,2,1,0:T(8,128)S(1)} %all_to_all.5.in_ref), custom_call_target="tpu_custom_call" | custom-call | tf_op jit(solution)/shard_map/composite/pallas_call | solution.py:245
  (9 shorter events, 0.0 us)
Async XLA Ops:
  0.8 12.4 %collective-permute-start.3 = (f32[8,8,128]{2,1,0:T(8,128)S(1)}, f32[8,8,128]{2,1,0:T(8,128)S(1)}, u32[]{:S(2)}, u32[]{:S(2)}) collective-permute-start(f32[8,8,128]{2,1,0:T(8,128)S(1)} %get-tuple-element.5), channel_id=1, source_target_pairs={{1,0},{2,1},{3,2},{4,3},{5,4},{6,5},{7,6},{9,8},{10,9},{11,10},{12... | collective-permute-start | bytes 98312 | tf_op jit(solution)/shard_map/ppermute | solution.py:229
  2.1 17.9 %copy-start = (f32[8,128,128]{2,1,0:T(8,128)S(1)}, f32[8,128,128]{2,1,0:T(8,128)}, u32[]{:S(2)}) copy-start(f32[8,128,128]{2,1,0:T(8,128)} %own_ref.1) | copy-start | bytes 1572868
  2.1 11.1 %collective-permute-start.2 = (f32[8,8,128]{2,1,0:T(8,128)S(1)}, f32[8,8,128]{2,1,0:T(8,128)S(1)}, u32[]{:S(2)}, u32[]{:S(2)}) collective-permute-start(f32[8,8,128]{2,1,0:T(8,128)S(1)} %get-tuple-element.6), channel_id=1, source_target_pairs={{0,1},{1,2},{2,3},{3,4},{4,5},{5,6},{6,7},{8,9},{9,10},{10,11},{11... | collective-permute-start | bytes 98312 | tf_op jit(solution)/shard_map/ppermute | solution.py:229
  8.8 11.2 %collective-permute-start.1 = (f32[5,128,128]{2,1,0:T(8,128)S(1)}, f32[5,128,128]{2,1,0:T(8,128)S(1)}, u32[]{:S(2)}, u32[]{:S(2)}) collective-permute-start(f32[5,128,128]{2,1,0:T(8,128)S(1)} %get-tuple-element.7), channel_id=1, source_target_pairs={{8,0},{16,8},{24,16},{9,1},{17,9},{25,17},{10,2},{18,10},{26,18},{... | collective-permute-start | bytes 983048 | tf_op jit(solution)/shard_map/ppermute | solution.py:229
  10.1 9.9 %collective-permute-start = (f32[5,128,128]{2,1,0:T(8,128)S(1)}, f32[5,128,128]{2,1,0:T(8,128)S(1)}, u32[]{:S(2)}, u32[]{:S(2)}) collective-permute-start(f32[5,128,128]{2,1,0:T(8,128)S(1)} %get-tuple-element.8), channel_id=1, source_target_pairs={{0,8},{8,16},{16,24},{1,9},{9,17},{17,25},{2,10},{10,18},{18,26},{... | collective-permute-start | bytes 983048 | tf_op jit(solution)/shard_map/ppermute | solution.py:229
  13.2 4.9 %collective-permute-start.4 = (f32[10,8,128]{2,1,0:T(8,128)S(1)}, f32[10,8,128]{2,1,0:T(8,128)S(1)}, u32[]{:S(2)}, u32[]{:S(2)}) collective-permute-start(f32[10,8,128]{2,1,0:T(8,128)S(1)} %pad_maximum_fusion), channel_id=1, source_target_pairs={{0,8},{8,16},{16,24},{1,9},{9,17},{17,25},{2,10},{10,18},{18,26},{... | collective-permute-start | bytes 122888 | tf_op jit(solution)/shard_map/ppermute | solution.py:229
  16.8 3.2 %copy-start.1 = (s32[4,8]{1,0:T(4,128)S(1)}, s32[4,8]{1,0:T(4,128)}, u32[]{:S(2)}) copy-start(s32[4,8]{1,0:T(4,128)} %live_ref.1) | copy-start | bytes 388
  16.8 3.2 %copy-start.2 = (s32[2,4]{1,0:T(2,128)S(1)}, s32[2,4]{1,0:T(2,128)}, u32[]{:S(2)}) copy-start(s32[2,4]{1,0:T(2,128)} %owner_ref.1) | copy-start | bytes 100
  16.8 3.2 %copy-start.4 = (f32[2]{0:T(128)S(1)}, f32[2]{0:T(128)}, u32[]{:S(2)}) copy-start(f32[2]{0:T(128)} %slopes_ref.1) | copy-start | bytes 28
  16.8 3.2 %copy-start.5 = (f32[3]{0:T(128)S(1)}, f32[3]{0:T(128)}, u32[]{:S(2)}) copy-start(f32[3]{0:T(128)} %palette_ref.1) | copy-start | bytes 40
  16.9 3.1 %collective-permute-start.5 = (f32[10,8,128]{2,1,0:T(8,128)S(1)}, f32[10,8,128]{2,1,0:T(8,128)S(1)}, u32[]{:S(2)}, u32[]{:S(2)}) collective-permute-start(f32[10,8,128]{2,1,0:T(8,128)S(1)} %pad_maximum_fusion.1), channel_id=1, source_target_pairs={{8,0},{16,8},{24,16},{9,1},{17,9},{25,17},{10,2},{18,10},{26,18},{... | collective-permute-start | bytes 122888 | tf_op jit(solution)/shard_map/ppermute | solution.py:229
  22.9 12.6 %copy-start.3 = (s32[2,4]{1,0:T(2,128)S(1)}, s32[2,4]{1,0:T(2,128)}, u32[]{:S(2)}) copy-start(s32[2,4]{1,0:T(2,128)} %order_ref.1) | copy-start | bytes 100

commit v2 on v1

--- a/solution.py
+++ b/solution.py
@@ -56,7 +56,7 @@
 
     def kernel(
         live_ref, slopes_ref, palette_ref, owner_ref,
-        own_ref, dlo_ref, dhi_ref, rlo_ref, rhi_ref, clo_ref, chi_ref,
+        own_ref, dlo_ref, dhi_ref, rlo_ref, rhi_ref,
         out_ref,
         deep, triple, smooth, across, sheared,
     ):
@@ -64,21 +64,18 @@
         row_index = lax.axis_index("xy")
 
         for chunk in range(padded_rows // ROW_TILE):
+            rows = pl.ds(chunk * ROW_TILE, ROW_TILE)
+            low = [dlo_ref[i, rows] for i in range(HALO)]
+            high = [dhi_ref[i, rows] for i in range(HALO)]
             if chunk == 0:
-                low = [clo_ref[i] for i in range(HALO)]
                 mid = [rlo_ref[i] for i in range(depth_cells)]
-                high = [chi_ref[i] for i in range(HALO)]
             elif chunk == padded_rows // ROW_TILE - 1:
-                low = [clo_ref[HALO + i] for i in range(HALO)]
                 mid = [rhi_ref[i] for i in range(depth_cells)]
-                high = [chi_ref[HALO + i] for i in range(HALO)]
             else:
-                rows = pl.ds((chunk - 1) * ROW_TILE, ROW_TILE)
-                low = [dlo_ref[i, rows] for i in range(HALO)]
-                mid = [own_ref[i, rows] for i in range(depth_cells)]
-                high = [dhi_ref[i, rows] for i in range(HALO)]
+                inner = pl.ds((chunk - 1) * ROW_TILE, ROW_TILE)
+                mid = [own_ref[i, inner] for i in range(depth_cells)]
             for z, total in enumerate(window_sums(low + mid + high, TAPS)):
-                deep[z, pl.ds(chunk * ROW_TILE, ROW_TILE)] = total
+                deep[z, rows] = total
 
         band = column_matrix(columns)
         weights = jnp.concatenate([band, band, band], axis=0)
@@ -186,7 +183,7 @@
     return pl.pallas_call(
         kernel,
         out_shape=jax.ShapeDtypeStruct((n_depth, VIEWS, 4, tile_rows, columns), jnp.float32),
-        in_specs=[smem] * 4 + [vmem] * 7,
+        in_specs=[smem] * 4 + [vmem] * 5,
         out_specs=vmem,
         scratch_shapes=[
             pltpu.VMEM((depth_cells + 2, padded_rows, columns), jnp.float32),
@@ -228,17 +225,17 @@
         backward = [(target, source) for source, target in forward]
         return lax.ppermute(to_next, axis, forward), lax.ppermute(to_previous, axis, backward)
 
-    dlo, dhi = both_ways("gz", density[depth_cells - HALO :], density[:HALO])
     rlo, rhi = both_ways("xy", density[:, row_cells - ROW_TILE :], density[:, :ROW_TILE])
-    clo, chi = both_ways(
+    edge = depth_cells - HALO
+    dlo, dhi = both_ways(
         "gz",
-        jnp.concatenate([rlo[depth_cells - HALO :], rhi[depth_cells - HALO :]], axis=0),
-        jnp.concatenate([rlo[:HALO], rhi[:HALO]], axis=0),
+        jnp.concatenate([rlo[edge:], density[edge:], rhi[edge:]], axis=1),
+        jnp.concatenate([rlo[:HALO], density[:HALO], rhi[:HALO]], axis=1),
     )
     render = make_render(n_depth, n_rows, depth_cells, row_cells, columns)
     outgoing = render(
         live_slices, shear_slopes, palette, tile_owner,
-        density, dlo, dhi, rlo, rhi, clo, chi,
+        density, dlo, dhi, rlo, rhi,
     )
     incoming = lax.all_to_all(outgoing, "gz", split_axis=0, concat_axis=0, tiled=True)
     tile_rows = row_cells // n_depth

time: 37.1 us -> 38.4 us (1.035)
  starting transfers between devices: 16.1 us -> 8.86 us
  waiting for transfers between devices: 1.83 us -> 7.37 us
  blocking collectives: 12.6 us -> 15.7 us
    ppermute x3 -> x2, starting transfers between devices: 12.2 us -> 6.28 us  [both_ways(): lax.ppermute(to_next, axis, forward)]
    ppermute x3 -> x2, waiting for transfers between devices: 1.83 us -> 7.36 us  [both_ways(): lax.ppermute(to_previous, axis, backward)]
    all_to_all x1, blocking collectives: 12.6 us -> 15.7 us  [body(): lax.all_to_all(outgoing, 'gz', split_axis=0, concat_axis=0, tiled=True)]
    ppermute x3 -> x2, starting transfers between devices: 3.86 us -> 2.58 us  [both_ways(): lax.ppermute(to_previous, axis, backward)]
  transfers between devices with their start and end apart: 6 -> 4, of which waited for: 1 -> 2; matrix products, arithmetic and copies ran while one was open for 3% -> 3% of each run, Pallas kernels for 0% -> 0%
where the time goes in v2:
time: 38.4 us; the launch traced here: 38.1 us
  blocking collectives  15.7 us (41%)
  starting transfers between devices  8.86 us (23%)
  waiting for transfers between devices  7.37 us (19%)
  Pallas kernels  4.05 us (11%)
  local copies, waits for them, and re-layouts  1.94 us (5%)
    all_to_all x1, blocking collectives, body(): lax.all_to_all(outgoing, 'gz', split_axis=0, concat_axis=0, tiled=True)  15.7 us
    ppermute x2, waiting for transfers between devices, both_ways(): lax.ppermute(to_previous, axis, backward)  7.36 us
    ppermute x2, starting transfers between devices, both_ways(): lax.ppermute(to_next, axis, forward)  6.28 us
    pallas_call x1, Pallas kernels, body(): render(live_slices, shear_slopes, palette, tile_owner, density, dlo, dhi,...  2.81 us
    ppermute x2, starting transfers between devices, both_ways(): lax.ppermute(to_previous, axis, backward)  2.58 us
    pallas_call x1, Pallas kernels, body(): pl.pallas_call(composite_kernel, out_shape=jax.ShapeDtypeStruct((VIEWS, 4...  1.24 us
    slice x1, local copies, waits for them, and re-layouts, body(): density[:HALO]  1.12 us
    slice x1, local copies, waits for them, and re-layouts, body(): density[:, row_cells - ROW_TILE:]  0.78 us
  transfers between devices with their start and end apart: 4, of which 2 were waited for; matrix products, arithmetic and copies ran while one was open for 3% of the time, Pallas kernels for 0%

profile of v2, /device:TPU:0, one launch (start us, length us, event | category | flops | bytes accessed | tf_op | source)
XLA Modules:
  0.0 38.1 jit_solution(10762592617952421608)
XLA Ops:
  0.0 0.8 %fusion.1 = (f32[8,8,128]{2,1,0:T(8,128)S(1)}, f32[8,8,128]{2,1,0:T(8,128)S(1)}) fusion(f32[8,128,128]{2,1,0:T(8,128)} %own_ref.1), kind=kLoop, calls=%fused_computation.3 | loop fusion | bytes 131072 | tf_op jit(solution)/shard_map/slice | solution.py:228
  0.8 4.8 %collective-permute-start = (f32[8,8,128]{2,1,0:T(8,128)S(1)}, f32[8,8,128]{2,1,0:T(8,128)S(1)}, u32[]{:S(2)}, u32[]{:S(2)}) collective-permute-start(f32[8,8,128]{2,1,0:T(8,128)S(1)} %get-tuple-element.7), channel_id=1, source_target_pairs={{0,1},{1,2},{2,3},{3,4},{4,5},{5,6},{6,7},{8,9},{9,10},{10,11},{11... | collective-permute-start | bytes 98312 | tf_op jit(solution)/shard_map/ppermute | solution.py:226
  5.6 1.3 %collective-permute-start.1 = (f32[8,8,128]{2,1,0:T(8,128)S(1)}, f32[8,8,128]{2,1,0:T(8,128)S(1)}, u32[]{:S(2)}, u32[]{:S(2)}) collective-permute-start(f32[8,8,128]{2,1,0:T(8,128)S(1)} %get-tuple-element.8), channel_id=1, source_target_pairs={{1,0},{2,1},{3,2},{4,3},{5,4},{6,5},{7,6},{9,8},{10,9},{11,10},{12... | collective-permute-start | bytes 98312 | tf_op jit(solution)/shard_map/ppermute | solution.py:226
  6.9 1.1 %fusion = (f32[5,128,128]{2,1,0:T(8,128)S(1)}, f32[5,128,128]{2,1,0:T(8,128)S(1)}) fusion(f32[8,128,128]{2,1,0:T(8,128)} %own_ref.1), kind=kLoop, calls=%fused_computation.2 | loop fusion | bytes 1310720 | tf_op jit(solution)/shard_map/slice | solution.py:233
  8.0 0.0 collective-permute-done.rlo_ref
  8.1 3.4 %collective-permute-done.1.rhi_ref = f32[8,8,128]{2,1,0:T(8,128)S(1)} collective-permute-done((f32[8,8,128]{2,1,0:T(8,128)S(1)}, f32[8,8,128]{2,1,0:T(8,128)S(1)}, u32[]{:S(2)}, u32[]{:S(2)}) %collective-permute-start.1) | collective-permute-done | bytes 32800 | tf_op jit(solution)/shard_map/ppermute | solution.py:226
  11.5 0.0 copy-start
  11.5 1.4 %collective-permute-start.2 = (f32[5,144,128]{2,1,0:T(8,128)S(1)}, f32[5,144,128]{2,1,0:T(8,128)S(1)}, u32[]{:S(2)}, u32[]{:S(2)}) collective-permute-start(f32[5,144,128]{2,1,0:T(8,128)S(1)} %pad_maximum_fusion), channel_id=1, source_target_pairs={{0,8},{8,16},{16,24},{1,9},{9,17},{17,25},{2,10},{10,18},{18,26},{... | collective-permute-start | bytes 1105928 | tf_op jit(solution)/shard_map/ppermute | solution.py:226
  12.9 0.0 copy-start.1
  12.9 0.0 copy-start.2
  13.0 0.0 copy-start.4
  13.0 0.0 copy-start.5
  13.0 1.3 %collective-permute-start.3 = (f32[5,144,128]{2,1,0:T(8,128)S(1)}, f32[5,144,128]{2,1,0:T(8,128)S(1)}, u32[]{:S(2)}, u32[]{:S(2)}) collective-permute-start(f32[5,144,128]{2,1,0:T(8,128)S(1)} %pad_maximum_fusion.1), channel_id=1, source_target_pairs={{8,0},{16,8},{24,16},{9,1},{17,9},{25,17},{10,2},{18,10},{26,18},{... | collective-permute-start | bytes 1105928 | tf_op jit(solution)/shard_map/ppermute | solution.py:226
  14.3 0.0 collective-permute-done.2.dlo_ref
  14.3 4.0 %collective-permute-done.3.dhi_ref = f32[5,144,128]{2,1,0:T(8,128)S(1)} collective-permute-done((f32[5,144,128]{2,1,0:T(8,128)S(1)}, f32[5,144,128]{2,1,0:T(8,128)S(1)}, u32[]{:S(2)}, u32[]{:S(2)}) %collective-permute-start.3) | collective-permute-done | bytes 368672 | tf_op jit(solution)/shard_map/ppermute | solution.py:226
  18.3 0.0 copy-done
  18.3 0.0 copy-done.1
  18.3 0.0 copy-done.2
  18.3 0.0 copy-done.4
  18.3 0.0 copy-done.5
  18.4 2.8 %render.1 = f32[4,2,4,32,128]{4,3,2,1,0:T(8,128)S(1)} custom-call(s32[4,8]{1,0:T(4,128)S(1)} %copy-done.1, f32[2]{0:T(128)S(1)} %copy-done.4, f32[3]{0:T(128)S(1)} %copy-done.5, s32[2,4]{1,0:T(2,128)S(1)} %copy-done.2, f32[8,128,128]{2,1,0:T(8,128)S(1)} %copy-done, f32[5,144,128]{2,1,0:T(8,128)S(1)} %collective-permute-done.2.dlo_ref, ...), custom_call_target="tpu_custom_call" | custom-call | tf_op jit(solution)/shard_map/render/pallas_call | solution.py:236
  21.2 0.0 copy-start.3
  21.2 15.7 %all_to_all.5.in_ref = f32[4,2,4,32,128]{4,3,2,1,0:T(8,128)S(1)} all-to-all(f32[4,2,4,32,128]{4,3,2,1,0:T(8,128)S(1)} %render.1), channel_id=1, replica_groups=mesh['gz'=4,'xy'=8] {'gz'}, dimensions={0} | all-to-all | bytes 1048576 | tf_op jit(solution)/shard_map/all_to_all | solution.py:240
  36.9 1.2 %composite.1 = f32[2,4,1,32,128]{4,3,2,1,0:T(8,128)} custom-call(s32[2,4]{1,0:T(2,128)S(1)} %copy-done.3, f32[4,2,4,32,128]{4,3,2,1,0:T(8,128)S(1)} %all_to_all.5.in_ref), custom_call_target="tpu_custom_call" | custom-call | tf_op jit(solution)/shard_map/composite/pallas_call | solution.py:242
  (5 shorter events, 0.1 us)
Async XLA Ops:
  0.8 7.3 %collective-permute-start = (f32[8,8,128]{2,1,0:T(8,128)S(1)}, f32[8,8,128]{2,1,0:T(8,128)S(1)}, u32[]{:S(2)}, u32[]{:S(2)}) collective-permute-start(f32[8,8,128]{2,1,0:T(8,128)S(1)} %get-tuple-element.7), channel_id=1, source_target_pairs={{0,1},{1,2},{2,3},{3,4},{4,5},{5,6},{6,7},{8,9},{9,10},{10,11},{11... | collective-permute-start | bytes 98312 | tf_op jit(solution)/shard_map/ppermute | solution.py:226
  5.6 5.8 %collective-permute-start.1 = (f32[8,8,128]{2,1,0:T(8,128)S(1)}, f32[8,8,128]{2,1,0:T(8,128)S(1)}, u32[]{:S(2)}, u32[]{:S(2)}) collective-permute-start(f32[8,8,128]{2,1,0:T(8,128)S(1)} %get-tuple-element.8), channel_id=1, source_target_pairs={{1,0},{2,1},{3,2},{4,3},{5,4},{6,5},{7,6},{9,8},{10,9},{11,10},{12... | collective-permute-start | bytes 98312 | tf_op jit(solution)/shard_map/ppermute | solution.py:226
  11.5 6.9 %copy-start = (f32[8,128,128]{2,1,0:T(8,128)S(1)}, f32[8,128,128]{2,1,0:T(8,128)}, u32[]{:S(2)}) copy-start(f32[8,128,128]{2,1,0:T(8,128)} %own_ref.1) | copy-start | bytes 1572868
  11.5 2.8 %collective-permute-start.2 = (f32[5,144,128]{2,1,0:T(8,128)S(1)}, f32[5,144,128]{2,1,0:T(8,128)S(1)}, u32[]{:S(2)}, u32[]{:S(2)}) collective-permute-start(f32[5,144,128]{2,1,0:T(8,128)S(1)} %pad_maximum_fusion), channel_id=1, source_target_pairs={{0,8},{8,16},{16,24},{1,9},{9,17},{17,25},{2,10},{10,18},{18,26},{... | collective-permute-start | bytes 1105928 | tf_op jit(solution)/shard_map/ppermute | solution.py:226
  12.9 5.4 %copy-start.1 = (s32[4,8]{1,0:T(4,128)S(1)}, s32[4,8]{1,0:T(4,128)}, u32[]{:S(2)}) copy-start(s32[4,8]{1,0:T(4,128)} %live_ref.1) | copy-start | bytes 388
  12.9 5.4 %copy-start.2 = (s32[2,4]{1,0:T(2,128)S(1)}, s32[2,4]{1,0:T(2,128)}, u32[]{:S(2)}) copy-start(s32[2,4]{1,0:T(2,128)} %owner_ref.1) | copy-start | bytes 100
  13.0 5.4 %copy-start.4 = (f32[2]{0:T(128)S(1)}, f32[2]{0:T(128)}, u32[]{:S(2)}) copy-start(f32[2]{0:T(128)} %slopes_ref.1) | copy-start | bytes 28
  13.0 5.4 %copy-start.5 = (f32[3]{0:T(128)S(1)}, f32[3]{0:T(128)}, u32[]{:S(2)}) copy-start(f32[3]{0:T(128)} %palette_ref.1) | copy-start | bytes 40
  13.0 5.3 %collective-permute-start.3 = (f32[5,144,128]{2,1,0:T(8,128)S(1)}, f32[5,144,128]{2,1,0:T(8,128)S(1)}, u32[]{:S(2)}, u32[]{:S(2)}) collective-permute-start(f32[5,144,128]{2,1,0:T(8,128)S(1)} %pad_maximum_fusion.1), channel_id=1, source_target_pairs={{8,0},{16,8},{24,16},{9,1},{17,9},{25,17},{10,2},{18,10},{26,18},{... | collective-permute-start | bytes 1105928 | tf_op jit(solution)/shard_map/ppermute | solution.py:226
  21.2 15.7 %copy-start.3 = (s32[2,4]{1,0:T(2,128)S(1)}, s32[2,4]{1,0:T(2,128)}, u32[]{:S(2)}) copy-start(s32[2,4]{1,0:T(2,128)} %order_ref.1) | copy-start | bytes 100

commit v3 on v1

--- a/solution.py
+++ b/solution.py
@@ -10,7 +10,11 @@
 HALO = REACH + 1
 TAPS = 2 * REACH + 1
 ROW_TILE = 8
+PACKED_ROWS = 16
 VIEWS = 2
+TOP = 2.2
+STEPS = 65535.0
+MIDDLE = 32768
 VMEM_BYTES = 40 * 1024 * 1024
 
 
@@ -45,12 +49,26 @@
     return [sums[i] + layers[i + width] for i in range(len(layers) - width)]
 
 
+def encode(value):
+    root = jnp.exp(0.125 * jnp.log(jnp.maximum(value, 1e-30) * (1.0 / TOP)))
+    level = jnp.minimum(root * STEPS + 0.5, STEPS)
+    return (level.astype(jnp.int32) - MIDDLE).astype(jnp.int16)
+
+
+def decode(code):
+    root = (code.astype(jnp.int32) + MIDDLE).astype(jnp.float32) * (TOP**0.125 / STEPS)
+    square = root * root
+    fourth = square * square
+    return fourth * fourth
+
+
 def make_render(n_depth, n_rows, depth_cells, row_cells, columns):
     total_depth = depth_cells * n_depth
     extinct = 3.0 / total_depth
     padded_rows = row_cells + 2 * ROW_TILE
     first, last = ROW_TILE, ROW_TILE + row_cells
     tile_rows = row_cells // n_depth
+    step_rows = min(tile_rows, PACKED_ROWS)
     cells = TAPS**3
     floor = 0.01 * (2.0 * cells) ** 2
 
@@ -157,35 +175,42 @@
             matrix = shear_matrices(slopes_ref, slab_start + float(z), columns, total_depth)
             sheared[z] = jnp.dot(rgba, matrix, preferred_element_type=jnp.float32)
 
-        for chunk in range(row_cells // ROW_TILE):
-            tile = chunk * ROW_TILE // tile_rows
-            inside = chunk * ROW_TILE - tile * tile_rows
-            for view in range(VIEWS):
-                lanes = pl.ds(view * columns, columns)
-                colour, transmit = None, None
-                for z in range(depth_cells):
-                    part = [
-                        sheared[z, pl.ds(c * row_cells + chunk * ROW_TILE, ROW_TILE), lanes]
-                        for c in range(4)
-                    ]
-                    clear = 1.0 - part[3]
-                    if z == 0:
-                        colour, transmit = part[:3], clear
-                    elif view == 0:
-                        colour = [colour[c] + transmit * part[c] for c in range(3)]
-                        transmit = transmit * clear
-                    else:
-                        colour = [part[c] + clear * colour[c] for c in range(3)]
-                        transmit = transmit * clear
-                place = owner_ref[view, tile]
-                for c, value in enumerate(colour + [1.0 - transmit]):
-                    out_ref[place, view, c, pl.ds(inside, ROW_TILE)] = value
+        for tile in range(n_depth):
+            place = [owner_ref[view, tile] for view in range(VIEWS)]
+            for inside in range(0, tile_rows, step_rows):
+                for view in range(VIEWS):
+                    lanes = pl.ds(view * columns, columns)
+                    colour, transmit = None, None
+                    for z in range(depth_cells):
+                        part = [
+                            sheared[
+                                z,
+                                pl.ds(c * row_cells + tile * tile_rows + inside, step_rows),
+                                lanes,
+                            ]
+                            for c in range(4)
+                        ]
+                        clear = 1.0 - part[3]
+                        if z == 0:
+                            colour, transmit = part[:3], clear
+                        elif view == 0:
+                            colour = [colour[c] + transmit * part[c] for c in range(3)]
+                            transmit = transmit * clear
+                        else:
+                            colour = [part[c] + clear * colour[c] for c in range(3)]
+                            transmit = transmit * clear
+                    values = colour + [1.0 - transmit]
+                    share = PACKED_ROWS // step_rows
+                    for c in range(0, 4, share):
+                        value = values[c] if share == 1 else jnp.concatenate(values[c : c + share])
+                        rows = pl.ds(c * tile_rows + inside, PACKED_ROWS)
+                        out_ref[place[view], view, rows] = encode(value)
 
     smem = pl.BlockSpec(memory_space=pltpu.SMEM)
     vmem = pl.BlockSpec(memory_space=pltpu.VMEM)
     return pl.pallas_call(
         kernel,
-        out_shape=jax.ShapeDtypeStruct((n_depth, VIEWS, 4, tile_rows, columns), jnp.float32),
+        out_shape=jax.ShapeDtypeStruct((n_depth, VIEWS, 4 * tile_rows, columns), jnp.int16),
         in_specs=[smem] * 4 + [vmem] * 7,
         out_specs=vmem,
         scratch_shapes=[
@@ -202,11 +227,13 @@
 
 def composite_kernel(order_ref, in_ref, out_ref):
     count = in_ref.shape[0]
+    rows = in_ref.shape[2] // 4
     for view in range(VIEWS):
         colour, transmit = None, None
         for k in range(count):
             source = order_ref[view, k]
-            part = [in_ref[source, view, c] for c in range(4)]
+            values = decode(in_ref[source, view])
+            part = [values[c * rows : (c + 1) * rows] for c in range(4)]
             clear = 1.0 - part[3]
             if k == 0:
                 colour, transmit = part[:3], clear

time: 37.1 us -> 38.5 us (1.038)
  the two profiles are of different devices: /device:TPU:0 before, /device:TPU:16 now
where the time goes in v3:
time: 38.5 us; the launch traced here: 38.2 us
  starting transfers between devices  13.5 us (35%)
  blocking collectives  9.81 us (25%)
  waiting for transfers between devices  8.32 us (22%)
  Pallas kernels  4.42 us (11%)
  local copies, waits for them, and re-layouts  1.94 us (5%)
    all_to_all x1, blocking collectives, body(): lax.all_to_all(outgoing, 'gz', split_axis=0, concat_axis=0, tiled=True)  9.81 us
    ppermute x3, starting transfers between devices, both_ways(): lax.ppermute(to_next, axis, forward)  7.49 us
    ppermute x3, starting transfers between devices, both_ways(): lax.ppermute(to_previous, axis, backward)  5.99 us
    ppermute x3, waiting for transfers between devices, both_ways(): lax.ppermute(to_previous, axis, backward)  4.2 us
    ppermute x3, waiting for transfers between devices, both_ways(): lax.ppermute(to_next, axis, forward)  4.12 us
    pallas_call x1, Pallas kernels, body(): render(live_slices, shear_slopes, palette, tile_owner, density, dlo, dhi,...  3.07 us
    pallas_call x1, Pallas kernels, body(): pl.pallas_call(composite_kernel, out_shape=jax.ShapeDtypeStruct((VIEWS, 4...  1.36 us
    slice x1, local copies, waits for them, and re-layouts, body(): dlo, dhi = both_ways('gz', density[depth_cells - HALO:], density[:HALO])  1.12 us
  transfers between devices with their start and end apart: 6, of which 2 were waited for; matrix products, arithmetic and copies ran while one was open for 3% of the time, Pallas kernels for 0%

profile of v3, /device:TPU:16, one launch (start us, length us, event | category | flops | bytes accessed | tf_op | source)
XLA Modules:
  0.0 38.2 jit_solution(1118461345621483611)
XLA Ops:
  0.0 0.8 %fusion = (f32[8,8,128]{2,1,0:T(8,128)S(1)}, f32[8,8,128]{2,1,0:T(8,128)S(1)}) fusion(f32[8,128,128]{2,1,0:T(8,128)} %own_ref.1), kind=kLoop, calls=%fused_computation.2 | loop fusion | bytes 131072 | tf_op jit(solution)/shard_map/slice | solution.py:259
  0.8 3.4 %collective-permute-start.3 = (f32[8,8,128]{2,1,0:T(8,128)S(1)}, f32[8,8,128]{2,1,0:T(8,128)S(1)}, u32[]{:S(2)}, u32[]{:S(2)}) collective-permute-start(f32[8,8,128]{2,1,0:T(8,128)S(1)} %get-tuple-element.5), channel_id=1, source_target_pairs={{1,0},{2,1},{3,2},{4,3},{5,4},{6,5},{7,6},{9,8},{10,9},{11,10},{12... | collective-permute-start | bytes 98312 | tf_op jit(solution)/shard_map/ppermute | solution.py:256
  4.2 1.1 %fusion.1 = (f32[5,128,128]{2,1,0:T(8,128)S(1)}, f32[5,128,128]{2,1,0:T(8,128)S(1)}) fusion(f32[8,128,128]{2,1,0:T(8,128)} %own_ref.1), kind=kLoop, calls=%fused_computation.3 | loop fusion | bytes 1310720 | tf_op jit(solution)/shard_map/slice | solution.py:258
  5.3 1.5 %collective-permute-start = (f32[5,128,128]{2,1,0:T(8,128)S(1)}, f32[5,128,128]{2,1,0:T(8,128)S(1)}, u32[]{:S(2)}, u32[]{:S(2)}) collective-permute-start(f32[5,128,128]{2,1,0:T(8,128)S(1)} %get-tuple-element.8), channel_id=1, source_target_pairs={{0,8},{8,16},{16,24},{1,9},{9,17},{17,25},{2,10},{10,18},{18,26},{... | collective-permute-start | bytes 983048 | tf_op jit(solution)/shard_map/ppermute | solution.py:256
  6.8 1.3 %collective-permute-start.1 = (f32[5,128,128]{2,1,0:T(8,128)S(1)}, f32[5,128,128]{2,1,0:T(8,128)S(1)}, u32[]{:S(2)}, u32[]{:S(2)}) collective-permute-start(f32[5,128,128]{2,1,0:T(8,128)S(1)} %get-tuple-element.7), channel_id=1, source_target_pairs={{8,0},{16,8},{24,16},{9,1},{17,9},{25,17},{10,2},{18,10},{26,18},{... | collective-permute-start | bytes 983048 | tf_op jit(solution)/shard_map/ppermute | solution.py:256
  8.1 2.6 %collective-permute-start.2 = (f32[8,8,128]{2,1,0:T(8,128)S(1)}, f32[8,8,128]{2,1,0:T(8,128)S(1)}, u32[]{:S(2)}, u32[]{:S(2)}) collective-permute-start(f32[8,8,128]{2,1,0:T(8,128)S(1)} %get-tuple-element.6), channel_id=1, source_target_pairs={{0,1},{1,2},{2,3},{3,4},{4,5},{5,6},{6,7},{8,9},{9,10},{10,11},{11... | collective-permute-start | bytes 98312 | tf_op jit(solution)/shard_map/ppermute | solution.py:256
  10.7 0.0 collective-permute-done.3.rhi_ref
  10.7 4.1 %collective-permute-done.2.rlo_ref = f32[8,8,128]{2,1,0:T(8,128)S(1)} collective-permute-done((f32[8,8,128]{2,1,0:T(8,128)S(1)}, f32[8,8,128]{2,1,0:T(8,128)S(1)}, u32[]{:S(2)}, u32[]{:S(2)}) %collective-permute-start.2) | collective-permute-done | bytes 32800 | tf_op jit(solution)/shard_map/ppermute | solution.py:256
  14.8 3.4 %collective-permute-start.4 = (f32[10,8,128]{2,1,0:T(8,128)S(1)}, f32[10,8,128]{2,1,0:T(8,128)S(1)}, u32[]{:S(2)}, u32[]{:S(2)}) collective-permute-start(f32[10,8,128]{2,1,0:T(8,128)S(1)} %pad_maximum_fusion), channel_id=1, source_target_pairs={{0,8},{8,16},{16,24},{1,9},{9,17},{17,25},{2,10},{10,18},{18,26},{... | collective-permute-start | bytes 122888 | tf_op jit(solution)/shard_map/ppermute | solution.py:256
  18.3 0.0 copy-start.1
  18.3 0.0 copy-start.2
  18.3 0.0 copy-start.4
  18.3 0.0 copy-start.5
  18.4 1.3 %collective-permute-start.5 = (f32[10,8,128]{2,1,0:T(8,128)S(1)}, f32[10,8,128]{2,1,0:T(8,128)S(1)}, u32[]{:S(2)}, u32[]{:S(2)}) collective-permute-start(f32[10,8,128]{2,1,0:T(8,128)S(1)} %pad_maximum_fusion.1), channel_id=1, source_target_pairs={{8,0},{16,8},{24,16},{9,1},{17,9},{25,17},{10,2},{18,10},{26,18},{... | collective-permute-start | bytes 122888 | tf_op jit(solution)/shard_map/ppermute | solution.py:256
  19.6 0.0 collective-permute-done.4.clo_ref
  19.7 4.2 %collective-permute-done.5.chi_ref = f32[10,8,128]{2,1,0:T(8,128)S(1)} collective-permute-done((f32[10,8,128]{2,1,0:T(8,128)S(1)}, f32[10,8,128]{2,1,0:T(8,128)S(1)}, u32[]{:S(2)}, u32[]{:S(2)}) %collective-permute-start.5) | collective-permute-done | bytes 40992 | tf_op jit(solution)/shard_map/ppermute | solution.py:256
  23.9 0.0 collective-permute-done.dlo_ref
  23.9 0.0 collective-permute-done.1.dhi_ref
  23.9 0.0 copy-done.1
  23.9 0.0 copy-done.2
  23.9 3.1 %render.1 = s16[4,2,128,128]{3,2,1,0:T(8,128)(2,1)S(1)} custom-call(s32[4,8]{1,0:T(4,128)S(1)} %copy-done.1, f32[2]{0:T(128)S(1)} %copy-done.4, f32[3]{0:T(128)S(1)} %copy-done.5, s32[2,4]{1,0:T(2,128)S(1)} %copy-done.2, f32[8,128,128]{2,1,0:T(8,128)S(1)} %copy-done, f32[5,128,128]{2,1,0:T(8,128)S(1)} %collective-permute-done.dlo_ref, ...), custom_call_target="tpu_custom_call" | custom-call | tf_op jit(solution)/shard_map/render/pallas_call | solution.py:266
  27.0 0.0 copy-start.3
  27.0 9.8 %all_to_all.5.in_ref = s16[4,2,128,128]{3,2,1,0:T(8,128)(2,1)S(1)} all-to-all(s16[4,2,128,128]{3,2,1,0:T(8,128)(2,1)S(1)} %render.1), channel_id=1, replica_groups=mesh['gz'=4,'xy'=8] {'gz'}, dimensions={0} | all-to-all | bytes 524288 | tf_op jit(solution)/shard_map/all_to_all | solution.py:270
  36.8 1.4 %composite.1 = f32[2,4,1,32,128]{4,3,2,1,0:T(8,128)} custom-call(s32[2,4]{1,0:T(2,128)S(1)} %copy-done.3, s16[4,2,128,128]{3,2,1,0:T(8,128)(2,1)S(1)} %all_to_all.5.in_ref), custom_call_target="tpu_custom_call" | custom-call | tf_op jit(solution)/shard_map/composite/pallas_call | solution.py:272
  (9 shorter events, 0.0 us)
Async XLA Ops:
  0.8 23.1 %copy-start = (f32[8,128,128]{2,1,0:T(8,128)S(1)}, f32[8,128,128]{2,1,0:T(8,128)}, u32[]{:S(2)}) copy-start(f32[8,128,128]{2,1,0:T(8,128)} %own_ref.1) | copy-start | bytes 1572868
  0.8 9.9 %collective-permute-start.3 = (f32[8,8,128]{2,1,0:T(8,128)S(1)}, f32[8,8,128]{2,1,0:T(8,128)S(1)}, u32[]{:S(2)}, u32[]{:S(2)}) collective-permute-start(f32[8,8,128]{2,1,0:T(8,128)S(1)} %get-tuple-element.5), channel_id=1, source_target_pairs={{1,0},{2,1},{3,2},{4,3},{5,4},{6,5},{7,6},{9,8},{10,9},{11,10},{12... | collective-permute-start | bytes 98312 | tf_op jit(solution)/shard_map/ppermute | solution.py:256
  5.3 18.5 %collective-permute-start = (f32[5,128,128]{2,1,0:T(8,128)S(1)}, f32[5,128,128]{2,1,0:T(8,128)S(1)}, u32[]{:S(2)}, u32[]{:S(2)}) collective-permute-start(f32[5,128,128]{2,1,0:T(8,128)S(1)} %get-tuple-element.8), channel_id=1, source_target_pairs={{0,8},{8,16},{16,24},{1,9},{9,17},{17,25},{2,10},{10,18},{18,26},{... | collective-permute-start | bytes 983048 | tf_op jit(solution)/shard_map/ppermute | solution.py:256
  6.8 17.0 %collective-permute-start.1 = (f32[5,128,128]{2,1,0:T(8,128)S(1)}, f32[5,128,128]{2,1,0:T(8,128)S(1)}, u32[]{:S(2)}, u32[]{:S(2)}) collective-permute-start(f32[5,128,128]{2,1,0:T(8,128)S(1)} %get-tuple-element.7), channel_id=1, source_target_pairs={{8,0},{16,8},{24,16},{9,1},{17,9},{25,17},{10,2},{18,10},{26,18},{... | collective-permute-start | bytes 983048 | tf_op jit(solution)/shard_map/ppermute | solution.py:256
  8.1 6.7 %collective-permute-start.2 = (f32[8,8,128]{2,1,0:T(8,128)S(1)}, f32[8,8,128]{2,1,0:T(8,128)S(1)}, u32[]{:S(2)}, u32[]{:S(2)}) collective-permute-start(f32[8,8,128]{2,1,0:T(8,128)S(1)} %get-tuple-element.6), channel_id=1, source_target_pairs={{0,1},{1,2},{2,3},{3,4},{4,5},{5,6},{6,7},{8,9},{9,10},{10,11},{11... | collective-permute-start | bytes 98312 | tf_op jit(solution)/shard_map/ppermute | solution.py:256
  14.8 4.8 %collective-permute-start.4 = (f32[10,8,128]{2,1,0:T(8,128)S(1)}, f32[10,8,128]{2,1,0:T(8,128)S(1)}, u32[]{:S(2)}, u32[]{:S(2)}) collective-permute-start(f32[10,8,128]{2,1,0:T(8,128)S(1)} %pad_maximum_fusion), channel_id=1, source_target_pairs={{0,8},{8,16},{16,24},{1,9},{9,17},{17,25},{2,10},{10,18},{18,26},{... | collective-permute-start | bytes 122888 | tf_op jit(solution)/shard_map/ppermute | solution.py:256
  18.3 5.6 %copy-start.1 = (s32[4,8]{1,0:T(4,128)S(1)}, s32[4,8]{1,0:T(4,128)}, u32[]{:S(2)}) copy-start(s32[4,8]{1,0:T(4,128)} %live_ref.1) | copy-start | bytes 388
  18.3 5.6 %copy-start.2 = (s32[2,4]{1,0:T(2,128)S(1)}, s32[2,4]{1,0:T(2,128)}, u32[]{:S(2)}) copy-start(s32[2,4]{1,0:T(2,128)} %owner_ref.1) | copy-start | bytes 100
  18.3 5.6 %copy-start.4 = (f32[2]{0:T(128)S(1)}, f32[2]{0:T(128)}, u32[]{:S(2)}) copy-start(f32[2]{0:T(128)} %slopes_ref.1) | copy-start | bytes 28
  18.3 5.6 %copy-start.5 = (f32[3]{0:T(128)S(1)}, f32[3]{0:T(128)}, u32[]{:S(2)}) copy-start(f32[3]{0:T(128)} %palette_ref.1) | copy-start | bytes 40
  18.4 5.5 %collective-permute-start.5 = (f32[10,8,128]{2,1,0:T(8,128)S(1)}, f32[10,8,128]{2,1,0:T(8,128)S(1)}, u32[]{:S(2)}, u32[]{:S(2)}) collective-permute-start(f32[10,8,128]{2,1,0:T(8,128)S(1)} %pad_maximum_fusion.1), channel_id=1, source_target_pairs={{8,0},{16,8},{24,16},{9,1},{17,9},{25,17},{10,2},{18,10},{26,18},{... | collective-permute-start | bytes 122888 | tf_op jit(solution)/shard_map/ppermute | solution.py:256
  27.0 9.8 %copy-start.3 = (s32[2,4]{1,0:T(2,128)S(1)}, s32[2,4]{1,0:T(2,128)}, u32[]{:S(2)}) copy-start(s32[2,4]{1,0:T(2,128)} %order_ref.1) | copy-start | bytes 100

commit v4 on v3

--- a/solution.py
+++ b/solution.py
@@ -74,29 +74,31 @@
 
     def kernel(
         live_ref, slopes_ref, palette_ref, owner_ref,
-        own_ref, dlo_ref, dhi_ref, rlo_ref, rhi_ref, clo_ref, chi_ref,
+        own_ref, even_ref, odd_ref, corner_ref, rlo_ref, rhi_ref,
         out_ref,
         deep, triple, smooth, across, sheared,
     ):
         depth_index = lax.axis_index("gz")
         row_index = lax.axis_index("xy")
+        odd_depth = depth_index % 2 == 1
 
         for chunk in range(padded_rows // ROW_TILE):
+            rows = pl.ds(chunk * ROW_TILE, ROW_TILE)
+            inner = pl.ds((chunk - 1) * ROW_TILE, ROW_TILE)
+            even = [even_ref[i, rows] for i in range(HALO)]
             if chunk == 0:
-                low = [clo_ref[i] for i in range(HALO)]
+                odd = [corner_ref[i, pl.ds(0, ROW_TILE)] for i in range(HALO)]
                 mid = [rlo_ref[i] for i in range(depth_cells)]
-                high = [chi_ref[i] for i in range(HALO)]
             elif chunk == padded_rows // ROW_TILE - 1:
-                low = [clo_ref[HALO + i] for i in range(HALO)]
+                odd = [corner_ref[i, pl.ds(ROW_TILE, ROW_TILE)] for i in range(HALO)]
                 mid = [rhi_ref[i] for i in range(depth_cells)]
-                high = [chi_ref[HALO + i] for i in range(HALO)]
             else:
-                rows = pl.ds((chunk - 1) * ROW_TILE, ROW_TILE)
-                low = [dlo_ref[i, rows] for i in range(HALO)]
-                mid = [own_ref[i, rows] for i in range(depth_cells)]
-                high = [dhi_ref[i, rows] for i in range(HALO)]
+                odd = [odd_ref[i, inner] for i in range(HALO)]
+                mid = [own_ref[i, inner] for i in range(depth_cells)]
+            low = [jnp.where(odd_depth, e, o) for e, o in zip(even, odd)]
+            high = [jnp.where(odd_depth, o, e) for e, o in zip(even, odd)]
             for z, total in enumerate(window_sums(low + mid + high, TAPS)):
-                deep[z, pl.ds(chunk * ROW_TILE, ROW_TILE)] = total
+                deep[z, rows] = total
 
         band = column_matrix(columns)
         weights = jnp.concatenate([band, band, band], axis=0)
@@ -211,7 +213,7 @@
     return pl.pallas_call(
         kernel,
         out_shape=jax.ShapeDtypeStruct((n_depth, VIEWS, 4 * tile_rows, columns), jnp.int16),
-        in_specs=[smem] * 4 + [vmem] * 7,
+        in_specs=[smem] * 4 + [vmem] * 6,
         out_specs=vmem,
         scratch_shapes=[
             pltpu.VMEM((depth_cells + 2, padded_rows, columns), jnp.float32),
@@ -249,23 +251,44 @@
     n_depth = lax.axis_size("gz")
     n_rows = lax.axis_size("xy")
 
-    def both_ways(axis, to_next, to_previous):
+    edge = depth_cells - HALO
+    odd_depth = lax.axis_index("gz") % 2 == 1
+    odd_row = lax.axis_index("xy") % 2 == 1
+
+    def pairs(axis, first):
         count = lax.axis_size(axis)
-        forward = [(i, i + 1) for i in range(count - 1)]
-        backward = [(target, source) for source, target in forward]
-        return lax.ppermute(to_next, axis, forward), lax.ppermute(to_previous, axis, backward)
-
-    dlo, dhi = both_ways("gz", density[depth_cells - HALO :], density[:HALO])
-    rlo, rhi = both_ways("xy", density[:, row_cells - ROW_TILE :], density[:, :ROW_TILE])
-    clo, chi = both_ways(
+        lower = range(first, count - 1, 2)
+        return [(i, i + 1) for i in lower] + [(i + 1, i) for i in lower]
+
+    low_rows, high_rows = density[:, :ROW_TILE], density[:, row_cells - ROW_TILE :]
+    row_even = lax.ppermute(jnp.where(odd_row, low_rows, high_rows), "xy", pairs("xy", 0))
+    row_odd = lax.ppermute(jnp.where(odd_row, high_rows, low_rows), "xy", pairs("xy", 1))
+    low_deep, high_deep = density[:HALO], density[edge:]
+    deep_odd = lax.ppermute(jnp.where(odd_depth, high_deep, low_deep), "gz", pairs("gz", 1))
+    rlo = jnp.where(odd_row, row_even, row_odd)
+    rhi = jnp.where(odd_row, row_odd, row_even)
+    deep_even = lax.ppermute(
+        jnp.where(
+            odd_depth,
+            jnp.concatenate([rlo[:HALO], low_deep, rhi[:HALO]], axis=1),
+            jnp.concatenate([rlo[edge:], high_deep, rhi[edge:]], axis=1),
+        ),
         "gz",
-        jnp.concatenate([rlo[depth_cells - HALO :], rhi[depth_cells - HALO :]], axis=0),
-        jnp.concatenate([rlo[:HALO], rhi[:HALO]], axis=0),
+        pairs("gz", 0),
+    )
+    corner_odd = lax.ppermute(
+        jnp.where(
+            odd_depth,
+            jnp.concatenate([rlo[edge:], rhi[edge:]], axis=1),
+            jnp.concatenate([rlo[:HALO], rhi[:HALO]], axis=1),
+        ),
+        "gz",
+        pairs("gz", 1),
     )
     render = make_render(n_depth, n_rows, depth_cells, row_cells, columns)
     outgoing = render(
         live_slices, shear_slopes, palette, tile_owner,
-        density, dlo, dhi, rlo, rhi, clo, chi,
+        density, deep_even, deep_odd, corner_odd, rlo, rhi,
     )
     incoming = lax.all_to_all(outgoing, "gz", split_axis=0, concat_axis=0, tiled=True)
     tile_rows = row_cells // n_depth

time: 38.5 us -> 31.6 us (0.82)
  the two profiles are of different devices: /device:TPU:16 before, /device:TPU:24 now
where the time goes in v4:
time: 31.6 us; the launch traced here: 31.3 us
  blocking collectives  16 us (51%)
  starting transfers between devices  5.36 us (17%)
  Pallas kernels  4.45 us (14%)
  waiting for transfers between devices  3.27 us (10%)
  other arithmetic  2.01 us (6%)
    all_to_all x1, blocking collectives, body(): lax.all_to_all(outgoing, 'gz', split_axis=0, concat_axis=0, tiled=True)  16 us
    ppermute x1, waiting for transfers between devices, body(): lax.ppermute(jnp.where(odd_row, high_rows, low_rows), 'xy', pairs('xy', 1))  3.17 us
    pallas_call x1, Pallas kernels, body(): render(live_slices, shear_slopes, palette, tile_owner, density, deep_even...  3.09 us
    ppermute x1, starting transfers between devices, body(): lax.ppermute(jnp.where(odd_row, high_rows, low_rows), 'xy', pairs('xy', 1))  2.32 us
    ppermute x1, starting transfers between devices, body(): lax.ppermute(jnp.where(odd_row, low_rows, high_rows), 'xy', pairs('xy', 0))  1.49 us
    pallas_call x1, Pallas kernels, body(): pl.pallas_call(composite_kernel, out_shape=jax.ShapeDtypeStruct((VIEWS, 4...  1.36 us
    select_n x1, other arithmetic, body(): jnp.where(odd_depth, high_deep, low_deep)  1.17 us
    ppermute x1, starting transfers between devices, body(): lax.ppermute(jnp.where(odd_depth, high_deep, low_deep), 'gz', pairs('gz',...  0.81 us
  transfers between devices with their start and end apart: 5, of which 2 were waited for; matrix products, arithmetic and copies ran while one was open for 4% of the time, Pallas kernels for 0%

profile of v4, /device:TPU:24, one launch (start us, length us, event | category | flops | bytes accessed | tf_op | source)
XLA Modules:
  0.0 31.3 jit_solution(12602004750011642279)
XLA Ops:
  0.0 0.8 %slice_select_fusion.1 = (f32[8,8,128]{2,1,0:T(8,128)S(1)}, f32[8,8,128]{2,1,0:T(8,128)S(1)}) fusion(f32[8,128,128]{2,1,0:T(8,128)} %own_ref.1, pred[]{:T(512)S(6)} %eq.10), kind=kLoop, calls=%fused_computation.4 | loop fusion | flops 16384 | bytes 131073 | tf_op jit(solution)/shard_map/jit(_where)/select_n | solution.py:264
  0.8 1.5 %collective-permute-start = (f32[8,8,128]{2,1,0:T(8,128)S(1)}, f32[8,8,128]{2,1,0:T(8,128)S(1)}, u32[]{:S(2)}, u32[]{:S(2)}) collective-permute-start(f32[8,8,128]{2,1,0:T(8,128)S(1)} %get-tuple-element.8), channel_id=1, source_target_pairs={{0,1},{2,3},{4,5},{6,7},{1,0},{3,2},{5,4},{7,6},{8,9},{10,11},{12,... | collective-permute-start | bytes 98312 | tf_op jit(solution)/shard_map/ppermute | solution.py:264
  2.3 2.3 %collective-permute-start.1 = (f32[8,8,128]{2,1,0:T(8,128)S(1)}, f32[8,8,128]{2,1,0:T(8,128)S(1)}, u32[]{:S(2)}, u32[]{:S(2)}) collective-permute-start(f32[8,8,128]{2,1,0:T(8,128)S(1)} %get-tuple-element.9), channel_id=1, source_target_pairs={{1,2},{3,4},{5,6},{2,1},{4,3},{6,5},{9,10},{11,12},{13,14},{10,9},... | collective-permute-start | bytes 98312 | tf_op jit(solution)/shard_map/ppermute | solution.py:265
  4.6 1.2 %broadcast_select_fusion = (f32[5,128,128]{2,1,0:T(8,128)S(1)}, f32[5,128,128]{2,1,0:T(8,128)S(1)}, f32[5,128,128]{2,1,0:T(8,128)S(1)}) fusion(pred[]{:T(512)S(6)} %eq.9, f32[8,128,128]{2,1,0:T(8,128)} %own_ref.1), kind=kLoop, calls=%fused_computation.1 | loop fusion | flops 81920 | bytes 1638401 | tf_op jit(solution)/shard_map/jit(_where)/select_n | solution.py:267
  5.8 0.0 collective-permute-done
  5.8 3.2 %collective-permute-done.1 = f32[8,8,128]{2,1,0:T(8,128)S(1)} collective-permute-done((f32[8,8,128]{2,1,0:T(8,128)S(1)}, f32[8,8,128]{2,1,0:T(8,128)S(1)}, u32[]{:S(2)}, u32[]{:S(2)}) %collective-permute-start.1) | collective-permute-done | bytes 32800 | tf_op jit(solution)/shard_map/ppermute | solution.py:265
  9.0 0.0 copy-start
  9.1 0.1 collective-permute-start.2
  9.1 0.0 copy-start.1
  9.2 0.0 copy-start.2
  9.2 0.0 copy-start.4
  9.2 0.0 copy-start.5
  9.2 0.8 %collective-permute-start.3 = (f32[5,128,128]{2,1,0:T(8,128)S(1)}, f32[5,128,128]{2,1,0:T(8,128)S(1)}, u32[]{:S(2)}, u32[]{:S(2)}) collective-permute-start(f32[5,128,128]{2,1,0:T(8,128)S(1)} %get-tuple-element.5), channel_id=1, source_target_pairs={{8,16},{16,8},{9,17},{17,9},{10,18},{18,10},{11,19},{19,11},{12,20... | collective-permute-start | bytes 983048 | tf_op jit(solution)/shard_map/ppermute | solution.py:267
  10.0 0.7 %collective-permute-start.4 = (f32[5,16,128]{2,1,0:T(8,128)S(1)}, f32[5,16,128]{2,1,0:T(8,128)S(1)}, u32[]{:S(2)}, u32[]{:S(2)}) collective-permute-start(f32[5,16,128]{2,1,0:T(8,128)S(1)} %maximum_select_fusion.1), channel_id=1, source_target_pairs={{8,16},{16,8},{9,17},{17,9},{10,18},{18,10},{11,19},{19,11},{12,20... | collective-permute-start | bytes 122888 | tf_op jit(solution)/shard_map/ppermute | solution.py:279
  10.7 0.0 collective-permute-done.4.corner_ref
  10.7 0.0 collective-permute-done.3.odd_ref
  10.7 0.1 collective-permute-done.2.even_ref
  10.8 0.0 copy-done
  10.8 0.0 copy-done.1
  10.8 0.0 copy-done.2
  10.8 3.1 %render.1 = s16[4,2,128,128]{3,2,1,0:T(8,128)(2,1)S(1)} custom-call(s32[4,8]{1,0:T(4,128)S(1)} %copy-done.1, f32[2]{0:T(128)S(1)} %copy-done.4, f32[3]{0:T(128)S(1)} %copy-done.5, s32[2,4]{1,0:T(2,128)S(1)} %copy-done.2, f32[8,128,128]{2,1,0:T(8,128)S(1)} %copy-done, f32[5,144,128]{2,1,0:T(8,128)S(1)} %collective-permute-done.2.even_ref, ...), custom_call_target="tpu_custom_call" | custom-call | tf_op jit(solution)/shard_map/render/pallas_call | solution.py:289
  13.9 0.0 copy-start.3
  14.0 16.0 %all_to_all.5.in_ref = s16[4,2,128,128]{3,2,1,0:T(8,128)(2,1)S(1)} all-to-all(s16[4,2,128,128]{3,2,1,0:T(8,128)(2,1)S(1)} %render.1), channel_id=1, replica_groups=mesh['gz'=4,'xy'=8] {'gz'}, dimensions={0} | all-to-all | bytes 524288 | tf_op jit(solution)/shard_map/all_to_all | solution.py:293
  29.9 1.4 %composite.1 = f32[2,4,1,32,128]{4,3,2,1,0:T(8,128)} custom-call(s32[2,4]{1,0:T(2,128)S(1)} %copy-done.3, s16[4,2,128,128]{3,2,1,0:T(8,128)(2,1)S(1)} %all_to_all.5.in_ref), custom_call_target="tpu_custom_call" | custom-call | tf_op jit(solution)/shard_map/composite/pallas_call | solution.py:295
  (7 shorter events, 0.1 us)
Async XLA Ops:
  0.8 5.0 %collective-permute-start = (f32[8,8,128]{2,1,0:T(8,128)S(1)}, f32[8,8,128]{2,1,0:T(8,128)S(1)}, u32[]{:S(2)}, u32[]{:S(2)}) collective-permute-start(f32[8,8,128]{2,1,0:T(8,128)S(1)} %get-tuple-element.8), channel_id=1, source_target_pairs={{0,1},{2,3},{4,5},{6,7},{1,0},{3,2},{5,4},{7,6},{8,9},{10,11},{12,... | collective-permute-start | bytes 98312 | tf_op jit(solution)/shard_map/ppermute | solution.py:264
  2.3 6.7 %collective-permute-start.1 = (f32[8,8,128]{2,1,0:T(8,128)S(1)}, f32[8,8,128]{2,1,0:T(8,128)S(1)}, u32[]{:S(2)}, u32[]{:S(2)}) collective-permute-start(f32[8,8,128]{2,1,0:T(8,128)S(1)} %get-tuple-element.9), channel_id=1, source_target_pairs={{1,2},{3,4},{5,6},{2,1},{4,3},{6,5},{9,10},{11,12},{13,14},{10,9},... | collective-permute-start | bytes 98312 | tf_op jit(solution)/shard_map/ppermute | solution.py:265
  9.0 1.8 %copy-start = (f32[8,128,128]{2,1,0:T(8,128)S(1)}, f32[8,128,128]{2,1,0:T(8,128)}, u32[]{:S(2)}) copy-start(f32[8,128,128]{2,1,0:T(8,128)} %own_ref.1) | copy-start | bytes 1572868
  9.1 1.8 %collective-permute-start.2 = (f32[5,144,128]{2,1,0:T(8,128)S(1)}, f32[5,144,128]{2,1,0:T(8,128)S(1)}, u32[]{:S(2)}, u32[]{:S(2)}) collective-permute-start(f32[5,144,128]{2,1,0:T(8,128)S(1)} %maximum_select_fusion), channel_id=1, source_target_pairs={{0,8},{16,24},{8,0},{24,16},{1,9},{17,25},{9,1},{25,17},{2,10},{18... | collective-permute-start | bytes 1105928 | tf_op jit(solution)/shard_map/ppermute | solution.py:270
  9.1 1.7 %copy-start.1 = (s32[4,8]{1,0:T(4,128)S(1)}, s32[4,8]{1,0:T(4,128)}, u32[]{:S(2)}) copy-start(s32[4,8]{1,0:T(4,128)} %live_ref.1) | copy-start | bytes 388
  9.2 1.7 %copy-start.2 = (s32[2,4]{1,0:T(2,128)S(1)}, s32[2,4]{1,0:T(2,128)}, u32[]{:S(2)}) copy-start(s32[2,4]{1,0:T(2,128)} %owner_ref.1) | copy-start | bytes 100
  9.2 1.7 %copy-start.4 = (f32[2]{0:T(128)S(1)}, f32[2]{0:T(128)}, u32[]{:S(2)}) copy-start(f32[2]{0:T(128)} %slopes_ref.1) | copy-start | bytes 28
  9.2 1.7 %copy-start.5 = (f32[3]{0:T(128)S(1)}, f32[3]{0:T(128)}, u32[]{:S(2)}) copy-start(f32[3]{0:T(128)} %palette_ref.1) | copy-start | bytes 40
  9.2 1.5 %collective-permute-start.3 = (f32[5,128,128]{2,1,0:T(8,128)S(1)}, f32[5,128,128]{2,1,0:T(8,128)S(1)}, u32[]{:S(2)}, u32[]{:S(2)}) collective-permute-start(f32[5,128,128]{2,1,0:T(8,128)S(1)} %get-tuple-element.5), channel_id=1, source_target_pairs={{8,16},{16,8},{9,17},{17,9},{10,18},{18,10},{11,19},{19,11},{12,20... | collective-permute-start | bytes 983048 | tf_op jit(solution)/shard_map/ppermute | solution.py:267
  10.0 0.7 %collective-permute-start.4 = (f32[5,16,128]{2,1,0:T(8,128)S(1)}, f32[5,16,128]{2,1,0:T(8,128)S(1)}, u32[]{:S(2)}, u32[]{:S(2)}) collective-permute-start(f32[5,16,128]{2,1,0:T(8,128)S(1)} %maximum_select_fusion.1), channel_id=1, source_target_pairs={{8,16},{16,8},{9,17},{17,9},{10,18},{18,10},{11,19},{19,11},{12,20... | collective-permute-start | bytes 122888 | tf_op jit(solution)/shard_map/ppermute | solution.py:279
  13.9 16.0 %copy-start.3 = (s32[2,4]{1,0:T(2,128)S(1)}, s32[2,4]{1,0:T(2,128)}, u32[]{:S(2)}) copy-start(s32[2,4]{1,0:T(2,128)} %order_ref.1) | copy-start | bytes 100

commit v5 on v4

--- a/solution.py
+++ b/solution.py
@@ -74,30 +74,31 @@
 
     def kernel(
         live_ref, slopes_ref, palette_ref, owner_ref,
-        own_ref, even_ref, odd_ref, corner_ref, rlo_ref, rhi_ref,
+        own_ref, even_ref, odd_ref, row_even_ref, row_odd_ref,
         out_ref,
         deep, triple, smooth, across, sheared,
     ):
         depth_index = lax.axis_index("gz")
         row_index = lax.axis_index("xy")
         odd_depth = depth_index % 2 == 1
+        odd_row = row_index % 2 == 1
 
         for chunk in range(padded_rows // ROW_TILE):
             rows = pl.ds(chunk * ROW_TILE, ROW_TILE)
             inner = pl.ds((chunk - 1) * ROW_TILE, ROW_TILE)
-            even = [even_ref[i, rows] for i in range(HALO)]
-            if chunk == 0:
-                odd = [corner_ref[i, pl.ds(0, ROW_TILE)] for i in range(HALO)]
-                mid = [rlo_ref[i] for i in range(depth_cells)]
-            elif chunk == padded_rows // ROW_TILE - 1:
-                odd = [corner_ref[i, pl.ds(ROW_TILE, ROW_TILE)] for i in range(HALO)]
-                mid = [rhi_ref[i] for i in range(depth_cells)]
+            if 0 < chunk < padded_rows // ROW_TILE - 1:
+                even = [even_ref[i, inner] for i in range(HALO)]
+                odd = [odd_ref[i, inner] for i in range(HALO)]
+                low = [jnp.where(odd_depth, e, o) for e, o in zip(even, odd)]
+                high = [jnp.where(odd_depth, o, e) for e, o in zip(even, odd)]
+                layers = low + [own_ref[i, inner] for i in range(depth_cells)] + high
             else:
-                odd = [odd_ref[i, inner] for i in range(HALO)]
-                mid = [own_ref[i, inner] for i in range(depth_cells)]
-            low = [jnp.where(odd_depth, e, o) for e, o in zip(even, odd)]
-            high = [jnp.where(odd_depth, o, e) for e, o in zip(even, odd)]
-            for z, total in enumerate(window_sums(low + mid + high, TAPS)):
+                take_even = odd_row if chunk == 0 else jnp.logical_not(odd_row)
+                layers = [
+                    jnp.where(take_even, row_even_ref[i], row_odd_ref[i])
+                    for i in range(depth_cells + 2 * HALO)
+                ]
+            for z, total in enumerate(window_sums(layers, TAPS)):
                 deep[z, rows] = total
 
         band = column_matrix(columns)
@@ -213,7 +214,7 @@
     return pl.pallas_call(
         kernel,
         out_shape=jax.ShapeDtypeStruct((n_depth, VIEWS, 4 * tile_rows, columns), jnp.int16),
-        in_specs=[smem] * 4 + [vmem] * 6,
+        in_specs=[smem] * 4 + [vmem] * 5,
         out_specs=vmem,
         scratch_shapes=[
             pltpu.VMEM((depth_cells + 2, padded_rows, columns), jnp.float32),
@@ -260,35 +261,23 @@
         lower = range(first, count - 1, 2)
         return [(i, i + 1) for i in lower] + [(i + 1, i) for i in lower]
 
-    low_rows, high_rows = density[:, :ROW_TILE], density[:, row_cells - ROW_TILE :]
-    row_even = lax.ppermute(jnp.where(odd_row, low_rows, high_rows), "xy", pairs("xy", 0))
-    row_odd = lax.ppermute(jnp.where(odd_row, high_rows, low_rows), "xy", pairs("xy", 1))
     low_deep, high_deep = density[:HALO], density[edge:]
     deep_odd = lax.ppermute(jnp.where(odd_depth, high_deep, low_deep), "gz", pairs("gz", 1))
-    rlo = jnp.where(odd_row, row_even, row_odd)
-    rhi = jnp.where(odd_row, row_odd, row_even)
-    deep_even = lax.ppermute(
-        jnp.where(
-            odd_depth,
-            jnp.concatenate([rlo[:HALO], low_deep, rhi[:HALO]], axis=1),
-            jnp.concatenate([rlo[edge:], high_deep, rhi[edge:]], axis=1),
-        ),
-        "gz",
-        pairs("gz", 0),
-    )
-    corner_odd = lax.ppermute(
-        jnp.where(
-            odd_depth,
-            jnp.concatenate([rlo[edge:], rhi[edge:]], axis=1),
-            jnp.concatenate([rlo[:HALO], rhi[:HALO]], axis=1),
-        ),
-        "gz",
-        pairs("gz", 1),
-    )
+    deep_even = lax.ppermute(jnp.where(odd_depth, low_deep, high_deep), "gz", pairs("gz", 0))
+
+    def rows_of(start):
+        rows = slice(start, start + ROW_TILE)
+        low = jnp.where(odd_depth, deep_even[:, rows], deep_odd[:, rows])
+        high = jnp.where(odd_depth, deep_odd[:, rows], deep_even[:, rows])
+        return jnp.concatenate([low, density[:, rows], high], axis=0)
+
+    low_rows, high_rows = rows_of(0), rows_of(row_cells - ROW_TILE)
+    row_odd = lax.ppermute(jnp.where(odd_row, high_rows, low_rows), "xy", pairs("xy", 1))
+    row_even = lax.ppermute(jnp.where(odd_row, low_rows, high_rows), "xy", pairs("xy", 0))
     render = make_render(n_depth, n_rows, depth_cells, row_cells, columns)
     outgoing = render(
         live_slices, shear_slopes, palette, tile_owner,
-        density, deep_even, deep_odd, corner_odd, rlo, rhi,
+        density, deep_even, deep_odd, row_even, row_odd,
     )
     incoming = lax.all_to_all(outgoing, "gz", split_axis=0, concat_axis=0, tiled=True)
     tile_rows = row_cells // n_depth

time: 31.6 us -> 32 us (1.013)
  the two profiles are of different devices: /device:TPU:24 before, /device:TPU:0 now
where the time goes in v5:
time: 32 us; the launch traced here: 31.8 us
  blocking collectives  12.2 us (38%)
  starting transfers between devices  10.2 us (32%)
  Pallas kernels  4.48 us (14%)
  waiting for transfers between devices  3.57 us (11%)
  other arithmetic  1.21 us (4%)
    all_to_all x1, blocking collectives, body(): lax.all_to_all(outgoing, 'gz', split_axis=0, concat_axis=0, tiled=True)  12.2 us
    ppermute x1, starting transfers between devices, body(): lax.ppermute(jnp.where(odd_depth, low_deep, high_deep), 'gz', pairs('gz',...  4.37 us
    ppermute x1, starting transfers between devices, body(): lax.ppermute(jnp.where(odd_row, low_rows, high_rows), 'xy', pairs('xy', 0))  4.35 us
    pallas_call x1, Pallas kernels, body(): render(live_slices, shear_slopes, palette, tile_owner, density, deep_even...  3.12 us
    ppermute x1, waiting for transfers between devices, body(): lax.ppermute(jnp.where(odd_row, low_rows, high_rows), 'xy', pairs('xy', 0))  2.33 us
    pallas_call x1, Pallas kernels, body(): pl.pallas_call(composite_kernel, out_shape=jax.ShapeDtypeStruct((VIEWS, 4...  1.36 us
    ppermute x1, waiting for transfers between devices, body(): lax.ppermute(jnp.where(odd_depth, low_deep, high_deep), 'gz', pairs('gz',...  1.23 us
    select_n x1, other arithmetic, body(): jnp.where(odd_depth, high_deep, low_deep)  1.18 us
  transfers between devices with their start and end apart: 4, of which 2 were waited for; matrix products, arithmetic and copies ran while one was open for 0% of the time, Pallas kernels for 0%

profile of v5, /device:TPU:0, one launch (start us, length us, event | category | flops | bytes accessed | tf_op | source)
XLA Modules:
  0.0 31.8 jit_solution(14383644717109146415)
XLA Ops:
  0.0 0.0 copy-start
  0.0 1.2 %slice_select_fusion = (f32[5,128,128]{2,1,0:T(8,128)S(1)}, f32[5,128,128]{2,1,0:T(8,128)S(1)}) fusion(f32[8,128,128]{2,1,0:T(8,128)} %own_ref.1, pred[]{:T(512)S(6)} %eq.9), kind=kLoop, calls=%fused_computation | loop fusion | flops 163840 | bytes 1310721 | tf_op jit(solution)/shard_map/jit(_where)/select_n | solution.py:265
  1.2 0.7 %collective-permute-start.1 = (f32[5,128,128]{2,1,0:T(8,128)S(1)}, f32[5,128,128]{2,1,0:T(8,128)S(1)}, u32[]{:S(2)}, u32[]{:S(2)}) collective-permute-start(f32[5,128,128]{2,1,0:T(8,128)S(1)} %get-tuple-element.11), channel_id=1, source_target_pairs={{8,16},{16,8},{9,17},{17,9},{10,18},{18,10},{11,19},{19,11},{12,20... | collective-permute-start | bytes 983048 | tf_op jit(solution)/shard_map/ppermute | solution.py:265
  1.9 4.4 %collective-permute-start = (f32[5,128,128]{2,1,0:T(8,128)S(1)}, f32[5,128,128]{2,1,0:T(8,128)S(1)}, u32[]{:S(2)}, u32[]{:S(2)}) collective-permute-start(f32[5,128,128]{2,1,0:T(8,128)S(1)} %get-tuple-element.12), channel_id=1, source_target_pairs={{0,8},{16,24},{8,0},{24,16},{1,9},{17,25},{9,1},{25,17},{2,10},{18... | collective-permute-start | bytes 983048 | tf_op jit(solution)/shard_map/ppermute | solution.py:266
  6.3 0.0 copy-done
  6.3 0.0 collective-permute-done.1.odd_ref
  6.3 1.2 %collective-permute-done.even_ref = f32[5,128,128]{2,1,0:T(8,128)S(1)} collective-permute-done((f32[5,128,128]{2,1,0:T(8,128)S(1)}, f32[5,128,128]{2,1,0:T(8,128)S(1)}, u32[]{:S(2)}, u32[]{:S(2)}) %collective-permute-start) | collective-permute-done | bytes 327712 | tf_op jit(solution)/shard_map/ppermute | solution.py:266
  7.5 0.0 copy-start.5
  7.6 0.0 copy-start.1
  7.6 0.0 copy-start.2
  7.6 0.0 copy-start.4
  7.6 0.8 %collective-permute-start.3 = (f32[18,8,128]{2,1,0:T(8,128)S(1)}, f32[18,8,128]{2,1,0:T(8,128)S(1)}, u32[]{:S(2)}, u32[]{:S(2)}) collective-permute-start(f32[18,8,128]{2,1,0:T(8,128)S(1)} %get-tuple-element.13), channel_id=1, source_target_pairs={{1,2},{3,4},{5,6},{2,1},{4,3},{6,5},{9,10},{11,12},{13,14},{10,9},... | collective-permute-start | bytes 221192 | tf_op jit(solution)/shard_map/ppermute | solution.py:275
  8.4 4.3 %collective-permute-start.2 = (f32[18,8,128]{2,1,0:T(8,128)S(1)}, f32[18,8,128]{2,1,0:T(8,128)S(1)}, u32[]{:S(2)}, u32[]{:S(2)}) collective-permute-start(f32[18,8,128]{2,1,0:T(8,128)S(1)} %get-tuple-element.14), channel_id=1, source_target_pairs={{0,1},{2,3},{4,5},{6,7},{1,0},{3,2},{5,4},{7,6},{8,9},{10,11},{12,... | collective-permute-start | bytes 221192 | tf_op jit(solution)/shard_map/ppermute | solution.py:276
  12.7 0.0 collective-permute-done.3.row_odd_ref
  12.8 2.3 %collective-permute-done.2.row_even_ref = f32[18,8,128]{2,1,0:T(8,128)S(1)} collective-permute-done((f32[18,8,128]{2,1,0:T(8,128)S(1)}, f32[18,8,128]{2,1,0:T(8,128)S(1)}, u32[]{:S(2)}, u32[]{:S(2)}) %collective-permute-start.2) | collective-permute-done | bytes 73760 | tf_op jit(solution)/shard_map/ppermute | solution.py:276
  15.1 0.0 copy-done.5
  15.1 0.0 copy-done.1
  15.1 0.0 copy-done.2
  15.1 0.0 copy-done.4
  15.1 3.1 %render.1 = s16[4,2,128,128]{3,2,1,0:T(8,128)(2,1)S(1)} custom-call(s32[4,8]{1,0:T(4,128)S(1)} %copy-done.1, f32[2]{0:T(128)S(1)} %copy-done.4, f32[3]{0:T(128)S(1)} %copy-done.5, s32[2,4]{1,0:T(2,128)S(1)} %copy-done.2, f32[8,128,128]{2,1,0:T(8,128)S(1)} %copy-done, f32[5,128,128]{2,1,0:T(8,128)S(1)} %collective-permute-done.even_ref, ...), custom_call_target="tpu_custom_call" | custom-call | tf_op jit(solution)/shard_map/render/pallas_call | solution.py:278
  18.2 0.0 copy-start.3
  18.2 12.2 %all_to_all.5.in_ref = s16[4,2,128,128]{3,2,1,0:T(8,128)(2,1)S(1)} all-to-all(s16[4,2,128,128]{3,2,1,0:T(8,128)(2,1)S(1)} %render.1), channel_id=1, replica_groups=mesh['gz'=4,'xy'=8] {'gz'}, dimensions={0} | all-to-all | bytes 524288 | tf_op jit(solution)/shard_map/all_to_all | solution.py:282
  30.4 0.0 copy-done.3
  30.4 1.4 %composite.1 = f32[2,4,1,32,128]{4,3,2,1,0:T(8,128)} custom-call(s32[2,4]{1,0:T(2,128)S(1)} %copy-done.3, s16[4,2,128,128]{3,2,1,0:T(8,128)(2,1)S(1)} %all_to_all.5.in_ref), custom_call_target="tpu_custom_call" | custom-call | tf_op jit(solution)/shard_map/composite/pallas_call | solution.py:284
  (3 shorter events, 0.0 us)
Async XLA Ops:
  0.0 6.3 %copy-start = (f32[8,128,128]{2,1,0:T(8,128)S(1)}, f32[8,128,128]{2,1,0:T(8,128)}, u32[]{:S(2)}) copy-start(f32[8,128,128]{2,1,0:T(8,128)} %own_ref.1) | copy-start | bytes 1572868
  1.2 5.1 %collective-permute-start.1 = (f32[5,128,128]{2,1,0:T(8,128)S(1)}, f32[5,128,128]{2,1,0:T(8,128)S(1)}, u32[]{:S(2)}, u32[]{:S(2)}) collective-permute-start(f32[5,128,128]{2,1,0:T(8,128)S(1)} %get-tuple-element.11), channel_id=1, source_target_pairs={{8,16},{16,8},{9,17},{17,9},{10,18},{18,10},{11,19},{19,11},{12,20... | collective-permute-start | bytes 983048 | tf_op jit(solution)/shard_map/ppermute | solution.py:265
  1.9 5.6 %collective-permute-start = (f32[5,128,128]{2,1,0:T(8,128)S(1)}, f32[5,128,128]{2,1,0:T(8,128)S(1)}, u32[]{:S(2)}, u32[]{:S(2)}) collective-permute-start(f32[5,128,128]{2,1,0:T(8,128)S(1)} %get-tuple-element.12), channel_id=1, source_target_pairs={{0,8},{16,24},{8,0},{24,16},{1,9},{17,25},{9,1},{25,17},{2,10},{18... | collective-permute-start | bytes 983048 | tf_op jit(solution)/shard_map/ppermute | solution.py:266
  7.5 7.6 %copy-start.5 = (f32[3]{0:T(128)S(1)}, f32[3]{0:T(128)}, u32[]{:S(2)}) copy-start(f32[3]{0:T(128)} %palette_ref.1) | copy-start | bytes 40
  7.6 7.5 %copy-start.1 = (s32[4,8]{1,0:T(4,128)S(1)}, s32[4,8]{1,0:T(4,128)}, u32[]{:S(2)}) copy-start(s32[4,8]{1,0:T(4,128)} %live_ref.1) | copy-start | bytes 388
  7.6 7.5 %copy-start.2 = (s32[2,4]{1,0:T(2,128)S(1)}, s32[2,4]{1,0:T(2,128)}, u32[]{:S(2)}) copy-start(s32[2,4]{1,0:T(2,128)} %owner_ref.1) | copy-start | bytes 100
  7.6 7.5 %copy-start.4 = (f32[2]{0:T(128)S(1)}, f32[2]{0:T(128)}, u32[]{:S(2)}) copy-start(f32[2]{0:T(128)} %slopes_ref.1) | copy-start | bytes 28
  7.6 5.2 %collective-permute-start.3 = (f32[18,8,128]{2,1,0:T(8,128)S(1)}, f32[18,8,128]{2,1,0:T(8,128)S(1)}, u32[]{:S(2)}, u32[]{:S(2)}) collective-permute-start(f32[18,8,128]{2,1,0:T(8,128)S(1)} %get-tuple-element.13), channel_id=1, source_target_pairs={{1,2},{3,4},{5,6},{2,1},{4,3},{6,5},{9,10},{11,12},{13,14},{10,9},... | collective-permute-start | bytes 221192 | tf_op jit(solution)/shard_map/ppermute | solution.py:275
  8.4 6.7 %collective-permute-start.2 = (f32[18,8,128]{2,1,0:T(8,128)S(1)}, f32[18,8,128]{2,1,0:T(8,128)S(1)}, u32[]{:S(2)}, u32[]{:S(2)}) collective-permute-start(f32[18,8,128]{2,1,0:T(8,128)S(1)} %get-tuple-element.14), channel_id=1, source_target_pairs={{0,1},{2,3},{4,5},{6,7},{1,0},{3,2},{5,4},{7,6},{8,9},{10,11},{12,... | collective-permute-start | bytes 221192 | tf_op jit(solution)/shard_map/ppermute | solution.py:276
  18.2 12.2 %copy-start.3 = (s32[2,4]{1,0:T(2,128)S(1)}, s32[2,4]{1,0:T(2,128)}, u32[]{:S(2)}) copy-start(s32[2,4]{1,0:T(2,128)} %order_ref.1) | copy-start | bytes 100

commit v6 on v4

--- a/solution.py
+++ b/solution.py
@@ -74,7 +74,7 @@
 
     def kernel(
         live_ref, slopes_ref, palette_ref, owner_ref,
-        own_ref, even_ref, odd_ref, corner_ref, rlo_ref, rhi_ref,
+        own_ref, even_ref, odd_ref, corner_even_ref, corner_odd_ref, rlo_ref, rhi_ref,
         out_ref,
         deep, triple, smooth, across, sheared,
     ):
@@ -85,16 +85,16 @@
         for chunk in range(padded_rows // ROW_TILE):
             rows = pl.ds(chunk * ROW_TILE, ROW_TILE)
             inner = pl.ds((chunk - 1) * ROW_TILE, ROW_TILE)
-            even = [even_ref[i, rows] for i in range(HALO)]
             if chunk == 0:
-                odd = [corner_ref[i, pl.ds(0, ROW_TILE)] for i in range(HALO)]
-                mid = [rlo_ref[i] for i in range(depth_cells)]
+                at, pair, mid_ref = pl.ds(0, ROW_TILE), (corner_even_ref, corner_odd_ref), rlo_ref
             elif chunk == padded_rows // ROW_TILE - 1:
-                odd = [corner_ref[i, pl.ds(ROW_TILE, ROW_TILE)] for i in range(HALO)]
-                mid = [rhi_ref[i] for i in range(depth_cells)]
+                at = pl.ds(ROW_TILE, ROW_TILE)
+                pair, mid_ref = (corner_even_ref, corner_odd_ref), rhi_ref
             else:
-                odd = [odd_ref[i, inner] for i in range(HALO)]
-                mid = [own_ref[i, inner] for i in range(depth_cells)]
+                at, pair, mid_ref = inner, (even_ref, odd_ref), own_ref
+            mid_at = at if mid_ref is own_ref else pl.ds(0, ROW_TILE)
+            even, odd = [[ref[i, at] for i in range(HALO)] for ref in pair]
+            mid = [mid_ref[i, mid_at] for i in range(depth_cells)]
             low = [jnp.where(odd_depth, e, o) for e, o in zip(even, odd)]
             high = [jnp.where(odd_depth, o, e) for e, o in zip(even, odd)]
             for z, total in enumerate(window_sums(low + mid + high, TAPS)):
@@ -213,7 +213,7 @@
     return pl.pallas_call(
         kernel,
         out_shape=jax.ShapeDtypeStruct((n_depth, VIEWS, 4 * tile_rows, columns), jnp.int16),
-        in_specs=[smem] * 4 + [vmem] * 6,
+        in_specs=[smem] * 4 + [vmem] * 7,
         out_specs=vmem,
         scratch_shapes=[
             pltpu.VMEM((depth_cells + 2, padded_rows, columns), jnp.float32),
@@ -265,30 +265,21 @@
     row_odd = lax.ppermute(jnp.where(odd_row, high_rows, low_rows), "xy", pairs("xy", 1))
     low_deep, high_deep = density[:HALO], density[edge:]
     deep_odd = lax.ppermute(jnp.where(odd_depth, high_deep, low_deep), "gz", pairs("gz", 1))
+    deep_even = lax.ppermute(jnp.where(odd_depth, low_deep, high_deep), "gz", pairs("gz", 0))
     rlo = jnp.where(odd_row, row_even, row_odd)
     rhi = jnp.where(odd_row, row_odd, row_even)
-    deep_even = lax.ppermute(
-        jnp.where(
-            odd_depth,
-            jnp.concatenate([rlo[:HALO], low_deep, rhi[:HALO]], axis=1),
-            jnp.concatenate([rlo[edge:], high_deep, rhi[edge:]], axis=1),
-        ),
-        "gz",
-        pairs("gz", 0),
-    )
+    low_corner = jnp.concatenate([rlo[:HALO], rhi[:HALO]], axis=1)
+    high_corner = jnp.concatenate([rlo[edge:], rhi[edge:]], axis=1)
     corner_odd = lax.ppermute(
-        jnp.where(
-            odd_depth,
-            jnp.concatenate([rlo[edge:], rhi[edge:]], axis=1),
-            jnp.concatenate([rlo[:HALO], rhi[:HALO]], axis=1),
-        ),
-        "gz",
-        pairs("gz", 1),
+        jnp.where(odd_depth, high_corner, low_corner), "gz", pairs("gz", 1)
+    )
+    corner_even = lax.ppermute(
+        jnp.where(odd_depth, low_corner, high_corner), "gz", pairs("gz", 0)
     )
     render = make_render(n_depth, n_rows, depth_cells, row_cells, columns)
     outgoing = render(
         live_slices, shear_slopes, palette, tile_owner,
-        density, deep_even, deep_odd, corner_odd, rlo, rhi,
+        density, deep_even, deep_odd, corner_even, corner_odd, rlo, rhi,
     )
     incoming = lax.all_to_all(outgoing, "gz", split_axis=0, concat_axis=0, tiled=True)
     tile_rows = row_cells // n_depth

time: 31.6 us -> 29.3 us (0.927)
  the two profiles are of different devices: /device:TPU:24 before, /device:TPU:2 now
where the time goes in v6:
time: 29.3 us; the launch traced here: 29 us
  blocking collectives  12.8 us (44%)
  starting transfers between devices  9.26 us (32%)
  Pallas kernels  4.47 us (15%)
  other arithmetic  1.98 us (7%)
    all_to_all x1, blocking collectives, body(): lax.all_to_all(outgoing, 'gz', split_axis=0, concat_axis=0, tiled=True)  12.8 us
    ppermute x1, starting transfers between devices, body(): lax.ppermute(jnp.where(odd_row, high_rows, low_rows), 'xy', pairs('xy', 1))  4.93 us
    pallas_call x1, Pallas kernels, body(): render(live_slices, shear_slopes, palette, tile_owner, density, deep_even...  3.11 us
    ppermute x1, starting transfers between devices, body(): lax.ppermute(jnp.where(odd_depth, low_corner, high_corner), 'gz', pairs('...  2.93 us
    pallas_call x1, Pallas kernels, body(): pl.pallas_call(composite_kernel, out_shape=jax.ShapeDtypeStruct((VIEWS, 4...  1.36 us
    select_n x1, other arithmetic, body(): jnp.where(odd_depth, high_deep, low_deep)  1.18 us
    select_n x1, other arithmetic, body(): jnp.where(odd_row, low_rows, high_rows)  0.78 us
    ppermute x1, starting transfers between devices, body(): lax.ppermute(jnp.where(odd_depth, high_deep, low_deep), 'gz', pairs('gz',...  0.68 us
  transfers between devices with their start and end apart: 6, of which 1 were waited for; matrix products, arithmetic and copies ran while one was open for 4% of the time, Pallas kernels for 0%

profile of v6, /device:TPU:2, one launch (start us, length us, event | category | flops | bytes accessed | tf_op | source)
XLA Modules:
  0.0 29.0 jit_solution(7556067061696977216)
XLA Ops:
  0.0 0.8 %slice_select_fusion.3 = (f32[8,8,128]{2,1,0:T(8,128)S(1)}, f32[8,8,128]{2,1,0:T(8,128)S(1)}) fusion(f32[8,128,128]{2,1,0:T(8,128)} %own_ref.1, pred[]{:T(512)S(6)} %eq.10), kind=kLoop, calls=%fused_computation.7 | loop fusion | flops 16384 | bytes 131073 | tf_op jit(solution)/shard_map/jit(_where)/select_n | solution.py:264
  0.8 0.0 collective-permute-start.2
  0.8 4.9 %collective-permute-start.3 = (f32[8,8,128]{2,1,0:T(8,128)S(1)}, f32[8,8,128]{2,1,0:T(8,128)S(1)}, u32[]{:S(2)}, u32[]{:S(2)}) collective-permute-start(f32[8,8,128]{2,1,0:T(8,128)S(1)} %get-tuple-element.6), channel_id=1, source_target_pairs={{1,2},{3,4},{5,6},{2,1},{4,3},{6,5},{9,10},{11,12},{13,14},{10,9},... | collective-permute-start | bytes 98312 | tf_op jit(solution)/shard_map/ppermute | solution.py:265
  5.7 0.0 copy-start
  5.8 1.2 %slice_select_fusion = (f32[5,128,128]{2,1,0:T(8,128)S(1)}, f32[5,128,128]{2,1,0:T(8,128)S(1)}) fusion(f32[8,128,128]{2,1,0:T(8,128)} %own_ref.1, pred[]{:T(512)S(6)} %eq.9), kind=kLoop, calls=%fused_computation | loop fusion | flops 163840 | bytes 1310721 | tf_op jit(solution)/shard_map/jit(_where)/select_n | solution.py:267
  6.9 0.1 collective-permute-start
  7.0 0.7 %collective-permute-start.1 = (f32[5,128,128]{2,1,0:T(8,128)S(1)}, f32[5,128,128]{2,1,0:T(8,128)S(1)}, u32[]{:S(2)}, u32[]{:S(2)}) collective-permute-start(f32[5,128,128]{2,1,0:T(8,128)S(1)} %get-tuple-element.7), channel_id=1, source_target_pairs={{8,16},{16,8},{9,17},{17,9},{10,18},{18,10},{11,19},{19,11},{12,20... | collective-permute-start | bytes 983048 | tf_op jit(solution)/shard_map/ppermute | solution.py:267
  7.7 0.0 collective-permute-done.2
  7.7 0.0 collective-permute-done.3
  7.8 0.0 copy-start.5
  7.8 0.0 copy-start.1
  7.8 0.0 copy-start.2
  7.8 0.0 copy-start.4
  7.8 2.9 %collective-permute-start.4 = (f32[5,16,128]{2,1,0:T(8,128)S(1)}, f32[5,16,128]{2,1,0:T(8,128)S(1)}, u32[]{:S(2)}, u32[]{:S(2)}) collective-permute-start(f32[5,16,128]{2,1,0:T(8,128)S(1)} %get-tuple-element.10), channel_id=1, source_target_pairs={{0,8},{16,24},{8,0},{24,16},{1,9},{17,25},{9,1},{25,17},{2,10},{18... | collective-permute-start | bytes 122888 | tf_op jit(solution)/shard_map/ppermute | solution.py:276
  10.7 0.7 %collective-permute-start.5 = (f32[5,16,128]{2,1,0:T(8,128)S(1)}, f32[5,16,128]{2,1,0:T(8,128)S(1)}, u32[]{:S(2)}, u32[]{:S(2)}) collective-permute-start(f32[5,16,128]{2,1,0:T(8,128)S(1)} %get-tuple-element.9), channel_id=1, source_target_pairs={{8,16},{16,8},{9,17},{17,9},{10,18},{18,10},{11,19},{19,11},{12,20... | collective-permute-start | bytes 122888 | tf_op jit(solution)/shard_map/ppermute | solution.py:273
  11.4 0.2 collective-permute-done.4.corner_even_ref
  11.6 0.0 collective-permute-done.5.corner_odd_ref
  11.6 0.0 collective-permute-done.even_ref
  11.6 0.0 collective-permute-done.1.odd_ref
  11.6 0.0 copy-done
  11.7 3.1 %render.1 = s16[4,2,128,128]{3,2,1,0:T(8,128)(2,1)S(1)} custom-call(s32[4,8]{1,0:T(4,128)S(1)} %copy-done.1, f32[2]{0:T(128)S(1)} %copy-done.4, f32[3]{0:T(128)S(1)} %copy-done.5, s32[2,4]{1,0:T(2,128)S(1)} %copy-done.2, f32[8,128,128]{2,1,0:T(8,128)S(1)} %copy-done, f32[5,128,128]{2,1,0:T(8,128)S(1)} %collective-permute-done.even_ref, ...), custom_call_target="tpu_custom_call" | custom-call | tf_op jit(solution)/shard_map/render/pallas_call | solution.py:280
  14.8 0.0 copy-start.3
  14.8 12.8 %all_to_all.5.in_ref = s16[4,2,128,128]{3,2,1,0:T(8,128)(2,1)S(1)} all-to-all(s16[4,2,128,128]{3,2,1,0:T(8,128)(2,1)S(1)} %render.1), channel_id=1, replica_groups=mesh['gz'=4,'xy'=8] {'gz'}, dimensions={0} | all-to-all | bytes 524288 | tf_op jit(solution)/shard_map/all_to_all | solution.py:284
  27.7 1.4 %composite.1 = f32[2,4,1,32,128]{4,3,2,1,0:T(8,128)} custom-call(s32[2,4]{1,0:T(2,128)S(1)} %copy-done.3, s16[4,2,128,128]{3,2,1,0:T(8,128)(2,1)S(1)} %all_to_all.5.in_ref), custom_call_target="tpu_custom_call" | custom-call | tf_op jit(solution)/shard_map/composite/pallas_call | solution.py:286
  (8 shorter events, 0.0 us)
Async XLA Ops:
  0.8 6.9 %collective-permute-start.2 = (f32[8,8,128]{2,1,0:T(8,128)S(1)}, f32[8,8,128]{2,1,0:T(8,128)S(1)}, u32[]{:S(2)}, u32[]{:S(2)}) collective-permute-start(f32[8,8,128]{2,1,0:T(8,128)S(1)} %get-tuple-element.5), channel_id=1, source_target_pairs={{0,1},{2,3},{4,5},{6,7},{1,0},{3,2},{5,4},{7,6},{8,9},{10,11},{12,... | collective-permute-start | bytes 98312 | tf_op jit(solution)/shard_map/ppermute | solution.py:264
  0.8 6.9 %collective-permute-start.3 = (f32[8,8,128]{2,1,0:T(8,128)S(1)}, f32[8,8,128]{2,1,0:T(8,128)S(1)}, u32[]{:S(2)}, u32[]{:S(2)}) collective-permute-start(f32[8,8,128]{2,1,0:T(8,128)S(1)} %get-tuple-element.6), channel_id=1, source_target_pairs={{1,2},{3,4},{5,6},{2,1},{4,3},{6,5},{9,10},{11,12},{13,14},{10,9},... | collective-permute-start | bytes 98312 | tf_op jit(solution)/shard_map/ppermute | solution.py:265
  5.7 5.9 %copy-start = (f32[8,128,128]{2,1,0:T(8,128)S(1)}, f32[8,128,128]{2,1,0:T(8,128)}, u32[]{:S(2)}) copy-start(f32[8,128,128]{2,1,0:T(8,128)} %own_ref.1) | copy-start | bytes 1572868
  6.9 4.7 %collective-permute-start = (f32[5,128,128]{2,1,0:T(8,128)S(1)}, f32[5,128,128]{2,1,0:T(8,128)S(1)}, u32[]{:S(2)}, u32[]{:S(2)}) collective-permute-start(f32[5,128,128]{2,1,0:T(8,128)S(1)} %get-tuple-element.8), channel_id=1, source_target_pairs={{0,8},{16,24},{8,0},{24,16},{1,9},{17,25},{9,1},{25,17},{2,10},{18... | collective-permute-start | bytes 983048 | tf_op jit(solution)/shard_map/ppermute | solution.py:268
  7.0 4.6 %collective-permute-start.1 = (f32[5,128,128]{2,1,0:T(8,128)S(1)}, f32[5,128,128]{2,1,0:T(8,128)S(1)}, u32[]{:S(2)}, u32[]{:S(2)}) collective-permute-start(f32[5,128,128]{2,1,0:T(8,128)S(1)} %get-tuple-element.7), channel_id=1, source_target_pairs={{8,16},{16,8},{9,17},{17,9},{10,18},{18,10},{11,19},{19,11},{12,20... | collective-permute-start | bytes 983048 | tf_op jit(solution)/shard_map/ppermute | solution.py:267
  7.8 3.9 %copy-start.5 = (f32[3]{0:T(128)S(1)}, f32[3]{0:T(128)}, u32[]{:S(2)}) copy-start(f32[3]{0:T(128)} %palette_ref.1) | copy-start | bytes 40
  7.8 3.9 %copy-start.1 = (s32[4,8]{1,0:T(4,128)S(1)}, s32[4,8]{1,0:T(4,128)}, u32[]{:S(2)}) copy-start(s32[4,8]{1,0:T(4,128)} %live_ref.1) | copy-start | bytes 388
  7.8 3.9 %copy-start.2 = (s32[2,4]{1,0:T(2,128)S(1)}, s32[2,4]{1,0:T(2,128)}, u32[]{:S(2)}) copy-start(s32[2,4]{1,0:T(2,128)} %owner_ref.1) | copy-start | bytes 100
  7.8 3.9 %copy-start.4 = (f32[2]{0:T(128)S(1)}, f32[2]{0:T(128)}, u32[]{:S(2)}) copy-start(f32[2]{0:T(128)} %slopes_ref.1) | copy-start | bytes 28
  7.8 3.8 %collective-permute-start.4 = (f32[5,16,128]{2,1,0:T(8,128)S(1)}, f32[5,16,128]{2,1,0:T(8,128)S(1)}, u32[]{:S(2)}, u32[]{:S(2)}) collective-permute-start(f32[5,16,128]{2,1,0:T(8,128)S(1)} %get-tuple-element.10), channel_id=1, source_target_pairs={{0,8},{16,24},{8,0},{24,16},{1,9},{17,25},{9,1},{25,17},{2,10},{18... | collective-permute-start | bytes 122888 | tf_op jit(solution)/shard_map/ppermute | solution.py:276
  10.7 0.9 %collective-permute-start.5 = (f32[5,16,128]{2,1,0:T(8,128)S(1)}, f32[5,16,128]{2,1,0:T(8,128)S(1)}, u32[]{:S(2)}, u32[]{:S(2)}) collective-permute-start(f32[5,16,128]{2,1,0:T(8,128)S(1)} %get-tuple-element.9), channel_id=1, source_target_pairs={{8,16},{16,8},{9,17},{17,9},{10,18},{18,10},{11,19},{19,11},{12,20... | collective-permute-start | bytes 122888 | tf_op jit(solution)/shard_map/ppermute | solution.py:273
  14.8 12.9 %copy-start.3 = (s32[2,4]{1,0:T(2,128)S(1)}, s32[2,4]{1,0:T(2,128)}, u32[]{:S(2)}) copy-start(s32[2,4]{1,0:T(2,128)} %order_ref.1) | copy-start | bytes 100

commit v7 on v6

--- a/solution.py
+++ b/solution.py
@@ -227,6 +227,44 @@
     )
 
 
+def cut_edges(density):
+    depth_cells, row_cells, columns = density.shape
+
+    def kernel(density_ref, row_even_ref, row_odd_ref, deep_even_ref, deep_odd_ref, sems):
+        row_bit = lax.axis_index("xy") % 2
+        depth_bit = lax.axis_index("gz") % 2
+        last_rows, last_deep = row_cells - ROW_TILE, depth_cells - HALO
+
+        def rows(bit):
+            return density_ref.at[:, pl.ds(pl.multiple_of(bit * last_rows, ROW_TILE), ROW_TILE)]
+
+        def deep(bit):
+            return density_ref.at[pl.ds(bit * last_deep, HALO)]
+
+        copies = [
+            pltpu.make_async_copy(deep(depth_bit), deep_odd_ref, sems.at[0]),
+            pltpu.make_async_copy(deep(1 - depth_bit), deep_even_ref, sems.at[1]),
+            pltpu.make_async_copy(rows(1 - row_bit), row_even_ref, sems.at[2]),
+            pltpu.make_async_copy(rows(row_bit), row_odd_ref, sems.at[3]),
+        ]
+        for copy in copies:
+            copy.start()
+        for copy in copies:
+            copy.wait()
+
+    rows = jax.ShapeDtypeStruct((depth_cells, ROW_TILE, columns), jnp.float32)
+    deep = jax.ShapeDtypeStruct((HALO, row_cells, columns), jnp.float32)
+    return pl.pallas_call(
+        kernel,
+        out_shape=(rows, rows, deep, deep),
+        in_specs=[pl.BlockSpec(memory_space=pltpu.HBM)],
+        out_specs=(pl.BlockSpec(memory_space=pltpu.VMEM),) * 4,
+        scratch_shapes=[pltpu.SemaphoreType.DMA((4,))],
+        compiler_params=pltpu.CompilerParams(vmem_limit_bytes=VMEM_BYTES),
+        name="cut_edges",
+    )(density)
+
+
 def composite_kernel(order_ref, in_ref, out_ref):
     count = in_ref.shape[0]
     rows = in_ref.shape[2] // 4
@@ -260,12 +298,11 @@
         lower = range(first, count - 1, 2)
         return [(i, i + 1) for i in lower] + [(i + 1, i) for i in lower]
 
-    low_rows, high_rows = density[:, :ROW_TILE], density[:, row_cells - ROW_TILE :]
-    row_even = lax.ppermute(jnp.where(odd_row, low_rows, high_rows), "xy", pairs("xy", 0))
-    row_odd = lax.ppermute(jnp.where(odd_row, high_rows, low_rows), "xy", pairs("xy", 1))
-    low_deep, high_deep = density[:HALO], density[edge:]
-    deep_odd = lax.ppermute(jnp.where(odd_depth, high_deep, low_deep), "gz", pairs("gz", 1))
-    deep_even = lax.ppermute(jnp.where(odd_depth, low_deep, high_deep), "gz", pairs("gz", 0))
+    row_even, row_odd, deep_even, deep_odd = cut_edges(density)
+    row_even = lax.ppermute(row_even, "xy", pairs("xy", 0))
+    row_odd = lax.ppermute(row_odd, "xy", pairs("xy", 1))
+    deep_odd = lax.ppermute(deep_odd, "gz", pairs("gz", 1))
+    deep_even = lax.ppermute(deep_even, "gz", pairs("gz", 0))
     rlo = jnp.where(odd_row, row_even, row_odd)
     rhi = jnp.where(odd_row, row_odd, row_even)
     low_corner = jnp.concatenate([rlo[:HALO], rhi[:HALO]], axis=1)

time: 29.3 us -> 28.7 us (0.980)
  other arithmetic: 1.98 us -> 0.02 us
  waiting for transfers between devices: 0.22 us -> 1.3 us
  local copies, waits for them, and re-layouts: 0.05 us -> 1.08 us
  starting transfers between devices: 9.26 us -> 8.26 us
    select_n x2 -> x0, other arithmetic: 1.96 us -> none  [the longest x1 1.18 us: body(): jnp.where(odd_depth, high_deep, low_deep)]
    ppermute x4, waiting for transfers between devices: 0.01 us -> 1.09 us  [the longest x1 1.08 us: body(): row_odd = lax.ppermute(row_odd, 'xy', pairs('xy', 1))]
    ppermute x1, starting transfers between devices: 2.93 us -> 1.86 us  [body(): lax.ppermute(jnp.where(odd_depth, low_corner, high_corner), 'gz', pairs('...]
    unnamed x12 -> x14, local copies, waits for them, and re-layouts: 0.04 us -> 1.08 us
  transfers between devices with their start and end apart: 6 -> 6, of which waited for: 1 -> 2; matrix products, arithmetic and copies ran while one was open for 4% -> 0% of each run, Pallas kernels for 0% -> 0%
where the time goes in v7:
time: 28.7 us; the launch traced here: 28.4 us
  blocking collectives  12.8 us (45%)
  starting transfers between devices  8.26 us (29%)
  Pallas kernels  4.73 us (16%)
  waiting for transfers between devices  1.3 us (5%)
  local copies, waits for them, and re-layouts  1.08 us (4%)
    all_to_all x1, blocking collectives, body(): lax.all_to_all(outgoing, 'gz', split_axis=0, concat_axis=0, tiled=True)  12.8 us
    ppermute x1, starting transfers between devices, body(): row_odd = lax.ppermute(row_odd, 'xy', pairs('xy', 1))  4.92 us
    pallas_call x1, Pallas kernels, body(): render(live_slices, shear_slopes, palette, tile_owner, density, deep_even...  3.11 us
    ppermute x1, starting transfers between devices, body(): lax.ppermute(jnp.where(odd_depth, low_corner, high_corner), 'gz', pairs('...  1.86 us
    pallas_call x1, Pallas kernels, body(): pl.pallas_call(composite_kernel, out_shape=jax.ShapeDtypeStruct((VIEWS, 4...  1.36 us
    ppermute x1, waiting for transfers between devices, body(): row_odd = lax.ppermute(row_odd, 'xy', pairs('xy', 1))  1.08 us
    unnamed x14, local copies, waits for them, and re-layouts  1.08 us
    ppermute x1, starting transfers between devices, body(): deep_odd = lax.ppermute(deep_odd, 'gz', pairs('gz', 1))  0.68 us
  transfers between devices with their start and end apart: 6, of which 2 were waited for; matrix products, arithmetic and copies ran while one was open for 0% of the time, Pallas kernels for 0%

profile of v7, /device:TPU:2, one launch (start us, length us, event | category | flops | bytes accessed | tf_op | source)
XLA Modules:
  0.0 28.4 jit_solution(18180416274340000087)
XLA Ops:
  0.0 1.0 %copy-done = f32[8,128,128]{2,1,0:T(8,128)S(1)} copy-done((f32[8,128,128]{2,1,0:T(8,128)S(1)}, f32[8,128,128]{2,1,0:T(8,128)}, u32[]{:S(2)}) %copy-start) | copy-done | bytes 524312
  1.0 0.3 cut_edges.1
  1.3 0.1 collective-permute-start.2
  1.4 4.9 %collective-permute-start.3 = (f32[8,8,128]{2,1,0:T(8,128)S(1)}, f32[8,8,128]{2,1,0:T(8,128)S(1)}, u32[]{:S(2)}, u32[]{:S(2)}) collective-permute-start(f32[8,8,128]{2,1,0:T(8,128)S(1)} %get-tuple-element.12), channel_id=1, source_target_pairs={{1,2},{3,4},{5,6},{2,1},{4,3},{6,5},{9,10},{11,12},{13,14},{10,9},... | collective-permute-start | bytes 98312 | tf_op jit(solution)/shard_map/ppermute | solution.py:303
  6.3 0.1 collective-permute-start
  6.4 0.7 %collective-permute-start.1 = (f32[5,128,128]{2,1,0:T(8,128)S(1)}, f32[5,128,128]{2,1,0:T(8,128)S(1)}, u32[]{:S(2)}, u32[]{:S(2)}) collective-permute-start(f32[5,128,128]{2,1,0:T(8,128)S(1)} %get-tuple-element.10), channel_id=1, source_target_pairs={{8,16},{16,8},{9,17},{17,9},{10,18},{18,10},{11,19},{19,11},{12,20... | collective-permute-start | bytes 983048 | tf_op jit(solution)/shard_map/ppermute | solution.py:304
  7.1 0.0 collective-permute-done.2
  7.1 1.1 %collective-permute-done.3 = f32[8,8,128]{2,1,0:T(8,128)S(1)} collective-permute-done((f32[8,8,128]{2,1,0:T(8,128)S(1)}, f32[8,8,128]{2,1,0:T(8,128)S(1)}, u32[]{:S(2)}, u32[]{:S(2)}) %collective-permute-start.3) | collective-permute-done | bytes 32800 | tf_op jit(solution)/shard_map/ppermute | solution.py:303
  8.2 0.0 copy-start.6
  8.3 0.0 copy-start.2
  8.3 0.0 copy-start.3
  8.3 0.0 copy-start.5
  8.3 1.9 %collective-permute-start.4 = (f32[5,16,128]{2,1,0:T(8,128)S(1)}, f32[5,16,128]{2,1,0:T(8,128)S(1)}, u32[]{:S(2)}, u32[]{:S(2)}) collective-permute-start(f32[5,16,128]{2,1,0:T(8,128)S(1)} %get-tuple-element.14), channel_id=1, source_target_pairs={{0,8},{16,24},{8,0},{24,16},{1,9},{17,25},{9,1},{25,17},{2,10},{18... | collective-permute-start | bytes 122888 | tf_op jit(solution)/shard_map/ppermute | solution.py:313
  10.2 0.7 %collective-permute-start.5 = (f32[5,16,128]{2,1,0:T(8,128)S(1)}, f32[5,16,128]{2,1,0:T(8,128)S(1)}, u32[]{:S(2)}, u32[]{:S(2)}) collective-permute-start(f32[5,16,128]{2,1,0:T(8,128)S(1)} %get-tuple-element.13), channel_id=1, source_target_pairs={{8,16},{16,8},{9,17},{17,9},{10,18},{18,10},{11,19},{19,11},{12,20... | collective-permute-start | bytes 122888 | tf_op jit(solution)/shard_map/ppermute | solution.py:310
  10.8 0.2 collective-permute-done.4.corner_even_ref
  11.0 0.0 collective-permute-done.5.corner_odd_ref
  11.0 0.0 collective-permute-done.even_ref
  11.0 0.0 collective-permute-done.1.odd_ref
  11.0 0.0 copy-done.1
  11.0 0.0 copy-done.6
  11.1 3.1 %render.1 = s16[4,2,128,128]{3,2,1,0:T(8,128)(2,1)S(1)} custom-call(s32[4,8]{1,0:T(4,128)S(1)} %copy-done.2, f32[2]{0:T(128)S(1)} %copy-done.5, f32[3]{0:T(128)S(1)} %copy-done.6, s32[2,4]{1,0:T(2,128)S(1)} %copy-done.3, f32[8,128,128]{2,1,0:T(8,128)S(1)} %copy-done.1, f32[5,128,128]{2,1,0:T(8,128)S(1)} %collective-permute-done.even_ref, ...), custom_call_target="tpu_custom_call" | custom-call | tf_op jit(solution)/shard_map/render/pallas_call | solution.py:317
  14.2 0.0 copy-start.4
  14.2 12.8 %all_to_all.5.in_ref = s16[4,2,128,128]{3,2,1,0:T(8,128)(2,1)S(1)} all-to-all(s16[4,2,128,128]{3,2,1,0:T(8,128)(2,1)S(1)} %render.1), channel_id=1, replica_groups=mesh['gz'=4,'xy'=8] {'gz'}, dimensions={0} | all-to-all | bytes 524288 | tf_op jit(solution)/shard_map/all_to_all | solution.py:321
  27.0 1.4 %composite.1 = f32[2,4,1,32,128]{4,3,2,1,0:T(8,128)} custom-call(s32[2,4]{1,0:T(2,128)S(1)} %copy-done.4, s16[4,2,128,128]{3,2,1,0:T(8,128)(2,1)S(1)} %all_to_all.5.in_ref), custom_call_target="tpu_custom_call" | custom-call | tf_op jit(solution)/shard_map/composite/pallas_call | solution.py:323
  (9 shorter events, 0.0 us)
Async XLA Ops:
  0.0 1.0 %copy-start = (f32[8,128,128]{2,1,0:T(8,128)S(1)}, f32[8,128,128]{2,1,0:T(8,128)}, u32[]{:S(2)}) copy-start(f32[8,128,128]{2,1,0:T(8,128)} %own_ref.1) | copy-start | bytes 1572868
  1.0 10.0 %copy-start.1 = (f32[8,128,128]{2,1,0:T(8,128)S(1)}, f32[8,128,128]{2,1,0:T(8,128)}, u32[]{:S(2)}) copy-start(f32[8,128,128]{2,1,0:T(8,128)} %own_ref.1) | copy-start | bytes 1572868
  1.3 5.8 %collective-permute-start.2 = (f32[8,8,128]{2,1,0:T(8,128)S(1)}, f32[8,8,128]{2,1,0:T(8,128)S(1)}, u32[]{:S(2)}, u32[]{:S(2)}) collective-permute-start(f32[8,8,128]{2,1,0:T(8,128)S(1)} %get-tuple-element.11), channel_id=1, source_target_pairs={{0,1},{2,3},{4,5},{6,7},{1,0},{3,2},{5,4},{7,6},{8,9},{10,11},{12,... | collective-permute-start | bytes 98312 | tf_op jit(solution)/shard_map/ppermute | solution.py:302
  1.4 6.8 %collective-permute-start.3 = (f32[8,8,128]{2,1,0:T(8,128)S(1)}, f32[8,8,128]{2,1,0:T(8,128)S(1)}, u32[]{:S(2)}, u32[]{:S(2)}) collective-permute-start(f32[8,8,128]{2,1,0:T(8,128)S(1)} %get-tuple-element.12), channel_id=1, source_target_pairs={{1,2},{3,4},{5,6},{2,1},{4,3},{6,5},{9,10},{11,12},{13,14},{10,9},... | collective-permute-start | bytes 98312 | tf_op jit(solution)/shard_map/ppermute | solution.py:303
  6.3 4.7 %collective-permute-start = (f32[5,128,128]{2,1,0:T(8,128)S(1)}, f32[5,128,128]{2,1,0:T(8,128)S(1)}, u32[]{:S(2)}, u32[]{:S(2)}) collective-permute-start(f32[5,128,128]{2,1,0:T(8,128)S(1)} %get-tuple-element.9), channel_id=1, source_target_pairs={{0,8},{16,24},{8,0},{24,16},{1,9},{17,25},{9,1},{25,17},{2,10},{18... | collective-permute-start | bytes 983048 | tf_op jit(solution)/shard_map/ppermute | solution.py:305
  6.4 4.6 %collective-permute-start.1 = (f32[5,128,128]{2,1,0:T(8,128)S(1)}, f32[5,128,128]{2,1,0:T(8,128)S(1)}, u32[]{:S(2)}, u32[]{:S(2)}) collective-permute-start(f32[5,128,128]{2,1,0:T(8,128)S(1)} %get-tuple-element.10), channel_id=1, source_target_pairs={{8,16},{16,8},{9,17},{17,9},{10,18},{18,10},{11,19},{19,11},{12,20... | collective-permute-start | bytes 983048 | tf_op jit(solution)/shard_map/ppermute | solution.py:304
  8.2 2.8 %copy-start.6 = (f32[3]{0:T(128)S(1)}, f32[3]{0:T(128)}, u32[]{:S(2)}) copy-start(f32[3]{0:T(128)} %palette_ref.1) | copy-start | bytes 40
  8.3 2.8 %copy-start.2 = (s32[4,8]{1,0:T(4,128)S(1)}, s32[4,8]{1,0:T(4,128)}, u32[]{:S(2)}) copy-start(s32[4,8]{1,0:T(4,128)} %live_ref.1) | copy-start | bytes 388
  8.3 2.8 %copy-start.3 = (s32[2,4]{1,0:T(2,128)S(1)}, s32[2,4]{1,0:T(2,128)}, u32[]{:S(2)}) copy-start(s32[2,4]{1,0:T(2,128)} %owner_ref.1) | copy-start | bytes 100
  8.3 2.8 %copy-start.5 = (f32[2]{0:T(128)S(1)}, f32[2]{0:T(128)}, u32[]{:S(2)}) copy-start(f32[2]{0:T(128)} %slopes_ref.1) | copy-start | bytes 28
  8.3 2.7 %collective-permute-start.4 = (f32[5,16,128]{2,1,0:T(8,128)S(1)}, f32[5,16,128]{2,1,0:T(8,128)S(1)}, u32[]{:S(2)}, u32[]{:S(2)}) collective-permute-start(f32[5,16,128]{2,1,0:T(8,128)S(1)} %get-tuple-element.14), channel_id=1, source_target_pairs={{0,8},{16,24},{8,0},{24,16},{1,9},{17,25},{9,1},{25,17},{2,10},{18... | collective-permute-start | bytes 122888 | tf_op jit(solution)/shard_map/ppermute | solution.py:313
  10.2 0.9 %collective-permute-start.5 = (f32[5,16,128]{2,1,0:T(8,128)S(1)}, f32[5,16,128]{2,1,0:T(8,128)S(1)}, u32[]{:S(2)}, u32[]{:S(2)}) collective-permute-start(f32[5,16,128]{2,1,0:T(8,128)S(1)} %get-tuple-element.13), channel_id=1, source_target_pairs={{8,16},{16,8},{9,17},{17,9},{10,18},{18,10},{11,19},{19,11},{12,20... | collective-permute-start | bytes 122888 | tf_op jit(solution)/shard_map/ppermute | solution.py:310
  14.2 12.8 %copy-start.4 = (s32[2,4]{1,0:T(2,128)S(1)}, s32[2,4]{1,0:T(2,128)}, u32[]{:S(2)}) copy-start(s32[2,4]{1,0:T(2,128)} %order_ref.1) | copy-start | bytes 100

commit v8 on v7

--- a/solution.py
+++ b/solution.py
@@ -49,6 +49,54 @@
     return [sums[i] + layers[i + width] for i in range(len(layers) - width)]
 
 
+def depth_sums(even, middle, odd, odd_depth):
+    low = [jnp.where(odd_depth, e, o) for e, o in zip(even, odd)]
+    high = [jnp.where(odd_depth, o, e) for e, o in zip(even, odd)]
+    return window_sums(low + middle + high, TAPS)
+
+
+def prepare(shear_slopes, density, deep_even, deep_odd, n_depth):
+    depth_cells, row_cells, columns = density.shape
+    total_depth = depth_cells * n_depth
+
+    def kernel(slopes_ref, own_ref, even_ref, odd_ref, deep_ref, shear_ref):
+        depth_index = lax.axis_index("gz")
+        odd_depth = depth_index % 2 == 1
+        for start in range(0, row_cells, ROW_TILE):
+            rows = pl.ds(start, ROW_TILE)
+            even = [even_ref[i, rows] for i in range(HALO)]
+            odd = [odd_ref[i, rows] for i in range(HALO)]
+            middle = [own_ref[i, rows] for i in range(depth_cells)]
+            for z, total in enumerate(depth_sums(even, middle, odd, odd_depth)):
+                deep_ref[z, rows] = total
+        slab_start = (depth_index * depth_cells).astype(jnp.float32)
+        for z in range(depth_cells):
+            shear_ref[z] = shear_matrices(
+                slopes_ref, slab_start + float(z), columns, total_depth
+            )
+
+    smem = pl.BlockSpec(memory_space=pltpu.SMEM)
+    vmem = pl.BlockSpec(memory_space=pltpu.VMEM)
+    layers = depth_cells + 2
+    plane = row_cells * columns
+    return pl.pallas_call(
+        kernel,
+        out_shape=(
+            jax.ShapeDtypeStruct((layers, row_cells, columns), jnp.float32),
+            jax.ShapeDtypeStruct((depth_cells, columns, VIEWS * columns), jnp.bfloat16),
+        ),
+        in_specs=[smem] + [vmem] * 3,
+        out_specs=(vmem, vmem),
+        compiler_params=pltpu.CompilerParams(vmem_limit_bytes=VMEM_BYTES),
+        cost_estimate=pl.CostEstimate(
+            flops=6 * layers * plane,
+            bytes_accessed=4 * plane * (2 * layers + 2 * HALO + depth_cells),
+            transcendentals=0,
+        ),
+        name="prepare",
+    )(shear_slopes, density, deep_even, deep_odd)
+
+
 def encode(value):
     root = jnp.exp(0.125 * jnp.log(jnp.maximum(value, 1e-30) * (1.0 / TOP)))
     level = jnp.minimum(root * STEPS + 0.5, STEPS)
@@ -73,8 +121,8 @@
     floor = 0.01 * (2.0 * cells) ** 2
 
     def kernel(
-        live_ref, slopes_ref, palette_ref, owner_ref,
-        own_ref, even_ref, odd_ref, corner_even_ref, corner_odd_ref, rlo_ref, rhi_ref,
+        live_ref, palette_ref, owner_ref,
+        deep_ref, shear_ref, corner_even_ref, corner_odd_ref, rlo_ref, rhi_ref,
         out_ref,
         deep, triple, smooth, across, sheared,
     ):
@@ -82,23 +130,14 @@
         row_index = lax.axis_index("xy")
         odd_depth = depth_index % 2 == 1
 
-        for chunk in range(padded_rows // ROW_TILE):
-            rows = pl.ds(chunk * ROW_TILE, ROW_TILE)
-            inner = pl.ds((chunk - 1) * ROW_TILE, ROW_TILE)
-            if chunk == 0:
-                at, pair, mid_ref = pl.ds(0, ROW_TILE), (corner_even_ref, corner_odd_ref), rlo_ref
-            elif chunk == padded_rows // ROW_TILE - 1:
-                at = pl.ds(ROW_TILE, ROW_TILE)
-                pair, mid_ref = (corner_even_ref, corner_odd_ref), rhi_ref
-            else:
-                at, pair, mid_ref = inner, (even_ref, odd_ref), own_ref
-            mid_at = at if mid_ref is own_ref else pl.ds(0, ROW_TILE)
-            even, odd = [[ref[i, at] for i in range(HALO)] for ref in pair]
-            mid = [mid_ref[i, mid_at] for i in range(depth_cells)]
-            low = [jnp.where(odd_depth, e, o) for e, o in zip(even, odd)]
-            high = [jnp.where(odd_depth, o, e) for e, o in zip(even, odd)]
-            for z, total in enumerate(window_sums(low + mid + high, TAPS)):
-                deep[z, rows] = total
+        deep[:, pl.ds(first, row_cells)] = deep_ref[...]
+        for at, mid_ref in ((0, rlo_ref), (ROW_TILE, rhi_ref)):
+            even = [corner_even_ref[i, pl.ds(at, ROW_TILE)] for i in range(HALO)]
+            odd = [corner_odd_ref[i, pl.ds(at, ROW_TILE)] for i in range(HALO)]
+            middle = [mid_ref[i] for i in range(depth_cells)]
+            row = 0 if at == 0 else last
+            for z, total in enumerate(depth_sums(even, middle, odd, odd_depth)):
+                deep[z, pl.ds(row, ROW_TILE)] = total
 
         band = column_matrix(columns)
         weights = jnp.concatenate([band, band, band], axis=0)
@@ -149,7 +188,6 @@
             smooth[depth_cells + 1] = jnp.zeros((padded_rows, columns), jnp.float32)
 
         own_live = live_ref[depth_index, row_index]
-        slab_start = (depth_index * depth_cells).astype(jnp.float32)
         for z in range(depth_cells):
             center = smooth[z + 1, pl.ds(first, row_cells)]
             diff_depth = (
@@ -174,8 +212,7 @@
                 + [opacity.astype(jnp.bfloat16)],
                 axis=0,
             )
-            matrix = shear_matrices(slopes_ref, slab_start + float(z), columns, total_depth)
-            sheared[z] = jnp.dot(rgba, matrix, preferred_element_type=jnp.float32)
+            sheared[z] = jnp.dot(rgba, shear_ref[z], preferred_element_type=jnp.float32)
 
         for tile in range(n_depth):
             place = [owner_ref[view, tile] for view in range(VIEWS)]
@@ -213,7 +250,7 @@
     return pl.pallas_call(
         kernel,
         out_shape=jax.ShapeDtypeStruct((n_depth, VIEWS, 4 * tile_rows, columns), jnp.int16),
-        in_specs=[smem] * 4 + [vmem] * 7,
+        in_specs=[smem] * 3 + [vmem] * 6,
         out_specs=vmem,
         scratch_shapes=[
             pltpu.VMEM((depth_cells + 2, padded_rows, columns), jnp.float32),
@@ -314,9 +351,9 @@
         jnp.where(odd_depth, low_corner, high_corner), "gz", pairs("gz", 0)
     )
     render = make_render(n_depth, n_rows, depth_cells, row_cells, columns)
+    deep, shear = prepare(shear_slopes, density, deep_even, deep_odd, n_depth)
     outgoing = render(
-        live_slices, shear_slopes, palette, tile_owner,
-        density, deep_even, deep_odd, corner_even, corner_odd, rlo, rhi,
+        live_slices, palette, tile_owner, deep, shear, corner_even, corner_odd, rlo, rhi
     )
     incoming = lax.all_to_all(outgoing, "gz", split_axis=0, concat_axis=0, tiled=True)
     tile_rows = row_cells // n_depth

time: 28.7 us -> 29.4 us (1.024)
  local copies, waits for them, and re-layouts: 1.08 us -> 1.74 us
  Pallas kernels: 4.73 us -> 5.25 us
    unnamed x14, local copies, waits for them, and re-layouts: 1.08 us -> 1.73 us
    pallas_call x1 -> x2, Pallas kernels: 3.11 us -> 3.64 us  [the longest x1 2.8 us: body(): render(live_slices, palette, tile_owner, deep, shear, corner_even, corner...]
  transfers between devices with their start and end apart: 6 -> 6, of which waited for: 2 -> 1; matrix products, arithmetic and copies ran while one was open for 0% -> 0% of each run, Pallas kernels for 0% -> 3%
where the time goes in v8:
time: 29.4 us; the launch traced here: 29.2 us
  blocking collectives  12.6 us (43%)
  starting transfers between devices  8.26 us (28%)
  Pallas kernels  5.25 us (18%)
  local copies, waits for them, and re-layouts  1.74 us (6%)
  waiting for transfers between devices  1.09 us (4%)
    all_to_all x1, blocking collectives, body(): lax.all_to_all(outgoing, 'gz', split_axis=0, concat_axis=0, tiled=True)  12.6 us
    ppermute x1, starting transfers between devices, body(): row_odd = lax.ppermute(row_odd, 'xy', pairs('xy', 1))  4.92 us
    pallas_call x1, Pallas kernels, body(): render(live_slices, palette, tile_owner, deep, shear, corner_even, corner...  2.8 us
    ppermute x1, starting transfers between devices, body(): lax.ppermute(jnp.where(odd_depth, low_corner, high_corner), 'gz', pairs('...  1.86 us
    unnamed x14, local copies, waits for them, and re-layouts  1.73 us
    pallas_call x1, Pallas kernels, body(): pl.pallas_call(composite_kernel, out_shape=jax.ShapeDtypeStruct((VIEWS, 4...  1.36 us
    ppermute x1, waiting for transfers between devices, body(): row_odd = lax.ppermute(row_odd, 'xy', pairs('xy', 1))  1.08 us
    pallas_call x1, Pallas kernels, prepare(): pl.pallas_call(kernel, out_shape=(jax.ShapeDtypeStruct((layers, row_cells...  0.84 us
  transfers between devices with their start and end apart: 6, of which 1 were waited for; matrix products, arithmetic and copies ran while one was open for 0% of the time, Pallas kernels for 3%

profile of v8, /device:TPU:2, one launch (start us, length us, event | category | flops | bytes accessed | tf_op | source)
XLA Modules:
  0.0 29.2 jit_solution(16214264017481041680)
XLA Ops:
  0.0 1.0 %copy-done = f32[8,128,128]{2,1,0:T(8,128)S(1)} copy-done((f32[8,128,128]{2,1,0:T(8,128)S(1)}, f32[8,128,128]{2,1,0:T(8,128)}, u32[]{:S(2)}) %copy-start) | copy-done | bytes 524312
  1.0 0.3 cut_edges.1
  1.3 0.1 collective-permute-start.2
  1.4 4.9 %collective-permute-start.3 = (f32[8,8,128]{2,1,0:T(8,128)S(1)}, f32[8,8,128]{2,1,0:T(8,128)S(1)}, u32[]{:S(2)}, u32[]{:S(2)}) collective-permute-start(f32[8,8,128]{2,1,0:T(8,128)S(1)} %get-tuple-element.16), channel_id=1, source_target_pairs={{1,2},{3,4},{5,6},{2,1},{4,3},{6,5},{9,10},{11,12},{13,14},{10,9},... | collective-permute-start | bytes 98312 | tf_op jit(solution)/shard_map/ppermute | solution.py:340
  6.3 0.1 collective-permute-start
  6.4 0.7 %collective-permute-start.1 = (f32[5,128,128]{2,1,0:T(8,128)S(1)}, f32[5,128,128]{2,1,0:T(8,128)S(1)}, u32[]{:S(2)}, u32[]{:S(2)}) collective-permute-start(f32[5,128,128]{2,1,0:T(8,128)S(1)} %get-tuple-element.12), channel_id=1, source_target_pairs={{8,16},{16,8},{9,17},{17,9},{10,18},{18,10},{11,19},{19,11},{12,20... | collective-permute-start | bytes 983048 | tf_op jit(solution)/shard_map/ppermute | solution.py:341
  7.1 0.0 collective-permute-done.2
  7.1 1.1 %collective-permute-done.3 = f32[8,8,128]{2,1,0:T(8,128)S(1)} collective-permute-done((f32[8,8,128]{2,1,0:T(8,128)S(1)}, f32[8,8,128]{2,1,0:T(8,128)S(1)}, u32[]{:S(2)}, u32[]{:S(2)}) %collective-permute-start.3) | collective-permute-done | bytes 32800 | tf_op jit(solution)/shard_map/ppermute | solution.py:340
  8.2 0.0 copy-start.6
  8.3 1.9 %collective-permute-start.4 = (f32[5,16,128]{2,1,0:T(8,128)S(1)}, f32[5,16,128]{2,1,0:T(8,128)S(1)}, u32[]{:S(2)}, u32[]{:S(2)}) collective-permute-start(f32[5,16,128]{2,1,0:T(8,128)S(1)} %get-tuple-element.18), channel_id=1, source_target_pairs={{0,8},{16,24},{8,0},{24,16},{1,9},{17,25},{9,1},{25,17},{2,10},{18... | collective-permute-start | bytes 122888 | tf_op jit(solution)/shard_map/ppermute | solution.py:350
  10.1 0.7 %collective-permute-start.5 = (f32[5,16,128]{2,1,0:T(8,128)S(1)}, f32[5,16,128]{2,1,0:T(8,128)S(1)}, u32[]{:S(2)}, u32[]{:S(2)}) collective-permute-start(f32[5,16,128]{2,1,0:T(8,128)S(1)} %get-tuple-element.17), channel_id=1, source_target_pairs={{8,16},{16,8},{9,17},{17,9},{10,18},{18,10},{11,19},{19,11},{12,20... | collective-permute-start | bytes 122888 | tf_op jit(solution)/shard_map/ppermute | solution.py:347
  10.8 0.0 collective-permute-done.even_ref
  10.8 0.0 collective-permute-done.1.odd_ref
  10.8 0.8 %prepare.1 = (f32[10,128,128]{2,1,0:T(8,128)S(1)}, bf16[8,128,256]{2,1,0:T(8,128)(2,1)S(1)}) custom-call(f32[2]{0:T(128)S(1)} %copy-done.6, f32[8,128,128]{2,1,0:T(8,128)S(1)} %copy-done.1, f32[5,128,128]{2,1,0:T(8,128)S(1)} %collective-permute-done.even_ref, f32[5,128,128]{2,1,0:T(8,128)S(1)} %collective-permute-done.1.odd_ref), custom_call_target="tpu_custom_call" | custom-call | flops 983040 | bytes 2490368 | tf_op jit(solution)/shard_map/prepare/pallas_call | solution.py:82
  11.7 0.0 copy-start.2
  11.7 0.0 collective-permute-done.5.corner_odd_ref
  11.7 0.0 copy-start.3
  11.7 0.0 copy-start.5
  11.7 0.6 %copy-done.2 = s32[4,8]{1,0:T(4,128)S(1)} copy-done((s32[4,8]{1,0:T(4,128)S(1)}, s32[4,8]{1,0:T(4,128)}, u32[]{:S(2)}) %copy-start.2) | copy-done | bytes 152
  12.4 0.0 copy-done.3
  12.4 2.8 %render.1 = s16[4,2,128,128]{3,2,1,0:T(8,128)(2,1)S(1)} custom-call(s32[4,8]{1,0:T(4,128)S(1)} %copy-done.2, f32[3]{0:T(128)S(1)} %copy-done.5, s32[2,4]{1,0:T(2,128)S(1)} %copy-done.3, f32[10,128,128]{2,1,0:T(8,128)S(1)} %get-tuple-element.13.deep_ref, bf16[8,128,256]{2,1,0:T(8,128)(2,1)S(1)} %get-tuple-element.14.shear_ref, ...), custom_call_target="tpu_custom_call" | custom-call | tf_op jit(solution)/shard_map/render/pallas_call | solution.py:355
  15.2 0.0 copy-start.4
  15.2 12.6 %all_to_all.5.in_ref = s16[4,2,128,128]{3,2,1,0:T(8,128)(2,1)S(1)} all-to-all(s16[4,2,128,128]{3,2,1,0:T(8,128)(2,1)S(1)} %render.1), channel_id=1, replica_groups=mesh['gz'=4,'xy'=8] {'gz'}, dimensions={0} | all-to-all | bytes 524288 | tf_op jit(solution)/shard_map/all_to_all | solution.py:358
  27.8 1.4 %composite.1 = f32[2,4,1,32,128]{4,3,2,1,0:T(8,128)} custom-call(s32[2,4]{1,0:T(2,128)S(1)} %copy-done.4, s16[4,2,128,128]{3,2,1,0:T(8,128)(2,1)S(1)} %all_to_all.5.in_ref), custom_call_target="tpu_custom_call" | custom-call | tf_op jit(solution)/shard_map/composite/pallas_call | solution.py:360
  (10 shorter events, 0.0 us)
Async XLA Ops:
  0.0 1.0 %copy-start = (f32[8,128,128]{2,1,0:T(8,128)S(1)}, f32[8,128,128]{2,1,0:T(8,128)}, u32[]{:S(2)}) copy-start(f32[8,128,128]{2,1,0:T(8,128)} %own_ref.1) | copy-start | bytes 1572868
  1.0 9.8 %copy-start.1 = (f32[8,128,128]{2,1,0:T(8,128)S(1)}, f32[8,128,128]{2,1,0:T(8,128)}, u32[]{:S(2)}) copy-start(f32[8,128,128]{2,1,0:T(8,128)} %own_ref.1) | copy-start | bytes 1572868
  1.3 5.8 %collective-permute-start.2 = (f32[8,8,128]{2,1,0:T(8,128)S(1)}, f32[8,8,128]{2,1,0:T(8,128)S(1)}, u32[]{:S(2)}, u32[]{:S(2)}) collective-permute-start(f32[8,8,128]{2,1,0:T(8,128)S(1)} %get-tuple-element.15), channel_id=1, source_target_pairs={{0,1},{2,3},{4,5},{6,7},{1,0},{3,2},{5,4},{7,6},{8,9},{10,11},{12,... | collective-permute-start | bytes 98312 | tf_op jit(solution)/shard_map/ppermute | solution.py:339
  1.4 6.8 %collective-permute-start.3 = (f32[8,8,128]{2,1,0:T(8,128)S(1)}, f32[8,8,128]{2,1,0:T(8,128)S(1)}, u32[]{:S(2)}, u32[]{:S(2)}) collective-permute-start(f32[8,8,128]{2,1,0:T(8,128)S(1)} %get-tuple-element.16), channel_id=1, source_target_pairs={{1,2},{3,4},{5,6},{2,1},{4,3},{6,5},{9,10},{11,12},{13,14},{10,9},... | collective-permute-start | bytes 98312 | tf_op jit(solution)/shard_map/ppermute | solution.py:340
  6.3 4.5 %collective-permute-start = (f32[5,128,128]{2,1,0:T(8,128)S(1)}, f32[5,128,128]{2,1,0:T(8,128)S(1)}, u32[]{:S(2)}, u32[]{:S(2)}) collective-permute-start(f32[5,128,128]{2,1,0:T(8,128)S(1)} %get-tuple-element.11), channel_id=1, source_target_pairs={{0,8},{16,24},{8,0},{24,16},{1,9},{17,25},{9,1},{25,17},{2,10},{18... | collective-permute-start | bytes 983048 | tf_op jit(solution)/shard_map/ppermute | solution.py:342
  6.4 4.4 %collective-permute-start.1 = (f32[5,128,128]{2,1,0:T(8,128)S(1)}, f32[5,128,128]{2,1,0:T(8,128)S(1)}, u32[]{:S(2)}, u32[]{:S(2)}) collective-permute-start(f32[5,128,128]{2,1,0:T(8,128)S(1)} %get-tuple-element.12), channel_id=1, source_target_pairs={{8,16},{16,8},{9,17},{17,9},{10,18},{18,10},{11,19},{19,11},{12,20... | collective-permute-start | bytes 983048 | tf_op jit(solution)/shard_map/ppermute | solution.py:341
  8.2 2.6 %copy-start.6 = (f32[2]{0:T(128)S(1)}, f32[2]{0:T(128)}, u32[]{:S(2)}) copy-start(f32[2]{0:T(128)} %slopes_ref.1) | copy-start | bytes 28
  8.3 3.4 %collective-permute-start.4 = (f32[5,16,128]{2,1,0:T(8,128)S(1)}, f32[5,16,128]{2,1,0:T(8,128)S(1)}, u32[]{:S(2)}, u32[]{:S(2)}) collective-permute-start(f32[5,16,128]{2,1,0:T(8,128)S(1)} %get-tuple-element.18), channel_id=1, source_target_pairs={{0,8},{16,24},{8,0},{24,16},{1,9},{17,25},{9,1},{25,17},{2,10},{18... | collective-permute-start | bytes 122888 | tf_op jit(solution)/shard_map/ppermute | solution.py:350
  10.1 1.6 %collective-permute-start.5 = (f32[5,16,128]{2,1,0:T(8,128)S(1)}, f32[5,16,128]{2,1,0:T(8,128)S(1)}, u32[]{:S(2)}, u32[]{:S(2)}) collective-permute-start(f32[5,16,128]{2,1,0:T(8,128)S(1)} %get-tuple-element.17), channel_id=1, source_target_pairs={{8,16},{16,8},{9,17},{17,9},{10,18},{18,10},{11,19},{19,11},{12,20... | collective-permute-start | bytes 122888 | tf_op jit(solution)/shard_map/ppermute | solution.py:347
  11.7 0.7 %copy-start.2 = (s32[4,8]{1,0:T(4,128)S(1)}, s32[4,8]{1,0:T(4,128)}, u32[]{:S(2)}) copy-start(s32[4,8]{1,0:T(4,128)} %live_ref.1) | copy-start | bytes 388
  11.7 0.7 %copy-start.3 = (s32[2,4]{1,0:T(2,128)S(1)}, s32[2,4]{1,0:T(2,128)}, u32[]{:S(2)}) copy-start(s32[2,4]{1,0:T(2,128)} %owner_ref.1) | copy-start | bytes 100
  11.7 0.7 %copy-start.5 = (f32[3]{0:T(128)S(1)}, f32[3]{0:T(128)}, u32[]{:S(2)}) copy-start(f32[3]{0:T(128)} %palette_ref.1) | copy-start | bytes 40
  15.2 12.6 %copy-start.4 = (s32[2,4]{1,0:T(2,128)S(1)}, s32[2,4]{1,0:T(2,128)}, u32[]{:S(2)}) copy-start(s32[2,4]{1,0:T(2,128)} %order_ref.1) | copy-start | bytes 100

commit v9 on v7

--- a/solution.py
+++ b/solution.py
@@ -74,7 +74,7 @@
 
     def kernel(
         live_ref, slopes_ref, palette_ref, owner_ref,
-        own_ref, even_ref, odd_ref, corner_even_ref, corner_odd_ref, rlo_ref, rhi_ref,
+        own_ref, odd_ref, even_ref, corner_odd_ref, corner_even_ref, rlo_ref, rhi_ref,
         out_ref,
         deep, triple, smooth, across, sheared,
     ):
@@ -316,7 +316,7 @@
     render = make_render(n_depth, n_rows, depth_cells, row_cells, columns)
     outgoing = render(
         live_slices, shear_slopes, palette, tile_owner,
-        density, deep_even, deep_odd, corner_even, corner_odd, rlo, rhi,
+        density, deep_odd, deep_even, corner_odd, corner_even, rlo, rhi,
     )
     incoming = lax.all_to_all(outgoing, "gz", split_axis=0, concat_axis=0, tiled=True)
     tile_rows = row_cells // n_depth

time: 28.7 us -> 28.6 us (level)
  starting transfers between devices: 8.26 us -> 11 us
  blocking collectives: 12.8 us -> 10.5 us
  waiting for transfers between devices: 1.3 us -> 0.88 us
    ppermute x1, starting transfers between devices: 0.07 us -> 2.93 us  [body(): deep_even = lax.ppermute(deep_even, 'gz', pairs('gz', 0))]
    all_to_all x1, blocking collectives: 12.8 us -> 10.5 us  [body(): lax.all_to_all(outgoing, 'gz', split_axis=0, concat_axis=0, tiled=True)]
    ppermute x1, waiting for transfers between devices: 1.08 us -> 0.01 us  [body(): row_odd = lax.ppermute(row_odd, 'xy', pairs('xy', 1))]
    ppermute x1, waiting for transfers between devices: 0.21 us -> 0.87 us  [body(): lax.ppermute(jnp.where(odd_depth, low_corner, high_corner), 'gz', pairs('...]
  transfers between devices with their start and end apart: 6 -> 6, of which waited for: 2 -> 1; matrix products, arithmetic and copies ran while one was open for 0% -> 0% of each run, Pallas kernels for 0% -> 0%
where the time goes in v9:
time: 28.6 us; the launch traced here: 28.3 us
  starting transfers between devices  11 us (38%)
  blocking collectives  10.5 us (37%)
  Pallas kernels  4.72 us (17%)
  local copies, waits for them, and re-layouts  1.08 us (4%)
  waiting for transfers between devices  0.88 us (3%)
    all_to_all x1, blocking collectives, body(): lax.all_to_all(outgoing, 'gz', split_axis=0, concat_axis=0, tiled=True)  10.5 us
    ppermute x1, starting transfers between devices, body(): row_odd = lax.ppermute(row_odd, 'xy', pairs('xy', 1))  4.92 us
    pallas_call x1, Pallas kernels, body(): render(live_slices, shear_slopes, palette, tile_owner, density, deep_odd,...  3.11 us
    ppermute x1, starting transfers between devices, body(): deep_even = lax.ppermute(deep_even, 'gz', pairs('gz', 0))  2.93 us
    ppermute x1, starting transfers between devices, body(): lax.ppermute(jnp.where(odd_depth, low_corner, high_corner), 'gz', pairs('...  1.61 us
    pallas_call x1, Pallas kernels, body(): pl.pallas_call(composite_kernel, out_shape=jax.ShapeDtypeStruct((VIEWS, 4...  1.36 us
    unnamed x14, local copies, waits for them, and re-layouts  1.08 us
    ppermute x1, waiting for transfers between devices, body(): lax.ppermute(jnp.where(odd_depth, low_corner, high_corner), 'gz', pairs('...  0.87 us
  transfers between devices with their start and end apart: 6, of which 1 were waited for; matrix products, arithmetic and copies ran while one was open for 0% of the time, Pallas kernels for 0%

profile of v9, /device:TPU:2, one launch (start us, length us, event | category | flops | bytes accessed | tf_op | source)
XLA Modules:
  0.0 28.3 jit_solution(15355470918546608607)
XLA Ops:
  0.0 1.0 %copy-done = f32[8,128,128]{2,1,0:T(8,128)S(1)} copy-done((f32[8,128,128]{2,1,0:T(8,128)S(1)}, f32[8,128,128]{2,1,0:T(8,128)}, u32[]{:S(2)}) %copy-start) | copy-done | bytes 524312
  1.0 0.3 cut_edges.1
  1.3 0.1 collective-permute-start.2
  1.4 4.9 %collective-permute-start.3 = (f32[8,8,128]{2,1,0:T(8,128)S(1)}, f32[8,8,128]{2,1,0:T(8,128)S(1)}, u32[]{:S(2)}, u32[]{:S(2)}) collective-permute-start(f32[8,8,128]{2,1,0:T(8,128)S(1)} %get-tuple-element.12), channel_id=1, source_target_pairs={{1,2},{3,4},{5,6},{2,1},{4,3},{6,5},{9,10},{11,12},{13,14},{10,9},... | collective-permute-start | bytes 98312 | tf_op jit(solution)/shard_map/ppermute | solution.py:303
  6.3 0.7 %collective-permute-start = (f32[5,128,128]{2,1,0:T(8,128)S(1)}, f32[5,128,128]{2,1,0:T(8,128)S(1)}, u32[]{:S(2)}, u32[]{:S(2)}) collective-permute-start(f32[5,128,128]{2,1,0:T(8,128)S(1)} %get-tuple-element.9), channel_id=1, source_target_pairs={{8,16},{16,8},{9,17},{17,9},{10,18},{18,10},{11,19},{19,11},{12,20... | collective-permute-start | bytes 983048 | tf_op jit(solution)/shard_map/ppermute | solution.py:304
  7.0 2.9 %collective-permute-start.1 = (f32[5,128,128]{2,1,0:T(8,128)S(1)}, f32[5,128,128]{2,1,0:T(8,128)S(1)}, u32[]{:S(2)}, u32[]{:S(2)}) collective-permute-start(f32[5,128,128]{2,1,0:T(8,128)S(1)} %get-tuple-element.10), channel_id=1, source_target_pairs={{0,8},{16,24},{8,0},{24,16},{1,9},{17,25},{9,1},{25,17},{2,10},{18... | collective-permute-start | bytes 983048 | tf_op jit(solution)/shard_map/ppermute | solution.py:305
  9.9 0.0 collective-permute-done.2
  9.9 0.0 collective-permute-done.3
  10.0 0.0 copy-start.6
  10.0 0.0 copy-start.2
  10.0 0.0 copy-start.3
  10.0 0.0 copy-start.5
  10.0 0.8 %collective-permute-start.4 = (f32[5,16,128]{2,1,0:T(8,128)S(1)}, f32[5,16,128]{2,1,0:T(8,128)S(1)}, u32[]{:S(2)}, u32[]{:S(2)}) collective-permute-start(f32[5,16,128]{2,1,0:T(8,128)S(1)} %get-tuple-element.14), channel_id=1, source_target_pairs={{8,16},{16,8},{9,17},{17,9},{10,18},{18,10},{11,19},{19,11},{12,20... | collective-permute-start | bytes 122888 | tf_op jit(solution)/shard_map/ppermute | solution.py:310
  10.8 1.6 %collective-permute-start.5 = (f32[5,16,128]{2,1,0:T(8,128)S(1)}, f32[5,16,128]{2,1,0:T(8,128)S(1)}, u32[]{:S(2)}, u32[]{:S(2)}) collective-permute-start(f32[5,16,128]{2,1,0:T(8,128)S(1)} %get-tuple-element.13), channel_id=1, source_target_pairs={{0,8},{16,24},{8,0},{24,16},{1,9},{17,25},{9,1},{25,17},{2,10},{18... | collective-permute-start | bytes 122888 | tf_op jit(solution)/shard_map/ppermute | solution.py:313
  12.4 0.0 collective-permute-done.4.corner_odd_ref
  12.5 0.9 %collective-permute-done.5.corner_even_ref = f32[5,16,128]{2,1,0:T(8,128)S(1)} collective-permute-done((f32[5,16,128]{2,1,0:T(8,128)S(1)}, f32[5,16,128]{2,1,0:T(8,128)S(1)}, u32[]{:S(2)}, u32[]{:S(2)}) %collective-permute-start.5) | collective-permute-done | bytes 40992 | tf_op jit(solution)/shard_map/ppermute | solution.py:313
  13.3 0.0 collective-permute-done.odd_ref
  13.3 0.0 collective-permute-done.1.even_ref
  13.3 0.0 copy-done.1
  13.3 0.0 copy-done.6
  13.4 3.1 %render.1 = s16[4,2,128,128]{3,2,1,0:T(8,128)(2,1)S(1)} custom-call(s32[4,8]{1,0:T(4,128)S(1)} %copy-done.2, f32[2]{0:T(128)S(1)} %copy-done.5, f32[3]{0:T(128)S(1)} %copy-done.6, s32[2,4]{1,0:T(2,128)S(1)} %copy-done.3, f32[8,128,128]{2,1,0:T(8,128)S(1)} %copy-done.1, f32[5,128,128]{2,1,0:T(8,128)S(1)} %collective-permute-done.odd_ref, ...), custom_call_target="tpu_custom_call" | custom-call | tf_op jit(solution)/shard_map/render/pallas_call | solution.py:317
  16.5 0.0 copy-start.4
  16.5 10.5 %all_to_all.5.in_ref = s16[4,2,128,128]{3,2,1,0:T(8,128)(2,1)S(1)} all-to-all(s16[4,2,128,128]{3,2,1,0:T(8,128)(2,1)S(1)} %render.1), channel_id=1, replica_groups=mesh['gz'=4,'xy'=8] {'gz'}, dimensions={0} | all-to-all | bytes 524288 | tf_op jit(solution)/shard_map/all_to_all | solution.py:321
  27.0 1.4 %composite.1 = f32[2,4,1,32,128]{4,3,2,1,0:T(8,128)} custom-call(s32[2,4]{1,0:T(2,128)S(1)} %copy-done.4, s16[4,2,128,128]{3,2,1,0:T(8,128)(2,1)S(1)} %all_to_all.5.in_ref), custom_call_target="tpu_custom_call" | custom-call | tf_op jit(solution)/shard_map/composite/pallas_call | solution.py:323
  (9 shorter events, 0.0 us)
Async XLA Ops:
  0.0 1.0 %copy-start = (f32[8,128,128]{2,1,0:T(8,128)S(1)}, f32[8,128,128]{2,1,0:T(8,128)}, u32[]{:S(2)}) copy-start(f32[8,128,128]{2,1,0:T(8,128)} %own_ref.1) | copy-start | bytes 1572868
  1.0 12.3 %copy-start.1 = (f32[8,128,128]{2,1,0:T(8,128)S(1)}, f32[8,128,128]{2,1,0:T(8,128)}, u32[]{:S(2)}) copy-start(f32[8,128,128]{2,1,0:T(8,128)} %own_ref.1) | copy-start | bytes 1572868
  1.3 8.6 %collective-permute-start.2 = (f32[8,8,128]{2,1,0:T(8,128)S(1)}, f32[8,8,128]{2,1,0:T(8,128)S(1)}, u32[]{:S(2)}, u32[]{:S(2)}) collective-permute-start(f32[8,8,128]{2,1,0:T(8,128)S(1)} %get-tuple-element.11), channel_id=1, source_target_pairs={{0,1},{2,3},{4,5},{6,7},{1,0},{3,2},{5,4},{7,6},{8,9},{10,11},{12,... | collective-permute-start | bytes 98312 | tf_op jit(solution)/shard_map/ppermute | solution.py:302
  1.4 8.6 %collective-permute-start.3 = (f32[8,8,128]{2,1,0:T(8,128)S(1)}, f32[8,8,128]{2,1,0:T(8,128)S(1)}, u32[]{:S(2)}, u32[]{:S(2)}) collective-permute-start(f32[8,8,128]{2,1,0:T(8,128)S(1)} %get-tuple-element.12), channel_id=1, source_target_pairs={{1,2},{3,4},{5,6},{2,1},{4,3},{6,5},{9,10},{11,12},{13,14},{10,9},... | collective-permute-start | bytes 98312 | tf_op jit(solution)/shard_map/ppermute | solution.py:303
  6.3 7.0 %collective-permute-start = (f32[5,128,128]{2,1,0:T(8,128)S(1)}, f32[5,128,128]{2,1,0:T(8,128)S(1)}, u32[]{:S(2)}, u32[]{:S(2)}) collective-permute-start(f32[5,128,128]{2,1,0:T(8,128)S(1)} %get-tuple-element.9), channel_id=1, source_target_pairs={{8,16},{16,8},{9,17},{17,9},{10,18},{18,10},{11,19},{19,11},{12,20... | collective-permute-start | bytes 983048 | tf_op jit(solution)/shard_map/ppermute | solution.py:304
  7.0 6.3 %collective-permute-start.1 = (f32[5,128,128]{2,1,0:T(8,128)S(1)}, f32[5,128,128]{2,1,0:T(8,128)S(1)}, u32[]{:S(2)}, u32[]{:S(2)}) collective-permute-start(f32[5,128,128]{2,1,0:T(8,128)S(1)} %get-tuple-element.10), channel_id=1, source_target_pairs={{0,8},{16,24},{8,0},{24,16},{1,9},{17,25},{9,1},{25,17},{2,10},{18... | collective-permute-start | bytes 983048 | tf_op jit(solution)/shard_map/ppermute | solution.py:305
  10.0 3.4 %copy-start.6 = (f32[3]{0:T(128)S(1)}, f32[3]{0:T(128)}, u32[]{:S(2)}) copy-start(f32[3]{0:T(128)} %palette_ref.1) | copy-start | bytes 40
  10.0 3.3 %copy-start.2 = (s32[4,8]{1,0:T(4,128)S(1)}, s32[4,8]{1,0:T(4,128)}, u32[]{:S(2)}) copy-start(s32[4,8]{1,0:T(4,128)} %live_ref.1) | copy-start | bytes 388
  10.0 3.3 %copy-start.3 = (s32[2,4]{1,0:T(2,128)S(1)}, s32[2,4]{1,0:T(2,128)}, u32[]{:S(2)}) copy-start(s32[2,4]{1,0:T(2,128)} %owner_ref.1) | copy-start | bytes 100
  10.0 3.3 %copy-start.5 = (f32[2]{0:T(128)S(1)}, f32[2]{0:T(128)}, u32[]{:S(2)}) copy-start(f32[2]{0:T(128)} %slopes_ref.1) | copy-start | bytes 28
  10.0 2.4 %collective-permute-start.4 = (f32[5,16,128]{2,1,0:T(8,128)S(1)}, f32[5,16,128]{2,1,0:T(8,128)S(1)}, u32[]{:S(2)}, u32[]{:S(2)}) collective-permute-start(f32[5,16,128]{2,1,0:T(8,128)S(1)} %get-tuple-element.14), channel_id=1, source_target_pairs={{8,16},{16,8},{9,17},{17,9},{10,18},{18,10},{11,19},{19,11},{12,20... | collective-permute-start | bytes 122888 | tf_op jit(solution)/shard_map/ppermute | solution.py:310
  10.8 2.5 %collective-permute-start.5 = (f32[5,16,128]{2,1,0:T(8,128)S(1)}, f32[5,16,128]{2,1,0:T(8,128)S(1)}, u32[]{:S(2)}, u32[]{:S(2)}) collective-permute-start(f32[5,16,128]{2,1,0:T(8,128)S(1)} %get-tuple-element.13), channel_id=1, source_target_pairs={{0,8},{16,24},{8,0},{24,16},{1,9},{17,25},{9,1},{25,17},{2,10},{18... | collective-permute-start | bytes 122888 | tf_op jit(solution)/shard_map/ppermute | solution.py:313
  16.5 10.5 %copy-start.4 = (s32[2,4]{1,0:T(2,128)S(1)}, s32[2,4]{1,0:T(2,128)}, u32[]{:S(2)}) copy-start(s32[2,4]{1,0:T(2,128)} %order_ref.1) | copy-start | bytes 100

commit v10 on v9

--- a/solution.py
+++ b/solution.py
@@ -74,7 +74,7 @@
 
     def kernel(
         live_ref, slopes_ref, palette_ref, owner_ref,
-        own_ref, odd_ref, even_ref, corner_odd_ref, corner_even_ref, rlo_ref, rhi_ref,
+        own_ref, odd_first_ref, odd_second_ref, even_ref, corner_odd_ref, corner_even_ref, rlo_ref, rhi_ref,
         out_ref,
         deep, triple, smooth, across, sheared,
     ):
@@ -91,9 +91,16 @@
                 at = pl.ds(ROW_TILE, ROW_TILE)
                 pair, mid_ref = (corner_even_ref, corner_odd_ref), rhi_ref
             else:
-                at, pair, mid_ref = inner, (even_ref, odd_ref), own_ref
+                at, pair, mid_ref = inner, (even_ref, None), own_ref
             mid_at = at if mid_ref is own_ref else pl.ds(0, ROW_TILE)
-            even, odd = [[ref[i, at] for i in range(HALO)] for ref in pair]
+            even = [pair[0][i, at] for i in range(HALO)]
+            if pair[1] is None:
+                start = (chunk - 1) * ROW_TILE
+                odd_ref = odd_first_ref if start < row_cells // 2 else odd_second_ref
+                part = pl.ds(start % (row_cells // 2), ROW_TILE)
+                odd = [odd_ref[i, part] for i in range(HALO)]
+            else:
+                odd = [pair[1][i, at] for i in range(HALO)]
             mid = [mid_ref[i, mid_at] for i in range(depth_cells)]
             low = [jnp.where(odd_depth, e, o) for e, o in zip(even, odd)]
             high = [jnp.where(odd_depth, o, e) for e, o in zip(even, odd)]
@@ -213,7 +220,7 @@
     return pl.pallas_call(
         kernel,
         out_shape=jax.ShapeDtypeStruct((n_depth, VIEWS, 4 * tile_rows, columns), jnp.int16),
-        in_specs=[smem] * 4 + [vmem] * 7,
+        in_specs=[smem] * 4 + [vmem] * 8,
         out_specs=vmem,
         scratch_shapes=[
             pltpu.VMEM((depth_cells + 2, padded_rows, columns), jnp.float32),
@@ -230,7 +237,9 @@
 def cut_edges(density):
     depth_cells, row_cells, columns = density.shape
 
-    def kernel(density_ref, row_even_ref, row_odd_ref, deep_even_ref, deep_odd_ref, sems):
+    half = row_cells // 2
+
+    def kernel(density_ref, row_even_ref, row_odd_ref, deep_even_ref, first_ref, second_ref, sems):
         row_bit = lax.axis_index("xy") % 2
         depth_bit = lax.axis_index("gz") % 2
         last_rows, last_deep = row_cells - ROW_TILE, depth_cells - HALO
@@ -238,12 +247,13 @@
         def rows(bit):
             return density_ref.at[:, pl.ds(pl.multiple_of(bit * last_rows, ROW_TILE), ROW_TILE)]
 
-        def deep(bit):
-            return density_ref.at[pl.ds(bit * last_deep, HALO)]
+        def deep(bit, start, size):
+            return density_ref.at[pl.ds(bit * last_deep, HALO), pl.ds(start, size)]
 
         copies = [
-            pltpu.make_async_copy(deep(depth_bit), deep_odd_ref, sems.at[0]),
-            pltpu.make_async_copy(deep(1 - depth_bit), deep_even_ref, sems.at[1]),
+            pltpu.make_async_copy(deep(depth_bit, 0, half), first_ref, sems.at[0]),
+            pltpu.make_async_copy(deep(depth_bit, half, half), second_ref, sems.at[4]),
+            pltpu.make_async_copy(deep(1 - depth_bit, 0, row_cells), deep_even_ref, sems.at[1]),
             pltpu.make_async_copy(rows(1 - row_bit), row_even_ref, sems.at[2]),
             pltpu.make_async_copy(rows(row_bit), row_odd_ref, sems.at[3]),
         ]
@@ -254,12 +264,13 @@
 
     rows = jax.ShapeDtypeStruct((depth_cells, ROW_TILE, columns), jnp.float32)
     deep = jax.ShapeDtypeStruct((HALO, row_cells, columns), jnp.float32)
+    part = jax.ShapeDtypeStruct((HALO, half, columns), jnp.float32)
     return pl.pallas_call(
         kernel,
-        out_shape=(rows, rows, deep, deep),
+        out_shape=(rows, rows, deep, part, part),
         in_specs=[pl.BlockSpec(memory_space=pltpu.HBM)],
-        out_specs=(pl.BlockSpec(memory_space=pltpu.VMEM),) * 4,
-        scratch_shapes=[pltpu.SemaphoreType.DMA((4,))],
+        out_specs=(pl.BlockSpec(memory_space=pltpu.VMEM),) * 5,
+        scratch_shapes=[pltpu.SemaphoreType.DMA((5,))],
         compiler_params=pltpu.CompilerParams(vmem_limit_bytes=VMEM_BYTES),
         name="cut_edges",
     )(density)
@@ -298,10 +309,10 @@
         lower = range(first, count - 1, 2)
         return [(i, i + 1) for i in lower] + [(i + 1, i) for i in lower]
 
-    row_even, row_odd, deep_even, deep_odd = cut_edges(density)
+    row_even, row_odd, deep_even, *deep_odd = cut_edges(density)
     row_even = lax.ppermute(row_even, "xy", pairs("xy", 0))
     row_odd = lax.ppermute(row_odd, "xy", pairs("xy", 1))
-    deep_odd = lax.ppermute(deep_odd, "gz", pairs("gz", 1))
+    deep_odd = [lax.ppermute(part, "gz", pairs("gz", 1)) for part in deep_odd]
     deep_even = lax.ppermute(deep_even, "gz", pairs("gz", 0))
     rlo = jnp.where(odd_row, row_even, row_odd)
     rhi = jnp.where(odd_row, row_odd, row_even)
@@ -316,7 +327,7 @@
     render = make_render(n_depth, n_rows, depth_cells, row_cells, columns)
     outgoing = render(
         live_slices, shear_slopes, palette, tile_owner,
-        density, deep_odd, deep_even, corner_odd, corner_even, rlo, rhi,
+        density, *deep_odd, deep_even, corner_odd, corner_even, rlo, rhi,
     )
     incoming = lax.all_to_all(outgoing, "gz", split_axis=0, concat_axis=0, tiled=True)
     tile_rows = row_cells // n_depth

time: 28.6 us -> 31 us (1.084)
  starting transfers between devices: 11 us -> 14.4 us
  blocking collectives: 10.5 us -> 9.47 us
    ppermute x1, starting transfers between devices: 1.61 us -> 3.1 us  [body(): lax.ppermute(jnp.where(odd_depth, low_corner, high_corner), 'gz', pairs('...]
    ppermute x1, starting transfers between devices: 2.93 us -> 4.19 us  [body(): deep_even = lax.ppermute(deep_even, 'gz', pairs('gz', 0))]
    all_to_all x1, blocking collectives: 10.5 us -> 9.47 us  [body(): lax.all_to_all(outgoing, 'gz', split_axis=0, concat_axis=0, tiled=True)]
    ppermute x1 -> x2, starting transfers between devices: 0.68 us -> 1.34 us  [body(): deep_odd = [lax.ppermute(part, 'gz', pairs('gz', 1)) for part in deep_odd]]
  transfers between devices with their start and end apart: 6 -> 7, of which waited for: 1 -> 1; matrix products, arithmetic and copies ran while one was open for 0% -> 0% of each run, Pallas kernels for 0% -> 0%
where the time goes in v10:
time: 31 us; the launch traced here: 30.7 us
  starting transfers between devices  14.4 us (46%)
  blocking collectives  9.47 us (31%)
  Pallas kernels  4.72 us (15%)
  local copies, waits for them, and re-layouts  1.08 us (3%)
  waiting for transfers between devices  0.88 us (3%)
    all_to_all x1, blocking collectives, body(): lax.all_to_all(outgoing, 'gz', split_axis=0, concat_axis=0, tiled=True)  9.47 us
    ppermute x1, starting transfers between devices, body(): row_odd = lax.ppermute(row_odd, 'xy', pairs('xy', 1))  4.92 us
    ppermute x1, starting transfers between devices, body(): deep_even = lax.ppermute(deep_even, 'gz', pairs('gz', 0))  4.19 us
    pallas_call x1, Pallas kernels, body(): render(live_slices, shear_slopes, palette, tile_owner, density, *deep_odd...  3.11 us
    ppermute x1, starting transfers between devices, body(): lax.ppermute(jnp.where(odd_depth, low_corner, high_corner), 'gz', pairs('...  3.1 us
    pallas_call x1, Pallas kernels, body(): pl.pallas_call(composite_kernel, out_shape=jax.ShapeDtypeStruct((VIEWS, 4...  1.36 us
    ppermute x2, starting transfers between devices, body(): deep_odd = [lax.ppermute(part, 'gz', pairs('gz', 1)) for part in deep_odd]  1.34 us
    unnamed x14, local copies, waits for them, and re-layouts  1.08 us
  transfers between devices with their start and end apart: 7, of which 1 were waited for; matrix products, arithmetic and copies ran while one was open for 0% of the time, Pallas kernels for 0%

profile of v10, /device:TPU:2, one launch (start us, length us, event | category | flops | bytes accessed | tf_op | source)
XLA Modules:
  0.0 30.7 jit_solution(3321380426747035586)
XLA Ops:
  0.0 1.0 %copy-done = f32[8,128,128]{2,1,0:T(8,128)S(1)} copy-done((f32[8,128,128]{2,1,0:T(8,128)S(1)}, f32[8,128,128]{2,1,0:T(8,128)}, u32[]{:S(2)}) %copy-start) | copy-done | bytes 524312
  1.0 0.2 cut_edges.1
  1.3 0.1 collective-permute-start.3
  1.4 4.9 %collective-permute-start.4 = (f32[8,8,128]{2,1,0:T(8,128)S(1)}, f32[8,8,128]{2,1,0:T(8,128)S(1)}, u32[]{:S(2)}, u32[]{:S(2)}) collective-permute-start(f32[8,8,128]{2,1,0:T(8,128)S(1)} %get-tuple-element.14), channel_id=1, source_target_pairs={{1,2},{3,4},{5,6},{2,1},{4,3},{6,5},{9,10},{11,12},{13,14},{10,9},... | collective-permute-start | bytes 98312 | tf_op jit(solution)/shard_map/ppermute | solution.py:314
  6.3 0.7 %collective-permute-start = (f32[5,64,128]{2,1,0:T(8,128)S(1)}, f32[5,64,128]{2,1,0:T(8,128)S(1)}, u32[]{:S(2)}, u32[]{:S(2)}) collective-permute-start(f32[5,64,128]{2,1,0:T(8,128)S(1)} %get-tuple-element.10), channel_id=1, source_target_pairs={{8,16},{16,8},{9,17},{17,9},{10,18},{18,10},{11,19},{19,11},{12,20... | collective-permute-start | bytes 491528 | tf_op jit(solution)/shard_map/ppermute | solution.py:315
  7.0 0.7 %collective-permute-start.1 = (f32[5,64,128]{2,1,0:T(8,128)S(1)}, f32[5,64,128]{2,1,0:T(8,128)S(1)}, u32[]{:S(2)}, u32[]{:S(2)}) collective-permute-start(f32[5,64,128]{2,1,0:T(8,128)S(1)} %get-tuple-element.11), channel_id=1, source_target_pairs={{8,16},{16,8},{9,17},{17,9},{10,18},{18,10},{11,19},{19,11},{12,20... | collective-permute-start | bytes 491528 | tf_op jit(solution)/shard_map/ppermute | solution.py:315
  7.7 4.2 %collective-permute-start.2 = (f32[5,128,128]{2,1,0:T(8,128)S(1)}, f32[5,128,128]{2,1,0:T(8,128)S(1)}, u32[]{:S(2)}, u32[]{:S(2)}) collective-permute-start(f32[5,128,128]{2,1,0:T(8,128)S(1)} %get-tuple-element.12), channel_id=1, source_target_pairs={{0,8},{16,24},{8,0},{24,16},{1,9},{17,25},{9,1},{25,17},{2,10},{18... | collective-permute-start | bytes 983048 | tf_op jit(solution)/shard_map/ppermute | solution.py:316
  11.9 0.0 collective-permute-done.3
  11.9 0.0 collective-permute-done.4
  11.9 0.0 copy-start.6
  11.9 0.0 copy-start.2
  11.9 0.0 copy-start.3
  11.9 0.0 copy-start.5
  12.0 0.8 %collective-permute-start.5 = (f32[5,16,128]{2,1,0:T(8,128)S(1)}, f32[5,16,128]{2,1,0:T(8,128)S(1)}, u32[]{:S(2)}, u32[]{:S(2)}) collective-permute-start(f32[5,16,128]{2,1,0:T(8,128)S(1)} %get-tuple-element.16), channel_id=1, source_target_pairs={{8,16},{16,8},{9,17},{17,9},{10,18},{18,10},{11,19},{19,11},{12,20... | collective-permute-start | bytes 122888 | tf_op jit(solution)/shard_map/ppermute | solution.py:321
  12.8 3.1 %collective-permute-start.6 = (f32[5,16,128]{2,1,0:T(8,128)S(1)}, f32[5,16,128]{2,1,0:T(8,128)S(1)}, u32[]{:S(2)}, u32[]{:S(2)}) collective-permute-start(f32[5,16,128]{2,1,0:T(8,128)S(1)} %get-tuple-element.15), channel_id=1, source_target_pairs={{0,8},{16,24},{8,0},{24,16},{1,9},{17,25},{9,1},{25,17},{2,10},{18... | collective-permute-start | bytes 122888 | tf_op jit(solution)/shard_map/ppermute | solution.py:324
  15.9 0.0 collective-permute-done.5.corner_odd_ref
  15.9 0.9 %collective-permute-done.6.corner_even_ref = f32[5,16,128]{2,1,0:T(8,128)S(1)} collective-permute-done((f32[5,16,128]{2,1,0:T(8,128)S(1)}, f32[5,16,128]{2,1,0:T(8,128)S(1)}, u32[]{:S(2)}, u32[]{:S(2)}) %collective-permute-start.6) | collective-permute-done | bytes 40992 | tf_op jit(solution)/shard_map/ppermute | solution.py:324
  16.7 0.0 collective-permute-done.odd_first_ref
  16.7 0.0 collective-permute-done.1.odd_second_ref
  16.7 0.0 collective-permute-done.2.even_ref
  16.8 3.1 %render.1 = s16[4,2,128,128]{3,2,1,0:T(8,128)(2,1)S(1)} custom-call(s32[4,8]{1,0:T(4,128)S(1)} %copy-done.2, f32[2]{0:T(128)S(1)} %copy-done.5, f32[3]{0:T(128)S(1)} %copy-done.6, s32[2,4]{1,0:T(2,128)S(1)} %copy-done.3, f32[8,128,128]{2,1,0:T(8,128)S(1)} %copy-done.1, f32[5,64,128]{2,1,0:T(8,128)S(1)} %collective-permute-done.odd_first_ref, ...), custom_call_target="tpu_custom_call" | custom-call | tf_op jit(solution)/shard_map/render/pallas_call | solution.py:328
  19.9 0.0 copy-start.4
  19.9 9.5 %all_to_all.5.in_ref = s16[4,2,128,128]{3,2,1,0:T(8,128)(2,1)S(1)} all-to-all(s16[4,2,128,128]{3,2,1,0:T(8,128)(2,1)S(1)} %render.1), channel_id=1, replica_groups=mesh['gz'=4,'xy'=8] {'gz'}, dimensions={0} | all-to-all | bytes 524288 | tf_op jit(solution)/shard_map/all_to_all | solution.py:332
  29.4 1.4 %composite.1 = f32[2,4,1,32,128]{4,3,2,1,0:T(8,128)} custom-call(s32[2,4]{1,0:T(2,128)S(1)} %copy-done.4, s16[4,2,128,128]{3,2,1,0:T(8,128)(2,1)S(1)} %all_to_all.5.in_ref), custom_call_target="tpu_custom_call" | custom-call | tf_op jit(solution)/shard_map/composite/pallas_call | solution.py:334
  (11 shorter events, 0.0 us)
Async XLA Ops:
  0.0 1.0 %copy-start = (f32[8,128,128]{2,1,0:T(8,128)S(1)}, f32[8,128,128]{2,1,0:T(8,128)}, u32[]{:S(2)}) copy-start(f32[8,128,128]{2,1,0:T(8,128)} %own_ref.1) | copy-start | bytes 1572868
  1.0 15.7 %copy-start.1 = (f32[8,128,128]{2,1,0:T(8,128)S(1)}, f32[8,128,128]{2,1,0:T(8,128)}, u32[]{:S(2)}) copy-start(f32[8,128,128]{2,1,0:T(8,128)} %own_ref.1) | copy-start | bytes 1572868
  1.3 10.6 %collective-permute-start.3 = (f32[8,8,128]{2,1,0:T(8,128)S(1)}, f32[8,8,128]{2,1,0:T(8,128)S(1)}, u32[]{:S(2)}, u32[]{:S(2)}) collective-permute-start(f32[8,8,128]{2,1,0:T(8,128)S(1)} %get-tuple-element.13), channel_id=1, source_target_pairs={{0,1},{2,3},{4,5},{6,7},{1,0},{3,2},{5,4},{7,6},{8,9},{10,11},{12,... | collective-permute-start | bytes 98312 | tf_op jit(solution)/shard_map/ppermute | solution.py:313
  1.4 10.5 %collective-permute-start.4 = (f32[8,8,128]{2,1,0:T(8,128)S(1)}, f32[8,8,128]{2,1,0:T(8,128)S(1)}, u32[]{:S(2)}, u32[]{:S(2)}) collective-permute-start(f32[8,8,128]{2,1,0:T(8,128)S(1)} %get-tuple-element.14), channel_id=1, source_target_pairs={{1,2},{3,4},{5,6},{2,1},{4,3},{6,5},{9,10},{11,12},{13,14},{10,9},... | collective-permute-start | bytes 98312 | tf_op jit(solution)/shard_map/ppermute | solution.py:314
  6.3 10.4 %collective-permute-start = (f32[5,64,128]{2,1,0:T(8,128)S(1)}, f32[5,64,128]{2,1,0:T(8,128)S(1)}, u32[]{:S(2)}, u32[]{:S(2)}) collective-permute-start(f32[5,64,128]{2,1,0:T(8,128)S(1)} %get-tuple-element.10), channel_id=1, source_target_pairs={{8,16},{16,8},{9,17},{17,9},{10,18},{18,10},{11,19},{19,11},{12,20... | collective-permute-start | bytes 491528 | tf_op jit(solution)/shard_map/ppermute | solution.py:315
  7.0 9.7 %collective-permute-start.1 = (f32[5,64,128]{2,1,0:T(8,128)S(1)}, f32[5,64,128]{2,1,0:T(8,128)S(1)}, u32[]{:S(2)}, u32[]{:S(2)}) collective-permute-start(f32[5,64,128]{2,1,0:T(8,128)S(1)} %get-tuple-element.11), channel_id=1, source_target_pairs={{8,16},{16,8},{9,17},{17,9},{10,18},{18,10},{11,19},{19,11},{12,20... | collective-permute-start | bytes 491528 | tf_op jit(solution)/shard_map/ppermute | solution.py:315
  7.7 9.1 %collective-permute-start.2 = (f32[5,128,128]{2,1,0:T(8,128)S(1)}, f32[5,128,128]{2,1,0:T(8,128)S(1)}, u32[]{:S(2)}, u32[]{:S(2)}) collective-permute-start(f32[5,128,128]{2,1,0:T(8,128)S(1)} %get-tuple-element.12), channel_id=1, source_target_pairs={{0,8},{16,24},{8,0},{24,16},{1,9},{17,25},{9,1},{25,17},{2,10},{18... | collective-permute-start | bytes 983048 | tf_op jit(solution)/shard_map/ppermute | solution.py:316
  11.9 4.9 %copy-start.6 = (f32[3]{0:T(128)S(1)}, f32[3]{0:T(128)}, u32[]{:S(2)}) copy-start(f32[3]{0:T(128)} %palette_ref.1) | copy-start | bytes 40
  11.9 4.8 %copy-start.2 = (s32[4,8]{1,0:T(4,128)S(1)}, s32[4,8]{1,0:T(4,128)}, u32[]{:S(2)}) copy-start(s32[4,8]{1,0:T(4,128)} %live_ref.1) | copy-start | bytes 388
  11.9 4.8 %copy-start.3 = (s32[2,4]{1,0:T(2,128)S(1)}, s32[2,4]{1,0:T(2,128)}, u32[]{:S(2)}) copy-start(s32[2,4]{1,0:T(2,128)} %owner_ref.1) | copy-start | bytes 100
  11.9 4.8 %copy-start.5 = (f32[2]{0:T(128)S(1)}, f32[2]{0:T(128)}, u32[]{:S(2)}) copy-start(f32[2]{0:T(128)} %slopes_ref.1) | copy-start | bytes 28
  12.0 3.9 %collective-permute-start.5 = (f32[5,16,128]{2,1,0:T(8,128)S(1)}, f32[5,16,128]{2,1,0:T(8,128)S(1)}, u32[]{:S(2)}, u32[]{:S(2)}) collective-permute-start(f32[5,16,128]{2,1,0:T(8,128)S(1)} %get-tuple-element.16), channel_id=1, source_target_pairs={{8,16},{16,8},{9,17},{17,9},{10,18},{18,10},{11,19},{19,11},{12,20... | collective-permute-start | bytes 122888 | tf_op jit(solution)/shard_map/ppermute | solution.py:321
  12.8 4.0 %collective-permute-start.6 = (f32[5,16,128]{2,1,0:T(8,128)S(1)}, f32[5,16,128]{2,1,0:T(8,128)S(1)}, u32[]{:S(2)}, u32[]{:S(2)}) collective-permute-start(f32[5,16,128]{2,1,0:T(8,128)S(1)} %get-tuple-element.15), channel_id=1, source_target_pairs={{0,8},{16,24},{8,0},{24,16},{1,9},{17,25},{9,1},{25,17},{2,10},{18... | collective-permute-start | bytes 122888 | tf_op jit(solution)/shard_map/ppermute | solution.py:324
  19.9 9.5 %copy-start.4 = (s32[2,4]{1,0:T(2,128)S(1)}, s32[2,4]{1,0:T(2,128)}, u32[]{:S(2)}) copy-start(s32[2,4]{1,0:T(2,128)} %order_ref.1) | copy-start | bytes 100

commit v11 on v9

--- a/solution.py
+++ b/solution.py
@@ -15,6 +15,9 @@
 TOP = 2.2
 STEPS = 65535.0
 MIDDLE = 32768
+LEVELS_PER_UNIT = 5461.0
+ZERO_LEVEL = 1 << 19
+GROUP, WORDS = 8, 5
 VMEM_BYTES = 40 * 1024 * 1024
 
 
@@ -49,6 +52,30 @@
     return [sums[i] + layers[i + width] for i in range(len(layers) - width)]
 
 
+def pack(values):
+    v = [(x * LEVELS_PER_UNIT + (ZERO_LEVEL + 0.5)).astype(jnp.int32) for x in values]
+    v = [(x - ZERO_LEVEL) & 0xFFFFF for x in v]
+    upper = [
+        v[5] & 0xFFF,
+        (v[5] >> 12) | ((v[6] & 0xF) << 8),
+        (v[6] >> 4) & 0xFFF,
+        (v[6] >> 16) | ((v[7] & 0xFF) << 4),
+        v[7] >> 8,
+    ]
+    return [v[i] | (upper[i] << 20) for i in range(WORDS)]
+
+
+def unpack(words):
+    upper = [lax.shift_right_logical(w, jnp.full_like(w, 20)) for w in words]
+    levels = words + [
+        upper[0] | ((upper[1] & 0xFF) << 12),
+        (upper[1] >> 8) | (upper[2] << 4) | ((upper[3] & 0xF) << 16),
+        (upper[3] >> 4) | (upper[4] << 8),
+    ]
+    levels = [(x << 12) >> 12 for x in levels]
+    return [x.astype(jnp.float32) * (1.0 / LEVELS_PER_UNIT) for x in levels]
+
+
 def encode(value):
     root = jnp.exp(0.125 * jnp.log(jnp.maximum(value, 1e-30) * (1.0 / TOP)))
     level = jnp.minimum(root * STEPS + 0.5, STEPS)
@@ -82,23 +109,26 @@
         row_index = lax.axis_index("xy")
         odd_depth = depth_index % 2 == 1
 
-        for chunk in range(padded_rows // ROW_TILE):
-            rows = pl.ds(chunk * ROW_TILE, ROW_TILE)
-            inner = pl.ds((chunk - 1) * ROW_TILE, ROW_TILE)
-            if chunk == 0:
-                at, pair, mid_ref = pl.ds(0, ROW_TILE), (corner_even_ref, corner_odd_ref), rlo_ref
-            elif chunk == padded_rows // ROW_TILE - 1:
-                at = pl.ds(ROW_TILE, ROW_TILE)
-                pair, mid_ref = (corner_even_ref, corner_odd_ref), rhi_ref
-            else:
-                at, pair, mid_ref = inner, (even_ref, odd_ref), own_ref
-            mid_at = at if mid_ref is own_ref else pl.ds(0, ROW_TILE)
-            even, odd = [[ref[i, at] for i in range(HALO)] for ref in pair]
-            mid = [mid_ref[i, mid_at] for i in range(depth_cells)]
+        for at, mid_ref in ((0, rlo_ref), (ROW_TILE, rhi_ref)):
+            even = [corner_even_ref[i, pl.ds(at, ROW_TILE)] for i in range(HALO)]
+            odd = [corner_odd_ref[i, pl.ds(at, ROW_TILE)] for i in range(HALO)]
             low = [jnp.where(odd_depth, e, o) for e, o in zip(even, odd)]
             high = [jnp.where(odd_depth, o, e) for e, o in zip(even, odd)]
-            for z, total in enumerate(window_sums(low + mid + high, TAPS)):
-                deep[z, rows] = total
+            layers = low + [mid_ref[i] for i in range(depth_cells)] + high
+            for z, total in enumerate(window_sums(layers, TAPS)):
+                deep[z, pl.ds(0 if at == 0 else last, ROW_TILE)] = total
+        low, high, word = [], [], 0
+        for start in range(0, row_cells, ROW_TILE):
+            while len(low) < HALO:
+                even = [even_ref[word + k] for k in range(WORDS)]
+                odd = [odd_ref[word + k] for k in range(WORDS)]
+                low += unpack([jnp.where(odd_depth, e, o) for e, o in zip(even, odd)])
+                high += unpack([jnp.where(odd_depth, o, e) for e, o in zip(even, odd)])
+                word += WORDS
+            own = [own_ref[i, pl.ds(start, ROW_TILE)] for i in range(depth_cells)]
+            for z, total in enumerate(window_sums(low[:HALO] + own + high[:HALO], TAPS)):
+                deep[z, pl.ds(first + start, ROW_TILE)] = total
+            low, high = low[HALO:], high[HALO:]
 
         band = column_matrix(columns)
         weights = jnp.concatenate([band, band, band], axis=0)
@@ -230,36 +260,33 @@
 def cut_edges(density):
     depth_cells, row_cells, columns = density.shape
 
-    def kernel(density_ref, row_even_ref, row_odd_ref, deep_even_ref, deep_odd_ref, sems):
+    places = [(i, start) for start in range(0, row_cells, ROW_TILE) for i in range(HALO)]
+    words = len(places) // GROUP * WORDS
+
+    def kernel(density_ref, row_even_ref, row_odd_ref, deep_even_ref, deep_odd_ref):
         row_bit = lax.axis_index("xy") % 2
         depth_bit = lax.axis_index("gz") % 2
         last_rows, last_deep = row_cells - ROW_TILE, depth_cells - HALO
-
-        def rows(bit):
-            return density_ref.at[:, pl.ds(pl.multiple_of(bit * last_rows, ROW_TILE), ROW_TILE)]
-
-        def deep(bit):
-            return density_ref.at[pl.ds(bit * last_deep, HALO)]
-
-        copies = [
-            pltpu.make_async_copy(deep(depth_bit), deep_odd_ref, sems.at[0]),
-            pltpu.make_async_copy(deep(1 - depth_bit), deep_even_ref, sems.at[1]),
-            pltpu.make_async_copy(rows(1 - row_bit), row_even_ref, sems.at[2]),
-            pltpu.make_async_copy(rows(row_bit), row_odd_ref, sems.at[3]),
-        ]
-        for copy in copies:
-            copy.start()
-        for copy in copies:
-            copy.wait()
+        for ref, bit in ((deep_odd_ref, depth_bit), (deep_even_ref, 1 - depth_bit)):
+            for group in range(len(places) // GROUP):
+                values = [
+                    density_ref[bit * last_deep + i, pl.ds(start, ROW_TILE)]
+                    for i, start in places[group * GROUP : (group + 1) * GROUP]
+                ]
+                for k, word in enumerate(pack(values)):
+                    ref[group * WORDS + k] = word
+        for ref, bit in ((row_even_ref, 1 - row_bit), (row_odd_ref, row_bit)):
+            start = pl.multiple_of(bit * last_rows, ROW_TILE)
+            ref[...] = density_ref[:, pl.ds(start, ROW_TILE)]
 
     rows = jax.ShapeDtypeStruct((depth_cells, ROW_TILE, columns), jnp.float32)
-    deep = jax.ShapeDtypeStruct((HALO, row_cells, columns), jnp.float32)
+    deep = jax.ShapeDtypeStruct((words, ROW_TILE, columns), jnp.int32)
+    vmem = pl.BlockSpec(memory_space=pltpu.VMEM)
     return pl.pallas_call(
         kernel,
         out_shape=(rows, rows, deep, deep),
-        in_specs=[pl.BlockSpec(memory_space=pltpu.HBM)],
-        out_specs=(pl.BlockSpec(memory_space=pltpu.VMEM),) * 4,
-        scratch_shapes=[pltpu.SemaphoreType.DMA((4,))],
+        in_specs=[vmem],
+        out_specs=(vmem,) * 4,
         compiler_params=pltpu.CompilerParams(vmem_limit_bytes=VMEM_BYTES),
         name="cut_edges",
     )(density)

time: 28.6 us -> 28.5 us (level)
  the two profiles are of different devices: /device:TPU:2 before, /device:TPU:8 now
where the time goes in v11:
time: 28.5 us; the launch traced here: 28.3 us
  blocking collectives  12.7 us (45%)
  starting transfers between devices  8.22 us (29%)
  Pallas kernels  4.77 us (17%)
  waiting for transfers between devices  1.29 us (5%)
  local copies, waits for them, and re-layouts  1.08 us (4%)
    all_to_all x1, blocking collectives, body(): lax.all_to_all(outgoing, 'gz', split_axis=0, concat_axis=0, tiled=True)  12.7 us
    ppermute x1, starting transfers between devices, body(): deep_even = lax.ppermute(deep_even, 'gz', pairs('gz', 0))  3.34 us
    pallas_call x1, Pallas kernels, body(): render(live_slices, shear_slopes, palette, tile_owner, density, deep_odd,...  3.22 us
    ppermute x1, starting transfers between devices, body(): row_odd = lax.ppermute(row_odd, 'xy', pairs('xy', 1))  1.91 us
    ppermute x1, starting transfers between devices, body(): row_even = lax.ppermute(row_even, 'xy', pairs('xy', 0))  1.56 us
    pallas_call x1, Pallas kernels, body(): pl.pallas_call(composite_kernel, out_shape=jax.ShapeDtypeStruct((VIEWS, 4...  1.36 us
    unnamed x14, local copies, waits for them, and re-layouts  1.08 us
    ppermute x1, waiting for transfers between devices, body(): row_odd = lax.ppermute(row_odd, 'xy', pairs('xy', 1))  0.75 us
  transfers between devices with their start and end apart: 6, of which 2 were waited for; matrix products, arithmetic and copies ran while one was open for 0% of the time, Pallas kernels for 0%

profile of v11, /device:TPU:8, one launch (start us, length us, event | category | flops | bytes accessed | tf_op | source)
XLA Modules:
  0.0 28.3 jit_solution(14262418522751246181)
XLA Ops:
  0.0 1.0 %copy-done = f32[8,128,128]{2,1,0:T(8,128)S(1)} copy-done((f32[8,128,128]{2,1,0:T(8,128)S(1)}, f32[8,128,128]{2,1,0:T(8,128)}, u32[]{:S(2)}) %copy-start) | copy-done | bytes 524312
  1.0 0.2 cut_edges.1
  1.2 1.6 %collective-permute-start.2 = (f32[8,8,128]{2,1,0:T(8,128)S(1)}, f32[8,8,128]{2,1,0:T(8,128)S(1)}, u32[]{:S(2)}, u32[]{:S(2)}) collective-permute-start(f32[8,8,128]{2,1,0:T(8,128)S(1)} %get-tuple-element.11), channel_id=1, source_target_pairs={{0,1},{2,3},{4,5},{6,7},{1,0},{3,2},{5,4},{7,6},{8,9},{10,11},{12,... | collective-permute-start | bytes 98312 | tf_op jit(solution)/shard_map/ppermute | solution.py:329
  2.8 1.9 %collective-permute-start.3 = (f32[8,8,128]{2,1,0:T(8,128)S(1)}, f32[8,8,128]{2,1,0:T(8,128)S(1)}, u32[]{:S(2)}, u32[]{:S(2)}) collective-permute-start(f32[8,8,128]{2,1,0:T(8,128)S(1)} %get-tuple-element.12), channel_id=1, source_target_pairs={{1,2},{3,4},{5,6},{2,1},{4,3},{6,5},{9,10},{11,12},{13,14},{10,9},... | collective-permute-start | bytes 98312 | tf_op jit(solution)/shard_map/ppermute | solution.py:330
  4.7 0.7 %collective-permute-start = (s32[50,8,128]{2,1,0:T(8,128)S(1)}, s32[50,8,128]{2,1,0:T(8,128)S(1)}, u32[]{:S(2)}, u32[]{:S(2)}) collective-permute-start(s32[50,8,128]{2,1,0:T(8,128)S(1)} %get-tuple-element.9), channel_id=1, source_target_pairs={{8,16},{16,8},{9,17},{17,9},{10,18},{18,10},{11,19},{19,11},{12,20... | collective-permute-start | bytes 614408 | tf_op jit(solution)/shard_map/ppermute | solution.py:331
  5.4 3.3 %collective-permute-start.1 = (s32[50,8,128]{2,1,0:T(8,128)S(1)}, s32[50,8,128]{2,1,0:T(8,128)S(1)}, u32[]{:S(2)}, u32[]{:S(2)}) collective-permute-start(s32[50,8,128]{2,1,0:T(8,128)S(1)} %get-tuple-element.10), channel_id=1, source_target_pairs={{0,8},{16,24},{8,0},{24,16},{1,9},{17,25},{9,1},{25,17},{2,10},{18... | collective-permute-start | bytes 614408 | tf_op jit(solution)/shard_map/ppermute | solution.py:332
  8.7 0.0 collective-permute-done.2
  8.7 0.8 %collective-permute-done.3 = f32[8,8,128]{2,1,0:T(8,128)S(1)} collective-permute-done((f32[8,8,128]{2,1,0:T(8,128)S(1)}, f32[8,8,128]{2,1,0:T(8,128)S(1)}, u32[]{:S(2)}, u32[]{:S(2)}) %collective-permute-start.3) | collective-permute-done | bytes 32800 | tf_op jit(solution)/shard_map/ppermute | solution.py:330
  9.5 0.0 copy-start.6
  9.6 0.0 copy-start.2
  9.6 0.0 copy-start.4
  9.6 0.0 copy-start.5
  9.6 0.1 collective-permute-start.5
  9.7 0.7 %collective-permute-start.4 = (f32[5,16,128]{2,1,0:T(8,128)S(1)}, f32[5,16,128]{2,1,0:T(8,128)S(1)}, u32[]{:S(2)}, u32[]{:S(2)}) collective-permute-start(f32[5,16,128]{2,1,0:T(8,128)S(1)} %get-tuple-element.14), channel_id=1, source_target_pairs={{8,16},{16,8},{9,17},{17,9},{10,18},{18,10},{11,19},{19,11},{12,20... | collective-permute-start | bytes 122888 | tf_op jit(solution)/shard_map/ppermute | solution.py:337
  10.3 0.5 %collective-permute-done.5.corner_even_ref = f32[5,16,128]{2,1,0:T(8,128)S(1)} collective-permute-done((f32[5,16,128]{2,1,0:T(8,128)S(1)}, f32[5,16,128]{2,1,0:T(8,128)S(1)}, u32[]{:S(2)}, u32[]{:S(2)}) %collective-permute-start.5) | collective-permute-done | bytes 40992 | tf_op jit(solution)/shard_map/ppermute | solution.py:340
  10.9 0.0 collective-permute-done.4.corner_odd_ref
  10.9 0.0 collective-permute-done.odd_ref
  10.9 0.0 collective-permute-done.1.even_ref
  10.9 0.0 copy-done.1
  10.9 0.0 copy-done.6
  10.9 3.2 %render.1 = s16[4,2,128,128]{3,2,1,0:T(8,128)(2,1)S(1)} custom-call(s32[4,8]{1,0:T(4,128)S(1)} %copy-done.2, f32[2]{0:T(128)S(1)} %copy-done.5, f32[3]{0:T(128)S(1)} %copy-done.6, s32[2,4]{1,0:T(2,128)S(1)} %copy-done.4, f32[8,128,128]{2,1,0:T(8,128)S(1)} %copy-done.1, s32[50,8,128]{2,1,0:T(8,128)S(1)} %collective-permute-done.odd_ref, ...), custom_call_target="tpu_custom_call" | custom-call | tf_op jit(solution)/shard_map/render/pallas_call | solution.py:344
  14.2 0.0 copy-start.3
  14.2 12.7 %all_to_all.5.in_ref = s16[4,2,128,128]{3,2,1,0:T(8,128)(2,1)S(1)} all-to-all(s16[4,2,128,128]{3,2,1,0:T(8,128)(2,1)S(1)} %render.1), channel_id=1, replica_groups=mesh['gz'=4,'xy'=8] {'gz'}, dimensions={0} | all-to-all | bytes 524288 | tf_op jit(solution)/shard_map/all_to_all | solution.py:348
  26.9 1.4 %composite.1 = f32[2,4,1,32,128]{4,3,2,1,0:T(8,128)} custom-call(s32[2,4]{1,0:T(2,128)S(1)} %copy-done.3, s16[4,2,128,128]{3,2,1,0:T(8,128)(2,1)S(1)} %all_to_all.5.in_ref), custom_call_target="tpu_custom_call" | custom-call | tf_op jit(solution)/shard_map/composite/pallas_call | solution.py:350
  (9 shorter events, 0.0 us)
Async XLA Ops:
  0.0 1.0 %copy-start = (f32[8,128,128]{2,1,0:T(8,128)S(1)}, f32[8,128,128]{2,1,0:T(8,128)}, u32[]{:S(2)}) copy-start(f32[8,128,128]{2,1,0:T(8,128)} %own_ref.1) | copy-start | bytes 1572868
  1.0 9.8 %copy-start.1 = (f32[8,128,128]{2,1,0:T(8,128)S(1)}, f32[8,128,128]{2,1,0:T(8,128)}, u32[]{:S(2)}) copy-start(f32[8,128,128]{2,1,0:T(8,128)} %own_ref.1) | copy-start | bytes 1572868
  1.2 7.5 %collective-permute-start.2 = (f32[8,8,128]{2,1,0:T(8,128)S(1)}, f32[8,8,128]{2,1,0:T(8,128)S(1)}, u32[]{:S(2)}, u32[]{:S(2)}) collective-permute-start(f32[8,8,128]{2,1,0:T(8,128)S(1)} %get-tuple-element.11), channel_id=1, source_target_pairs={{0,1},{2,3},{4,5},{6,7},{1,0},{3,2},{5,4},{7,6},{8,9},{10,11},{12,... | collective-permute-start | bytes 98312 | tf_op jit(solution)/shard_map/ppermute | solution.py:329
  2.8 6.7 %collective-permute-start.3 = (f32[8,8,128]{2,1,0:T(8,128)S(1)}, f32[8,8,128]{2,1,0:T(8,128)S(1)}, u32[]{:S(2)}, u32[]{:S(2)}) collective-permute-start(f32[8,8,128]{2,1,0:T(8,128)S(1)} %get-tuple-element.12), channel_id=1, source_target_pairs={{1,2},{3,4},{5,6},{2,1},{4,3},{6,5},{9,10},{11,12},{13,14},{10,9},... | collective-permute-start | bytes 98312 | tf_op jit(solution)/shard_map/ppermute | solution.py:330
  4.7 6.2 %collective-permute-start = (s32[50,8,128]{2,1,0:T(8,128)S(1)}, s32[50,8,128]{2,1,0:T(8,128)S(1)}, u32[]{:S(2)}, u32[]{:S(2)}) collective-permute-start(s32[50,8,128]{2,1,0:T(8,128)S(1)} %get-tuple-element.9), channel_id=1, source_target_pairs={{8,16},{16,8},{9,17},{17,9},{10,18},{18,10},{11,19},{19,11},{12,20... | collective-permute-start | bytes 614408 | tf_op jit(solution)/shard_map/ppermute | solution.py:331
  5.4 5.5 %collective-permute-start.1 = (s32[50,8,128]{2,1,0:T(8,128)S(1)}, s32[50,8,128]{2,1,0:T(8,128)S(1)}, u32[]{:S(2)}, u32[]{:S(2)}) collective-permute-start(s32[50,8,128]{2,1,0:T(8,128)S(1)} %get-tuple-element.10), channel_id=1, source_target_pairs={{0,8},{16,24},{8,0},{24,16},{1,9},{17,25},{9,1},{25,17},{2,10},{18... | collective-permute-start | bytes 614408 | tf_op jit(solution)/shard_map/ppermute | solution.py:332
  9.5 1.4 %copy-start.6 = (f32[3]{0:T(128)S(1)}, f32[3]{0:T(128)}, u32[]{:S(2)}) copy-start(f32[3]{0:T(128)} %palette_ref.1) | copy-start | bytes 40
  9.6 1.4 %copy-start.2 = (s32[4,8]{1,0:T(4,128)S(1)}, s32[4,8]{1,0:T(4,128)}, u32[]{:S(2)}) copy-start(s32[4,8]{1,0:T(4,128)} %live_ref.1) | copy-start | bytes 388
  9.6 1.4 %copy-start.4 = (s32[2,4]{1,0:T(2,128)S(1)}, s32[2,4]{1,0:T(2,128)}, u32[]{:S(2)}) copy-start(s32[2,4]{1,0:T(2,128)} %owner_ref.1) | copy-start | bytes 100
  9.6 1.4 %copy-start.5 = (f32[2]{0:T(128)S(1)}, f32[2]{0:T(128)}, u32[]{:S(2)}) copy-start(f32[2]{0:T(128)} %slopes_ref.1) | copy-start | bytes 28
  9.6 1.3 %collective-permute-start.5 = (f32[5,16,128]{2,1,0:T(8,128)S(1)}, f32[5,16,128]{2,1,0:T(8,128)S(1)}, u32[]{:S(2)}, u32[]{:S(2)}) collective-permute-start(f32[5,16,128]{2,1,0:T(8,128)S(1)} %get-tuple-element.13), channel_id=1, source_target_pairs={{0,8},{16,24},{8,0},{24,16},{1,9},{17,25},{9,1},{25,17},{2,10},{18... | collective-permute-start | bytes 122888 | tf_op jit(solution)/shard_map/ppermute | solution.py:340
  9.7 1.2 %collective-permute-start.4 = (f32[5,16,128]{2,1,0:T(8,128)S(1)}, f32[5,16,128]{2,1,0:T(8,128)S(1)}, u32[]{:S(2)}, u32[]{:S(2)}) collective-permute-start(f32[5,16,128]{2,1,0:T(8,128)S(1)} %get-tuple-element.14), channel_id=1, source_target_pairs={{8,16},{16,8},{9,17},{17,9},{10,18},{18,10},{11,19},{19,11},{12,20... | collective-permute-start | bytes 122888 | tf_op jit(solution)/shard_map/ppermute | solution.py:337
  14.2 12.7 %copy-start.3 = (s32[2,4]{1,0:T(2,128)S(1)}, s32[2,4]{1,0:T(2,128)}, u32[]{:S(2)}) copy-start(s32[2,4]{1,0:T(2,128)} %order_ref.1) | copy-start | bytes 100

commit v12 on v11

--- a/solution.py
+++ b/solution.py
@@ -101,33 +101,30 @@
 
     def kernel(
         live_ref, slopes_ref, palette_ref, owner_ref,
-        own_ref, odd_ref, even_ref, corner_odd_ref, corner_even_ref, rlo_ref, rhi_ref,
+        own_ref, odd_ref, even_ref, row_even_ref, row_odd_ref,
         out_ref,
         deep, triple, smooth, across, sheared,
     ):
         depth_index = lax.axis_index("gz")
         row_index = lax.axis_index("xy")
         odd_depth = depth_index % 2 == 1
-
-        for at, mid_ref in ((0, rlo_ref), (ROW_TILE, rhi_ref)):
-            even = [corner_even_ref[i, pl.ds(at, ROW_TILE)] for i in range(HALO)]
-            odd = [corner_odd_ref[i, pl.ds(at, ROW_TILE)] for i in range(HALO)]
-            low = [jnp.where(odd_depth, e, o) for e, o in zip(even, odd)]
-            high = [jnp.where(odd_depth, o, e) for e, o in zip(even, odd)]
-            layers = low + [mid_ref[i] for i in range(depth_cells)] + high
-            for z, total in enumerate(window_sums(layers, TAPS)):
-                deep[z, pl.ds(0 if at == 0 else last, ROW_TILE)] = total
+        odd_row = row_index % 2 == 1
+
+        chunks = padded_rows // ROW_TILE
         low, high, word = [], [], 0
-        for start in range(0, row_cells, ROW_TILE):
+        for chunk in range(chunks):
             while len(low) < HALO:
                 even = [even_ref[word + k] for k in range(WORDS)]
                 odd = [odd_ref[word + k] for k in range(WORDS)]
                 low += unpack([jnp.where(odd_depth, e, o) for e, o in zip(even, odd)])
                 high += unpack([jnp.where(odd_depth, o, e) for e, o in zip(even, odd)])
                 word += WORDS
-            own = [own_ref[i, pl.ds(start, ROW_TILE)] for i in range(depth_cells)]
+            own = [
+                layer_rows(own_ref, row_even_ref, row_odd_ref, odd_row, i, chunk, chunks)
+                for i in range(depth_cells)
+            ]
             for z, total in enumerate(window_sums(low[:HALO] + own + high[:HALO], TAPS)):
-                deep[z, pl.ds(first + start, ROW_TILE)] = total
+                deep[z, pl.ds(chunk * ROW_TILE, ROW_TILE)] = total
             low, high = low[HALO:], high[HALO:]
 
         band = column_matrix(columns)
@@ -243,7 +240,7 @@
     return pl.pallas_call(
         kernel,
         out_shape=jax.ShapeDtypeStruct((n_depth, VIEWS, 4 * tile_rows, columns), jnp.int16),
-        in_specs=[smem] * 4 + [vmem] * 7,
+        in_specs=[smem] * 4 + [vmem] * 5,
         out_specs=vmem,
         scratch_shapes=[
             pltpu.VMEM((depth_cells + 2, padded_rows, columns), jnp.float32),
@@ -257,39 +254,46 @@
     )
 
 
-def cut_edges(density):
+def layer_rows(own_ref, row_even_ref, row_odd_ref, odd_row, layer, chunk, chunks):
+    if 0 < chunk < chunks - 1:
+        return own_ref[layer, pl.ds((chunk - 1) * ROW_TILE, ROW_TILE)]
+    take_even = odd_row if chunk == 0 else jnp.logical_not(odd_row)
+    return jnp.where(take_even, row_even_ref[layer], row_odd_ref[layer])
+
+
+def cut_layers(density, row_even, row_odd):
     depth_cells, row_cells, columns = density.shape
-
-    places = [(i, start) for start in range(0, row_cells, ROW_TILE) for i in range(HALO)]
-    words = len(places) // GROUP * WORDS
-
-    def kernel(density_ref, row_even_ref, row_odd_ref, deep_even_ref, deep_odd_ref):
-        row_bit = lax.axis_index("xy") % 2
+    chunks = row_cells // ROW_TILE + 2
+    places = [(i, chunk) for chunk in range(chunks) for i in range(HALO)]
+    groups = pl.cdiv(len(places), GROUP)
+
+    def kernel(own_ref, row_even_ref, row_odd_ref, deep_even_ref, deep_odd_ref):
+        odd_row = lax.axis_index("xy") % 2 == 1
         depth_bit = lax.axis_index("gz") % 2
-        last_rows, last_deep = row_cells - ROW_TILE, depth_cells - HALO
+        last_deep = depth_cells - HALO
         for ref, bit in ((deep_odd_ref, depth_bit), (deep_even_ref, 1 - depth_bit)):
-            for group in range(len(places) // GROUP):
+            for group in range(groups):
                 values = [
-                    density_ref[bit * last_deep + i, pl.ds(start, ROW_TILE)]
-                    for i, start in places[group * GROUP : (group + 1) * GROUP]
+                    layer_rows(
+                        own_ref, row_even_ref, row_odd_ref, odd_row,
+                        bit * last_deep + i, chunk, chunks,
+                    )
+                    for i, chunk in places[group * GROUP : (group + 1) * GROUP]
                 ]
+                values += [jnp.zeros_like(values[0])] * (GROUP - len(values))
                 for k, word in enumerate(pack(values)):
                     ref[group * WORDS + k] = word
-        for ref, bit in ((row_even_ref, 1 - row_bit), (row_odd_ref, row_bit)):
-            start = pl.multiple_of(bit * last_rows, ROW_TILE)
-            ref[...] = density_ref[:, pl.ds(start, ROW_TILE)]
-
-    rows = jax.ShapeDtypeStruct((depth_cells, ROW_TILE, columns), jnp.float32)
-    deep = jax.ShapeDtypeStruct((words, ROW_TILE, columns), jnp.int32)
+
+    deep = jax.ShapeDtypeStruct((groups * WORDS, ROW_TILE, columns), jnp.int32)
     vmem = pl.BlockSpec(memory_space=pltpu.VMEM)
     return pl.pallas_call(
         kernel,
-        out_shape=(rows, rows, deep, deep),
-        in_specs=[vmem],
-        out_specs=(vmem,) * 4,
+        out_shape=(deep, deep),
+        in_specs=[vmem] * 3,
+        out_specs=(vmem,) * 2,
         compiler_params=pltpu.CompilerParams(vmem_limit_bytes=VMEM_BYTES),
-        name="cut_edges",
-    )(density)
+        name="cut_layers",
+    )(density, row_even, row_odd)
 
 
 def composite_kernel(order_ref, in_ref, out_ref):
@@ -316,8 +320,6 @@
     n_depth = lax.axis_size("gz")
     n_rows = lax.axis_size("xy")
 
-    edge = depth_cells - HALO
-    odd_depth = lax.axis_index("gz") % 2 == 1
     odd_row = lax.axis_index("xy") % 2 == 1
 
     def pairs(axis, first):
@@ -325,25 +327,16 @@
         lower = range(first, count - 1, 2)
         return [(i, i + 1) for i in lower] + [(i + 1, i) for i in lower]
 
-    row_even, row_odd, deep_even, deep_odd = cut_edges(density)
-    row_even = lax.ppermute(row_even, "xy", pairs("xy", 0))
-    row_odd = lax.ppermute(row_odd, "xy", pairs("xy", 1))
+    low_rows, high_rows = density[:, :ROW_TILE], density[:, row_cells - ROW_TILE :]
+    row_even = lax.ppermute(jnp.where(odd_row, low_rows, high_rows), "xy", pairs("xy", 0))
+    row_odd = lax.ppermute(jnp.where(odd_row, high_rows, low_rows), "xy", pairs("xy", 1))
+    deep_even, deep_odd = cut_layers(density, row_even, row_odd)
     deep_odd = lax.ppermute(deep_odd, "gz", pairs("gz", 1))
     deep_even = lax.ppermute(deep_even, "gz", pairs("gz", 0))
-    rlo = jnp.where(odd_row, row_even, row_odd)
-    rhi = jnp.where(odd_row, row_odd, row_even)
-    low_corner = jnp.concatenate([rlo[:HALO], rhi[:HALO]], axis=1)
-    high_corner = jnp.concatenate([rlo[edge:], rhi[edge:]], axis=1)
-    corner_odd = lax.ppermute(
-        jnp.where(odd_depth, high_corner, low_corner), "gz", pairs("gz", 1)
-    )
-    corner_even = lax.ppermute(
-        jnp.where(odd_depth, low_corner, high_corner), "gz", pairs("gz", 0)
-    )
     render = make_render(n_depth, n_rows, depth_cells, row_cells, columns)
     outgoing = render(
         live_slices, shear_slopes, palette, tile_owner,
-        density, deep_odd, deep_even, corner_odd, corner_even, rlo, rhi,
+        density, deep_odd, deep_even, row_even, row_odd,
     )
     incoming = lax.all_to_all(outgoing, "gz", split_axis=0, concat_axis=0, tiled=True)
     tile_rows = row_cells // n_depth

time: 28.5 us -> 31.6 us (1.11)
  the two profiles are of different devices: /device:TPU:8 before, /device:TPU:0 now
where the time goes in v12:
time: 31.6 us; the launch traced here: 31.3 us
  blocking collectives  11.4 us (36%)
  starting transfers between devices  10.2 us (32%)
  Pallas kernels  4.8 us (15%)
  waiting for transfers between devices  3.03 us (10%)
  local copies, waits for them, and re-layouts  1.07 us (3%)
  other arithmetic  0.78 us (2%)
    all_to_all x1, blocking collectives, body(): lax.all_to_all(outgoing, 'gz', split_axis=0, concat_axis=0, tiled=True)  11.4 us
    ppermute x1, starting transfers between devices, body(): lax.ppermute(jnp.where(odd_row, low_rows, high_rows), 'xy', pairs('xy', 0))  5.8 us
    pallas_call x1, Pallas kernels, body(): render(live_slices, shear_slopes, palette, tile_owner, density, deep_odd,...  3.22 us
    ppermute x1, starting transfers between devices, body(): deep_even = lax.ppermute(deep_even, 'gz', pairs('gz', 0))  2.93 us
    ppermute x1, waiting for transfers between devices, body(): lax.ppermute(jnp.where(odd_row, low_rows, high_rows), 'xy', pairs('xy', 0))  1.89 us
    pallas_call x1, Pallas kernels, body(): pl.pallas_call(composite_kernel, out_shape=jax.ShapeDtypeStruct((VIEWS, 4...  1.36 us
    ppermute x1, waiting for transfers between devices, body(): deep_even = lax.ppermute(deep_even, 'gz', pairs('gz', 0))  1.14 us
    unnamed x12, local copies, waits for them, and re-layouts  1.07 us
  transfers between devices with their start and end apart: 4, of which 2 were waited for; matrix products, arithmetic and copies ran while one was open for 0% of the time, Pallas kernels for 0%

profile of v12, /device:TPU:0, one launch (start us, length us, event | category | flops | bytes accessed | tf_op | source)
XLA Modules:
  0.0 31.3 jit_solution(15652072210101337328)
XLA Ops:
  0.0 0.8 %slice_select_fusion = (f32[8,8,128]{2,1,0:T(8,128)S(1)}, f32[8,8,128]{2,1,0:T(8,128)S(1)}) fusion(f32[8,128,128]{2,1,0:T(8,128)} %own_ref.3, pred[]{:T(512)S(6)} %eq.5), kind=kLoop, calls=%fused_computation | loop fusion | flops 16384 | bytes 131073 | tf_op jit(solution)/shard_map/jit(_where)/select_n | solution.py:332
  0.8 0.7 %collective-permute-start.1 = (f32[8,8,128]{2,1,0:T(8,128)S(1)}, f32[8,8,128]{2,1,0:T(8,128)S(1)}, u32[]{:S(2)}, u32[]{:S(2)}) collective-permute-start(f32[8,8,128]{2,1,0:T(8,128)S(1)} %get-tuple-element.9), channel_id=1, source_target_pairs={{1,2},{3,4},{5,6},{2,1},{4,3},{6,5},{9,10},{11,12},{13,14},{10,9},... | collective-permute-start | bytes 98312 | tf_op jit(solution)/shard_map/ppermute | solution.py:332
  1.4 5.8 %collective-permute-start = (f32[8,8,128]{2,1,0:T(8,128)S(1)}, f32[8,8,128]{2,1,0:T(8,128)S(1)}, u32[]{:S(2)}, u32[]{:S(2)}) collective-permute-start(f32[8,8,128]{2,1,0:T(8,128)S(1)} %get-tuple-element.10), channel_id=1, source_target_pairs={{0,1},{2,3},{4,5},{6,7},{1,0},{3,2},{5,4},{7,6},{8,9},{10,11},{12,... | collective-permute-start | bytes 98312 | tf_op jit(solution)/shard_map/ppermute | solution.py:331
  7.2 0.0 collective-permute-done.1.row_odd_ref
  7.2 1.9 %collective-permute-done.row_even_ref = f32[8,8,128]{2,1,0:T(8,128)S(1)} collective-permute-done((f32[8,8,128]{2,1,0:T(8,128)S(1)}, f32[8,8,128]{2,1,0:T(8,128)S(1)}, u32[]{:S(2)}, u32[]{:S(2)}) %collective-permute-start) | collective-permute-done | bytes 32800 | tf_op jit(solution)/shard_map/ppermute | solution.py:331
  9.1 0.0 copy-start
  9.1 1.0 %copy-done = f32[8,128,128]{2,1,0:T(8,128)S(1)} copy-done((f32[8,128,128]{2,1,0:T(8,128)S(1)}, f32[8,128,128]{2,1,0:T(8,128)}, u32[]{:S(2)}) %copy-start) | copy-done | bytes 524312
  10.2 0.2 cut_layers.1
  10.4 0.0 copy-start.1
  10.4 0.0 copy-start.3
  10.4 0.0 copy-start.4
  10.4 0.8 %collective-permute-start.2 = (s32[60,8,128]{2,1,0:T(8,128)S(1)}, s32[60,8,128]{2,1,0:T(8,128)S(1)}, u32[]{:S(2)}, u32[]{:S(2)}) collective-permute-start(s32[60,8,128]{2,1,0:T(8,128)S(1)} %get-tuple-element.7), channel_id=1, source_target_pairs={{8,16},{16,8},{9,17},{17,9},{10,18},{18,10},{11,19},{19,11},{12,20... | collective-permute-start | bytes 737288 | tf_op jit(solution)/shard_map/ppermute | solution.py:334
  11.2 2.9 %collective-permute-start.3 = (s32[60,8,128]{2,1,0:T(8,128)S(1)}, s32[60,8,128]{2,1,0:T(8,128)S(1)}, u32[]{:S(2)}, u32[]{:S(2)}) collective-permute-start(s32[60,8,128]{2,1,0:T(8,128)S(1)} %get-tuple-element.8), channel_id=1, source_target_pairs={{0,8},{16,24},{8,0},{24,16},{1,9},{17,25},{9,1},{25,17},{2,10},{18... | collective-permute-start | bytes 737288 | tf_op jit(solution)/shard_map/ppermute | solution.py:335
  14.2 0.0 collective-permute-done.2.odd_ref
  14.2 1.1 %collective-permute-done.3.even_ref = s32[60,8,128]{2,1,0:T(8,128)S(1)} collective-permute-done((s32[60,8,128]{2,1,0:T(8,128)S(1)}, s32[60,8,128]{2,1,0:T(8,128)S(1)}, u32[]{:S(2)}, u32[]{:S(2)}) %collective-permute-start.3) | collective-permute-done | bytes 245792 | tf_op jit(solution)/shard_map/ppermute | solution.py:335
  15.3 0.0 copy-done.5
  15.3 0.0 copy-done.1
  15.3 0.0 copy-done.3
  15.3 0.0 copy-done.4
  15.3 3.2 %render.1 = s16[4,2,128,128]{3,2,1,0:T(8,128)(2,1)S(1)} custom-call(s32[4,8]{1,0:T(4,128)S(1)} %copy-done.1, f32[2]{0:T(128)S(1)} %copy-done.4, f32[3]{0:T(128)S(1)} %copy-done.5, s32[2,4]{1,0:T(2,128)S(1)} %copy-done.3, f32[8,128,128]{2,1,0:T(8,128)S(1)} %copy-done, s32[60,8,128]{2,1,0:T(8,128)S(1)} %collective-permute-done.2.odd_ref, ...), custom_call_target="tpu_custom_call" | custom-call | tf_op jit(solution)/shard_map/render/pallas_call | solution.py:337
  18.6 0.0 copy-start.2
  18.6 11.4 %all_to_all.5.in_ref = s16[4,2,128,128]{3,2,1,0:T(8,128)(2,1)S(1)} all-to-all(s16[4,2,128,128]{3,2,1,0:T(8,128)(2,1)S(1)} %render.1), channel_id=1, replica_groups=mesh['gz'=4,'xy'=8] {'gz'}, dimensions={0} | all-to-all | bytes 524288 | tf_op jit(solution)/shard_map/all_to_all | solution.py:341
  30.0 0.0 copy-done.2
  30.0 1.4 %composite.1 = f32[2,4,1,32,128]{4,3,2,1,0:T(8,128)} custom-call(s32[2,4]{1,0:T(2,128)S(1)} %copy-done.2, s16[4,2,128,128]{3,2,1,0:T(8,128)(2,1)S(1)} %all_to_all.5.in_ref), custom_call_target="tpu_custom_call" | custom-call | tf_op jit(solution)/shard_map/composite/pallas_call | solution.py:343
  (1 shorter events, 0.0 us)
Async XLA Ops:
  0.8 6.5 %collective-permute-start.1 = (f32[8,8,128]{2,1,0:T(8,128)S(1)}, f32[8,8,128]{2,1,0:T(8,128)S(1)}, u32[]{:S(2)}, u32[]{:S(2)}) collective-permute-start(f32[8,8,128]{2,1,0:T(8,128)S(1)} %get-tuple-element.9), channel_id=1, source_target_pairs={{1,2},{3,4},{5,6},{2,1},{4,3},{6,5},{9,10},{11,12},{13,14},{10,9},... | collective-permute-start | bytes 98312 | tf_op jit(solution)/shard_map/ppermute | solution.py:332
  1.4 7.7 %collective-permute-start = (f32[8,8,128]{2,1,0:T(8,128)S(1)}, f32[8,8,128]{2,1,0:T(8,128)S(1)}, u32[]{:S(2)}, u32[]{:S(2)}) collective-permute-start(f32[8,8,128]{2,1,0:T(8,128)S(1)} %get-tuple-element.10), channel_id=1, source_target_pairs={{0,1},{2,3},{4,5},{6,7},{1,0},{3,2},{5,4},{7,6},{8,9},{10,11},{12,... | collective-permute-start | bytes 98312 | tf_op jit(solution)/shard_map/ppermute | solution.py:331
  9.1 1.0 %copy-start = (f32[8,128,128]{2,1,0:T(8,128)S(1)}, f32[8,128,128]{2,1,0:T(8,128)}, u32[]{:S(2)}) copy-start(f32[8,128,128]{2,1,0:T(8,128)} %own_ref.3) | copy-start | bytes 1572868
  10.2 5.1 %copy-start.5 = (f32[3]{0:T(128)S(1)}, f32[3]{0:T(128)}, u32[]{:S(2)}) copy-start(f32[3]{0:T(128)} %palette_ref.1) | copy-start | bytes 40
  10.4 4.9 %copy-start.1 = (s32[4,8]{1,0:T(4,128)S(1)}, s32[4,8]{1,0:T(4,128)}, u32[]{:S(2)}) copy-start(s32[4,8]{1,0:T(4,128)} %live_ref.1) | copy-start | bytes 388
  10.4 4.9 %copy-start.3 = (s32[2,4]{1,0:T(2,128)S(1)}, s32[2,4]{1,0:T(2,128)}, u32[]{:S(2)}) copy-start(s32[2,4]{1,0:T(2,128)} %owner_ref.1) | copy-start | bytes 100
  10.4 4.9 %copy-start.4 = (f32[2]{0:T(128)S(1)}, f32[2]{0:T(128)}, u32[]{:S(2)}) copy-start(f32[2]{0:T(128)} %slopes_ref.1) | copy-start | bytes 28
  10.4 3.8 %collective-permute-start.2 = (s32[60,8,128]{2,1,0:T(8,128)S(1)}, s32[60,8,128]{2,1,0:T(8,128)S(1)}, u32[]{:S(2)}, u32[]{:S(2)}) collective-permute-start(s32[60,8,128]{2,1,0:T(8,128)S(1)} %get-tuple-element.7), channel_id=1, source_target_pairs={{8,16},{16,8},{9,17},{17,9},{10,18},{18,10},{11,19},{19,11},{12,20... | collective-permute-start | bytes 737288 | tf_op jit(solution)/shard_map/ppermute | solution.py:334
  11.2 4.1 %collective-permute-start.3 = (s32[60,8,128]{2,1,0:T(8,128)S(1)}, s32[60,8,128]{2,1,0:T(8,128)S(1)}, u32[]{:S(2)}, u32[]{:S(2)}) collective-permute-start(s32[60,8,128]{2,1,0:T(8,128)S(1)} %get-tuple-element.8), channel_id=1, source_target_pairs={{0,8},{16,24},{8,0},{24,16},{1,9},{17,25},{9,1},{25,17},{2,10},{18... | collective-permute-start | bytes 737288 | tf_op jit(solution)/shard_map/ppermute | solution.py:335
  18.6 11.4 %copy-start.2 = (s32[2,4]{1,0:T(2,128)S(1)}, s32[2,4]{1,0:T(2,128)}, u32[]{:S(2)}) copy-start(s32[2,4]{1,0:T(2,128)} %order_ref.1) | copy-start | bytes 100

commit v13 on v11

v13 whole, which is shorter than its diff:
```python
import jax
import jax.numpy as jnp
from jax import lax
from jax.experimental import pallas as pl
from jax.experimental.pallas import tpu as pltpu
from jax.sharding import PartitionSpec as P

LIGHT = (0.48, 0.6, 0.64)
REACH = 4
HALO = REACH + 1
TAPS = 2 * REACH + 1
ROW_TILE = 8
PACKED_ROWS = 16
EDGE = 16
VIEWS = 2
TOP = 2.2
STEPS = 65535.0
MIDDLE = 32768
LEVELS_PER_UNIT = 5461.0
ZERO_LEVEL = 1 << 19
GROUP, WORDS = 8, 5
VMEM_BYTES = 40 * 1024 * 1024


def column_matrix(columns):
    source = lax.broadcasted_iota(jnp.int32, (columns, columns), 0)
    target = lax.broadcasted_iota(jnp.int32, (columns, columns), 1)

    def band(shift):
        at = target + shift
        inside = (jnp.abs(source - at) <= REACH) & (at >= 0) & (at < columns)
        return jnp.where(inside, 1.0, 0.0).astype(jnp.float32)

    return jnp.concatenate([band(0), band(1) - band(-1)], axis=1).astype(jnp.bfloat16)


def shear_matrices(slopes_ref, slice_depth, columns, total_depth):
    source = lax.broadcasted_iota(jnp.int32, (columns, columns), 0)
    target = lax.broadcasted_iota(jnp.int32, (columns, columns), 1)
    distance = (source - target).astype(jnp.float32)
    parts = []
    for view in range(VIEWS):
        shift = slopes_ref[view] * (slice_depth + 0.5 - 0.5 * total_depth)
        parts.append(jnp.maximum(0.0, 1.0 - jnp.abs(distance + shift)))
    return jnp.concatenate(parts, axis=1).astype(jnp.bfloat16)


def window_sums(layers, taps):
    sums, width = layers, 1
    while 2 * width < taps:
        sums = [sums[i] + sums[i + width] for i in range(len(sums) - width)]
        width *= 2
    return [sums[i] + layers[i + width] for i in range(len(layers) - width)]


def pack(values):
    v = [(x * LEVELS_PER_UNIT + (ZERO_LEVEL + 0.5)).astype(jnp.int32) for x in values]
    v = [(x - ZERO_LEVEL) & 0xFFFFF for x in v]
    upper = [
        v[5] & 0xFFF,
        (v[5] >> 12) | ((v[6] & 0xF) << 8),
        (v[6] >> 4) & 0xFFF,
        (v[6] >> 16) | ((v[7] & 0xFF) << 4),
        v[7] >> 8,
    ]
    return [v[i] | (upper[i] << 20) for i in range(WORDS)]


def unpack(words):
    upper = [lax.shift_right_logical(w, jnp.full_like(w, 20)) for w in words]
    levels = words + [
        upper[0] | ((upper[1] & 0xFF) << 12),
        (upper[1] >> 8) | (upper[2] << 4) | ((upper[3] & 0xF) << 16),
        (upper[3] >> 4) | (upper[4] << 8),
    ]
    levels = [(x << 12) >> 12 for x in levels]
    return [x.astype(jnp.float32) * (1.0 / LEVELS_PER_UNIT) for x in levels]


def encode(value):
    root = jnp.exp(0.125 * jnp.log(jnp.maximum(value, 1e-30) * (1.0 / TOP)))
    level = jnp.minimum(root * STEPS + 0.5, STEPS)
    return (level.astype(jnp.int32) - MIDDLE).astype(jnp.int16)


def decode(code):
    root = (code.astype(jnp.int32) + MIDDLE).astype(jnp.float32) * (TOP**0.125 / STEPS)
    square = root * root
    fourth = square * square
    return fourth * fourth


def column_sums(total, weights):
    hi = total.astype(jnp.bfloat16)
    rest = total - hi.astype(jnp.float32)
    mid = rest.astype(jnp.bfloat16)
    lo = (rest - mid.astype(jnp.float32)).astype(jnp.bfloat16)
    split = jnp.concatenate([hi, mid, lo], axis=1)
    return jnp.dot(split, weights, preferred_element_type=jnp.float32)


def column_weights(columns):
    band = column_matrix(columns)
    return jnp.concatenate([band, band, band], axis=0)


def shade(center, diff_depth, diff_rows, diff_cols, live, palette_ref, extinct):
    cells = TAPS**3
    floor = 0.01 * (2.0 * cells) ** 2
    square = diff_depth * diff_depth + diff_rows * diff_rows + diff_cols * diff_cols
    toward = LIGHT[0] * diff_depth + LIGHT[1] * diff_rows + LIGHT[2] * diff_cols
    facing = jnp.maximum(0.0, toward) * lax.rsqrt(square + floor)
    twice = center * (2.0 / cells)
    small = jnp.exp(-jnp.abs(twice))
    log1p = jnp.where(small < 1e-4, small * (1.0 - 0.5 * small), jnp.log(1.0 + small))
    softplus = jnp.maximum(twice, 0.0) + log1p
    opacity = jnp.where(live, 1.0 - jnp.exp(-extinct * softplus), 0.0)
    bright = opacity * (0.25 + 0.75 * facing)
    channels = [bright * palette_ref[c] for c in range(3)] + [opacity]
    return [channel.astype(jnp.bfloat16) for channel in channels]


def march(layer, depth_cells, view):
    colour, transmit = None, None
    for z in range(depth_cells):
        part = [layer(z, c) for c in range(4)]
        clear = 1.0 - part[3]
        if z == 0:
            colour, transmit = part[:3], clear
        elif view == 0:
            colour = [colour[c] + transmit * part[c] for c in range(3)]
            transmit = transmit * clear
        else:
            colour = [part[c] + clear * colour[c] for c in range(3)]
            transmit = transmit * clear
    return colour + [1.0 - transmit]


def march_rows(sheared, out_ref, owner_ref, rows, base, height, depth_cells, tile_rows, columns):
    step = min(tile_rows, PACKED_ROWS)
    share = PACKED_ROWS // step
    for row in range(rows.start, rows.stop, step):
        tile, inside = row // tile_rows, row % tile_rows
        at = row - rows.start + base
        for view in range(VIEWS):
            place = owner_ref[view, tile]
            lanes = pl.ds(view * columns, columns)
            values = march(
                lambda z, c: sheared[z, pl.ds(c * height + at, step), lanes], depth_cells, view
            )
            for c in range(0, 4, share):
                value = values[c] if share == 1 else jnp.concatenate(values[c : c + share])
                at_rows = pl.ds(c * tile_rows + inside, PACKED_ROWS)
                out_ref[place, view, at_rows] = encode(value)


def zero_outside(smooth, depth_index, n_depth, layers):
    @pl.when(depth_index == 0)
    def _():
        smooth[0] = jnp.zeros_like(smooth[0])

    @pl.when(depth_index == n_depth - 1)
    def _():
        smooth[layers - 1] = jnp.zeros_like(smooth[layers - 1])


def render_inner(live_slices, slopes, palette, owner, density, deep_odd, deep_even, n_depth):
    depth_cells, row_cells, columns = density.shape
    total_depth = depth_cells * n_depth
    extinct = 3.0 / total_depth
    tile_rows = row_cells // n_depth
    layers = depth_cells + 2
    rows = range(EDGE, row_cells - EDGE)
    height = len(rows)
    lead, span = EDGE - ROW_TILE, height + 2 * ROW_TILE

    def kernel(
        live_ref, slopes_ref, palette_ref, owner_ref, own_ref, odd_ref, even_ref,
        out_ref, deep, shear_ref, triple, smooth, across, sheared,
    ):
        depth_index = lax.axis_index("gz")
        row_index = lax.axis_index("xy")
        odd_depth = depth_index % 2 == 1

        low, high, word = [], [], 0
        for start in range(0, row_cells, ROW_TILE):
            while len(low) < HALO:
                even = [even_ref[word + k] for k in range(WORDS)]
                odd = [odd_ref[word + k] for k in range(WORDS)]
                low += unpack([jnp.where(odd_depth, e, o) for e, o in zip(even, odd)])
                high += unpack([jnp.where(odd_depth, o, e) for e, o in zip(even, odd)])
                word += WORDS
            own = [own_ref[i, pl.ds(start, ROW_TILE)] for i in range(depth_cells)]
            for z, total in enumerate(window_sums(low[:HALO] + own + high[:HALO], TAPS)):
                deep[z, pl.ds(start, ROW_TILE)] = total
            low, high = low[HALO:], high[HALO:]

        slab_start = (depth_index * depth_cells).astype(jnp.float32)
        for z in range(depth_cells):
            shear_ref[z] = shear_matrices(slopes_ref, slab_start + float(z), columns, total_depth)

        weights = column_weights(columns)
        for z in range(layers):
            triple[...] = (
                deep[z, pl.ds(lead - 4, span + ROW_TILE)]
                + deep[z, pl.ds(lead - 3, span + ROW_TILE)]
                + deep[z, pl.ds(lead - 2, span + ROW_TILE)]
            )
            total = triple[pl.ds(0, span)] + triple[pl.ds(3, span)] + triple[pl.ds(6, span)]
            if 1 <= z <= depth_cells:
                both = column_sums(total, weights)
                smooth[z] = both[:, :columns]
                across[z - 1] = both[ROW_TILE : ROW_TILE + height, columns:]
            else:
                smooth[z] = column_sums(total, weights[:, :columns])
        zero_outside(smooth, depth_index, n_depth, layers)

        own_live = live_ref[depth_index, row_index]
        middle = pl.ds(ROW_TILE, height)
        for z in range(depth_cells):
            channels = shade(
                smooth[z + 1, middle],
                smooth[z + 2, middle] - smooth[z, middle],
                smooth[z + 1, pl.ds(ROW_TILE + 1, height)]
                - smooth[z + 1, pl.ds(ROW_TILE - 1, height)],
                across[z],
                z < own_live,
                palette_ref,
                extinct,
            )
            sheared[z] = jnp.dot(
                jnp.concatenate(channels), shear_ref[z], preferred_element_type=jnp.float32
            )
        march_rows(sheared, out_ref, owner_ref, rows, 0, height, depth_cells, tile_rows, columns)

    smem = pl.BlockSpec(memory_space=pltpu.SMEM)
    vmem = pl.BlockSpec(memory_space=pltpu.VMEM)
    return pl.pallas_call(
        kernel,
        out_shape=(
            jax.ShapeDtypeStruct((n_depth, VIEWS, 4 * tile_rows, columns), jnp.int16),
            jax.ShapeDtypeStruct((layers, row_cells, columns), jnp.float32),
            jax.ShapeDtypeStruct((depth_cells, columns, VIEWS * columns), jnp.bfloat16),
        ),
        in_specs=[smem] * 4 + [vmem] * 3,
        out_specs=(vmem,) * 3,
        scratch_shapes=[
            pltpu.VMEM((span + ROW_TILE, columns), jnp.float32),
            pltpu.VMEM((layers, span, columns), jnp.float32),
            pltpu.VMEM((depth_cells, height, columns), jnp.float32),
            pltpu.VMEM((depth_cells, 4 * height, VIEWS * columns), jnp.float32),
        ],
        compiler_params=pltpu.CompilerParams(vmem_limit_bytes=VMEM_BYTES),
        cost_estimate=pl.CostEstimate(
            flops=100 * depth_cells * row_cells * columns,
            bytes_accessed=16 * 4 * depth_cells * row_cells * columns,
            transcendentals=4 * depth_cells * row_cells * columns,
        ),
        name="render_inner",
    )(live_slices, slopes, palette, owner, density, deep_odd, deep_even)


def render_edges(
    live_slices, palette, owner, inner, deep, shear, corner_odd, corner_even, rlo, rhi, n_depth
):
    layers, row_cells, columns = deep.shape
    depth_cells = layers - 2
    n_rows = lax.axis_size("xy")
    extinct = 3.0 / (depth_cells * n_depth)
    tile_rows = row_cells // n_depth
    band = EDGE + 2 * ROW_TILE
    height = 2 * EDGE

    def kernel(
        live_ref, palette_ref, owner_ref, inner_ref, deep_ref, shear_ref,
        corner_odd_ref, corner_even_ref, rlo_ref, rhi_ref,
        out_ref, halo, triple, split_sums, smooth, across, sheared,
    ):
        depth_index = lax.axis_index("gz")
        row_index = lax.axis_index("xy")
        odd_depth = depth_index % 2 == 1

        for side, mid_ref in ((0, rlo_ref), (1, rhi_ref)):
            at = pl.ds(side * ROW_TILE, ROW_TILE)
            even = [corner_even_ref[i, at] for i in range(HALO)]
            odd = [corner_odd_ref[i, at] for i in range(HALO)]
            low = [jnp.where(odd_depth, e, o) for e, o in zip(even, odd)]
            high = [jnp.where(odd_depth, o, e) for e, o in zip(even, odd)]
            outer = 0 if side == 0 else band - ROW_TILE
            inner_at = ROW_TILE if side == 0 else 0
            own_at = 0 if side == 0 else row_cells - (band - ROW_TILE)
            sums = window_sums(low + [mid_ref[i] for i in range(depth_cells)] + high, TAPS)
            for z in range(layers):
                halo[z, side, pl.ds(outer, ROW_TILE)] = sums[z]
                halo[z, side, pl.ds(inner_at, band - ROW_TILE)] = deep_ref[
                    z, pl.ds(own_at, band - ROW_TILE)
                ]

        span = band - ROW_TILE
        for z in range(layers):
            for side in range(2):
                triple[pl.ds(0, span)] = (
                    halo[z, side, pl.ds(3, span)]
                    + halo[z, side, pl.ds(4, span)]
                    + halo[z, side, pl.ds(5, span)]
                )
                split_sums[z, side] = (
                    triple[pl.ds(0, band)] + triple[pl.ds(3, band)] + triple[pl.ds(6, band)]
                )
        both = column_sums(
            split_sums[...].reshape(layers * 2 * band, columns), column_weights(columns)
        ).reshape(layers, 2, band, 2 * columns)
        smooth[...] = both[..., :columns]
        across[...] = both[1:-1, :, :, columns:]

        @pl.when(row_index == 0)
        def _():
            smooth[:, 0, :1] = jnp.zeros((layers, 1, columns), jnp.float32)

        @pl.when(row_index == n_rows - 1)
        def _():
            smooth[:, 1, EDGE + 1 : EDGE + 2] = jnp.zeros((layers, 1, columns), jnp.float32)

        zero_outside(smooth, depth_index, n_depth, layers)

        own_live = live_ref[depth_index, row_index]
        middle = pl.ds(1, EDGE)
        for z in range(depth_cells):
            sides = [
                shade(
                    smooth[z + 1, side, middle],
                    smooth[z + 2, side, middle] - smooth[z, side, middle],
                    smooth[z + 1, side, pl.ds(2, EDGE)] - smooth[z + 1, side, pl.ds(0, EDGE)],
                    across[z, side, middle],
                    z < own_live,
                    palette_ref,
                    extinct,
                )
                for side in range(2)
            ]
            rgba = jnp.concatenate([side[c] for c in range(4) for side in sides])
            sheared[z] = jnp.dot(rgba, shear_ref[z], preferred_element_type=jnp.float32)
        out_ref[...] = inner_ref[...]
        for side, rows in enumerate((range(EDGE), range(row_cells - EDGE, row_cells))):
            march_rows(
                sheared, out_ref, owner_ref, rows, side * EDGE, height,
                depth_cells, tile_rows, columns,
            )

    smem = pl.BlockSpec(memory_space=pltpu.SMEM)
    vmem = pl.BlockSpec(memory_space=pltpu.VMEM)
    return pl.pallas_call(
        kernel,
        out_shape=jax.ShapeDtypeStruct(inner.shape, inner.dtype),
        in_specs=[smem] * 3 + [vmem] * 7,
        out_specs=vmem,
        scratch_shapes=[
            pltpu.VMEM((layers, 2, band, columns), jnp.float32),
            pltpu.VMEM((band + ROW_TILE, columns), jnp.float32),
            pltpu.VMEM((layers, 2, band, columns), jnp.float32),
            pltpu.VMEM((layers, 2, band, columns), jnp.float32),
            pltpu.VMEM((depth_cells, 2, band, columns), jnp.float32),
            pltpu.VMEM((depth_cells, 4 * height, VIEWS * columns), jnp.float32),
        ],
        compiler_params=pltpu.CompilerParams(vmem_limit_bytes=VMEM_BYTES),
        name="render_edges",
    )(live_slices, palette, owner, inner, deep, shear, corner_odd, corner_even, rlo, rhi)


def cut_edges(density):
    depth_cells, row_cells, columns = density.shape

    places = [(i, start) for start in range(0, row_cells, ROW_TILE) for i in range(HALO)]
    words = len(places) // GROUP * WORDS

    def kernel(density_ref, row_even_ref, row_odd_ref, deep_even_ref, deep_odd_ref):
        row_bit = lax.axis_index("xy") % 2
        depth_bit = lax.axis_index("gz") % 2
        last_rows, last_deep = row_cells - ROW_TILE, depth_cells - HALO
        for ref, bit in ((deep_odd_ref, depth_bit), (deep_even_ref, 1 - depth_bit)):
            for group in range(len(places) // GROUP):
                values = [
                    density_ref[bit * last_deep + i, pl.ds(start, ROW_TILE)]
                    for i, start in places[group * GROUP : (group + 1) * GROUP]
                ]
                for k, word in enumerate(pack(values)):
                    ref[group * WORDS + k] = word
        for ref, bit in ((row_even_ref, 1 - row_bit), (row_odd_ref, row_bit)):
            start = pl.multiple_of(bit * last_rows, ROW_TILE)
            ref[...] = density_ref[:, pl.ds(start, ROW_TILE)]

    rows = jax.ShapeDtypeStruct((depth_cells, ROW_TILE, columns), jnp.float32)
    deep = jax.ShapeDtypeStruct((words, ROW_TILE, columns), jnp.int32)
    vmem = pl.BlockSpec(memory_space=pltpu.VMEM)
    return pl.pallas_call(
        kernel,
        out_shape=(rows, rows, deep, deep),
        in_specs=[vmem],
        out_specs=(vmem,) * 4,
        compiler_params=pltpu.CompilerParams(vmem_limit_bytes=VMEM_BYTES),
        name="cut_edges",
    )(density)


def composite_kernel(order_ref, in_ref, out_ref):
    count = in_ref.shape[0]
    rows = in_ref.shape[2] // 4
    for view in range(VIEWS):
        colour, transmit = None, None
        for k in range(count):
            source = order_ref[view, k]
            values = decode(in_ref[source, view])
            part = [values[c * rows : (c + 1) * rows] for c in range(4)]
            clear = 1.0 - part[3]
            if k == 0:
                colour, transmit = part[:3], clear
            else:
                colour = [colour[c] + transmit * part[c] for c in range(3)]
                transmit = transmit * clear
        for c, value in enumerate(colour + [1.0 - transmit]):
            out_ref[view, c, 0] = value


def body(density, live_slices, shear_slopes, palette, depth_order, tile_owner):
    depth_cells, row_cells, columns = density.shape
    n_depth = lax.axis_size("gz")
    edge = depth_cells - HALO
    odd_depth = lax.axis_index("gz") % 2 == 1
    odd_row = lax.axis_index("xy") % 2 == 1

    def pairs(axis, first):
        count = lax.axis_size(axis)
        lower = range(first, count - 1, 2)
        return [(i, i + 1) for i in lower] + [(i + 1, i) for i in lower]

    row_even, row_odd, deep_even, deep_odd = cut_edges(density)
    row_even = lax.ppermute(row_even, "xy", pairs("xy", 0))
    row_odd = lax.ppermute(row_odd, "xy", pairs("xy", 1))
    deep_odd = lax.ppermute(deep_odd, "gz", pairs("gz", 1))
    deep_even = lax.ppermute(deep_even, "gz", pairs("gz", 0))
    rlo = jnp.where(odd_row, row_even, row_odd)
    rhi = jnp.where(odd_row, row_odd, row_even)
    low_corner = jnp.concatenate([rlo[:HALO], rhi[:HALO]], axis=1)
    high_corner = jnp.concatenate([rlo[edge:], rhi[edge:]], axis=1)
    corner_odd = lax.ppermute(
        jnp.where(odd_depth, high_corner, low_corner), "gz", pairs("gz", 1)
    )
    corner_even = lax.ppermute(
        jnp.where(odd_depth, low_corner, high_corner), "gz", pairs("gz", 0)
    )
    inner, deep, shear = render_inner(
        live_slices, shear_slopes, palette, tile_owner, density, deep_odd, deep_even, n_depth
    )
    outgoing = render_edges(
        live_slices, palette, tile_owner, inner, deep, shear,
        corner_odd, corner_even, rlo, rhi, n_depth,
    )
    incoming = lax.all_to_all(outgoing, "gz", split_axis=0, concat_axis=0, tiled=True)
    tile_rows = row_cells // n_depth
    return pl.pallas_call(
        composite_kernel,
        out_shape=jax.ShapeDtypeStruct((VIEWS, 4, 1, tile_rows, columns), jnp.float32),
        in_specs=[pl.BlockSpec(memory_space=pltpu.SMEM), pl.BlockSpec(memory_space=pltpu.VMEM)],
        out_specs=pl.BlockSpec(memory_space=pltpu.VMEM),
        compiler_params=pltpu.CompilerParams(vmem_limit_bytes=VMEM_BYTES),
        name="composite",
    )(depth_order, incoming)


def solution(mesh):
    placed = (P("gz", "xy", None), P(), P(), P(), P(), P())
    return jax.shard_map(
        body, mesh=mesh, in_specs=placed, out_specs=P(None, None, "gz", "xy", None), check_vma=False
    )
```

time: 28.5 us -> 28 us (0.982)
  the two profiles are of different devices: /device:TPU:8 before, /device:TPU:2 now
where the time goes in v13:
time: 28 us; the launch traced here: 27.8 us
  starting transfers between devices  11 us (39%)
  blocking collectives  9.57 us (34%)
  Pallas kernels  5.91 us (21%)
  local copies, waits for them, and re-layouts  1.09 us (4%)
    all_to_all x1, blocking collectives, body(): lax.all_to_all(outgoing, 'gz', split_axis=0, concat_axis=0, tiled=True)  9.57 us
    ppermute x1, starting transfers between devices, body(): row_odd = lax.ppermute(row_odd, 'xy', pairs('xy', 1))  4.92 us
    ppermute x1, starting transfers between devices, body(): deep_even = lax.ppermute(deep_even, 'gz', pairs('gz', 0))  2.93 us
    pallas_call x1, Pallas kernels, render_inner(): pl.pallas_call(kernel, out_shape=(jax.ShapeDtypeStruct((n_depth, VIEWS, 4...  2.76 us
    ppermute x1, starting transfers between devices, body(): lax.ppermute(jnp.where(odd_depth, low_corner, high_corner), 'gz', pairs('...  1.61 us
    pallas_call x1, Pallas kernels, render_edges(): pl.pallas_call(kernel, out_shape=jax.ShapeDtypeStruct(inner.shape, inner....  1.6 us
    pallas_call x1, Pallas kernels, body(): pl.pallas_call(composite_kernel, out_shape=jax.ShapeDtypeStruct((VIEWS, 4...  1.36 us
    unnamed x14, local copies, waits for them, and re-layouts  1.08 us
  transfers between devices with their start and end apart: 6, of which 0 were waited for; matrix products, arithmetic and copies ran while one was open for 0% of the time, Pallas kernels for 10%

profile of v13, /device:TPU:2, one launch (start us, length us, event | category | flops | bytes accessed | tf_op | source)
XLA Modules:
  0.0 27.8 jit_solution(1824800452392562619)
XLA Ops:
  0.0 1.0 %copy-done = f32[8,128,128]{2,1,0:T(8,128)S(1)} copy-done((f32[8,128,128]{2,1,0:T(8,128)S(1)}, f32[8,128,128]{2,1,0:T(8,128)}, u32[]{:S(2)}) %copy-start) | copy-done | bytes 524312
  1.0 0.2 cut_edges.1
  1.2 0.1 collective-permute-start.2
  1.3 4.9 %collective-permute-start.3 = (f32[8,8,128]{2,1,0:T(8,128)S(1)}, f32[8,8,128]{2,1,0:T(8,128)S(1)}, u32[]{:S(2)}, u32[]{:S(2)}) collective-permute-start(f32[8,8,128]{2,1,0:T(8,128)S(1)} %get-tuple-element.18), channel_id=1, source_target_pairs={{1,2},{3,4},{5,6},{2,1},{4,3},{6,5},{9,10},{11,12},{13,14},{10,9},... | collective-permute-start | bytes 98312 | tf_op jit(solution)/shard_map/ppermute | solution.py:438
  6.2 0.7 %collective-permute-start = (s32[50,8,128]{2,1,0:T(8,128)S(1)}, s32[50,8,128]{2,1,0:T(8,128)S(1)}, u32[]{:S(2)}, u32[]{:S(2)}) collective-permute-start(s32[50,8,128]{2,1,0:T(8,128)S(1)} %get-tuple-element.12), channel_id=1, source_target_pairs={{8,16},{16,8},{9,17},{17,9},{10,18},{18,10},{11,19},{19,11},{12,20... | collective-permute-start | bytes 614408 | tf_op jit(solution)/shard_map/ppermute | solution.py:439
  6.9 2.9 %collective-permute-start.1 = (s32[50,8,128]{2,1,0:T(8,128)S(1)}, s32[50,8,128]{2,1,0:T(8,128)S(1)}, u32[]{:S(2)}, u32[]{:S(2)}) collective-permute-start(s32[50,8,128]{2,1,0:T(8,128)S(1)} %get-tuple-element.13), channel_id=1, source_target_pairs={{0,8},{16,24},{8,0},{24,16},{1,9},{17,25},{9,1},{25,17},{2,10},{18... | collective-permute-start | bytes 614408 | tf_op jit(solution)/shard_map/ppermute | solution.py:440
  9.9 0.0 collective-permute-done.2
  9.9 0.0 collective-permute-done.3
  9.9 0.0 copy-start.6
  9.9 0.0 copy-start.2
  9.9 0.0 copy-start.3
  10.0 0.0 copy-start.5
  10.0 0.8 %collective-permute-start.4 = (f32[5,16,128]{2,1,0:T(8,128)S(1)}, f32[5,16,128]{2,1,0:T(8,128)S(1)}, u32[]{:S(2)}, u32[]{:S(2)}) collective-permute-start(f32[5,16,128]{2,1,0:T(8,128)S(1)} %get-tuple-element.20), channel_id=1, source_target_pairs={{8,16},{16,8},{9,17},{17,9},{10,18},{18,10},{11,19},{19,11},{12,20... | collective-permute-start | bytes 122888 | tf_op jit(solution)/shard_map/ppermute | solution.py:445
  10.8 1.6 %collective-permute-start.5 = (f32[5,16,128]{2,1,0:T(8,128)S(1)}, f32[5,16,128]{2,1,0:T(8,128)S(1)}, u32[]{:S(2)}, u32[]{:S(2)}) collective-permute-start(f32[5,16,128]{2,1,0:T(8,128)S(1)} %get-tuple-element.19), channel_id=1, source_target_pairs={{0,8},{16,24},{8,0},{24,16},{1,9},{17,25},{9,1},{25,17},{2,10},{18... | collective-permute-start | bytes 122888 | tf_op jit(solution)/shard_map/ppermute | solution.py:448
  12.4 0.0 collective-permute-done.odd_ref
  12.4 0.0 collective-permute-done.1.even_ref
  12.4 0.0 copy-done.1
  12.4 2.8 %render_inner.1 = (s16[4,2,128,128]{3,2,1,0:T(8,128)(2,1)S(1)}, f32[10,128,128]{2,1,0:T(8,128)S(1)}, bf16[8,128,256]{2,1,0:T(8,128)(2,1)S(1)}) custom-call(s32[4,8]{1,0:T(4,128)S(1)} %copy-done.2, f32[2]{0:T(128)S(1)} %copy-done.6, f32[3]{0:T(128)S(1)} %copy-done.5, s32[2,4]{1,0:T(2,128)S(1)} %copy-done.3, f32[8,128,128]{2,1,0:T(8,128)S(1)} %copy-done.1, ...), custom_call_target="tpu_custom_call" | custom-call | flops 13107200 | bytes 8388608 | tf_op jit(solution)/shard_map/render_inner/pallas_call | solution.py:238
  15.2 0.0 collective-permute-done.4.corner_odd_ref
  15.2 0.0 collective-permute-done.5.corner_even_ref
  15.2 1.6 %render_edges.1 = s16[4,2,128,128]{3,2,1,0:T(8,128)(2,1)S(1)} custom-call(s32[4,8]{1,0:T(4,128)S(1)} %copy-done.2, f32[3]{0:T(128)S(1)} %copy-done.5, s32[2,4]{1,0:T(2,128)S(1)} %copy-done.3, s16[4,2,128,128]{3,2,1,0:T(8,128)(2,1)S(1)} %get-tuple-element.14.inner_ref, f32[10,128,128]{2,1,0:T(8,128)S(1)} %get-tuple-element.15.deep_ref, ...), custom_call_target="tpu_custom_call" | custom-call | tf_op jit(solution)/shard_map/render_edges/pallas_call | solution.py:352
  16.8 0.0 copy-start.4
  16.8 9.6 %all_to_all.5.in_ref = s16[4,2,128,128]{3,2,1,0:T(8,128)(2,1)S(1)} all-to-all(s16[4,2,128,128]{3,2,1,0:T(8,128)(2,1)S(1)} %render_edges.1), channel_id=1, replica_groups=mesh['gz'=4,'xy'=8] {'gz'}, dimensions={0} | all-to-all | bytes 524288 | tf_op jit(solution)/shard_map/all_to_all | solution.py:458
  26.4 1.4 %composite.1 = f32[2,4,1,32,128]{4,3,2,1,0:T(8,128)} custom-call(s32[2,4]{1,0:T(2,128)S(1)} %copy-done.4, s16[4,2,128,128]{3,2,1,0:T(8,128)(2,1)S(1)} %all_to_all.5.in_ref), custom_call_target="tpu_custom_call" | custom-call | tf_op jit(solution)/shard_map/composite/pallas_call | solution.py:460
  (10 shorter events, 0.0 us)
Async XLA Ops:
  0.0 1.0 %copy-start = (f32[8,128,128]{2,1,0:T(8,128)S(1)}, f32[8,128,128]{2,1,0:T(8,128)}, u32[]{:S(2)}) copy-start(f32[8,128,128]{2,1,0:T(8,128)} %own_ref.1) | copy-start | bytes 1572868
  1.0 11.3 %copy-start.1 = (f32[8,128,128]{2,1,0:T(8,128)S(1)}, f32[8,128,128]{2,1,0:T(8,128)}, u32[]{:S(2)}) copy-start(f32[8,128,128]{2,1,0:T(8,128)} %own_ref.1) | copy-start | bytes 1572868
  1.2 8.6 %collective-permute-start.2 = (f32[8,8,128]{2,1,0:T(8,128)S(1)}, f32[8,8,128]{2,1,0:T(8,128)S(1)}, u32[]{:S(2)}, u32[]{:S(2)}) collective-permute-start(f32[8,8,128]{2,1,0:T(8,128)S(1)} %get-tuple-element.17), channel_id=1, source_target_pairs={{0,1},{2,3},{4,5},{6,7},{1,0},{3,2},{5,4},{7,6},{8,9},{10,11},{12,... | collective-permute-start | bytes 98312 | tf_op jit(solution)/shard_map/ppermute | solution.py:437
  1.3 8.6 %collective-permute-start.3 = (f32[8,8,128]{2,1,0:T(8,128)S(1)}, f32[8,8,128]{2,1,0:T(8,128)S(1)}, u32[]{:S(2)}, u32[]{:S(2)}) collective-permute-start(f32[8,8,128]{2,1,0:T(8,128)S(1)} %get-tuple-element.18), channel_id=1, source_target_pairs={{1,2},{3,4},{5,6},{2,1},{4,3},{6,5},{9,10},{11,12},{13,14},{10,9},... | collective-permute-start | bytes 98312 | tf_op jit(solution)/shard_map/ppermute | solution.py:438
  6.2 6.1 %collective-permute-start = (s32[50,8,128]{2,1,0:T(8,128)S(1)}, s32[50,8,128]{2,1,0:T(8,128)S(1)}, u32[]{:S(2)}, u32[]{:S(2)}) collective-permute-start(s32[50,8,128]{2,1,0:T(8,128)S(1)} %get-tuple-element.12), channel_id=1, source_target_pairs={{8,16},{16,8},{9,17},{17,9},{10,18},{18,10},{11,19},{19,11},{12,20... | collective-permute-start | bytes 614408 | tf_op jit(solution)/shard_map/ppermute | solution.py:439
  6.9 5.5 %collective-permute-start.1 = (s32[50,8,128]{2,1,0:T(8,128)S(1)}, s32[50,8,128]{2,1,0:T(8,128)S(1)}, u32[]{:S(2)}, u32[]{:S(2)}) collective-permute-start(s32[50,8,128]{2,1,0:T(8,128)S(1)} %get-tuple-element.13), channel_id=1, source_target_pairs={{0,8},{16,24},{8,0},{24,16},{1,9},{17,25},{9,1},{25,17},{2,10},{18... | collective-permute-start | bytes 614408 | tf_op jit(solution)/shard_map/ppermute | solution.py:440
  9.9 2.5 %copy-start.6 = (f32[2]{0:T(128)S(1)}, f32[2]{0:T(128)}, u32[]{:S(2)}) copy-start(f32[2]{0:T(128)} %slopes_ref.1) | copy-start | bytes 28
  9.9 2.5 %copy-start.2 = (s32[4,8]{1,0:T(4,128)S(1)}, s32[4,8]{1,0:T(4,128)}, u32[]{:S(2)}) copy-start(s32[4,8]{1,0:T(4,128)} %live_ref.3) | copy-start | bytes 388
  9.9 2.5 %copy-start.3 = (s32[2,4]{1,0:T(2,128)S(1)}, s32[2,4]{1,0:T(2,128)}, u32[]{:S(2)}) copy-start(s32[2,4]{1,0:T(2,128)} %owner_ref.3) | copy-start | bytes 100
  10.0 2.5 %copy-start.5 = (f32[3]{0:T(128)S(1)}, f32[3]{0:T(128)}, u32[]{:S(2)}) copy-start(f32[3]{0:T(128)} %palette_ref.3) | copy-start | bytes 40
  10.0 5.2 %collective-permute-start.4 = (f32[5,16,128]{2,1,0:T(8,128)S(1)}, f32[5,16,128]{2,1,0:T(8,128)S(1)}, u32[]{:S(2)}, u32[]{:S(2)}) collective-permute-start(f32[5,16,128]{2,1,0:T(8,128)S(1)} %get-tuple-element.20), channel_id=1, source_target_pairs={{8,16},{16,8},{9,17},{17,9},{10,18},{18,10},{11,19},{19,11},{12,20... | collective-permute-start | bytes 122888 | tf_op jit(solution)/shard_map/ppermute | solution.py:445
  10.8 4.4 %collective-permute-start.5 = (f32[5,16,128]{2,1,0:T(8,128)S(1)}, f32[5,16,128]{2,1,0:T(8,128)S(1)}, u32[]{:S(2)}, u32[]{:S(2)}) collective-permute-start(f32[5,16,128]{2,1,0:T(8,128)S(1)} %get-tuple-element.19), channel_id=1, source_target_pairs={{0,8},{16,24},{8,0},{24,16},{1,9},{17,25},{9,1},{25,17},{2,10},{18... | collective-permute-start | bytes 122888 | tf_op jit(solution)/shard_map/ppermute | solution.py:448
  16.8 9.6 %copy-start.4 = (s32[2,4]{1,0:T(2,128)S(1)}, s32[2,4]{1,0:T(2,128)}, u32[]{:S(2)}) copy-start(s32[2,4]{1,0:T(2,128)} %order_ref.1) | copy-start | bytes 100

commit v14 on v13

--- a/solution.py
+++ b/solution.py
@@ -90,18 +90,36 @@
     return fourth * fourth
 
 
-def column_sums(total, weights):
+def split_parts(total):
     hi = total.astype(jnp.bfloat16)
     rest = total - hi.astype(jnp.float32)
     mid = rest.astype(jnp.bfloat16)
     lo = (rest - mid.astype(jnp.float32)).astype(jnp.bfloat16)
-    split = jnp.concatenate([hi, mid, lo], axis=1)
+    return jnp.concatenate([hi, mid, lo], axis=1)
+
+
+def column_sums(split, columns):
+    band = column_matrix(columns)
+    weights = jnp.concatenate([band, band, band], axis=0)
     return jnp.dot(split, weights, preferred_element_type=jnp.float32)
 
 
-def column_weights(columns):
-    band = column_matrix(columns)
-    return jnp.concatenate([band, band, band], axis=0)
+def shear_tables(slopes, depth_cells, columns, n_depth):
+    def kernel(slopes_ref, shear_ref):
+        slab_start = (lax.axis_index("gz") * depth_cells).astype(jnp.float32)
+        for z in range(depth_cells):
+            shear_ref[z] = shear_matrices(
+                slopes_ref, slab_start + float(z), columns, depth_cells * n_depth
+            )
+
+    return pl.pallas_call(
+        kernel,
+        out_shape=jax.ShapeDtypeStruct((depth_cells, columns, VIEWS * columns), jnp.bfloat16),
+        in_specs=[pl.BlockSpec(memory_space=pltpu.SMEM)],
+        out_specs=pl.BlockSpec(memory_space=pltpu.VMEM),
+        compiler_params=pltpu.CompilerParams(vmem_limit_bytes=VMEM_BYTES),
+        name="shear_tables",
+    )(slopes)
 
 
 def shade(center, diff_depth, diff_rows, diff_cols, live, palette_ref, extinct):
@@ -164,10 +182,9 @@
         smooth[layers - 1] = jnp.zeros_like(smooth[layers - 1])
 
 
-def render_inner(live_slices, slopes, palette, owner, density, deep_odd, deep_even, n_depth):
+def render_inner(live_slices, palette, owner, shear, density, deep_odd, deep_even, n_depth):
     depth_cells, row_cells, columns = density.shape
-    total_depth = depth_cells * n_depth
-    extinct = 3.0 / total_depth
+    extinct = 3.0 / (depth_cells * n_depth)
     tile_rows = row_cells // n_depth
     layers = depth_cells + 2
     rows = range(EDGE, row_cells - EDGE)
@@ -175,8 +192,8 @@
     lead, span = EDGE - ROW_TILE, height + 2 * ROW_TILE
 
     def kernel(
-        live_ref, slopes_ref, palette_ref, owner_ref, own_ref, odd_ref, even_ref,
-        out_ref, deep, shear_ref, triple, smooth, across, sheared,
+        live_ref, palette_ref, owner_ref, shear_ref, own_ref, odd_ref, even_ref,
+        out_ref, deep, triple, split, smooth, across, sheared,
     ):
         depth_index = lax.axis_index("gz")
         row_index = lax.axis_index("xy")
@@ -195,24 +212,18 @@
                 deep[z, pl.ds(start, ROW_TILE)] = total
             low, high = low[HALO:], high[HALO:]
 
-        slab_start = (depth_index * depth_cells).astype(jnp.float32)
-        for z in range(depth_cells):
-            shear_ref[z] = shear_matrices(slopes_ref, slab_start + float(z), columns, total_depth)
-
-        weights = column_weights(columns)
         for z in range(layers):
             triple[...] = (
                 deep[z, pl.ds(lead - 4, span + ROW_TILE)]
                 + deep[z, pl.ds(lead - 3, span + ROW_TILE)]
                 + deep[z, pl.ds(lead - 2, span + ROW_TILE)]
             )
-            total = triple[pl.ds(0, span)] + triple[pl.ds(3, span)] + triple[pl.ds(6, span)]
-            if 1 <= z <= depth_cells:
-                both = column_sums(total, weights)
-                smooth[z] = both[:, :columns]
-                across[z - 1] = both[ROW_TILE : ROW_TILE + height, columns:]
-            else:
-                smooth[z] = column_sums(total, weights[:, :columns])
+            split[pl.ds(z * span, span)] = split_parts(
+                triple[pl.ds(0, span)] + triple[pl.ds(3, span)] + triple[pl.ds(6, span)]
+            )
+        both = column_sums(split[...], columns).reshape(layers, span, 2 * columns)
+        smooth[...] = both[..., :columns]
+        across[...] = both[1:-1, ROW_TILE : ROW_TILE + height, columns:]
         zero_outside(smooth, depth_index, n_depth, layers)
 
         own_live = live_ref[depth_index, row_index]
@@ -240,12 +251,12 @@
         out_shape=(
             jax.ShapeDtypeStruct((n_depth, VIEWS, 4 * tile_rows, columns), jnp.int16),
             jax.ShapeDtypeStruct((layers, row_cells, columns), jnp.float32),
-            jax.ShapeDtypeStruct((depth_cells, columns, VIEWS * columns), jnp.bfloat16),
         ),
-        in_specs=[smem] * 4 + [vmem] * 3,
-        out_specs=(vmem,) * 3,
+        in_specs=[smem] * 3 + [vmem] * 4,
+        out_specs=(vmem,) * 2,
         scratch_shapes=[
             pltpu.VMEM((span + ROW_TILE, columns), jnp.float32),
+            pltpu.VMEM((layers * span, 3 * columns), jnp.bfloat16),
             pltpu.VMEM((layers, span, columns), jnp.float32),
             pltpu.VMEM((depth_cells, height, columns), jnp.float32),
             pltpu.VMEM((depth_cells, 4 * height, VIEWS * columns), jnp.float32),
@@ -257,7 +268,7 @@
             transcendentals=4 * depth_cells * row_cells * columns,
         ),
         name="render_inner",
-    )(live_slices, slopes, palette, owner, density, deep_odd, deep_even)
+    )(live_slices, palette, owner, shear, density, deep_odd, deep_even)
 
 
 def render_edges(
@@ -274,7 +285,7 @@
     def kernel(
         live_ref, palette_ref, owner_ref, inner_ref, deep_ref, shear_ref,
         corner_odd_ref, corner_even_ref, rlo_ref, rhi_ref,
-        out_ref, halo, triple, split_sums, smooth, across, sheared,
+        out_ref, halo, triple, split, smooth, across, sheared,
     ):
         depth_index = lax.axis_index("gz")
         row_index = lax.axis_index("xy")
@@ -304,12 +315,10 @@
                     + halo[z, side, pl.ds(4, span)]
                     + halo[z, side, pl.ds(5, span)]
                 )
-                split_sums[z, side] = (
+                split[pl.ds((2 * z + side) * band, band)] = split_parts(
                     triple[pl.ds(0, band)] + triple[pl.ds(3, band)] + triple[pl.ds(6, band)]
                 )
-        both = column_sums(
-            split_sums[...].reshape(layers * 2 * band, columns), column_weights(columns)
-        ).reshape(layers, 2, band, 2 * columns)
+        both = column_sums(split[...], columns).reshape(layers, 2, band, 2 * columns)
         smooth[...] = both[..., :columns]
         across[...] = both[1:-1, :, :, columns:]
 
@@ -357,7 +366,7 @@
         scratch_shapes=[
             pltpu.VMEM((layers, 2, band, columns), jnp.float32),
             pltpu.VMEM((band + ROW_TILE, columns), jnp.float32),
-            pltpu.VMEM((layers, 2, band, columns), jnp.float32),
+            pltpu.VMEM((layers * 2 * band, 3 * columns), jnp.bfloat16),
             pltpu.VMEM((layers, 2, band, columns), jnp.float32),
             pltpu.VMEM((depth_cells, 2, band, columns), jnp.float32),
             pltpu.VMEM((depth_cells, 4 * height, VIEWS * columns), jnp.float32),
@@ -448,8 +457,9 @@
     corner_even = lax.ppermute(
         jnp.where(odd_depth, low_corner, high_corner), "gz", pairs("gz", 0)
     )
-    inner, deep, shear = render_inner(
-        live_slices, shear_slopes, palette, tile_owner, density, deep_odd, deep_even, n_depth
+    shear = shear_tables(shear_slopes, depth_cells, columns, n_depth)
+    inner, deep = render_inner(
+        live_slices, palette, tile_owner, shear, density, deep_odd, deep_even, n_depth
     )
     outgoing = render_edges(
         live_slices, palette, tile_owner, inner, deep, shear,

time: 28 us -> 28.5 us (1.018)
  the two profiles are of different devices: /device:TPU:2 before, /device:TPU:8 now
where the time goes in v14:
time: 28.5 us; the launch traced here: 28.2 us
  starting transfers between devices  11.1 us (39%)
  blocking collectives  8.42 us (30%)
  Pallas kernels  6.7 us (24%)
  local copies, waits for them, and re-layouts  1.08 us (4%)
  waiting for transfers between devices  0.76 us (3%)
    all_to_all x1, blocking collectives, body(): lax.all_to_all(outgoing, 'gz', split_axis=0, concat_axis=0, tiled=True)  8.42 us
    ppermute x1, starting transfers between devices, body(): deep_even = lax.ppermute(deep_even, 'gz', pairs('gz', 0))  3.34 us
    ppermute x1, starting transfers between devices, body(): lax.ppermute(jnp.where(odd_depth, low_corner, high_corner), 'gz', pairs('...  2.94 us
    pallas_call x1, Pallas kernels, render_inner(): pl.pallas_call(kernel, out_shape=(jax.ShapeDtypeStruct((n_depth, VIEWS, 4...  2.83 us
    ppermute x1, starting transfers between devices, body(): row_odd = lax.ppermute(row_odd, 'xy', pairs('xy', 1))  1.91 us
    pallas_call x1, Pallas kernels, render_edges(): pl.pallas_call(kernel, out_shape=jax.ShapeDtypeStruct(inner.shape, inner....  1.6 us
    ppermute x1, starting transfers between devices, body(): row_even = lax.ppermute(row_even, 'xy', pairs('xy', 0))  1.56 us
    pallas_call x1, Pallas kernels, body(): pl.pallas_call(composite_kernel, out_shape=jax.ShapeDtypeStruct((VIEWS, 4...  1.36 us
  transfers between devices with their start and end apart: 6, of which 1 were waited for; matrix products, arithmetic and copies ran while one was open for 0% of the time, Pallas kernels for 13%

profile of v14, /device:TPU:8, one launch (start us, length us, event | category | flops | bytes accessed | tf_op | source)
XLA Modules:
  0.0 28.2 jit_solution(11731646918274508243)
XLA Ops:
  0.0 1.0 %copy-done = f32[8,128,128]{2,1,0:T(8,128)S(1)} copy-done((f32[8,128,128]{2,1,0:T(8,128)S(1)}, f32[8,128,128]{2,1,0:T(8,128)}, u32[]{:S(2)}) %copy-start) | copy-done | bytes 524312
  1.0 0.2 cut_edges.1
  1.2 1.6 %collective-permute-start.2 = (f32[8,8,128]{2,1,0:T(8,128)S(1)}, f32[8,8,128]{2,1,0:T(8,128)S(1)}, u32[]{:S(2)}, u32[]{:S(2)}) collective-permute-start(f32[8,8,128]{2,1,0:T(8,128)S(1)} %get-tuple-element.15), channel_id=1, source_target_pairs={{0,1},{2,3},{4,5},{6,7},{1,0},{3,2},{5,4},{7,6},{8,9},{10,11},{12,... | collective-permute-start | bytes 98312 | tf_op jit(solution)/shard_map/ppermute | solution.py:446
  2.8 1.9 %collective-permute-start.3 = (f32[8,8,128]{2,1,0:T(8,128)S(1)}, f32[8,8,128]{2,1,0:T(8,128)S(1)}, u32[]{:S(2)}, u32[]{:S(2)}) collective-permute-start(f32[8,8,128]{2,1,0:T(8,128)S(1)} %get-tuple-element.16), channel_id=1, source_target_pairs={{1,2},{3,4},{5,6},{2,1},{4,3},{6,5},{9,10},{11,12},{13,14},{10,9},... | collective-permute-start | bytes 98312 | tf_op jit(solution)/shard_map/ppermute | solution.py:447
  4.7 0.7 %collective-permute-start = (s32[50,8,128]{2,1,0:T(8,128)S(1)}, s32[50,8,128]{2,1,0:T(8,128)S(1)}, u32[]{:S(2)}, u32[]{:S(2)}) collective-permute-start(s32[50,8,128]{2,1,0:T(8,128)S(1)} %get-tuple-element.11), channel_id=1, source_target_pairs={{8,16},{16,8},{9,17},{17,9},{10,18},{18,10},{11,19},{19,11},{12,20... | collective-permute-start | bytes 614408 | tf_op jit(solution)/shard_map/ppermute | solution.py:448
  5.4 3.3 %collective-permute-start.1 = (s32[50,8,128]{2,1,0:T(8,128)S(1)}, s32[50,8,128]{2,1,0:T(8,128)S(1)}, u32[]{:S(2)}, u32[]{:S(2)}) collective-permute-start(s32[50,8,128]{2,1,0:T(8,128)S(1)} %get-tuple-element.12), channel_id=1, source_target_pairs={{0,8},{16,24},{8,0},{24,16},{1,9},{17,25},{9,1},{25,17},{2,10},{18... | collective-permute-start | bytes 614408 | tf_op jit(solution)/shard_map/ppermute | solution.py:449
  8.7 0.0 collective-permute-done.2
  8.7 0.7 %collective-permute-done.3 = f32[8,8,128]{2,1,0:T(8,128)S(1)} collective-permute-done((f32[8,8,128]{2,1,0:T(8,128)S(1)}, f32[8,8,128]{2,1,0:T(8,128)S(1)}, u32[]{:S(2)}, u32[]{:S(2)}) %collective-permute-start.3) | collective-permute-done | bytes 32800 | tf_op jit(solution)/shard_map/ppermute | solution.py:447
  9.5 0.7 %collective-permute-start.4 = (f32[5,16,128]{2,1,0:T(8,128)S(1)}, f32[5,16,128]{2,1,0:T(8,128)S(1)}, u32[]{:S(2)}, u32[]{:S(2)}) collective-permute-start(f32[5,16,128]{2,1,0:T(8,128)S(1)} %get-tuple-element.18), channel_id=1, source_target_pairs={{8,16},{16,8},{9,17},{17,9},{10,18},{18,10},{11,19},{19,11},{12,20... | collective-permute-start | bytes 122888 | tf_op jit(solution)/shard_map/ppermute | solution.py:454
  10.2 0.0 copy-start.2
  10.2 0.0 copy-start.3
  10.2 0.0 copy-start.4
  10.2 2.9 %collective-permute-start.5 = (f32[5,16,128]{2,1,0:T(8,128)S(1)}, f32[5,16,128]{2,1,0:T(8,128)S(1)}, u32[]{:S(2)}, u32[]{:S(2)}) collective-permute-start(f32[5,16,128]{2,1,0:T(8,128)S(1)} %get-tuple-element.17), channel_id=1, source_target_pairs={{0,8},{16,24},{8,0},{24,16},{1,9},{17,25},{9,1},{25,17},{2,10},{18... | collective-permute-start | bytes 122888 | tf_op jit(solution)/shard_map/ppermute | solution.py:457
  13.2 0.0 copy-done.6
  13.2 0.7 %shear_tables.1.shear_ref = bf16[8,128,256]{2,1,0:T(8,128)(2,1)S(1)} custom-call(f32[2]{0:T(128)S(1)} %copy-done.6), custom_call_target="tpu_custom_call" | custom-call | tf_op jit(solution)/shard_map/shear_tables/pallas_call | solution.py:115
  13.9 0.0 collective-permute-done.odd_ref
  13.9 0.0 collective-permute-done.1.even_ref
  14.0 2.8 %render_inner.1 = (s16[4,2,128,128]{3,2,1,0:T(8,128)(2,1)S(1)}, f32[10,128,128]{2,1,0:T(8,128)S(1)}) custom-call(s32[4,8]{1,0:T(4,128)S(1)} %copy-done.2, f32[3]{0:T(128)S(1)} %copy-done.4, s32[2,4]{1,0:T(2,128)S(1)} %copy-done.3, bf16[8,128,256]{2,1,0:T(8,128)(2,1)S(1)} %shear_tables.1.shear_ref, f32[8,128,128]{2,1,0:T(8,128)S(1)} %copy-done.1, ...), custom_call_target="tpu_custom_call" | custom-call | flops 13107200 | bytes 8388608 | tf_op jit(solution)/shard_map/render_inner/pallas_call | solution.py:249
  16.8 0.0 collective-permute-done.4.corner_odd_ref
  16.8 0.0 collective-permute-done.5.corner_even_ref
  16.8 1.6 %render_edges.1 = s16[4,2,128,128]{3,2,1,0:T(8,128)(2,1)S(1)} custom-call(s32[4,8]{1,0:T(4,128)S(1)} %copy-done.2, f32[3]{0:T(128)S(1)} %copy-done.4, s32[2,4]{1,0:T(2,128)S(1)} %copy-done.3, s16[4,2,128,128]{3,2,1,0:T(8,128)(2,1)S(1)} %get-tuple-element.13.inner_ref, f32[10,128,128]{2,1,0:T(8,128)S(1)} %get-tuple-element.14.deep_ref, ...), custom_call_target="tpu_custom_call" | custom-call | tf_op jit(solution)/shard_map/render_edges/pallas_call | solution.py:361
  18.4 0.0 copy-start.5
  18.5 8.4 %all_to_all.5.in_ref = s16[4,2,128,128]{3,2,1,0:T(8,128)(2,1)S(1)} all-to-all(s16[4,2,128,128]{3,2,1,0:T(8,128)(2,1)S(1)} %render_edges.1), channel_id=1, replica_groups=mesh['gz'=4,'xy'=8] {'gz'}, dimensions={0} | all-to-all | bytes 524288 | tf_op jit(solution)/shard_map/all_to_all | solution.py:468
  26.9 1.4 %composite.1 = f32[2,4,1,32,128]{4,3,2,1,0:T(8,128)} custom-call(s32[2,4]{1,0:T(2,128)S(1)} %copy-done.5, s16[4,2,128,128]{3,2,1,0:T(8,128)(2,1)S(1)} %all_to_all.5.in_ref), custom_call_target="tpu_custom_call" | custom-call | tf_op jit(solution)/shard_map/composite/pallas_call | solution.py:470
  (11 shorter events, 0.0 us)
Async XLA Ops:
  0.0 1.0 %copy-start = (f32[8,128,128]{2,1,0:T(8,128)S(1)}, f32[8,128,128]{2,1,0:T(8,128)}, u32[]{:S(2)}) copy-start(f32[8,128,128]{2,1,0:T(8,128)} %own_ref.1) | copy-start | bytes 1572868
  1.2 7.5 %collective-permute-start.2 = (f32[8,8,128]{2,1,0:T(8,128)S(1)}, f32[8,8,128]{2,1,0:T(8,128)S(1)}, u32[]{:S(2)}, u32[]{:S(2)}) collective-permute-start(f32[8,8,128]{2,1,0:T(8,128)S(1)} %get-tuple-element.15), channel_id=1, source_target_pairs={{0,1},{2,3},{4,5},{6,7},{1,0},{3,2},{5,4},{7,6},{8,9},{10,11},{12,... | collective-permute-start | bytes 98312 | tf_op jit(solution)/shard_map/ppermute | solution.py:446
  2.8 6.7 %collective-permute-start.3 = (f32[8,8,128]{2,1,0:T(8,128)S(1)}, f32[8,8,128]{2,1,0:T(8,128)S(1)}, u32[]{:S(2)}, u32[]{:S(2)}) collective-permute-start(f32[8,8,128]{2,1,0:T(8,128)S(1)} %get-tuple-element.16), channel_id=1, source_target_pairs={{1,2},{3,4},{5,6},{2,1},{4,3},{6,5},{9,10},{11,12},{13,14},{10,9},... | collective-permute-start | bytes 98312 | tf_op jit(solution)/shard_map/ppermute | solution.py:447
  4.7 9.2 %collective-permute-start = (s32[50,8,128]{2,1,0:T(8,128)S(1)}, s32[50,8,128]{2,1,0:T(8,128)S(1)}, u32[]{:S(2)}, u32[]{:S(2)}) collective-permute-start(s32[50,8,128]{2,1,0:T(8,128)S(1)} %get-tuple-element.11), channel_id=1, source_target_pairs={{8,16},{16,8},{9,17},{17,9},{10,18},{18,10},{11,19},{19,11},{12,20... | collective-permute-start | bytes 614408 | tf_op jit(solution)/shard_map/ppermute | solution.py:448
  5.4 8.5 %collective-permute-start.1 = (s32[50,8,128]{2,1,0:T(8,128)S(1)}, s32[50,8,128]{2,1,0:T(8,128)S(1)}, u32[]{:S(2)}, u32[]{:S(2)}) collective-permute-start(s32[50,8,128]{2,1,0:T(8,128)S(1)} %get-tuple-element.12), channel_id=1, source_target_pairs={{0,8},{16,24},{8,0},{24,16},{1,9},{17,25},{9,1},{25,17},{2,10},{18... | collective-permute-start | bytes 614408 | tf_op jit(solution)/shard_map/ppermute | solution.py:449
  8.7 4.5 %copy-start.6 = (f32[2]{0:T(128)S(1)}, f32[2]{0:T(128)}, u32[]{:S(2)}) copy-start(f32[2]{0:T(128)} %slopes_ref.1) | copy-start | bytes 28
  8.7 5.2 %copy-start.1 = (f32[8,128,128]{2,1,0:T(8,128)S(1)}, f32[8,128,128]{2,1,0:T(8,128)}, u32[]{:S(2)}) copy-start(f32[8,128,128]{2,1,0:T(8,128)} %own_ref.1) | copy-start | bytes 1572868
  9.5 7.3 %collective-permute-start.4 = (f32[5,16,128]{2,1,0:T(8,128)S(1)}, f32[5,16,128]{2,1,0:T(8,128)S(1)}, u32[]{:S(2)}, u32[]{:S(2)}) collective-permute-start(f32[5,16,128]{2,1,0:T(8,128)S(1)} %get-tuple-element.18), channel_id=1, source_target_pairs={{8,16},{16,8},{9,17},{17,9},{10,18},{18,10},{11,19},{19,11},{12,20... | collective-permute-start | bytes 122888 | tf_op jit(solution)/shard_map/ppermute | solution.py:454
  10.2 3.7 %copy-start.2 = (s32[4,8]{1,0:T(4,128)S(1)}, s32[4,8]{1,0:T(4,128)}, u32[]{:S(2)}) copy-start(s32[4,8]{1,0:T(4,128)} %live_ref.3) | copy-start | bytes 388
  10.2 3.7 %copy-start.3 = (s32[2,4]{1,0:T(2,128)S(1)}, s32[2,4]{1,0:T(2,128)}, u32[]{:S(2)}) copy-start(s32[2,4]{1,0:T(2,128)} %owner_ref.3) | copy-start | bytes 100
  10.2 3.7 %copy-start.4 = (f32[3]{0:T(128)S(1)}, f32[3]{0:T(128)}, u32[]{:S(2)}) copy-start(f32[3]{0:T(128)} %palette_ref.3) | copy-start | bytes 40
  10.2 6.6 %collective-permute-start.5 = (f32[5,16,128]{2,1,0:T(8,128)S(1)}, f32[5,16,128]{2,1,0:T(8,128)S(1)}, u32[]{:S(2)}, u32[]{:S(2)}) collective-permute-start(f32[5,16,128]{2,1,0:T(8,128)S(1)} %get-tuple-element.17), channel_id=1, source_target_pairs={{0,8},{16,24},{8,0},{24,16},{1,9},{17,25},{9,1},{25,17},{2,10},{18... | collective-permute-start | bytes 122888 | tf_op jit(solution)/shard_map/ppermute | solution.py:457
  18.4 8.4 %copy-start.5 = (s32[2,4]{1,0:T(2,128)S(1)}, s32[2,4]{1,0:T(2,128)}, u32[]{:S(2)}) copy-start(s32[2,4]{1,0:T(2,128)} %order_ref.1) | copy-start | bytes 100

commit v15 on v13

--- a/solution.py
+++ b/solution.py
@@ -434,10 +434,15 @@
         return [(i, i + 1) for i in lower] + [(i + 1, i) for i in lower]
 
     row_even, row_odd, deep_even, deep_odd = cut_edges(density)
-    row_even = lax.ppermute(row_even, "xy", pairs("xy", 0))
-    row_odd = lax.ppermute(row_odd, "xy", pairs("xy", 1))
     deep_odd = lax.ppermute(deep_odd, "gz", pairs("gz", 1))
     deep_even = lax.ppermute(deep_even, "gz", pairs("gz", 0))
+
+    def exchange_rows(even, odd):
+        return lax.ppermute(even, "xy", pairs("xy", 0)), lax.ppermute(odd, "xy", pairs("xy", 1))
+
+    row_even, row_odd = lax.cond(
+        lax.axis_index("gz") < 0, lambda even, odd: (even, odd), exchange_rows, row_even, row_odd
+    )
     rlo = jnp.where(odd_row, row_even, row_odd)
     rhi = jnp.where(odd_row, row_odd, row_even)
     low_corner = jnp.concatenate([rlo[:HALO], rhi[:HALO]], axis=1)

time: 28 us -> 29.9 us (1.068)
  the two profiles are of different devices: /device:TPU:2 before, /device:TPU:24 now
where the time goes in v15:
time: 29.9 us; the launch traced here: 29.6 us
  starting transfers between devices  9.63 us (32%)
  blocking collectives  8.42 us (28%)
  Pallas kernels  5.91 us (20%)
  waiting for transfers between devices  4.38 us (15%)
  local copies, waits for them, and re-layouts  1.08 us (4%)
    all_to_all x1, blocking collectives, body(): lax.all_to_all(outgoing, 'gz', split_axis=0, concat_axis=0, tiled=True)  8.42 us
    ppermute x1, waiting for transfers between devices, exchange_rows(): lax.ppermute(odd, 'xy', pairs('xy', 1))  4.27 us
    ppermute x1, starting transfers between devices, body(): deep_even = lax.ppermute(deep_even, 'gz', pairs('gz', 0))  2.93 us
    pallas_call x1, Pallas kernels, render_inner(): pl.pallas_call(kernel, out_shape=(jax.ShapeDtypeStruct((n_depth, VIEWS, 4...  2.76 us
    ppermute x1, starting transfers between devices, exchange_rows(): lax.ppermute(odd, 'xy', pairs('xy', 1))  2.32 us
    pallas_call x1, Pallas kernels, render_edges(): pl.pallas_call(kernel, out_shape=jax.ShapeDtypeStruct(inner.shape, inner....  1.6 us
    ppermute x1, starting transfers between devices, exchange_rows(): lax.ppermute(even, 'xy', pairs('xy', 0))  1.49 us
    ppermute x1, starting transfers between devices, body(): lax.ppermute(jnp.where(odd_depth, low_corner, high_corner), 'gz', pairs('...  1.42 us
  transfers between devices with their start and end apart: 6, of which 2 were waited for; matrix products, arithmetic and copies ran while one was open for 0% of the time, Pallas kernels for 9%

profile of v15, /device:TPU:24, one launch (start us, length us, event | category | flops | bytes accessed | tf_op | source)
XLA Modules:
  0.0 29.6 jit_solution(5533889354357926584)
XLA Ops:
  0.0 1.0 %copy-done = f32[8,128,128]{2,1,0:T(8,128)S(1)} copy-done((f32[8,128,128]{2,1,0:T(8,128)S(1)}, f32[8,128,128]{2,1,0:T(8,128)}, u32[]{:S(2)}) %copy-start) | copy-done | bytes 524312
  1.0 0.2 cut_edges.1
  1.2 0.7 %collective-permute-start.2 = (s32[50,8,128]{2,1,0:T(8,128)S(1)}, s32[50,8,128]{2,1,0:T(8,128)S(1)}, u32[]{:S(2)}, u32[]{:S(2)}) collective-permute-start(s32[50,8,128]{2,1,0:T(8,128)S(1)} %get-tuple-element.24), channel_id=1, source_target_pairs={{8,16},{16,8},{9,17},{17,9},{10,18},{18,10},{11,19},{19,11},{12,20... | collective-permute-start | bytes 614408 | tf_op jit(solution)/shard_map/ppermute | solution.py:437
  1.9 2.9 %collective-permute-start.3 = (s32[50,8,128]{2,1,0:T(8,128)S(1)}, s32[50,8,128]{2,1,0:T(8,128)S(1)}, u32[]{:S(2)}, u32[]{:S(2)}) collective-permute-start(s32[50,8,128]{2,1,0:T(8,128)S(1)} %get-tuple-element.25), channel_id=1, source_target_pairs={{0,8},{16,24},{8,0},{24,16},{1,9},{17,25},{9,1},{25,17},{2,10},{18... | collective-permute-start | bytes 614408 | tf_op jit(solution)/shard_map/ppermute | solution.py:438
  4.9 8.2 %conditional.1 = (f32[8,8,128]{2,1,0:T(8,128)S(1)}, f32[8,8,128]{2,1,0:T(8,128)S(1)}) conditional(s32[]{:T(128)} %convert_element_type.3, (f32[8,8,128]{2,1,0:T(8,128)S(1)}, f32[8,8,128]{2,1,0:T(8,128)S(1)}) %tuple.12, (f32[8,8,128]{2,1,0:T(8,128)S(1)}, f32[8,8,128]{2,1,0:T(8,128)S(1)}) %tuple.12), branch_computations={%region_0.1_spmd, %region_1.2_spmd} | conditional | bytes 262240 | solution.py:443
  4.9 1.5 %collective-permute-start = (f32[8,8,128]{2,1,0:T(8,128)S(1)}, f32[8,8,128]{2,1,0:T(8,128)S(1)}, u32[]{:S(2)}, u32[]{:S(2)}) collective-permute-start(f32[8,8,128]{2,1,0:T(8,128)S(1)} %get-tuple-element.13), channel_id=1, source_target_pairs={{0,1},{2,3},{4,5},{6,7},{1,0},{3,2},{5,4},{7,6},{8,9},{10,11},{12,... | collective-permute-start | bytes 98312 | tf_op jit(solution)/shard_map/cond/branch_0_fun/ppermute | solution.py:441
  6.3 2.3 %collective-permute-start.1 = (f32[8,8,128]{2,1,0:T(8,128)S(1)}, f32[8,8,128]{2,1,0:T(8,128)S(1)}, u32[]{:S(2)}, u32[]{:S(2)}) collective-permute-start(f32[8,8,128]{2,1,0:T(8,128)S(1)} %get-tuple-element.14), channel_id=1, source_target_pairs={{1,2},{3,4},{5,6},{2,1},{4,3},{6,5},{9,10},{11,12},{13,14},{10,9},... | collective-permute-start | bytes 98312 | tf_op jit(solution)/shard_map/cond/branch_0_fun/ppermute | solution.py:441
  8.7 0.1 collective-permute-done
  8.8 4.3 %collective-permute-done.1 = f32[8,8,128]{2,1,0:T(8,128)S(1)} collective-permute-done((f32[8,8,128]{2,1,0:T(8,128)S(1)}, f32[8,8,128]{2,1,0:T(8,128)S(1)}, u32[]{:S(2)}, u32[]{:S(2)}) %collective-permute-start.1) | collective-permute-done | bytes 32800 | tf_op jit(solution)/shard_map/cond/branch_0_fun/ppermute | solution.py:441
  13.1 0.0 copy-start.6
  13.1 0.0 copy-start.2
  13.1 0.0 copy-start.3
  13.1 0.0 copy-start.5
  13.2 0.8 %collective-permute-start.4 = (f32[5,16,128]{2,1,0:T(8,128)S(1)}, f32[5,16,128]{2,1,0:T(8,128)S(1)}, u32[]{:S(2)}, u32[]{:S(2)}) collective-permute-start(f32[5,16,128]{2,1,0:T(8,128)S(1)} %get-tuple-element.34), channel_id=1, source_target_pairs={{8,16},{16,8},{9,17},{17,9},{10,18},{18,10},{11,19},{19,11},{12,20... | collective-permute-start | bytes 122888 | tf_op jit(solution)/shard_map/ppermute | solution.py:450
  14.0 1.4 %collective-permute-start.5 = (f32[5,16,128]{2,1,0:T(8,128)S(1)}, f32[5,16,128]{2,1,0:T(8,128)S(1)}, u32[]{:S(2)}, u32[]{:S(2)}) collective-permute-start(f32[5,16,128]{2,1,0:T(8,128)S(1)} %get-tuple-element.33), channel_id=1, source_target_pairs={{0,8},{16,24},{8,0},{24,16},{1,9},{17,25},{9,1},{25,17},{2,10},{18... | collective-permute-start | bytes 122888 | tf_op jit(solution)/shard_map/ppermute | solution.py:453
  15.4 0.0 collective-permute-done.2.odd_ref
  15.4 0.0 collective-permute-done.3.even_ref
  15.4 2.8 %render_inner.1 = (s16[4,2,128,128]{3,2,1,0:T(8,128)(2,1)S(1)}, f32[10,128,128]{2,1,0:T(8,128)S(1)}, bf16[8,128,256]{2,1,0:T(8,128)(2,1)S(1)}) custom-call(s32[4,8]{1,0:T(4,128)S(1)} %copy-done.2, f32[2]{0:T(128)S(1)} %copy-done.6, f32[3]{0:T(128)S(1)} %copy-done.5, s32[2,4]{1,0:T(2,128)S(1)} %copy-done.3, f32[8,128,128]{2,1,0:T(8,128)S(1)} %copy-done.1, ...), custom_call_target="tpu_custom_call" | custom-call | flops 13107200 | bytes 8388608 | tf_op jit(solution)/shard_map/render_inner/pallas_call | solution.py:238
  18.2 0.0 collective-permute-done.4.corner_odd_ref
  18.2 0.0 collective-permute-done.5.corner_even_ref
  18.2 1.6 %render_edges.1 = s16[4,2,128,128]{3,2,1,0:T(8,128)(2,1)S(1)} custom-call(s32[4,8]{1,0:T(4,128)S(1)} %copy-done.2, f32[3]{0:T(128)S(1)} %copy-done.5, s32[2,4]{1,0:T(2,128)S(1)} %copy-done.3, s16[4,2,128,128]{3,2,1,0:T(8,128)(2,1)S(1)} %get-tuple-element.26.inner_ref, f32[10,128,128]{2,1,0:T(8,128)S(1)} %get-tuple-element.27.deep_ref, ...), custom_call_target="tpu_custom_call" | custom-call | tf_op jit(solution)/shard_map/render_edges/pallas_call | solution.py:352
  19.8 0.0 copy-start.4
  19.8 8.4 %all_to_all.5.in_ref = s16[4,2,128,128]{3,2,1,0:T(8,128)(2,1)S(1)} all-to-all(s16[4,2,128,128]{3,2,1,0:T(8,128)(2,1)S(1)} %render_edges.1), channel_id=1, replica_groups=mesh['gz'=4,'xy'=8] {'gz'}, dimensions={0} | all-to-all | bytes 524288 | tf_op jit(solution)/shard_map/all_to_all | solution.py:463
  28.3 1.4 %composite.1 = f32[2,4,1,32,128]{4,3,2,1,0:T(8,128)} custom-call(s32[2,4]{1,0:T(2,128)S(1)} %copy-done.4, s16[4,2,128,128]{3,2,1,0:T(8,128)(2,1)S(1)} %all_to_all.5.in_ref), custom_call_target="tpu_custom_call" | custom-call | tf_op jit(solution)/shard_map/composite/pallas_call | solution.py:465
  (11 shorter events, 0.0 us)
Async XLA Ops:
  0.0 1.0 %copy-start = (f32[8,128,128]{2,1,0:T(8,128)S(1)}, f32[8,128,128]{2,1,0:T(8,128)}, u32[]{:S(2)}) copy-start(f32[8,128,128]{2,1,0:T(8,128)} %own_ref.1) | copy-start | bytes 1572868
  1.0 14.3 %copy-start.1 = (f32[8,128,128]{2,1,0:T(8,128)S(1)}, f32[8,128,128]{2,1,0:T(8,128)}, u32[]{:S(2)}) copy-start(f32[8,128,128]{2,1,0:T(8,128)} %own_ref.1) | copy-start | bytes 1572868
  1.2 14.1 %collective-permute-start.2 = (s32[50,8,128]{2,1,0:T(8,128)S(1)}, s32[50,8,128]{2,1,0:T(8,128)S(1)}, u32[]{:S(2)}, u32[]{:S(2)}) collective-permute-start(s32[50,8,128]{2,1,0:T(8,128)S(1)} %get-tuple-element.24), channel_id=1, source_target_pairs={{8,16},{16,8},{9,17},{17,9},{10,18},{18,10},{11,19},{19,11},{12,20... | collective-permute-start | bytes 614408 | tf_op jit(solution)/shard_map/ppermute | solution.py:437
  1.9 13.5 %collective-permute-start.3 = (s32[50,8,128]{2,1,0:T(8,128)S(1)}, s32[50,8,128]{2,1,0:T(8,128)S(1)}, u32[]{:S(2)}, u32[]{:S(2)}) collective-permute-start(s32[50,8,128]{2,1,0:T(8,128)S(1)} %get-tuple-element.25), channel_id=1, source_target_pairs={{0,8},{16,24},{8,0},{24,16},{1,9},{17,25},{9,1},{25,17},{2,10},{18... | collective-permute-start | bytes 614408 | tf_op jit(solution)/shard_map/ppermute | solution.py:438
  4.9 3.9 %collective-permute-start = (f32[8,8,128]{2,1,0:T(8,128)S(1)}, f32[8,8,128]{2,1,0:T(8,128)S(1)}, u32[]{:S(2)}, u32[]{:S(2)}) collective-permute-start(f32[8,8,128]{2,1,0:T(8,128)S(1)} %get-tuple-element.13), channel_id=1, source_target_pairs={{0,1},{2,3},{4,5},{6,7},{1,0},{3,2},{5,4},{7,6},{8,9},{10,11},{12,... | collective-permute-start | bytes 98312 | tf_op jit(solution)/shard_map/cond/branch_0_fun/ppermute | solution.py:441
  6.3 6.7 %collective-permute-start.1 = (f32[8,8,128]{2,1,0:T(8,128)S(1)}, f32[8,8,128]{2,1,0:T(8,128)S(1)}, u32[]{:S(2)}, u32[]{:S(2)}) collective-permute-start(f32[8,8,128]{2,1,0:T(8,128)S(1)} %get-tuple-element.14), channel_id=1, source_target_pairs={{1,2},{3,4},{5,6},{2,1},{4,3},{6,5},{9,10},{11,12},{13,14},{10,9},... | collective-permute-start | bytes 98312 | tf_op jit(solution)/shard_map/cond/branch_0_fun/ppermute | solution.py:441
  13.1 2.3 %copy-start.6 = (f32[2]{0:T(128)S(1)}, f32[2]{0:T(128)}, u32[]{:S(2)}) copy-start(f32[2]{0:T(128)} %slopes_ref.1) | copy-start | bytes 28
  13.1 2.3 %copy-start.2 = (s32[4,8]{1,0:T(4,128)S(1)}, s32[4,8]{1,0:T(4,128)}, u32[]{:S(2)}) copy-start(s32[4,8]{1,0:T(4,128)} %live_ref.3) | copy-start | bytes 388
  13.1 2.3 %copy-start.3 = (s32[2,4]{1,0:T(2,128)S(1)}, s32[2,4]{1,0:T(2,128)}, u32[]{:S(2)}) copy-start(s32[2,4]{1,0:T(2,128)} %owner_ref.3) | copy-start | bytes 100
  13.1 2.3 %copy-start.5 = (f32[3]{0:T(128)S(1)}, f32[3]{0:T(128)}, u32[]{:S(2)}) copy-start(f32[3]{0:T(128)} %palette_ref.3) | copy-start | bytes 40
  13.2 5.0 %collective-permute-start.4 = (f32[5,16,128]{2,1,0:T(8,128)S(1)}, f32[5,16,128]{2,1,0:T(8,128)S(1)}, u32[]{:S(2)}, u32[]{:S(2)}) collective-permute-start(f32[5,16,128]{2,1,0:T(8,128)S(1)} %get-tuple-element.34), channel_id=1, source_target_pairs={{8,16},{16,8},{9,17},{17,9},{10,18},{18,10},{11,19},{19,11},{12,20... | collective-permute-start | bytes 122888 | tf_op jit(solution)/shard_map/ppermute | solution.py:450
  14.0 4.3 %collective-permute-start.5 = (f32[5,16,128]{2,1,0:T(8,128)S(1)}, f32[5,16,128]{2,1,0:T(8,128)S(1)}, u32[]{:S(2)}, u32[]{:S(2)}) collective-permute-start(f32[5,16,128]{2,1,0:T(8,128)S(1)} %get-tuple-element.33), channel_id=1, source_target_pairs={{0,8},{16,24},{8,0},{24,16},{1,9},{17,25},{9,1},{25,17},{2,10},{18... | collective-permute-start | bytes 122888 | tf_op jit(solution)/shard_map/ppermute | solution.py:453
  19.8 8.4 %copy-start.4 = (s32[2,4]{1,0:T(2,128)S(1)}, s32[2,4]{1,0:T(2,128)}, u32[]{:S(2)}) copy-start(s32[2,4]{1,0:T(2,128)} %order_ref.1) | copy-start | bytes 100

commit v16 on v13

--- a/solution.py
+++ b/solution.py
@@ -1,3 +1,5 @@
+import math
+
 import jax
 import jax.numpy as jnp
 from jax import lax
@@ -78,9 +80,9 @@
 
 
 def encode(value):
-    root = jnp.exp(0.125 * jnp.log(jnp.maximum(value, 1e-30) * (1.0 / TOP)))
-    level = jnp.minimum(root * STEPS + 0.5, STEPS)
-    return (level.astype(jnp.int32) - MIDDLE).astype(jnp.int16)
+    scale = math.log2(STEPS) - 0.125 * math.log2(TOP)
+    root = jnp.exp2(0.125 * jnp.log2(jnp.maximum(value, 1e-30)) + scale)
+    return ((root + 0.5).astype(jnp.int32) - MIDDLE).astype(jnp.int16)
 
 
 def decode(code):
@@ -107,15 +109,14 @@
 def shade(center, diff_depth, diff_rows, diff_cols, live, palette_ref, extinct):
     cells = TAPS**3
     floor = 0.01 * (2.0 * cells) ** 2
-    square = diff_depth * diff_depth + diff_rows * diff_rows + diff_cols * diff_cols
-    toward = LIGHT[0] * diff_depth + LIGHT[1] * diff_rows + LIGHT[2] * diff_cols
-    facing = jnp.maximum(0.0, toward) * lax.rsqrt(square + floor)
-    twice = center * (2.0 / cells)
-    small = jnp.exp(-jnp.abs(twice))
-    log1p = jnp.where(small < 1e-4, small * (1.0 - 0.5 * small), jnp.log(1.0 + small))
-    softplus = jnp.maximum(twice, 0.0) + log1p
-    opacity = jnp.where(live, 1.0 - jnp.exp(-extinct * softplus), 0.0)
-    bright = opacity * (0.25 + 0.75 * facing)
+    square = diff_depth * diff_depth + diff_rows * diff_rows + diff_cols * diff_cols + floor
+    light = [0.75 * part for part in LIGHT]
+    toward = light[0] * diff_depth + light[1] * diff_rows + light[2] * diff_cols
+    facing = jnp.maximum(0.0, toward) * lax.rsqrt(square)
+    t = center * (2.0 * math.log2(math.e) / cells)
+    softplus = jnp.maximum(t, 0.0) + jnp.log2(1.0 + jnp.exp2(-jnp.abs(t)))
+    opacity = 1.0 - jnp.exp2(jnp.where(live, -extinct, 0.0) * softplus)
+    bright = opacity * (0.25 + facing)
     channels = [bright * palette_ref[c] for c in range(3)] + [opacity]
     return [channel.astype(jnp.bfloat16) for channel in channels]
 

time: 28 us -> 27.8 us (level)
  transfers between devices with their start and end apart: 6 -> 6, of which waited for: 0 -> 0; matrix products, arithmetic and copies ran while one was open for 0% -> 0% of each run, Pallas kernels for 10% -> 9%
where the time goes in v16:
time: 27.8 us; the launch traced here: 27.6 us
  starting transfers between devices  11 us (40%)
  blocking collectives  9.57 us (34%)
  Pallas kernels  5.72 us (21%)
  local copies, waits for them, and re-layouts  1.09 us (4%)
    all_to_all x1, blocking collectives, body(): lax.all_to_all(outgoing, 'gz', split_axis=0, concat_axis=0, tiled=True)  9.57 us
    ppermute x1, starting transfers between devices, body(): row_odd = lax.ppermute(row_odd, 'xy', pairs('xy', 1))  4.92 us
    ppermute x1, starting transfers between devices, body(): deep_even = lax.ppermute(deep_even, 'gz', pairs('gz', 0))  2.93 us
    pallas_call x1, Pallas kernels, render_inner(): pl.pallas_call(kernel, out_shape=(jax.ShapeDtypeStruct((n_depth, VIEWS, 4...  2.59 us
    ppermute x1, starting transfers between devices, body(): lax.ppermute(jnp.where(odd_depth, low_corner, high_corner), 'gz', pairs('...  1.61 us
    pallas_call x1, Pallas kernels, render_edges(): pl.pallas_call(kernel, out_shape=jax.ShapeDtypeStruct(inner.shape, inner....  1.58 us
    pallas_call x1, Pallas kernels, body(): pl.pallas_call(composite_kernel, out_shape=jax.ShapeDtypeStruct((VIEWS, 4...  1.36 us
    unnamed x14, local copies, waits for them, and re-layouts  1.08 us
  transfers between devices with their start and end apart: 6, of which 0 were waited for; matrix products, arithmetic and copies ran while one was open for 0% of the time, Pallas kernels for 9%

profile of v16, /device:TPU:2, one launch (start us, length us, event | category | flops | bytes accessed | tf_op | source)
XLA Modules:
  0.0 27.6 jit_solution(7810434734841285568)
XLA Ops:
  0.0 1.0 %copy-done = f32[8,128,128]{2,1,0:T(8,128)S(1)} copy-done((f32[8,128,128]{2,1,0:T(8,128)S(1)}, f32[8,128,128]{2,1,0:T(8,128)}, u32[]{:S(2)}) %copy-start) | copy-done | bytes 524312
  1.0 0.2 cut_edges.1
  1.2 0.1 collective-permute-start.2
  1.3 4.9 %collective-permute-start.3 = (f32[8,8,128]{2,1,0:T(8,128)S(1)}, f32[8,8,128]{2,1,0:T(8,128)S(1)}, u32[]{:S(2)}, u32[]{:S(2)}) collective-permute-start(f32[8,8,128]{2,1,0:T(8,128)S(1)} %get-tuple-element.18), channel_id=1, source_target_pairs={{1,2},{3,4},{5,6},{2,1},{4,3},{6,5},{9,10},{11,12},{13,14},{10,9},... | collective-permute-start | bytes 98312 | tf_op jit(solution)/shard_map/ppermute | solution.py:439
  6.2 0.7 %collective-permute-start = (s32[50,8,128]{2,1,0:T(8,128)S(1)}, s32[50,8,128]{2,1,0:T(8,128)S(1)}, u32[]{:S(2)}, u32[]{:S(2)}) collective-permute-start(s32[50,8,128]{2,1,0:T(8,128)S(1)} %get-tuple-element.12), channel_id=1, source_target_pairs={{8,16},{16,8},{9,17},{17,9},{10,18},{18,10},{11,19},{19,11},{12,20... | collective-permute-start | bytes 614408 | tf_op jit(solution)/shard_map/ppermute | solution.py:440
  6.9 2.9 %collective-permute-start.1 = (s32[50,8,128]{2,1,0:T(8,128)S(1)}, s32[50,8,128]{2,1,0:T(8,128)S(1)}, u32[]{:S(2)}, u32[]{:S(2)}) collective-permute-start(s32[50,8,128]{2,1,0:T(8,128)S(1)} %get-tuple-element.13), channel_id=1, source_target_pairs={{0,8},{16,24},{8,0},{24,16},{1,9},{17,25},{9,1},{25,17},{2,10},{18... | collective-permute-start | bytes 614408 | tf_op jit(solution)/shard_map/ppermute | solution.py:441
  9.9 0.0 collective-permute-done.2
  9.9 0.0 collective-permute-done.3
  9.9 0.0 copy-start.6
  9.9 0.0 copy-start.2
  9.9 0.0 copy-start.3
  10.0 0.0 copy-start.5
  10.0 0.8 %collective-permute-start.4 = (f32[5,16,128]{2,1,0:T(8,128)S(1)}, f32[5,16,128]{2,1,0:T(8,128)S(1)}, u32[]{:S(2)}, u32[]{:S(2)}) collective-permute-start(f32[5,16,128]{2,1,0:T(8,128)S(1)} %get-tuple-element.20), channel_id=1, source_target_pairs={{8,16},{16,8},{9,17},{17,9},{10,18},{18,10},{11,19},{19,11},{12,20... | collective-permute-start | bytes 122888 | tf_op jit(solution)/shard_map/ppermute | solution.py:446
  10.8 1.6 %collective-permute-start.5 = (f32[5,16,128]{2,1,0:T(8,128)S(1)}, f32[5,16,128]{2,1,0:T(8,128)S(1)}, u32[]{:S(2)}, u32[]{:S(2)}) collective-permute-start(f32[5,16,128]{2,1,0:T(8,128)S(1)} %get-tuple-element.19), channel_id=1, source_target_pairs={{0,8},{16,24},{8,0},{24,16},{1,9},{17,25},{9,1},{25,17},{2,10},{18... | collective-permute-start | bytes 122888 | tf_op jit(solution)/shard_map/ppermute | solution.py:449
  12.4 0.0 collective-permute-done.odd_ref
  12.4 0.0 collective-permute-done.1.even_ref
  12.4 0.0 copy-done.1
  12.4 2.6 %render_inner.1 = (s16[4,2,128,128]{3,2,1,0:T(8,128)(2,1)S(1)}, f32[10,128,128]{2,1,0:T(8,128)S(1)}, bf16[8,128,256]{2,1,0:T(8,128)(2,1)S(1)}) custom-call(s32[4,8]{1,0:T(4,128)S(1)} %copy-done.2, f32[2]{0:T(128)S(1)} %copy-done.6, f32[3]{0:T(128)S(1)} %copy-done.5, s32[2,4]{1,0:T(2,128)S(1)} %copy-done.3, f32[8,128,128]{2,1,0:T(8,128)S(1)} %copy-done.1, ...), custom_call_target="tpu_custom_call" | custom-call | flops 13107200 | bytes 8388608 | tf_op jit(solution)/shard_map/render_inner/pallas_call | solution.py:239
  15.0 0.0 collective-permute-done.4.corner_odd_ref
  15.0 0.0 collective-permute-done.5.corner_even_ref
  15.0 1.6 %render_edges.1 = s16[4,2,128,128]{3,2,1,0:T(8,128)(2,1)S(1)} custom-call(s32[4,8]{1,0:T(4,128)S(1)} %copy-done.2, f32[3]{0:T(128)S(1)} %copy-done.5, s32[2,4]{1,0:T(2,128)S(1)} %copy-done.3, s16[4,2,128,128]{3,2,1,0:T(8,128)(2,1)S(1)} %get-tuple-element.14.inner_ref, f32[10,128,128]{2,1,0:T(8,128)S(1)} %get-tuple-element.15.deep_ref, ...), custom_call_target="tpu_custom_call" | custom-call | tf_op jit(solution)/shard_map/render_edges/pallas_call | solution.py:353
  16.6 0.0 copy-start.4
  16.6 9.6 %all_to_all.5.in_ref = s16[4,2,128,128]{3,2,1,0:T(8,128)(2,1)S(1)} all-to-all(s16[4,2,128,128]{3,2,1,0:T(8,128)(2,1)S(1)} %render_edges.1), channel_id=1, replica_groups=mesh['gz'=4,'xy'=8] {'gz'}, dimensions={0} | all-to-all | bytes 524288 | tf_op jit(solution)/shard_map/all_to_all | solution.py:459
  26.2 1.4 %composite.1 = f32[2,4,1,32,128]{4,3,2,1,0:T(8,128)} custom-call(s32[2,4]{1,0:T(2,128)S(1)} %copy-done.4, s16[4,2,128,128]{3,2,1,0:T(8,128)(2,1)S(1)} %all_to_all.5.in_ref), custom_call_target="tpu_custom_call" | custom-call | tf_op jit(solution)/shard_map/composite/pallas_call | solution.py:461
  (10 shorter events, 0.0 us)
Async XLA Ops:
  0.0 1.0 %copy-start = (f32[8,128,128]{2,1,0:T(8,128)S(1)}, f32[8,128,128]{2,1,0:T(8,128)}, u32[]{:S(2)}) copy-start(f32[8,128,128]{2,1,0:T(8,128)} %own_ref.1) | copy-start | bytes 1572868
  1.0 11.3 %copy-start.1 = (f32[8,128,128]{2,1,0:T(8,128)S(1)}, f32[8,128,128]{2,1,0:T(8,128)}, u32[]{:S(2)}) copy-start(f32[8,128,128]{2,1,0:T(8,128)} %own_ref.1) | copy-start | bytes 1572868
  1.2 8.6 %collective-permute-start.2 = (f32[8,8,128]{2,1,0:T(8,128)S(1)}, f32[8,8,128]{2,1,0:T(8,128)S(1)}, u32[]{:S(2)}, u32[]{:S(2)}) collective-permute-start(f32[8,8,128]{2,1,0:T(8,128)S(1)} %get-tuple-element.17), channel_id=1, source_target_pairs={{0,1},{2,3},{4,5},{6,7},{1,0},{3,2},{5,4},{7,6},{8,9},{10,11},{12,... | collective-permute-start | bytes 98312 | tf_op jit(solution)/shard_map/ppermute | solution.py:438
  1.3 8.6 %collective-permute-start.3 = (f32[8,8,128]{2,1,0:T(8,128)S(1)}, f32[8,8,128]{2,1,0:T(8,128)S(1)}, u32[]{:S(2)}, u32[]{:S(2)}) collective-permute-start(f32[8,8,128]{2,1,0:T(8,128)S(1)} %get-tuple-element.18), channel_id=1, source_target_pairs={{1,2},{3,4},{5,6},{2,1},{4,3},{6,5},{9,10},{11,12},{13,14},{10,9},... | collective-permute-start | bytes 98312 | tf_op jit(solution)/shard_map/ppermute | solution.py:439
  6.2 6.1 %collective-permute-start = (s32[50,8,128]{2,1,0:T(8,128)S(1)}, s32[50,8,128]{2,1,0:T(8,128)S(1)}, u32[]{:S(2)}, u32[]{:S(2)}) collective-permute-start(s32[50,8,128]{2,1,0:T(8,128)S(1)} %get-tuple-element.12), channel_id=1, source_target_pairs={{8,16},{16,8},{9,17},{17,9},{10,18},{18,10},{11,19},{19,11},{12,20... | collective-permute-start | bytes 614408 | tf_op jit(solution)/shard_map/ppermute | solution.py:440
  6.9 5.5 %collective-permute-start.1 = (s32[50,8,128]{2,1,0:T(8,128)S(1)}, s32[50,8,128]{2,1,0:T(8,128)S(1)}, u32[]{:S(2)}, u32[]{:S(2)}) collective-permute-start(s32[50,8,128]{2,1,0:T(8,128)S(1)} %get-tuple-element.13), channel_id=1, source_target_pairs={{0,8},{16,24},{8,0},{24,16},{1,9},{17,25},{9,1},{25,17},{2,10},{18... | collective-permute-start | bytes 614408 | tf_op jit(solution)/shard_map/ppermute | solution.py:441
  9.9 2.5 %copy-start.6 = (f32[2]{0:T(128)S(1)}, f32[2]{0:T(128)}, u32[]{:S(2)}) copy-start(f32[2]{0:T(128)} %slopes_ref.1) | copy-start | bytes 28
  9.9 2.5 %copy-start.2 = (s32[4,8]{1,0:T(4,128)S(1)}, s32[4,8]{1,0:T(4,128)}, u32[]{:S(2)}) copy-start(s32[4,8]{1,0:T(4,128)} %live_ref.3) | copy-start | bytes 388
  9.9 2.5 %copy-start.3 = (s32[2,4]{1,0:T(2,128)S(1)}, s32[2,4]{1,0:T(2,128)}, u32[]{:S(2)}) copy-start(s32[2,4]{1,0:T(2,128)} %owner_ref.3) | copy-start | bytes 100
  10.0 2.5 %copy-start.5 = (f32[3]{0:T(128)S(1)}, f32[3]{0:T(128)}, u32[]{:S(2)}) copy-start(f32[3]{0:T(128)} %palette_ref.3) | copy-start | bytes 40
  10.0 5.1 %collective-permute-start.4 = (f32[5,16,128]{2,1,0:T(8,128)S(1)}, f32[5,16,128]{2,1,0:T(8,128)S(1)}, u32[]{:S(2)}, u32[]{:S(2)}) collective-permute-start(f32[5,16,128]{2,1,0:T(8,128)S(1)} %get-tuple-element.20), channel_id=1, source_target_pairs={{8,16},{16,8},{9,17},{17,9},{10,18},{18,10},{11,19},{19,11},{12,20... | collective-permute-start | bytes 122888 | tf_op jit(solution)/shard_map/ppermute | solution.py:446
  10.8 4.3 %collective-permute-start.5 = (f32[5,16,128]{2,1,0:T(8,128)S(1)}, f32[5,16,128]{2,1,0:T(8,128)S(1)}, u32[]{:S(2)}, u32[]{:S(2)}) collective-permute-start(f32[5,16,128]{2,1,0:T(8,128)S(1)} %get-tuple-element.19), channel_id=1, source_target_pairs={{0,8},{16,24},{8,0},{24,16},{1,9},{17,25},{9,1},{25,17},{2,10},{18... | collective-permute-start | bytes 122888 | tf_op jit(solution)/shard_map/ppermute | solution.py:449
  16.6 9.6 %copy-start.4 = (s32[2,4]{1,0:T(2,128)S(1)}, s32[2,4]{1,0:T(2,128)}, u32[]{:S(2)}) copy-start(s32[2,4]{1,0:T(2,128)} %order_ref.1) | copy-start | bytes 100

commit v17 on v16

--- a/solution.py
+++ b/solution.py
@@ -101,11 +101,6 @@
     return jnp.dot(split, weights, preferred_element_type=jnp.float32)
 
 
-def column_weights(columns):
-    band = column_matrix(columns)
-    return jnp.concatenate([band, band, band], axis=0)
-
-
 def shade(center, diff_depth, diff_rows, diff_cols, live, palette_ref, extinct):
     cells = TAPS**3
     floor = 0.01 * (2.0 * cells) ** 2
@@ -177,7 +172,7 @@
 
     def kernel(
         live_ref, slopes_ref, palette_ref, owner_ref, own_ref, odd_ref, even_ref,
-        out_ref, deep, shear_ref, triple, smooth, across, sheared,
+        out_ref, deep, shear_ref, band_ref, triple, smooth, across, sheared,
     ):
         depth_index = lax.axis_index("gz")
         row_index = lax.axis_index("xy")
@@ -200,14 +195,18 @@
         for z in range(depth_cells):
             shear_ref[z] = shear_matrices(slopes_ref, slab_start + float(z), columns, total_depth)
 
-        weights = column_weights(columns)
+        band = column_matrix(columns)
+        band_ref[...] = band
+        weights = jnp.concatenate([band, band, band], axis=0)
         for z in range(layers):
-            triple[...] = (
+            triple[z] = (
                 deep[z, pl.ds(lead - 4, span + ROW_TILE)]
                 + deep[z, pl.ds(lead - 3, span + ROW_TILE)]
                 + deep[z, pl.ds(lead - 2, span + ROW_TILE)]
             )
-            total = triple[pl.ds(0, span)] + triple[pl.ds(3, span)] + triple[pl.ds(6, span)]
+            total = (
+                triple[z, pl.ds(0, span)] + triple[z, pl.ds(3, span)] + triple[z, pl.ds(6, span)]
+            )
             if 1 <= z <= depth_cells:
                 both = column_sums(total, weights)
                 smooth[z] = both[:, :columns]
@@ -242,11 +241,12 @@
             jax.ShapeDtypeStruct((n_depth, VIEWS, 4 * tile_rows, columns), jnp.int16),
             jax.ShapeDtypeStruct((layers, row_cells, columns), jnp.float32),
             jax.ShapeDtypeStruct((depth_cells, columns, VIEWS * columns), jnp.bfloat16),
+            jax.ShapeDtypeStruct((columns, 2 * columns), jnp.bfloat16),
         ),
         in_specs=[smem] * 4 + [vmem] * 3,
-        out_specs=(vmem,) * 3,
+        out_specs=(vmem,) * 4,
         scratch_shapes=[
-            pltpu.VMEM((span + ROW_TILE, columns), jnp.float32),
+            pltpu.VMEM((layers, span + ROW_TILE, columns), jnp.float32),
             pltpu.VMEM((layers, span, columns), jnp.float32),
             pltpu.VMEM((depth_cells, height, columns), jnp.float32),
             pltpu.VMEM((depth_cells, 4 * height, VIEWS * columns), jnp.float32),
@@ -262,7 +262,8 @@
 
 
 def render_edges(
-    live_slices, palette, owner, inner, deep, shear, corner_odd, corner_even, rlo, rhi, n_depth
+    live_slices, palette, owner, inner, deep, shear, band_weights,
+    corner_odd, corner_even, rlo, rhi, n_depth,
 ):
     layers, row_cells, columns = deep.shape
     depth_cells = layers - 2
@@ -273,7 +274,7 @@
     height = 2 * EDGE
 
     def kernel(
-        live_ref, palette_ref, owner_ref, inner_ref, deep_ref, shear_ref,
+        live_ref, palette_ref, owner_ref, inner_ref, deep_ref, shear_ref, band_ref,
         corner_odd_ref, corner_even_ref, rlo_ref, rhi_ref,
         out_ref, halo, triple, split_sums, smooth, across, sheared,
     ):
@@ -300,17 +301,19 @@
         span = band - ROW_TILE
         for z in range(layers):
             for side in range(2):
-                triple[pl.ds(0, span)] = (
+                triple[z, side, pl.ds(0, span)] = (
                     halo[z, side, pl.ds(3, span)]
                     + halo[z, side, pl.ds(4, span)]
                     + halo[z, side, pl.ds(5, span)]
                 )
                 split_sums[z, side] = (
-                    triple[pl.ds(0, band)] + triple[pl.ds(3, band)] + triple[pl.ds(6, band)]
+                    triple[z, side, pl.ds(0, band)]
+                    + triple[z, side, pl.ds(3, band)]
+                    + triple[z, side, pl.ds(6, band)]
                 )
-        both = column_sums(
-            split_sums[...].reshape(layers * 2 * band, columns), column_weights(columns)
-        ).reshape(layers, 2, band, 2 * columns)
+        weights = jnp.concatenate([band_ref[...]] * 3, axis=0)
+        both = column_sums(split_sums[...].reshape(layers * 2 * band, columns), weights)
+        both = both.reshape(layers, 2, band, 2 * columns)
         smooth[...] = both[..., :columns]
         across[...] = both[1:-1, :, :, columns:]
 
@@ -353,11 +356,11 @@
     return pl.pallas_call(
         kernel,
         out_shape=jax.ShapeDtypeStruct(inner.shape, inner.dtype),
-        in_specs=[smem] * 3 + [vmem] * 7,
+        in_specs=[smem] * 3 + [vmem] * 8,
         out_specs=vmem,
         scratch_shapes=[
             pltpu.VMEM((layers, 2, band, columns), jnp.float32),
-            pltpu.VMEM((band + ROW_TILE, columns), jnp.float32),
+            pltpu.VMEM((layers, 2, band + ROW_TILE, columns), jnp.float32),
             pltpu.VMEM((layers, 2, band, columns), jnp.float32),
             pltpu.VMEM((layers, 2, band, columns), jnp.float32),
             pltpu.VMEM((depth_cells, 2, band, columns), jnp.float32),
@@ -365,7 +368,10 @@
         ],
         compiler_params=pltpu.CompilerParams(vmem_limit_bytes=VMEM_BYTES),
         name="render_edges",
-    )(live_slices, palette, owner, inner, deep, shear, corner_odd, corner_even, rlo, rhi)
+    )(
+        live_slices, palette, owner, inner, deep, shear, band_weights,
+        corner_odd, corner_even, rlo, rhi,
+    )
 
 
 def cut_edges(density):
@@ -449,11 +455,11 @@
     corner_even = lax.ppermute(
         jnp.where(odd_depth, low_corner, high_corner), "gz", pairs("gz", 0)
     )
-    inner, deep, shear = render_inner(
+    inner, deep, shear, band_weights = render_inner(
         live_slices, shear_slopes, palette, tile_owner, density, deep_odd, deep_even, n_depth
     )
     outgoing = render_edges(
-        live_slices, palette, tile_owner, inner, deep, shear,
+        live_slices, palette, tile_owner, inner, deep, shear, band_weights,
         corner_odd, corner_even, rlo, rhi, n_depth,
     )
     incoming = lax.all_to_all(outgoing, "gz", split_axis=0, concat_axis=0, tiled=True)

time: 27.8 us -> 27.7 us (level)
  no operation moved by 1% of the time
where the time goes in v17:
time: 27.7 us; the launch traced here: 27.5 us
  starting transfers between devices  11 us (40%)
  blocking collectives  9.56 us (35%)
  Pallas kernels  5.63 us (20%)
  local copies, waits for them, and re-layouts  1.09 us (4%)
    all_to_all x1, blocking collectives, body(): lax.all_to_all(outgoing, 'gz', split_axis=0, concat_axis=0, tiled=True)  9.56 us
    ppermute x1, starting transfers between devices, body(): row_odd = lax.ppermute(row_odd, 'xy', pairs('xy', 1))  4.92 us
    ppermute x1, starting transfers between devices, body(): deep_even = lax.ppermute(deep_even, 'gz', pairs('gz', 0))  2.93 us
    pallas_call x1, Pallas kernels, render_inner(): pl.pallas_call(kernel, out_shape=(jax.ShapeDtypeStruct((n_depth, VIEWS, 4...  2.54 us
    ppermute x1, starting transfers between devices, body(): lax.ppermute(jnp.where(odd_depth, low_corner, high_corner), 'gz', pairs('...  1.61 us
    pallas_call x1, Pallas kernels, render_edges(): pl.pallas_call(kernel, out_shape=jax.ShapeDtypeStruct(inner.shape, inner....  1.55 us
    pallas_call x1, Pallas kernels, body(): pl.pallas_call(composite_kernel, out_shape=jax.ShapeDtypeStruct((VIEWS, 4...  1.36 us
    unnamed x14, local copies, waits for them, and re-layouts  1.08 us
  transfers between devices with their start and end apart: 6, of which 0 were waited for; matrix products, arithmetic and copies ran while one was open for 0% of the time, Pallas kernels for 9%

profile of v17, /device:TPU:2, one launch (start us, length us, event | category | flops | bytes accessed | tf_op | source)
XLA Modules:
  0.0 27.5 jit_solution(11495973692199671873)
XLA Ops:
  0.0 1.0 %copy-done = f32[8,128,128]{2,1,0:T(8,128)S(1)} copy-done((f32[8,128,128]{2,1,0:T(8,128)S(1)}, f32[8,128,128]{2,1,0:T(8,128)}, u32[]{:S(2)}) %copy-start) | copy-done | bytes 524312
  1.0 0.2 cut_edges.1
  1.2 0.1 collective-permute-start.2
  1.3 4.9 %collective-permute-start.3 = (f32[8,8,128]{2,1,0:T(8,128)S(1)}, f32[8,8,128]{2,1,0:T(8,128)S(1)}, u32[]{:S(2)}, u32[]{:S(2)}) collective-permute-start(f32[8,8,128]{2,1,0:T(8,128)S(1)} %get-tuple-element.20), channel_id=1, source_target_pairs={{1,2},{3,4},{5,6},{2,1},{4,3},{6,5},{9,10},{11,12},{13,14},{10,9},... | collective-permute-start | bytes 98312 | tf_op jit(solution)/shard_map/ppermute | solution.py:445
  6.2 0.7 %collective-permute-start = (s32[50,8,128]{2,1,0:T(8,128)S(1)}, s32[50,8,128]{2,1,0:T(8,128)S(1)}, u32[]{:S(2)}, u32[]{:S(2)}) collective-permute-start(s32[50,8,128]{2,1,0:T(8,128)S(1)} %get-tuple-element.13), channel_id=1, source_target_pairs={{8,16},{16,8},{9,17},{17,9},{10,18},{18,10},{11,19},{19,11},{12,20... | collective-permute-start | bytes 614408 | tf_op jit(solution)/shard_map/ppermute | solution.py:446
  6.9 2.9 %collective-permute-start.1 = (s32[50,8,128]{2,1,0:T(8,128)S(1)}, s32[50,8,128]{2,1,0:T(8,128)S(1)}, u32[]{:S(2)}, u32[]{:S(2)}) collective-permute-start(s32[50,8,128]{2,1,0:T(8,128)S(1)} %get-tuple-element.14), channel_id=1, source_target_pairs={{0,8},{16,24},{8,0},{24,16},{1,9},{17,25},{9,1},{25,17},{2,10},{18... | collective-permute-start | bytes 614408 | tf_op jit(solution)/shard_map/ppermute | solution.py:447
  9.9 0.0 collective-permute-done.2
  9.9 0.0 collective-permute-done.3
  9.9 0.0 copy-start.6
  9.9 0.0 copy-start.2
  9.9 0.0 copy-start.3
  10.0 0.0 copy-start.5
  10.0 0.8 %collective-permute-start.4 = (f32[5,16,128]{2,1,0:T(8,128)S(1)}, f32[5,16,128]{2,1,0:T(8,128)S(1)}, u32[]{:S(2)}, u32[]{:S(2)}) collective-permute-start(f32[5,16,128]{2,1,0:T(8,128)S(1)} %get-tuple-element.22), channel_id=1, source_target_pairs={{8,16},{16,8},{9,17},{17,9},{10,18},{18,10},{11,19},{19,11},{12,20... | collective-permute-start | bytes 122888 | tf_op jit(solution)/shard_map/ppermute | solution.py:452
  10.8 1.6 %collective-permute-start.5 = (f32[5,16,128]{2,1,0:T(8,128)S(1)}, f32[5,16,128]{2,1,0:T(8,128)S(1)}, u32[]{:S(2)}, u32[]{:S(2)}) collective-permute-start(f32[5,16,128]{2,1,0:T(8,128)S(1)} %get-tuple-element.21), channel_id=1, source_target_pairs={{0,8},{16,24},{8,0},{24,16},{1,9},{17,25},{9,1},{25,17},{2,10},{18... | collective-permute-start | bytes 122888 | tf_op jit(solution)/shard_map/ppermute | solution.py:455
  12.4 0.0 collective-permute-done.odd_ref
  12.4 0.0 collective-permute-done.1.even_ref
  12.4 2.5 %render_inner.1 = (s16[4,2,128,128]{3,2,1,0:T(8,128)(2,1)S(1)}, f32[10,128,128]{2,1,0:T(8,128)S(1)}, bf16[8,128,256]{2,1,0:T(8,128)(2,1)S(1)}, bf16[128,256]{1,0:T(8,128)(2,1)S(1)}) custom-call(s32[4,8]{1,0:T(4,128)S(1)} %copy-done.2, f32[2]{0:T(128)S(1)} %copy-done.6, f32[3]{0:T(128)S(1)} %copy-done.5, s32[2,4]{1,0:T(2,128)S(1)} %copy-done.3, ...), custom_call_target="tpu_custom_call" | custom-call | flops 13107200 | bytes 8388608 | tf_op jit(solution)/shard_map/render_inner/pallas_call | solution.py:238
  15.0 0.0 collective-permute-done.4.corner_odd_ref
  15.0 0.0 collective-permute-done.5.corner_even_ref
  15.0 1.5 %render_edges.1 = s16[4,2,128,128]{3,2,1,0:T(8,128)(2,1)S(1)} custom-call(s32[4,8]{1,0:T(4,128)S(1)} %copy-done.2, f32[3]{0:T(128)S(1)} %copy-done.5, s32[2,4]{1,0:T(2,128)S(1)} %copy-done.3, s16[4,2,128,128]{3,2,1,0:T(8,128)(2,1)S(1)} %get-tuple-element.15.inner_ref, f32[10,128,128]{2,1,0:T(8,128)S(1)} %get-tuple-element.16.deep_ref, ...), custom_call_target="tpu_custom_call" | custom-call | tf_op jit(solution)/shard_map/render_edges/pallas_call | solution.py:356
  16.5 0.0 copy-start.4
  16.6 9.6 %all_to_all.5.in_ref = s16[4,2,128,128]{3,2,1,0:T(8,128)(2,1)S(1)} all-to-all(s16[4,2,128,128]{3,2,1,0:T(8,128)(2,1)S(1)} %render_edges.1), channel_id=1, replica_groups=mesh['gz'=4,'xy'=8] {'gz'}, dimensions={0} | all-to-all | bytes 524288 | tf_op jit(solution)/shard_map/all_to_all | solution.py:465
  26.1 0.0 copy-done.4
  26.1 1.4 %composite.1 = f32[2,4,1,32,128]{4,3,2,1,0:T(8,128)} custom-call(s32[2,4]{1,0:T(2,128)S(1)} %copy-done.4, s16[4,2,128,128]{3,2,1,0:T(8,128)(2,1)S(1)} %all_to_all.5.in_ref), custom_call_target="tpu_custom_call" | custom-call | tf_op jit(solution)/shard_map/composite/pallas_call | solution.py:467
  (10 shorter events, 0.0 us)
Async XLA Ops:
  0.0 1.0 %copy-start = (f32[8,128,128]{2,1,0:T(8,128)S(1)}, f32[8,128,128]{2,1,0:T(8,128)}, u32[]{:S(2)}) copy-start(f32[8,128,128]{2,1,0:T(8,128)} %own_ref.1) | copy-start | bytes 1572868
  1.0 11.3 %copy-start.1 = (f32[8,128,128]{2,1,0:T(8,128)S(1)}, f32[8,128,128]{2,1,0:T(8,128)}, u32[]{:S(2)}) copy-start(f32[8,128,128]{2,1,0:T(8,128)} %own_ref.1) | copy-start | bytes 1572868
  1.2 8.6 %collective-permute-start.2 = (f32[8,8,128]{2,1,0:T(8,128)S(1)}, f32[8,8,128]{2,1,0:T(8,128)S(1)}, u32[]{:S(2)}, u32[]{:S(2)}) collective-permute-start(f32[8,8,128]{2,1,0:T(8,128)S(1)} %get-tuple-element.19), channel_id=1, source_target_pairs={{0,1},{2,3},{4,5},{6,7},{1,0},{3,2},{5,4},{7,6},{8,9},{10,11},{12,... | collective-permute-start | bytes 98312 | tf_op jit(solution)/shard_map/ppermute | solution.py:444
  1.3 8.6 %collective-permute-start.3 = (f32[8,8,128]{2,1,0:T(8,128)S(1)}, f32[8,8,128]{2,1,0:T(8,128)S(1)}, u32[]{:S(2)}, u32[]{:S(2)}) collective-permute-start(f32[8,8,128]{2,1,0:T(8,128)S(1)} %get-tuple-element.20), channel_id=1, source_target_pairs={{1,2},{3,4},{5,6},{2,1},{4,3},{6,5},{9,10},{11,12},{13,14},{10,9},... | collective-permute-start | bytes 98312 | tf_op jit(solution)/shard_map/ppermute | solution.py:445
  6.2 6.1 %collective-permute-start = (s32[50,8,128]{2,1,0:T(8,128)S(1)}, s32[50,8,128]{2,1,0:T(8,128)S(1)}, u32[]{:S(2)}, u32[]{:S(2)}) collective-permute-start(s32[50,8,128]{2,1,0:T(8,128)S(1)} %get-tuple-element.13), channel_id=1, source_target_pairs={{8,16},{16,8},{9,17},{17,9},{10,18},{18,10},{11,19},{19,11},{12,20... | collective-permute-start | bytes 614408 | tf_op jit(solution)/shard_map/ppermute | solution.py:446
  6.9 5.5 %collective-permute-start.1 = (s32[50,8,128]{2,1,0:T(8,128)S(1)}, s32[50,8,128]{2,1,0:T(8,128)S(1)}, u32[]{:S(2)}, u32[]{:S(2)}) collective-permute-start(s32[50,8,128]{2,1,0:T(8,128)S(1)} %get-tuple-element.14), channel_id=1, source_target_pairs={{0,8},{16,24},{8,0},{24,16},{1,9},{17,25},{9,1},{25,17},{2,10},{18... | collective-permute-start | bytes 614408 | tf_op jit(solution)/shard_map/ppermute | solution.py:447
  9.9 2.5 %copy-start.6 = (f32[2]{0:T(128)S(1)}, f32[2]{0:T(128)}, u32[]{:S(2)}) copy-start(f32[2]{0:T(128)} %slopes_ref.1) | copy-start | bytes 28
  9.9 2.5 %copy-start.2 = (s32[4,8]{1,0:T(4,128)S(1)}, s32[4,8]{1,0:T(4,128)}, u32[]{:S(2)}) copy-start(s32[4,8]{1,0:T(4,128)} %live_ref.3) | copy-start | bytes 388
  9.9 2.5 %copy-start.3 = (s32[2,4]{1,0:T(2,128)S(1)}, s32[2,4]{1,0:T(2,128)}, u32[]{:S(2)}) copy-start(s32[2,4]{1,0:T(2,128)} %owner_ref.3) | copy-start | bytes 100
  10.0 2.5 %copy-start.5 = (f32[3]{0:T(128)S(1)}, f32[3]{0:T(128)}, u32[]{:S(2)}) copy-start(f32[3]{0:T(128)} %palette_ref.3) | copy-start | bytes 40
  10.0 5.0 %collective-permute-start.4 = (f32[5,16,128]{2,1,0:T(8,128)S(1)}, f32[5,16,128]{2,1,0:T(8,128)S(1)}, u32[]{:S(2)}, u32[]{:S(2)}) collective-permute-start(f32[5,16,128]{2,1,0:T(8,128)S(1)} %get-tuple-element.22), channel_id=1, source_target_pairs={{8,16},{16,8},{9,17},{17,9},{10,18},{18,10},{11,19},{19,11},{12,20... | collective-permute-start | bytes 122888 | tf_op jit(solution)/shard_map/ppermute | solution.py:452
  10.8 4.2 %collective-permute-start.5 = (f32[5,16,128]{2,1,0:T(8,128)S(1)}, f32[5,16,128]{2,1,0:T(8,128)S(1)}, u32[]{:S(2)}, u32[]{:S(2)}) collective-permute-start(f32[5,16,128]{2,1,0:T(8,128)S(1)} %get-tuple-element.21), channel_id=1, source_target_pairs={{0,8},{16,24},{8,0},{24,16},{1,9},{17,25},{9,1},{25,17},{2,10},{18... | collective-permute-start | bytes 122888 | tf_op jit(solution)/shard_map/ppermute | solution.py:455
  16.5 9.6 %copy-start.4 = (s32[2,4]{1,0:T(2,128)S(1)}, s32[2,4]{1,0:T(2,128)}, u32[]{:S(2)}) copy-start(s32[2,4]{1,0:T(2,128)} %order_ref.1) | copy-start | bytes 100

commit v18 on v17

--- a/solution.py
+++ b/solution.py
@@ -178,13 +178,15 @@
         row_index = lax.axis_index("xy")
         odd_depth = depth_index % 2 == 1
 
+        below = jnp.where(depth_index > 0, -1, 0)
+        above = jnp.where(depth_index < n_depth - 1, -1, 0)
         low, high, word = [], [], 0
         for start in range(0, row_cells, ROW_TILE):
             while len(low) < HALO:
                 even = [even_ref[word + k] for k in range(WORDS)]
                 odd = [odd_ref[word + k] for k in range(WORDS)]
-                low += unpack([jnp.where(odd_depth, e, o) for e, o in zip(even, odd)])
-                high += unpack([jnp.where(odd_depth, o, e) for e, o in zip(even, odd)])
+                low += unpack([jnp.where(odd_depth, e, o) & below for e, o in zip(even, odd)])
+                high += unpack([jnp.where(odd_depth, o, e) & above for e, o in zip(even, odd)])
                 word += WORDS
             own = [own_ref[i, pl.ds(start, ROW_TILE)] for i in range(depth_cells)]
             for z, total in enumerate(window_sums(low[:HALO] + own + high[:HALO], TAPS)):
@@ -282,12 +284,14 @@
         row_index = lax.axis_index("xy")
         odd_depth = depth_index % 2 == 1
 
+        below = jnp.where(depth_index > 0, 1.0, 0.0)
+        above = jnp.where(depth_index < n_depth - 1, 1.0, 0.0)
         for side, mid_ref in ((0, rlo_ref), (1, rhi_ref)):
             at = pl.ds(side * ROW_TILE, ROW_TILE)
             even = [corner_even_ref[i, at] for i in range(HALO)]
             odd = [corner_odd_ref[i, at] for i in range(HALO)]
-            low = [jnp.where(odd_depth, e, o) for e, o in zip(even, odd)]
-            high = [jnp.where(odd_depth, o, e) for e, o in zip(even, odd)]
+            low = [jnp.where(odd_depth, e, o) * below for e, o in zip(even, odd)]
+            high = [jnp.where(odd_depth, o, e) * above for e, o in zip(even, odd)]
             outer = 0 if side == 0 else band - ROW_TILE
             inner_at = ROW_TILE if side == 0 else 0
             own_at = 0 if side == 0 else row_cells - (band - ROW_TILE)
@@ -438,15 +442,18 @@
     def pairs(axis, first):
         count = lax.axis_size(axis)
         lower = range(first, count - 1, 2)
-        return [(i, i + 1) for i in lower] + [(i + 1, i) for i in lower]
+        met = [(i, i + 1) for i in lower] + [(i + 1, i) for i in lower]
+        alone = set(range(count)) - {source for source, _ in met}
+        return met + [(i, i) for i in sorted(alone)]
 
     row_even, row_odd, deep_even, deep_odd = cut_edges(density)
     row_even = lax.ppermute(row_even, "xy", pairs("xy", 0))
     row_odd = lax.ppermute(row_odd, "xy", pairs("xy", 1))
     deep_odd = lax.ppermute(deep_odd, "gz", pairs("gz", 1))
     deep_even = lax.ppermute(deep_even, "gz", pairs("gz", 0))
-    rlo = jnp.where(odd_row, row_even, row_odd)
-    rhi = jnp.where(odd_row, row_odd, row_even)
+    row_index, n_rows = lax.axis_index("xy"), lax.axis_size("xy")
+    rlo = jnp.where(row_index > 0, jnp.where(odd_row, row_even, row_odd), 0.0)
+    rhi = jnp.where(row_index < n_rows - 1, jnp.where(odd_row, row_odd, row_even), 0.0)
     low_corner = jnp.concatenate([rlo[:HALO], rhi[:HALO]], axis=1)
     high_corner = jnp.concatenate([rlo[edge:], rhi[edge:]], axis=1)
     corner_odd = lax.ppermute(

time: 27.7 us -> 27.8 us (level)
  no operation moved by 1% of the time
where the time goes in v18:
time: 27.8 us; the launch traced here: 27.5 us
  starting transfers between devices  11 us (40%)
  blocking collectives  9.56 us (34%)
  Pallas kernels  5.67 us (20%)
  local copies, waits for them, and re-layouts  1.09 us (4%)
    all_to_all x1, blocking collectives, body(): lax.all_to_all(outgoing, 'gz', split_axis=0, concat_axis=0, tiled=True)  9.56 us
    ppermute x1, starting transfers between devices, body(): row_odd = lax.ppermute(row_odd, 'xy', pairs('xy', 1))  4.92 us
    ppermute x1, starting transfers between devices, body(): deep_even = lax.ppermute(deep_even, 'gz', pairs('gz', 0))  2.93 us
    pallas_call x1, Pallas kernels, render_inner(): pl.pallas_call(kernel, out_shape=(jax.ShapeDtypeStruct((n_depth, VIEWS, 4...  2.57 us
    ppermute x1, starting transfers between devices, body(): lax.ppermute(jnp.where(odd_depth, low_corner, high_corner), 'gz', pairs('...  1.61 us
    pallas_call x1, Pallas kernels, render_edges(): pl.pallas_call(kernel, out_shape=jax.ShapeDtypeStruct(inner.shape, inner....  1.55 us
    pallas_call x1, Pallas kernels, body(): pl.pallas_call(composite_kernel, out_shape=jax.ShapeDtypeStruct((VIEWS, 4...  1.36 us
    unnamed x14, local copies, waits for them, and re-layouts  1.08 us
  transfers between devices with their start and end apart: 6, of which 0 were waited for; matrix products, arithmetic and copies ran while one was open for 0% of the time, Pallas kernels for 9%

profile of v18, /device:TPU:2, one launch (start us, length us, event | category | flops | bytes accessed | tf_op | source)
XLA Modules:
  0.0 27.5 jit_solution(16255002273613080915)
XLA Ops:
  0.0 1.0 %copy-done = f32[8,128,128]{2,1,0:T(8,128)S(1)} copy-done((f32[8,128,128]{2,1,0:T(8,128)S(1)}, f32[8,128,128]{2,1,0:T(8,128)}, u32[]{:S(2)}) %copy-start) | copy-done | bytes 524312
  1.0 0.2 cut_edges.1
  1.2 0.1 collective-permute-start.2
  1.3 4.9 %collective-permute-start.3 = (f32[8,8,128]{2,1,0:T(8,128)S(1)}, f32[8,8,128]{2,1,0:T(8,128)S(1)}, u32[]{:S(2)}, u32[]{:S(2)}) collective-permute-start(f32[8,8,128]{2,1,0:T(8,128)S(1)} %get-tuple-element.20), channel_id=1, source_target_pairs={{1,2},{3,4},{5,6},{2,1},{4,3},{6,5},{0,0},{7,7},{9,10},{11,12},{13... | collective-permute-start | bytes 98312 | tf_op jit(solution)/shard_map/ppermute | solution.py:451
  6.2 0.7 %collective-permute-start = (s32[50,8,128]{2,1,0:T(8,128)S(1)}, s32[50,8,128]{2,1,0:T(8,128)S(1)}, u32[]{:S(2)}, u32[]{:S(2)}) collective-permute-start(s32[50,8,128]{2,1,0:T(8,128)S(1)} %get-tuple-element.13), channel_id=1, source_target_pairs={{8,16},{16,8},{0,0},{24,24},{9,17},{17,9},{1,1},{25,25},{10,18},{1... | collective-permute-start | bytes 614408 | tf_op jit(solution)/shard_map/ppermute | solution.py:452
  6.9 2.9 %collective-permute-start.1 = (s32[50,8,128]{2,1,0:T(8,128)S(1)}, s32[50,8,128]{2,1,0:T(8,128)S(1)}, u32[]{:S(2)}, u32[]{:S(2)}) collective-permute-start(s32[50,8,128]{2,1,0:T(8,128)S(1)} %get-tuple-element.14), channel_id=1, source_target_pairs={{0,8},{16,24},{8,0},{24,16},{1,9},{17,25},{9,1},{25,17},{2,10},{18... | collective-permute-start | bytes 614408 | tf_op jit(solution)/shard_map/ppermute | solution.py:453
  9.9 0.0 collective-permute-done.2
  9.9 0.0 collective-permute-done.3
  9.9 0.0 copy-start.6
  9.9 0.0 copy-start.2
  9.9 0.0 copy-start.3
  10.0 0.0 copy-start.5
  10.0 0.8 %collective-permute-start.4 = (f32[5,16,128]{2,1,0:T(8,128)S(1)}, f32[5,16,128]{2,1,0:T(8,128)S(1)}, u32[]{:S(2)}, u32[]{:S(2)}) collective-permute-start(f32[5,16,128]{2,1,0:T(8,128)S(1)} %get-tuple-element.22), channel_id=1, source_target_pairs={{8,16},{16,8},{0,0},{24,24},{9,17},{17,9},{1,1},{25,25},{10,18},{1... | collective-permute-start | bytes 122888 | tf_op jit(solution)/shard_map/ppermute | solution.py:459
  10.8 1.6 %collective-permute-start.5 = (f32[5,16,128]{2,1,0:T(8,128)S(1)}, f32[5,16,128]{2,1,0:T(8,128)S(1)}, u32[]{:S(2)}, u32[]{:S(2)}) collective-permute-start(f32[5,16,128]{2,1,0:T(8,128)S(1)} %get-tuple-element.21), channel_id=1, source_target_pairs={{0,8},{16,24},{8,0},{24,16},{1,9},{17,25},{9,1},{25,17},{2,10},{18... | collective-permute-start | bytes 122888 | tf_op jit(solution)/shard_map/ppermute | solution.py:462
  12.4 0.0 collective-permute-done.odd_ref
  12.4 0.0 collective-permute-done.1.even_ref
  12.4 0.0 copy-done.6
  12.4 2.6 %render_inner.1 = (s16[4,2,128,128]{3,2,1,0:T(8,128)(2,1)S(1)}, f32[10,128,128]{2,1,0:T(8,128)S(1)}, bf16[8,128,256]{2,1,0:T(8,128)(2,1)S(1)}, bf16[128,256]{1,0:T(8,128)(2,1)S(1)}) custom-call(s32[4,8]{1,0:T(4,128)S(1)} %copy-done.2, f32[2]{0:T(128)S(1)} %copy-done.6, f32[3]{0:T(128)S(1)} %copy-done.5, s32[2,4]{1,0:T(2,128)S(1)} %copy-done.3, ...), custom_call_target="tpu_custom_call" | custom-call | flops 13107200 | bytes 8388608 | tf_op jit(solution)/shard_map/render_inner/pallas_call | solution.py:240
  15.0 0.0 collective-permute-done.4.corner_odd_ref
  15.0 0.0 collective-permute-done.5.corner_even_ref
  15.0 1.5 %render_edges.1 = s16[4,2,128,128]{3,2,1,0:T(8,128)(2,1)S(1)} custom-call(s32[4,8]{1,0:T(4,128)S(1)} %copy-done.2, f32[3]{0:T(128)S(1)} %copy-done.5, s32[2,4]{1,0:T(2,128)S(1)} %copy-done.3, s16[4,2,128,128]{3,2,1,0:T(8,128)(2,1)S(1)} %get-tuple-element.15.inner_ref, f32[10,128,128]{2,1,0:T(8,128)S(1)} %get-tuple-element.16.deep_ref, ...), custom_call_target="tpu_custom_call" | custom-call | tf_op jit(solution)/shard_map/render_edges/pallas_call | solution.py:360
  16.6 0.0 copy-start.4
  16.6 9.6 %all_to_all.5.in_ref = s16[4,2,128,128]{3,2,1,0:T(8,128)(2,1)S(1)} all-to-all(s16[4,2,128,128]{3,2,1,0:T(8,128)(2,1)S(1)} %render_edges.1), channel_id=1, replica_groups=mesh['gz'=4,'xy'=8] {'gz'}, dimensions={0} | all-to-all | bytes 524288 | tf_op jit(solution)/shard_map/all_to_all | solution.py:472
  26.2 1.4 %composite.1 = f32[2,4,1,32,128]{4,3,2,1,0:T(8,128)} custom-call(s32[2,4]{1,0:T(2,128)S(1)} %copy-done.4, s16[4,2,128,128]{3,2,1,0:T(8,128)(2,1)S(1)} %all_to_all.5.in_ref), custom_call_target="tpu_custom_call" | custom-call | tf_op jit(solution)/shard_map/composite/pallas_call | solution.py:474
  (10 shorter events, 0.0 us)
Async XLA Ops:
  0.0 1.0 %copy-start = (f32[8,128,128]{2,1,0:T(8,128)S(1)}, f32[8,128,128]{2,1,0:T(8,128)}, u32[]{:S(2)}) copy-start(f32[8,128,128]{2,1,0:T(8,128)} %own_ref.1) | copy-start | bytes 1572868
  1.0 11.3 %copy-start.1 = (f32[8,128,128]{2,1,0:T(8,128)S(1)}, f32[8,128,128]{2,1,0:T(8,128)}, u32[]{:S(2)}) copy-start(f32[8,128,128]{2,1,0:T(8,128)} %own_ref.1) | copy-start | bytes 1572868
  1.2 8.6 %collective-permute-start.2 = (f32[8,8,128]{2,1,0:T(8,128)S(1)}, f32[8,8,128]{2,1,0:T(8,128)S(1)}, u32[]{:S(2)}, u32[]{:S(2)}) collective-permute-start(f32[8,8,128]{2,1,0:T(8,128)S(1)} %get-tuple-element.19), channel_id=1, source_target_pairs={{0,1},{2,3},{4,5},{6,7},{1,0},{3,2},{5,4},{7,6},{8,9},{10,11},{12,... | collective-permute-start | bytes 98312 | tf_op jit(solution)/shard_map/ppermute | solution.py:450
  1.3 8.6 %collective-permute-start.3 = (f32[8,8,128]{2,1,0:T(8,128)S(1)}, f32[8,8,128]{2,1,0:T(8,128)S(1)}, u32[]{:S(2)}, u32[]{:S(2)}) collective-permute-start(f32[8,8,128]{2,1,0:T(8,128)S(1)} %get-tuple-element.20), channel_id=1, source_target_pairs={{1,2},{3,4},{5,6},{2,1},{4,3},{6,5},{0,0},{7,7},{9,10},{11,12},{13... | collective-permute-start | bytes 98312 | tf_op jit(solution)/shard_map/ppermute | solution.py:451
  6.2 6.1 %collective-permute-start = (s32[50,8,128]{2,1,0:T(8,128)S(1)}, s32[50,8,128]{2,1,0:T(8,128)S(1)}, u32[]{:S(2)}, u32[]{:S(2)}) collective-permute-start(s32[50,8,128]{2,1,0:T(8,128)S(1)} %get-tuple-element.13), channel_id=1, source_target_pairs={{8,16},{16,8},{0,0},{24,24},{9,17},{17,9},{1,1},{25,25},{10,18},{1... | collective-permute-start | bytes 614408 | tf_op jit(solution)/shard_map/ppermute | solution.py:452
  6.9 5.5 %collective-permute-start.1 = (s32[50,8,128]{2,1,0:T(8,128)S(1)}, s32[50,8,128]{2,1,0:T(8,128)S(1)}, u32[]{:S(2)}, u32[]{:S(2)}) collective-permute-start(s32[50,8,128]{2,1,0:T(8,128)S(1)} %get-tuple-element.14), channel_id=1, source_target_pairs={{0,8},{16,24},{8,0},{24,16},{1,9},{17,25},{9,1},{25,17},{2,10},{18... | collective-permute-start | bytes 614408 | tf_op jit(solution)/shard_map/ppermute | solution.py:453
  9.9 2.5 %copy-start.6 = (f32[2]{0:T(128)S(1)}, f32[2]{0:T(128)}, u32[]{:S(2)}) copy-start(f32[2]{0:T(128)} %slopes_ref.1) | copy-start | bytes 28
  9.9 2.5 %copy-start.2 = (s32[4,8]{1,0:T(4,128)S(1)}, s32[4,8]{1,0:T(4,128)}, u32[]{:S(2)}) copy-start(s32[4,8]{1,0:T(4,128)} %live_ref.3) | copy-start | bytes 388
  9.9 2.5 %copy-start.3 = (s32[2,4]{1,0:T(2,128)S(1)}, s32[2,4]{1,0:T(2,128)}, u32[]{:S(2)}) copy-start(s32[2,4]{1,0:T(2,128)} %owner_ref.3) | copy-start | bytes 100
  10.0 2.5 %copy-start.5 = (f32[3]{0:T(128)S(1)}, f32[3]{0:T(128)}, u32[]{:S(2)}) copy-start(f32[3]{0:T(128)} %palette_ref.3) | copy-start | bytes 40
  10.0 5.0 %collective-permute-start.4 = (f32[5,16,128]{2,1,0:T(8,128)S(1)}, f32[5,16,128]{2,1,0:T(8,128)S(1)}, u32[]{:S(2)}, u32[]{:S(2)}) collective-permute-start(f32[5,16,128]{2,1,0:T(8,128)S(1)} %get-tuple-element.22), channel_id=1, source_target_pairs={{8,16},{16,8},{0,0},{24,24},{9,17},{17,9},{1,1},{25,25},{10,18},{1... | collective-permute-start | bytes 122888 | tf_op jit(solution)/shard_map/ppermute | solution.py:459
  10.8 4.2 %collective-permute-start.5 = (f32[5,16,128]{2,1,0:T(8,128)S(1)}, f32[5,16,128]{2,1,0:T(8,128)S(1)}, u32[]{:S(2)}, u32[]{:S(2)}) collective-permute-start(f32[5,16,128]{2,1,0:T(8,128)S(1)} %get-tuple-element.21), channel_id=1, source_target_pairs={{0,8},{16,24},{8,0},{24,16},{1,9},{17,25},{9,1},{25,17},{2,10},{18... | collective-permute-start | bytes 122888 | tf_op jit(solution)/shard_map/ppermute | solution.py:462
  16.6 9.6 %copy-start.4 = (s32[2,4]{1,0:T(2,128)S(1)}, s32[2,4]{1,0:T(2,128)}, u32[]{:S(2)}) copy-start(s32[2,4]{1,0:T(2,128)} %order_ref.1) | copy-start | bytes 100

commit v19 on v17

--- a/solution.py
+++ b/solution.py
@@ -13,7 +13,7 @@
 TAPS = 2 * REACH + 1
 ROW_TILE = 8
 PACKED_ROWS = 16
-EDGE = 16
+EDGE = 8
 VIEWS = 2
 TOP = 2.2
 STEPS = 65535.0
@@ -82,7 +82,7 @@
 def encode(value):
     scale = math.log2(STEPS) - 0.125 * math.log2(TOP)
     root = jnp.exp2(0.125 * jnp.log2(jnp.maximum(value, 1e-30)) + scale)
-    return ((root + 0.5).astype(jnp.int32) - MIDDLE).astype(jnp.int16)
+    return (root + 0.5).astype(jnp.int32) - MIDDLE
 
 
 def decode(code):
@@ -132,22 +132,23 @@
     return colour + [1.0 - transmit]
 
 
-def march_rows(sheared, out_ref, owner_ref, rows, base, height, depth_cells, tile_rows, columns):
-    step = min(tile_rows, PACKED_ROWS)
-    share = PACKED_ROWS // step
-    for row in range(rows.start, rows.stop, step):
-        tile, inside = row // tile_rows, row % tile_rows
-        at = row - rows.start + base
-        for view in range(VIEWS):
-            place = owner_ref[view, tile]
-            lanes = pl.ds(view * columns, columns)
-            values = march(
-                lambda z, c: sheared[z, pl.ds(c * height + at, step), lanes], depth_cells, view
-            )
-            for c in range(0, 4, share):
-                value = values[c] if share == 1 else jnp.concatenate(values[c : c + share])
-                at_rows = pl.ds(c * tile_rows + inside, PACKED_ROWS)
-                out_ref[place, view, at_rows] = encode(value)
+def store_codes(out_ref, place, view, codes, row, tile_rows, other=None):
+    if tile_rows < PACKED_ROWS:
+        for c in range(0, 4, 2):
+            pair = jnp.concatenate(codes[c : c + 2])
+            out_ref[place, view, pl.ds(c * tile_rows, PACKED_ROWS)] = pair.astype(jnp.int16)
+        return
+    for c in range(4):
+        at = pl.ds(c * tile_rows + row // PACKED_ROWS * PACKED_ROWS, PACKED_ROWS)
+        code = codes[c]
+        if code.shape[0] < PACKED_ROWS:
+            half = row % PACKED_ROWS
+            rest = jnp.zeros_like(code)
+            if other is not None:
+                rest = other[place, view, at].astype(jnp.int32)
+                rest = rest[ROW_TILE:] if half == 0 else rest[:ROW_TILE]
+            code = jnp.concatenate([code, rest] if half == 0 else [rest, code])
+        out_ref[place, view, at] = code.astype(jnp.int16)
 
 
 def zero_outside(smooth, depth_index, n_depth, layers):
@@ -168,7 +169,7 @@
     layers = depth_cells + 2
     rows = range(EDGE, row_cells - EDGE)
     height = len(rows)
-    lead, span = EDGE - ROW_TILE, height + 2 * ROW_TILE
+    lead, span = EDGE, height + 2 * ROW_TILE
 
     def kernel(
         live_ref, slopes_ref, palette_ref, owner_ref, own_ref, odd_ref, even_ref,
@@ -188,7 +189,7 @@
                 word += WORDS
             own = [own_ref[i, pl.ds(start, ROW_TILE)] for i in range(depth_cells)]
             for z, total in enumerate(window_sums(low[:HALO] + own + high[:HALO], TAPS)):
-                deep[z, pl.ds(start, ROW_TILE)] = total
+                deep[z, pl.ds(ROW_TILE + start, ROW_TILE)] = total
             low, high = low[HALO:], high[HALO:]
 
         slab_start = (depth_index * depth_cells).astype(jnp.float32)
@@ -231,7 +232,22 @@
             sheared[z] = jnp.dot(
                 jnp.concatenate(channels), shear_ref[z], preferred_element_type=jnp.float32
             )
-        march_rows(sheared, out_ref, owner_ref, rows, 0, height, depth_cells, tile_rows, columns)
+        row = rows.start
+        while row < rows.stop:
+            whole = tile_rows >= PACKED_ROWS and row % PACKED_ROWS == 0
+            count = PACKED_ROWS if whole and row + PACKED_ROWS <= rows.stop else ROW_TILE
+            at = row - rows.start
+            for view in range(VIEWS):
+                lanes = pl.ds(view * columns, columns)
+                values = march(
+                    lambda z, c: sheared[z, pl.ds(c * height + at, count), lanes],
+                    depth_cells,
+                    view,
+                )
+                place = owner_ref[view, row // tile_rows]
+                codes = [encode(value) for value in values]
+                store_codes(out_ref, place, view, codes, row % tile_rows, tile_rows)
+            row += count
 
     smem = pl.BlockSpec(memory_space=pltpu.SMEM)
     vmem = pl.BlockSpec(memory_space=pltpu.VMEM)
@@ -239,7 +255,7 @@
         kernel,
         out_shape=(
             jax.ShapeDtypeStruct((n_depth, VIEWS, 4 * tile_rows, columns), jnp.int16),
-            jax.ShapeDtypeStruct((layers, row_cells, columns), jnp.float32),
+            jax.ShapeDtypeStruct((layers, row_cells + 2 * ROW_TILE, columns), jnp.float32),
             jax.ShapeDtypeStruct((depth_cells, columns, VIEWS * columns), jnp.bfloat16),
             jax.ShapeDtypeStruct((columns, 2 * columns), jnp.bfloat16),
         ),
@@ -265,12 +281,14 @@
     live_slices, palette, owner, inner, deep, shear, band_weights,
     corner_odd, corner_even, rlo, rhi, n_depth,
 ):
-    layers, row_cells, columns = deep.shape
+    layers, padded_rows, columns = deep.shape
+    row_cells = padded_rows - 2 * ROW_TILE
     depth_cells = layers - 2
     n_rows = lax.axis_size("xy")
     extinct = 3.0 / (depth_cells * n_depth)
     tile_rows = row_cells // n_depth
     band = EDGE + 2 * ROW_TILE
+    piece = 2 * ROW_TILE
     height = 2 * EDGE
 
     def kernel(
@@ -290,7 +308,7 @@
             high = [jnp.where(odd_depth, o, e) for e, o in zip(even, odd)]
             outer = 0 if side == 0 else band - ROW_TILE
             inner_at = ROW_TILE if side == 0 else 0
-            own_at = 0 if side == 0 else row_cells - (band - ROW_TILE)
+            own_at = ROW_TILE if side == 0 else padded_rows - band
             sums = window_sums(low + [mid_ref[i] for i in range(depth_cells)] + high, TAPS)
             for z in range(layers):
                 halo[z, side, pl.ds(outer, ROW_TILE)] = sums[z]
@@ -307,13 +325,13 @@
                     + halo[z, side, pl.ds(5, span)]
                 )
                 split_sums[z, side] = (
-                    triple[z, side, pl.ds(0, band)]
-                    + triple[z, side, pl.ds(3, band)]
-                    + triple[z, side, pl.ds(6, band)]
+                    triple[z, side, pl.ds(0, piece)]
+                    + triple[z, side, pl.ds(3, piece)]
+                    + triple[z, side, pl.ds(6, piece)]
                 )
         weights = jnp.concatenate([band_ref[...]] * 3, axis=0)
-        both = column_sums(split_sums[...].reshape(layers * 2 * band, columns), weights)
-        both = both.reshape(layers, 2, band, 2 * columns)
+        both = column_sums(split_sums[...].reshape(layers * 2 * piece, columns), weights)
+        both = both.reshape(layers, 2, piece, 2 * columns)
         smooth[...] = both[..., :columns]
         across[...] = both[1:-1, :, :, columns:]
 
@@ -328,28 +346,34 @@
         zero_outside(smooth, depth_index, n_depth, layers)
 
         own_live = live_ref[depth_index, row_index]
-        middle = pl.ds(1, EDGE)
+
+        def both_sides(ref, z, start):
+            return ref[z, :, pl.ds(start, EDGE)].reshape(height, columns)
+
         for z in range(depth_cells):
-            sides = [
-                shade(
-                    smooth[z + 1, side, middle],
-                    smooth[z + 2, side, middle] - smooth[z, side, middle],
-                    smooth[z + 1, side, pl.ds(2, EDGE)] - smooth[z + 1, side, pl.ds(0, EDGE)],
-                    across[z, side, middle],
-                    z < own_live,
-                    palette_ref,
-                    extinct,
-                )
-                for side in range(2)
-            ]
-            rgba = jnp.concatenate([side[c] for c in range(4) for side in sides])
-            sheared[z] = jnp.dot(rgba, shear_ref[z], preferred_element_type=jnp.float32)
+            channels = shade(
+                both_sides(smooth, z + 1, 1),
+                both_sides(smooth, z + 2, 1) - both_sides(smooth, z, 1),
+                both_sides(smooth, z + 1, 2) - both_sides(smooth, z + 1, 0),
+                both_sides(across, z, 1),
+                z < own_live,
+                palette_ref,
+                extinct,
+            )
+            sheared[z] = jnp.dot(
+                jnp.concatenate(channels), shear_ref[z], preferred_element_type=jnp.float32
+            )
         out_ref[...] = inner_ref[...]
-        for side, rows in enumerate((range(EDGE), range(row_cells - EDGE, row_cells))):
-            march_rows(
-                sheared, out_ref, owner_ref, rows, side * EDGE, height,
-                depth_cells, tile_rows, columns,
-            )
+        for view in range(VIEWS):
+            lanes = pl.ds(view * columns, columns)
+            values = march(
+                lambda z, c: sheared[z, pl.ds(c * height, height), lanes], depth_cells, view
+            )
+            codes = [encode(value) for value in values]
+            for side, row in enumerate((0, row_cells - EDGE)):
+                place = owner_ref[view, row // tile_rows]
+                part = [code[side * EDGE : (side + 1) * EDGE] for code in codes]
+                store_codes(out_ref, place, view, part, row % tile_rows, tile_rows, inner_ref)
 
     smem = pl.BlockSpec(memory_space=pltpu.SMEM)
     vmem = pl.BlockSpec(memory_space=pltpu.VMEM)
@@ -360,10 +384,10 @@
         out_specs=vmem,
         scratch_shapes=[
             pltpu.VMEM((layers, 2, band, columns), jnp.float32),
-            pltpu.VMEM((layers, 2, band + ROW_TILE, columns), jnp.float32),
-            pltpu.VMEM((layers, 2, band, columns), jnp.float32),
-            pltpu.VMEM((layers, 2, band, columns), jnp.float32),
-            pltpu.VMEM((depth_cells, 2, band, columns), jnp.float32),
+            pltpu.VMEM((layers, 2, piece + ROW_TILE, columns), jnp.float32),
+            pltpu.VMEM((layers, 2, piece, columns), jnp.float32),
+            pltpu.VMEM((layers, 2, piece, columns), jnp.float32),
+            pltpu.VMEM((depth_cells, 2, piece, columns), jnp.float32),
             pltpu.VMEM((depth_cells, 4 * height, VIEWS * columns), jnp.float32),
         ],
         compiler_params=pltpu.CompilerParams(vmem_limit_bytes=VMEM_BYTES),

time: 27.7 us -> 27.6 us (level)
    pallas_call x1, Pallas kernels: 1.55 us -> 1.23 us  [render_edges(): pl.pallas_call(kernel, out_shape=jax.ShapeDtypeStruct(inner.shape, inner....]
  transfers between devices with their start and end apart: 6 -> 6, of which waited for: 0 -> 0; matrix products, arithmetic and copies ran while one was open for 0% -> 0% of each run, Pallas kernels for 9% -> 10%
where the time goes in v19:
time: 27.6 us; the launch traced here: 27.4 us
  starting transfers between devices  11 us (40%)
  blocking collectives  9.56 us (35%)
  Pallas kernels  5.53 us (20%)
  local copies, waits for them, and re-layouts  1.08 us (4%)
    all_to_all x1, blocking collectives, body(): lax.all_to_all(outgoing, 'gz', split_axis=0, concat_axis=0, tiled=True)  9.56 us
    ppermute x1, starting transfers between devices, body(): row_odd = lax.ppermute(row_odd, 'xy', pairs('xy', 1))  4.92 us
    ppermute x1, starting transfers between devices, body(): deep_even = lax.ppermute(deep_even, 'gz', pairs('gz', 0))  2.93 us
    pallas_call x1, Pallas kernels, render_inner(): pl.pallas_call(kernel, out_shape=(jax.ShapeDtypeStruct((n_depth, VIEWS, 4...  2.76 us
    ppermute x1, starting transfers between devices, body(): lax.ppermute(jnp.where(odd_depth, low_corner, high_corner), 'gz', pairs('...  1.61 us
    pallas_call x1, Pallas kernels, body(): pl.pallas_call(composite_kernel, out_shape=jax.ShapeDtypeStruct((VIEWS, 4...  1.36 us
    pallas_call x1, Pallas kernels, render_edges(): pl.pallas_call(kernel, out_shape=jax.ShapeDtypeStruct(inner.shape, inner....  1.23 us
    unnamed x14, local copies, waits for them, and re-layouts  1.08 us
  transfers between devices with their start and end apart: 6, of which 0 were waited for; matrix products, arithmetic and copies ran while one was open for 0% of the time, Pallas kernels for 10%

profile of v19, /device:TPU:2, one launch (start us, length us, event | category | flops | bytes accessed | tf_op | source)
XLA Modules:
  0.0 27.4 jit_solution(5048172266603072618)
XLA Ops:
  0.0 1.0 %copy-done = f32[8,128,128]{2,1,0:T(8,128)S(1)} copy-done((f32[8,128,128]{2,1,0:T(8,128)S(1)}, f32[8,128,128]{2,1,0:T(8,128)}, u32[]{:S(2)}) %copy-start) | copy-done | bytes 524312
  1.0 0.2 cut_edges.1
  1.2 0.1 collective-permute-start.2
  1.3 4.9 %collective-permute-start.3 = (f32[8,8,128]{2,1,0:T(8,128)S(1)}, f32[8,8,128]{2,1,0:T(8,128)S(1)}, u32[]{:S(2)}, u32[]{:S(2)}) collective-permute-start(f32[8,8,128]{2,1,0:T(8,128)S(1)} %get-tuple-element.20), channel_id=1, source_target_pairs={{1,2},{3,4},{5,6},{2,1},{4,3},{6,5},{9,10},{11,12},{13,14},{10,9},... | collective-permute-start | bytes 98312 | tf_op jit(solution)/shard_map/ppermute | solution.py:469
  6.2 0.7 %collective-permute-start = (s32[50,8,128]{2,1,0:T(8,128)S(1)}, s32[50,8,128]{2,1,0:T(8,128)S(1)}, u32[]{:S(2)}, u32[]{:S(2)}) collective-permute-start(s32[50,8,128]{2,1,0:T(8,128)S(1)} %get-tuple-element.13), channel_id=1, source_target_pairs={{8,16},{16,8},{9,17},{17,9},{10,18},{18,10},{11,19},{19,11},{12,20... | collective-permute-start | bytes 614408 | tf_op jit(solution)/shard_map/ppermute | solution.py:470
  6.9 2.9 %collective-permute-start.1 = (s32[50,8,128]{2,1,0:T(8,128)S(1)}, s32[50,8,128]{2,1,0:T(8,128)S(1)}, u32[]{:S(2)}, u32[]{:S(2)}) collective-permute-start(s32[50,8,128]{2,1,0:T(8,128)S(1)} %get-tuple-element.14), channel_id=1, source_target_pairs={{0,8},{16,24},{8,0},{24,16},{1,9},{17,25},{9,1},{25,17},{2,10},{18... | collective-permute-start | bytes 614408 | tf_op jit(solution)/shard_map/ppermute | solution.py:471
  9.9 0.0 collective-permute-done.2
  9.9 0.0 collective-permute-done.3
  9.9 0.0 copy-start.6
  9.9 0.0 copy-start.2
  9.9 0.0 copy-start.3
  10.0 0.0 copy-start.5
  10.0 0.8 %collective-permute-start.4 = (f32[5,16,128]{2,1,0:T(8,128)S(1)}, f32[5,16,128]{2,1,0:T(8,128)S(1)}, u32[]{:S(2)}, u32[]{:S(2)}) collective-permute-start(f32[5,16,128]{2,1,0:T(8,128)S(1)} %get-tuple-element.22), channel_id=1, source_target_pairs={{8,16},{16,8},{9,17},{17,9},{10,18},{18,10},{11,19},{19,11},{12,20... | collective-permute-start | bytes 122888 | tf_op jit(solution)/shard_map/ppermute | solution.py:476
  10.8 1.6 %collective-permute-start.5 = (f32[5,16,128]{2,1,0:T(8,128)S(1)}, f32[5,16,128]{2,1,0:T(8,128)S(1)}, u32[]{:S(2)}, u32[]{:S(2)}) collective-permute-start(f32[5,16,128]{2,1,0:T(8,128)S(1)} %get-tuple-element.21), channel_id=1, source_target_pairs={{0,8},{16,24},{8,0},{24,16},{1,9},{17,25},{9,1},{25,17},{2,10},{18... | collective-permute-start | bytes 122888 | tf_op jit(solution)/shard_map/ppermute | solution.py:479
  12.4 0.0 collective-permute-done.odd_ref
  12.4 0.0 collective-permute-done.1.even_ref
  12.4 0.0 copy-done.1
  12.4 2.8 %render_inner.1 = (s16[4,2,128,128]{3,2,1,0:T(8,128)(2,1)S(1)}, f32[10,144,128]{2,1,0:T(8,128)S(1)}, bf16[8,128,256]{2,1,0:T(8,128)(2,1)S(1)}, bf16[128,256]{1,0:T(8,128)(2,1)S(1)}) custom-call(s32[4,8]{1,0:T(4,128)S(1)} %copy-done.2, f32[2]{0:T(128)S(1)} %copy-done.6, f32[3]{0:T(128)S(1)} %copy-done.5, s32[2,4]{1,0:T(2,128)S(1)} %copy-done.3, ...), custom_call_target="tpu_custom_call" | custom-call | flops 13107200 | bytes 8388608 | tf_op jit(solution)/shard_map/render_inner/pallas_call | solution.py:254
  15.2 0.0 collective-permute-done.4.corner_odd_ref
  15.2 0.0 collective-permute-done.5.corner_even_ref
  15.2 1.2 %render_edges.1 = s16[4,2,128,128]{3,2,1,0:T(8,128)(2,1)S(1)} custom-call(s32[4,8]{1,0:T(4,128)S(1)} %copy-done.2, f32[3]{0:T(128)S(1)} %copy-done.5, s32[2,4]{1,0:T(2,128)S(1)} %copy-done.3, s16[4,2,128,128]{3,2,1,0:T(8,128)(2,1)S(1)} %get-tuple-element.15.inner_ref, f32[10,144,128]{2,1,0:T(8,128)S(1)} %get-tuple-element.16.deep_ref, ...), custom_call_target="tpu_custom_call" | custom-call | tf_op jit(solution)/shard_map/render_edges/pallas_call | solution.py:380
  16.4 0.0 copy-start.4
  16.5 9.6 %all_to_all.5.in_ref = s16[4,2,128,128]{3,2,1,0:T(8,128)(2,1)S(1)} all-to-all(s16[4,2,128,128]{3,2,1,0:T(8,128)(2,1)S(1)} %render_edges.1), channel_id=1, replica_groups=mesh['gz'=4,'xy'=8] {'gz'}, dimensions={0} | all-to-all | bytes 524288 | tf_op jit(solution)/shard_map/all_to_all | solution.py:489
  26.0 1.4 %composite.1 = f32[2,4,1,32,128]{4,3,2,1,0:T(8,128)} custom-call(s32[2,4]{1,0:T(2,128)S(1)} %copy-done.4, s16[4,2,128,128]{3,2,1,0:T(8,128)(2,1)S(1)} %all_to_all.5.in_ref), custom_call_target="tpu_custom_call" | custom-call | tf_op jit(solution)/shard_map/composite/pallas_call | solution.py:491
  (10 shorter events, 0.0 us)
Async XLA Ops:
  0.0 1.0 %copy-start = (f32[8,128,128]{2,1,0:T(8,128)S(1)}, f32[8,128,128]{2,1,0:T(8,128)}, u32[]{:S(2)}) copy-start(f32[8,128,128]{2,1,0:T(8,128)} %own_ref.1) | copy-start | bytes 1572868
  1.0 11.3 %copy-start.1 = (f32[8,128,128]{2,1,0:T(8,128)S(1)}, f32[8,128,128]{2,1,0:T(8,128)}, u32[]{:S(2)}) copy-start(f32[8,128,128]{2,1,0:T(8,128)} %own_ref.1) | copy-start | bytes 1572868
  1.2 8.6 %collective-permute-start.2 = (f32[8,8,128]{2,1,0:T(8,128)S(1)}, f32[8,8,128]{2,1,0:T(8,128)S(1)}, u32[]{:S(2)}, u32[]{:S(2)}) collective-permute-start(f32[8,8,128]{2,1,0:T(8,128)S(1)} %get-tuple-element.19), channel_id=1, source_target_pairs={{0,1},{2,3},{4,5},{6,7},{1,0},{3,2},{5,4},{7,6},{8,9},{10,11},{12,... | collective-permute-start | bytes 98312 | tf_op jit(solution)/shard_map/ppermute | solution.py:468
  1.3 8.6 %collective-permute-start.3 = (f32[8,8,128]{2,1,0:T(8,128)S(1)}, f32[8,8,128]{2,1,0:T(8,128)S(1)}, u32[]{:S(2)}, u32[]{:S(2)}) collective-permute-start(f32[8,8,128]{2,1,0:T(8,128)S(1)} %get-tuple-element.20), channel_id=1, source_target_pairs={{1,2},{3,4},{5,6},{2,1},{4,3},{6,5},{9,10},{11,12},{13,14},{10,9},... | collective-permute-start | bytes 98312 | tf_op jit(solution)/shard_map/ppermute | solution.py:469
  6.2 6.1 %collective-permute-start = (s32[50,8,128]{2,1,0:T(8,128)S(1)}, s32[50,8,128]{2,1,0:T(8,128)S(1)}, u32[]{:S(2)}, u32[]{:S(2)}) collective-permute-start(s32[50,8,128]{2,1,0:T(8,128)S(1)} %get-tuple-element.13), channel_id=1, source_target_pairs={{8,16},{16,8},{9,17},{17,9},{10,18},{18,10},{11,19},{19,11},{12,20... | collective-permute-start | bytes 614408 | tf_op jit(solution)/shard_map/ppermute | solution.py:470
  6.9 5.5 %collective-permute-start.1 = (s32[50,8,128]{2,1,0:T(8,128)S(1)}, s32[50,8,128]{2,1,0:T(8,128)S(1)}, u32[]{:S(2)}, u32[]{:S(2)}) collective-permute-start(s32[50,8,128]{2,1,0:T(8,128)S(1)} %get-tuple-element.14), channel_id=1, source_target_pairs={{0,8},{16,24},{8,0},{24,16},{1,9},{17,25},{9,1},{25,17},{2,10},{18... | collective-permute-start | bytes 614408 | tf_op jit(solution)/shard_map/ppermute | solution.py:471
  9.9 2.5 %copy-start.6 = (f32[2]{0:T(128)S(1)}, f32[2]{0:T(128)}, u32[]{:S(2)}) copy-start(f32[2]{0:T(128)} %slopes_ref.1) | copy-start | bytes 28
  9.9 2.5 %copy-start.2 = (s32[4,8]{1,0:T(4,128)S(1)}, s32[4,8]{1,0:T(4,128)}, u32[]{:S(2)}) copy-start(s32[4,8]{1,0:T(4,128)} %live_ref.3) | copy-start | bytes 388
  9.9 2.5 %copy-start.3 = (s32[2,4]{1,0:T(2,128)S(1)}, s32[2,4]{1,0:T(2,128)}, u32[]{:S(2)}) copy-start(s32[2,4]{1,0:T(2,128)} %owner_ref.3) | copy-start | bytes 100
  10.0 2.5 %copy-start.5 = (f32[3]{0:T(128)S(1)}, f32[3]{0:T(128)}, u32[]{:S(2)}) copy-start(f32[3]{0:T(128)} %palette_ref.3) | copy-start | bytes 40
  10.0 5.2 %collective-permute-start.4 = (f32[5,16,128]{2,1,0:T(8,128)S(1)}, f32[5,16,128]{2,1,0:T(8,128)S(1)}, u32[]{:S(2)}, u32[]{:S(2)}) collective-permute-start(f32[5,16,128]{2,1,0:T(8,128)S(1)} %get-tuple-element.22), channel_id=1, source_target_pairs={{8,16},{16,8},{9,17},{17,9},{10,18},{18,10},{11,19},{19,11},{12,20... | collective-permute-start | bytes 122888 | tf_op jit(solution)/shard_map/ppermute | solution.py:476
  10.8 4.4 %collective-permute-start.5 = (f32[5,16,128]{2,1,0:T(8,128)S(1)}, f32[5,16,128]{2,1,0:T(8,128)S(1)}, u32[]{:S(2)}, u32[]{:S(2)}) collective-permute-start(f32[5,16,128]{2,1,0:T(8,128)S(1)} %get-tuple-element.21), channel_id=1, source_target_pairs={{0,8},{16,24},{8,0},{24,16},{1,9},{17,25},{9,1},{25,17},{2,10},{18... | collective-permute-start | bytes 122888 | tf_op jit(solution)/shard_map/ppermute | solution.py:479
  16.4 9.6 %copy-start.4 = (s32[2,4]{1,0:T(2,128)S(1)}, s32[2,4]{1,0:T(2,128)}, u32[]{:S(2)}) copy-start(s32[2,4]{1,0:T(2,128)} %order_ref.1) | copy-start | bytes 100

commit v20 on v19

--- a/solution.py
+++ b/solution.py
@@ -151,6 +151,20 @@
         out_ref[place, view, at] = code.astype(jnp.int16)
 
 
+def fetch_scalars(pairs, sems):
+    copies = [
+        pltpu.make_async_copy(source, target, sems.at[i]) for i, (source, target) in enumerate(pairs)
+    ]
+    for copy in copies:
+        copy.start()
+
+    def wait():
+        for copy in copies:
+            copy.wait()
+
+    return wait
+
+
 def zero_outside(smooth, depth_index, n_depth, layers):
     @pl.when(depth_index == 0)
     def _():
@@ -172,9 +186,19 @@
     lead, span = EDGE, height + 2 * ROW_TILE
 
     def kernel(
-        live_ref, slopes_ref, palette_ref, owner_ref, own_ref, odd_ref, even_ref,
+        live_in, slopes_in, palette_in, owner_in, own_ref, odd_ref, even_ref,
         out_ref, deep, shear_ref, band_ref, triple, smooth, across, sheared,
+        live_ref, slopes_ref, palette_ref, owner_ref, sems,
     ):
+        wait_scalars = fetch_scalars(
+            [
+                (live_in, live_ref),
+                (slopes_in, slopes_ref),
+                (palette_in, palette_ref),
+                (owner_in, owner_ref),
+            ],
+            sems,
+        )
         depth_index = lax.axis_index("gz")
         row_index = lax.axis_index("xy")
         odd_depth = depth_index % 2 == 1
@@ -192,10 +216,6 @@
                 deep[z, pl.ds(ROW_TILE + start, ROW_TILE)] = total
             low, high = low[HALO:], high[HALO:]
 
-        slab_start = (depth_index * depth_cells).astype(jnp.float32)
-        for z in range(depth_cells):
-            shear_ref[z] = shear_matrices(slopes_ref, slab_start + float(z), columns, total_depth)
-
         band = column_matrix(columns)
         band_ref[...] = band
         weights = jnp.concatenate([band, band, band], axis=0)
@@ -215,6 +235,11 @@
             else:
                 smooth[z] = column_sums(total, weights[:, :columns])
         zero_outside(smooth, depth_index, n_depth, layers)
+
+        wait_scalars()
+        slab_start = (depth_index * depth_cells).astype(jnp.float32)
+        for z in range(depth_cells):
+            shear_ref[z] = shear_matrices(slopes_ref, slab_start + float(z), columns, total_depth)
 
         own_live = live_ref[depth_index, row_index]
         middle = pl.ds(ROW_TILE, height)
@@ -249,7 +274,6 @@
                 store_codes(out_ref, place, view, codes, row % tile_rows, tile_rows)
             row += count
 
-    smem = pl.BlockSpec(memory_space=pltpu.SMEM)
     vmem = pl.BlockSpec(memory_space=pltpu.VMEM)
     return pl.pallas_call(
         kernel,
@@ -259,13 +283,18 @@
             jax.ShapeDtypeStruct((depth_cells, columns, VIEWS * columns), jnp.bfloat16),
             jax.ShapeDtypeStruct((columns, 2 * columns), jnp.bfloat16),
         ),
-        in_specs=[smem] * 4 + [vmem] * 3,
+        in_specs=[vmem] * 7,
         out_specs=(vmem,) * 4,
         scratch_shapes=[
             pltpu.VMEM((layers, span + ROW_TILE, columns), jnp.float32),
             pltpu.VMEM((layers, span, columns), jnp.float32),
             pltpu.VMEM((depth_cells, height, columns), jnp.float32),
             pltpu.VMEM((depth_cells, 4 * height, VIEWS * columns), jnp.float32),
+            pltpu.SMEM(live_slices.shape, jnp.int32),
+            pltpu.SMEM(slopes.shape, jnp.float32),
+            pltpu.SMEM(palette.shape, jnp.float32),
+            pltpu.SMEM(owner.shape, jnp.int32),
+            pltpu.SemaphoreType.DMA((4,)),
         ],
         compiler_params=pltpu.CompilerParams(vmem_limit_bytes=VMEM_BYTES),
         cost_estimate=pl.CostEstimate(
@@ -292,10 +321,14 @@
     height = 2 * EDGE
 
     def kernel(
-        live_ref, palette_ref, owner_ref, inner_ref, deep_ref, shear_ref, band_ref,
+        live_in, palette_in, owner_in, inner_ref, deep_ref, shear_ref, band_ref,
         corner_odd_ref, corner_even_ref, rlo_ref, rhi_ref,
         out_ref, halo, triple, split_sums, smooth, across, sheared,
+        live_ref, palette_ref, owner_ref, sems,
     ):
+        wait_scalars = fetch_scalars(
+            [(live_in, live_ref), (palette_in, palette_ref), (owner_in, owner_ref)], sems
+        )
         depth_index = lax.axis_index("gz")
         row_index = lax.axis_index("xy")
         odd_depth = depth_index % 2 == 1
@@ -345,6 +378,7 @@
 
         zero_outside(smooth, depth_index, n_depth, layers)
 
+        wait_scalars()
         own_live = live_ref[depth_index, row_index]
 
         def both_sides(ref, z, start):
@@ -375,12 +409,11 @@
                 part = [code[side * EDGE : (side + 1) * EDGE] for code in codes]
                 store_codes(out_ref, place, view, part, row % tile_rows, tile_rows, inner_ref)
 
-    smem = pl.BlockSpec(memory_space=pltpu.SMEM)
     vmem = pl.BlockSpec(memory_space=pltpu.VMEM)
     return pl.pallas_call(
         kernel,
         out_shape=jax.ShapeDtypeStruct(inner.shape, inner.dtype),
-        in_specs=[smem] * 3 + [vmem] * 8,
+        in_specs=[vmem] * 11,
         out_specs=vmem,
         scratch_shapes=[
             pltpu.VMEM((layers, 2, band, columns), jnp.float32),
@@ -389,6 +422,10 @@
             pltpu.VMEM((layers, 2, piece, columns), jnp.float32),
             pltpu.VMEM((depth_cells, 2, piece, columns), jnp.float32),
             pltpu.VMEM((depth_cells, 4 * height, VIEWS * columns), jnp.float32),
+            pltpu.SMEM(live_slices.shape, jnp.int32),
+            pltpu.SMEM(palette.shape, jnp.float32),
+            pltpu.SMEM(owner.shape, jnp.int32),
+            pltpu.SemaphoreType.DMA((3,)),
         ],
         compiler_params=pltpu.CompilerParams(vmem_limit_bytes=VMEM_BYTES),
         name="render_edges",
@@ -433,15 +470,19 @@
     )(density)
 
 
-def composite_kernel(order_ref, in_ref, out_ref):
+def composite_kernel(order_in, in_ref, out_ref, values, order_ref, sems):
+    wait_scalars = fetch_scalars([(order_in, order_ref)], sems)
     count = in_ref.shape[0]
     rows = in_ref.shape[2] // 4
+    for source in range(count):
+        for view in range(VIEWS):
+            values[source, view] = decode(in_ref[source, view])
+    wait_scalars()
     for view in range(VIEWS):
         colour, transmit = None, None
         for k in range(count):
             source = order_ref[view, k]
-            values = decode(in_ref[source, view])
-            part = [values[c * rows : (c + 1) * rows] for c in range(4)]
+            part = [values[source, view, pl.ds(c * rows, rows)] for c in range(4)]
             clear = 1.0 - part[3]
             if k == 0:
                 colour, transmit = part[:3], clear
@@ -491,8 +532,13 @@
     return pl.pallas_call(
         composite_kernel,
         out_shape=jax.ShapeDtypeStruct((VIEWS, 4, 1, tile_rows, columns), jnp.float32),
-        in_specs=[pl.BlockSpec(memory_space=pltpu.SMEM), pl.BlockSpec(memory_space=pltpu.VMEM)],
+        in_specs=[pl.BlockSpec(memory_space=pltpu.VMEM)] * 2,
         out_specs=pl.BlockSpec(memory_space=pltpu.VMEM),
+        scratch_shapes=[
+            pltpu.VMEM(incoming.shape, jnp.float32),
+            pltpu.SMEM(depth_order.shape, jnp.int32),
+            pltpu.SemaphoreType.DMA((1,)),
+        ],
         compiler_params=pltpu.CompilerParams(vmem_limit_bytes=VMEM_BYTES),
         name="composite",
     )(depth_order, incoming)

time: 27.6 us -> 27.1 us (0.982)
  Pallas kernels: 5.53 us -> 5 us
    pallas_call x1, Pallas kernels: 1.23 us -> 0.94 us  [render_edges(): pl.pallas_call(kernel, out_shape=jax.ShapeDtypeStruct(inner.shape, inner....]
where the time goes in v20:
time: 27.1 us; the launch traced here: 26.9 us
  starting transfers between devices  11 us (41%)
  blocking collectives  9.57 us (35%)
  Pallas kernels  5 us (18%)
  local copies, waits for them, and re-layouts  1.08 us (4%)
    all_to_all x1, blocking collectives, body(): lax.all_to_all(outgoing, 'gz', split_axis=0, concat_axis=0, tiled=True)  9.57 us
    ppermute x1, starting transfers between devices, body(): row_odd = lax.ppermute(row_odd, 'xy', pairs('xy', 1))  4.92 us
    ppermute x1, starting transfers between devices, body(): deep_even = lax.ppermute(deep_even, 'gz', pairs('gz', 0))  2.93 us
    pallas_call x1, Pallas kernels, render_inner(): pl.pallas_call(kernel, out_shape=(jax.ShapeDtypeStruct((n_depth, VIEWS, 4...  2.61 us
    ppermute x1, starting transfers between devices, body(): lax.ppermute(jnp.where(odd_depth, low_corner, high_corner), 'gz', pairs('...  1.61 us
    pallas_call x1, Pallas kernels, body(): pl.pallas_call(composite_kernel, out_shape=jax.ShapeDtypeStruct((VIEWS, 4...  1.25 us
    unnamed x14, local copies, waits for them, and re-layouts  1.08 us
    pallas_call x1, Pallas kernels, render_edges(): pl.pallas_call(kernel, out_shape=jax.ShapeDtypeStruct(inner.shape, inner....  0.94 us
  transfers between devices with their start and end apart: 6, of which 0 were waited for; matrix products, arithmetic and copies ran while one was open for 0% of the time, Pallas kernels for 10%

profile of v20, /device:TPU:2, one launch (start us, length us, event | category | flops | bytes accessed | tf_op | source)
XLA Modules:
  0.0 26.9 jit_solution(2823567764948869719)
XLA Ops:
  0.0 1.0 %copy-done = f32[8,128,128]{2,1,0:T(8,128)S(1)} copy-done((f32[8,128,128]{2,1,0:T(8,128)S(1)}, f32[8,128,128]{2,1,0:T(8,128)}, u32[]{:S(2)}) %copy-start) | copy-done | bytes 524312
  1.0 0.2 cut_edges.1
  1.2 0.1 collective-permute-start.2
  1.3 4.9 %collective-permute-start.3 = (f32[8,8,128]{2,1,0:T(8,128)S(1)}, f32[8,8,128]{2,1,0:T(8,128)S(1)}, u32[]{:S(2)}, u32[]{:S(2)}) collective-permute-start(f32[8,8,128]{2,1,0:T(8,128)S(1)} %get-tuple-element.20), channel_id=1, source_target_pairs={{1,2},{3,4},{5,6},{2,1},{4,3},{6,5},{9,10},{11,12},{13,14},{10,9},... | collective-permute-start | bytes 98312 | tf_op jit(solution)/shard_map/ppermute | solution.py:510
  6.2 0.7 %collective-permute-start = (s32[50,8,128]{2,1,0:T(8,128)S(1)}, s32[50,8,128]{2,1,0:T(8,128)S(1)}, u32[]{:S(2)}, u32[]{:S(2)}) collective-permute-start(s32[50,8,128]{2,1,0:T(8,128)S(1)} %get-tuple-element.13), channel_id=1, source_target_pairs={{8,16},{16,8},{9,17},{17,9},{10,18},{18,10},{11,19},{19,11},{12,20... | collective-permute-start | bytes 614408 | tf_op jit(solution)/shard_map/ppermute | solution.py:511
  6.9 2.9 %collective-permute-start.1 = (s32[50,8,128]{2,1,0:T(8,128)S(1)}, s32[50,8,128]{2,1,0:T(8,128)S(1)}, u32[]{:S(2)}, u32[]{:S(2)}) collective-permute-start(s32[50,8,128]{2,1,0:T(8,128)S(1)} %get-tuple-element.14), channel_id=1, source_target_pairs={{0,8},{16,24},{8,0},{24,16},{1,9},{17,25},{9,1},{25,17},{2,10},{18... | collective-permute-start | bytes 614408 | tf_op jit(solution)/shard_map/ppermute | solution.py:512
  9.9 0.0 collective-permute-done.2
  9.9 0.0 collective-permute-done.3
  9.9 0.0 copy-start.6
  9.9 0.0 copy-start.2
  9.9 0.0 copy-start.3
  10.0 0.0 copy-start.5
  10.0 0.8 %collective-permute-start.4 = (f32[5,16,128]{2,1,0:T(8,128)S(1)}, f32[5,16,128]{2,1,0:T(8,128)S(1)}, u32[]{:S(2)}, u32[]{:S(2)}) collective-permute-start(f32[5,16,128]{2,1,0:T(8,128)S(1)} %get-tuple-element.22), channel_id=1, source_target_pairs={{8,16},{16,8},{9,17},{17,9},{10,18},{18,10},{11,19},{19,11},{12,20... | collective-permute-start | bytes 122888 | tf_op jit(solution)/shard_map/ppermute | solution.py:517
  10.8 1.6 %collective-permute-start.5 = (f32[5,16,128]{2,1,0:T(8,128)S(1)}, f32[5,16,128]{2,1,0:T(8,128)S(1)}, u32[]{:S(2)}, u32[]{:S(2)}) collective-permute-start(f32[5,16,128]{2,1,0:T(8,128)S(1)} %get-tuple-element.21), channel_id=1, source_target_pairs={{0,8},{16,24},{8,0},{24,16},{1,9},{17,25},{9,1},{25,17},{2,10},{18... | collective-permute-start | bytes 122888 | tf_op jit(solution)/shard_map/ppermute | solution.py:520
  12.4 0.0 collective-permute-done.odd_ref
  12.4 0.0 collective-permute-done.1.even_ref
  12.4 0.0 copy-done.1
  12.4 2.6 %render_inner.1 = (s16[4,2,128,128]{3,2,1,0:T(8,128)(2,1)S(1)}, f32[10,144,128]{2,1,0:T(8,128)S(1)}, bf16[8,128,256]{2,1,0:T(8,128)(2,1)S(1)}, bf16[128,256]{1,0:T(8,128)(2,1)S(1)}) custom-call(s32[4,8]{1,0:T(4,128)S(1)} %copy-done.2, f32[2]{0:T(128)S(1)} %copy-done.6, f32[3]{0:T(128)S(1)} %copy-done.5, s32[2,4]{1,0:T(2,128)S(1)} %copy-done.3, ...), custom_call_target="tpu_custom_call" | custom-call | flops 13107200 | bytes 8388608 | tf_op jit(solution)/shard_map/render_inner/pallas_call | solution.py:278
  15.1 0.0 collective-permute-done.4.corner_odd_ref
  15.1 0.0 collective-permute-done.5.corner_even_ref
  15.1 0.9 %render_edges.1 = s16[4,2,128,128]{3,2,1,0:T(8,128)(2,1)S(1)} custom-call(s32[4,8]{1,0:T(4,128)S(1)} %copy-done.2, f32[3]{0:T(128)S(1)} %copy-done.5, s32[2,4]{1,0:T(2,128)S(1)} %copy-done.3, s16[4,2,128,128]{3,2,1,0:T(8,128)(2,1)S(1)} %get-tuple-element.15.inner_ref, f32[10,144,128]{2,1,0:T(8,128)S(1)} %get-tuple-element.16.deep_ref, ...), custom_call_target="tpu_custom_call" | custom-call | tf_op jit(solution)/shard_map/render_edges/pallas_call | solution.py:413
  16.0 0.0 copy-start.4
  16.0 9.6 %all_to_all.5.in_ref = s16[4,2,128,128]{3,2,1,0:T(8,128)(2,1)S(1)} all-to-all(s16[4,2,128,128]{3,2,1,0:T(8,128)(2,1)S(1)} %render_edges.1), channel_id=1, replica_groups=mesh['gz'=4,'xy'=8] {'gz'}, dimensions={0} | all-to-all | bytes 524288 | tf_op jit(solution)/shard_map/all_to_all | solution.py:530
  25.6 1.2 %composite.1 = f32[2,4,1,32,128]{4,3,2,1,0:T(8,128)} custom-call(s32[2,4]{1,0:T(2,128)S(1)} %copy-done.4, s16[4,2,128,128]{3,2,1,0:T(8,128)(2,1)S(1)} %all_to_all.5.in_ref), custom_call_target="tpu_custom_call" | custom-call | tf_op jit(solution)/shard_map/composite/pallas_call | solution.py:532
  (10 shorter events, 0.0 us)
Async XLA Ops:
  0.0 1.0 %copy-start = (f32[8,128,128]{2,1,0:T(8,128)S(1)}, f32[8,128,128]{2,1,0:T(8,128)}, u32[]{:S(2)}) copy-start(f32[8,128,128]{2,1,0:T(8,128)} %own_ref.1) | copy-start | bytes 1572868
  1.0 11.3 %copy-start.1 = (f32[8,128,128]{2,1,0:T(8,128)S(1)}, f32[8,128,128]{2,1,0:T(8,128)}, u32[]{:S(2)}) copy-start(f32[8,128,128]{2,1,0:T(8,128)} %own_ref.1) | copy-start | bytes 1572868
  1.2 8.6 %collective-permute-start.2 = (f32[8,8,128]{2,1,0:T(8,128)S(1)}, f32[8,8,128]{2,1,0:T(8,128)S(1)}, u32[]{:S(2)}, u32[]{:S(2)}) collective-permute-start(f32[8,8,128]{2,1,0:T(8,128)S(1)} %get-tuple-element.19), channel_id=1, source_target_pairs={{0,1},{2,3},{4,5},{6,7},{1,0},{3,2},{5,4},{7,6},{8,9},{10,11},{12,... | collective-permute-start | bytes 98312 | tf_op jit(solution)/shard_map/ppermute | solution.py:509
  1.3 8.6 %collective-permute-start.3 = (f32[8,8,128]{2,1,0:T(8,128)S(1)}, f32[8,8,128]{2,1,0:T(8,128)S(1)}, u32[]{:S(2)}, u32[]{:S(2)}) collective-permute-start(f32[8,8,128]{2,1,0:T(8,128)S(1)} %get-tuple-element.20), channel_id=1, source_target_pairs={{1,2},{3,4},{5,6},{2,1},{4,3},{6,5},{9,10},{11,12},{13,14},{10,9},... | collective-permute-start | bytes 98312 | tf_op jit(solution)/shard_map/ppermute | solution.py:510
  6.2 6.1 %collective-permute-start = (s32[50,8,128]{2,1,0:T(8,128)S(1)}, s32[50,8,128]{2,1,0:T(8,128)S(1)}, u32[]{:S(2)}, u32[]{:S(2)}) collective-permute-start(s32[50,8,128]{2,1,0:T(8,128)S(1)} %get-tuple-element.13), channel_id=1, source_target_pairs={{8,16},{16,8},{9,17},{17,9},{10,18},{18,10},{11,19},{19,11},{12,20... | collective-permute-start | bytes 614408 | tf_op jit(solution)/shard_map/ppermute | solution.py:511
  6.9 5.5 %collective-permute-start.1 = (s32[50,8,128]{2,1,0:T(8,128)S(1)}, s32[50,8,128]{2,1,0:T(8,128)S(1)}, u32[]{:S(2)}, u32[]{:S(2)}) collective-permute-start(s32[50,8,128]{2,1,0:T(8,128)S(1)} %get-tuple-element.14), channel_id=1, source_target_pairs={{0,8},{16,24},{8,0},{24,16},{1,9},{17,25},{9,1},{25,17},{2,10},{18... | collective-permute-start | bytes 614408 | tf_op jit(solution)/shard_map/ppermute | solution.py:512
  9.9 2.5 %copy-start.6 = (f32[2]{0:T(128)S(1)}, f32[2]{0:T(128)}, u32[]{:S(2)}) copy-start(f32[2]{0:T(128)} %slopes_in.1) | copy-start | bytes 28
  9.9 2.5 %copy-start.2 = (s32[4,8]{1,0:T(4,128)S(1)}, s32[4,8]{1,0:T(4,128)}, u32[]{:S(2)}) copy-start(s32[4,8]{1,0:T(4,128)} %live_in.3) | copy-start | bytes 388
  9.9 2.5 %copy-start.3 = (s32[2,4]{1,0:T(2,128)S(1)}, s32[2,4]{1,0:T(2,128)}, u32[]{:S(2)}) copy-start(s32[2,4]{1,0:T(2,128)} %owner_in.3) | copy-start | bytes 100
  10.0 2.5 %copy-start.5 = (f32[3]{0:T(128)S(1)}, f32[3]{0:T(128)}, u32[]{:S(2)}) copy-start(f32[3]{0:T(128)} %palette_in.3) | copy-start | bytes 40
  10.0 5.1 %collective-permute-start.4 = (f32[5,16,128]{2,1,0:T(8,128)S(1)}, f32[5,16,128]{2,1,0:T(8,128)S(1)}, u32[]{:S(2)}, u32[]{:S(2)}) collective-permute-start(f32[5,16,128]{2,1,0:T(8,128)S(1)} %get-tuple-element.22), channel_id=1, source_target_pairs={{8,16},{16,8},{9,17},{17,9},{10,18},{18,10},{11,19},{19,11},{12,20... | collective-permute-start | bytes 122888 | tf_op jit(solution)/shard_map/ppermute | solution.py:517
  10.8 4.3 %collective-permute-start.5 = (f32[5,16,128]{2,1,0:T(8,128)S(1)}, f32[5,16,128]{2,1,0:T(8,128)S(1)}, u32[]{:S(2)}, u32[]{:S(2)}) collective-permute-start(f32[5,16,128]{2,1,0:T(8,128)S(1)} %get-tuple-element.21), channel_id=1, source_target_pairs={{0,8},{16,24},{8,0},{24,16},{1,9},{17,25},{9,1},{25,17},{2,10},{18... | collective-permute-start | bytes 122888 | tf_op jit(solution)/shard_map/ppermute | solution.py:520
  16.0 9.6 %copy-start.4 = (s32[2,4]{1,0:T(2,128)S(1)}, s32[2,4]{1,0:T(2,128)}, u32[]{:S(2)}) copy-start(s32[2,4]{1,0:T(2,128)} %order_in.1) | copy-start | bytes 100

commit v21 on v20

--- a/solution.py
+++ b/solution.py
@@ -308,7 +308,7 @@
 
 def render_edges(
     live_slices, palette, owner, inner, deep, shear, band_weights,
-    corner_odd, corner_even, rlo, rhi, n_depth,
+    corner_odd, corner_even, row_even, row_odd, n_depth,
 ):
     layers, padded_rows, columns = deep.shape
     row_cells = padded_rows - 2 * ROW_TILE
@@ -322,7 +322,7 @@
 
     def kernel(
         live_in, palette_in, owner_in, inner_ref, deep_ref, shear_ref, band_ref,
-        corner_odd_ref, corner_even_ref, rlo_ref, rhi_ref,
+        corner_odd_ref, corner_even_ref, row_even_ref, row_odd_ref,
         out_ref, halo, triple, split_sums, smooth, across, sheared,
         live_ref, palette_ref, owner_ref, sems,
     ):
@@ -333,16 +333,25 @@
         row_index = lax.axis_index("xy")
         odd_depth = depth_index % 2 == 1
 
-        for side, mid_ref in ((0, rlo_ref), (1, rhi_ref)):
-            at = pl.ds(side * ROW_TILE, ROW_TILE)
-            even = [corner_even_ref[i, at] for i in range(HALO)]
-            odd = [corner_odd_ref[i, at] for i in range(HALO)]
+        odd_row = row_index % 2 == 1
+        from_even, from_odd = pl.ds(0, ROW_TILE), pl.ds(ROW_TILE, ROW_TILE)
+        for side in range(2):
+            take_even = odd_row if side == 0 else jnp.logical_not(odd_row)
+
+            def facing_rows(ref, i):
+                return jnp.where(take_even, ref[i, from_even], ref[i, from_odd])
+
+            even = [facing_rows(corner_even_ref, i) for i in range(HALO)]
+            odd = [facing_rows(corner_odd_ref, i) for i in range(HALO)]
+            middle = [
+                jnp.where(take_even, row_even_ref[i], row_odd_ref[i]) for i in range(depth_cells)
+            ]
             low = [jnp.where(odd_depth, e, o) for e, o in zip(even, odd)]
             high = [jnp.where(odd_depth, o, e) for e, o in zip(even, odd)]
             outer = 0 if side == 0 else band - ROW_TILE
             inner_at = ROW_TILE if side == 0 else 0
             own_at = ROW_TILE if side == 0 else padded_rows - band
-            sums = window_sums(low + [mid_ref[i] for i in range(depth_cells)] + high, TAPS)
+            sums = window_sums(low + middle + high, TAPS)
             for z in range(layers):
                 halo[z, side, pl.ds(outer, ROW_TILE)] = sums[z]
                 halo[z, side, pl.ds(inner_at, band - ROW_TILE)] = deep_ref[
@@ -431,7 +440,7 @@
         name="render_edges",
     )(
         live_slices, palette, owner, inner, deep, shear, band_weights,
-        corner_odd, corner_even, rlo, rhi,
+        corner_odd, corner_even, row_even, row_odd,
     )
 
 
@@ -498,7 +507,6 @@
     n_depth = lax.axis_size("gz")
     edge = depth_cells - HALO
     odd_depth = lax.axis_index("gz") % 2 == 1
-    odd_row = lax.axis_index("xy") % 2 == 1
 
     def pairs(axis, first):
         count = lax.axis_size(axis)
@@ -510,22 +518,20 @@
     row_odd = lax.ppermute(row_odd, "xy", pairs("xy", 1))
     deep_odd = lax.ppermute(deep_odd, "gz", pairs("gz", 1))
     deep_even = lax.ppermute(deep_even, "gz", pairs("gz", 0))
-    rlo = jnp.where(odd_row, row_even, row_odd)
-    rhi = jnp.where(odd_row, row_odd, row_even)
-    low_corner = jnp.concatenate([rlo[:HALO], rhi[:HALO]], axis=1)
-    high_corner = jnp.concatenate([rlo[edge:], rhi[edge:]], axis=1)
+    rows = jnp.concatenate([row_even, row_odd], axis=1)
+    facing = jnp.where(odd_depth, edge, 0)
     corner_odd = lax.ppermute(
-        jnp.where(odd_depth, high_corner, low_corner), "gz", pairs("gz", 1)
+        lax.dynamic_slice_in_dim(rows, facing, HALO), "gz", pairs("gz", 1)
     )
     corner_even = lax.ppermute(
-        jnp.where(odd_depth, low_corner, high_corner), "gz", pairs("gz", 0)
+        lax.dynamic_slice_in_dim(rows, edge - facing, HALO), "gz", pairs("gz", 0)
     )
     inner, deep, shear, band_weights = render_inner(
         live_slices, shear_slopes, palette, tile_owner, density, deep_odd, deep_even, n_depth
     )
     outgoing = render_edges(
         live_slices, palette, tile_owner, inner, deep, shear, band_weights,
-        corner_odd, corner_even, rlo, rhi, n_depth,
+        corner_odd, corner_even, row_even, row_odd, n_depth,
     )
     incoming = lax.all_to_all(outgoing, "gz", split_axis=0, concat_axis=0, tiled=True)
     tile_rows = row_cells // n_depth

time: 27.1 us -> 28.9 us (1.066)
  the two profiles are of different devices: /device:TPU:2 before, /device:TPU:24 now
where the time goes in v21:
time: 28.9 us; the launch traced here: 28.6 us
  starting transfers between devices  9.61 us (33%)
  blocking collectives  8.42 us (29%)
  Pallas kernels  4.99 us (17%)
  waiting for transfers between devices  4.35 us (15%)
  local copies, waits for them, and re-layouts  1.09 us (4%)
    all_to_all x1, blocking collectives, body(): lax.all_to_all(outgoing, 'gz', split_axis=0, concat_axis=0, tiled=True)  8.42 us
    ppermute x1, waiting for transfers between devices, body(): row_odd = lax.ppermute(row_odd, 'xy', pairs('xy', 1))  4.33 us
    ppermute x1, starting transfers between devices, body(): deep_even = lax.ppermute(deep_even, 'gz', pairs('gz', 0))  2.93 us
    pallas_call x1, Pallas kernels, render_inner(): pl.pallas_call(kernel, out_shape=(jax.ShapeDtypeStruct((n_depth, VIEWS, 4...  2.6 us
    ppermute x1, starting transfers between devices, body(): row_odd = lax.ppermute(row_odd, 'xy', pairs('xy', 1))  2.32 us
    ppermute x1, starting transfers between devices, body(): row_even = lax.ppermute(row_even, 'xy', pairs('xy', 0))  1.56 us
    ppermute x1, starting transfers between devices, body(): lax.ppermute(lax.dynamic_slice_in_dim(rows, edge - facing, HALO), 'gz', p...  1.35 us
    pallas_call x1, Pallas kernels, body(): pl.pallas_call(composite_kernel, out_shape=jax.ShapeDtypeStruct((VIEWS, 4...  1.25 us
  transfers between devices with their start and end apart: 6, of which 1 were waited for; matrix products, arithmetic and copies ran while one was open for 0% of the time, Pallas kernels for 9%

profile of v21, /device:TPU:24, one launch (start us, length us, event | category | flops | bytes accessed | tf_op | source)
XLA Modules:
  0.0 28.6 jit_solution(10148232832181537217)
XLA Ops:
  0.0 1.0 %copy-done = f32[8,128,128]{2,1,0:T(8,128)S(1)} copy-done((f32[8,128,128]{2,1,0:T(8,128)S(1)}, f32[8,128,128]{2,1,0:T(8,128)}, u32[]{:S(2)}) %copy-start) | copy-done | bytes 524312
  1.0 0.2 cut_edges.1
  1.2 1.6 %collective-permute-start.2 = (f32[8,8,128]{2,1,0:T(8,128)S(1)}, f32[8,8,128]{2,1,0:T(8,128)S(1)}, u32[]{:S(2)}, u32[]{:S(2)}) collective-permute-start(f32[8,8,128]{2,1,0:T(8,128)S(1)} %get-tuple-element.19), channel_id=1, source_target_pairs={{0,1},{2,3},{4,5},{6,7},{1,0},{3,2},{5,4},{7,6},{8,9},{10,11},{12,... | collective-permute-start | bytes 98312 | tf_op jit(solution)/shard_map/ppermute | solution.py:517
  2.8 0.7 %collective-permute-start = (s32[50,8,128]{2,1,0:T(8,128)S(1)}, s32[50,8,128]{2,1,0:T(8,128)S(1)}, u32[]{:S(2)}, u32[]{:S(2)}) collective-permute-start(s32[50,8,128]{2,1,0:T(8,128)S(1)} %get-tuple-element.13), channel_id=1, source_target_pairs={{8,16},{16,8},{9,17},{17,9},{10,18},{18,10},{11,19},{19,11},{12,20... | collective-permute-start | bytes 614408 | tf_op jit(solution)/shard_map/ppermute | solution.py:519
  3.5 2.9 %collective-permute-start.1 = (s32[50,8,128]{2,1,0:T(8,128)S(1)}, s32[50,8,128]{2,1,0:T(8,128)S(1)}, u32[]{:S(2)}, u32[]{:S(2)}) collective-permute-start(s32[50,8,128]{2,1,0:T(8,128)S(1)} %get-tuple-element.14), channel_id=1, source_target_pairs={{0,8},{16,24},{8,0},{24,16},{1,9},{17,25},{9,1},{25,17},{2,10},{18... | collective-permute-start | bytes 614408 | tf_op jit(solution)/shard_map/ppermute | solution.py:520
  6.4 2.3 %collective-permute-start.3 = (f32[8,8,128]{2,1,0:T(8,128)S(1)}, f32[8,8,128]{2,1,0:T(8,128)S(1)}, u32[]{:S(2)}, u32[]{:S(2)}) collective-permute-start(f32[8,8,128]{2,1,0:T(8,128)S(1)} %get-tuple-element.20), channel_id=1, source_target_pairs={{1,2},{3,4},{5,6},{2,1},{4,3},{6,5},{9,10},{11,12},{13,14},{10,9},... | collective-permute-start | bytes 98312 | tf_op jit(solution)/shard_map/ppermute | solution.py:518
  8.7 0.0 collective-permute-done.2.row_even_ref
  8.8 4.3 %collective-permute-done.3.row_odd_ref = f32[8,8,128]{2,1,0:T(8,128)S(1)} collective-permute-done((f32[8,8,128]{2,1,0:T(8,128)S(1)}, f32[8,8,128]{2,1,0:T(8,128)S(1)}, u32[]{:S(2)}, u32[]{:S(2)}) %collective-permute-start.3) | collective-permute-done | bytes 32800 | tf_op jit(solution)/shard_map/ppermute | solution.py:518
  13.1 0.0 copy-start.2
  13.1 0.0 copy-start.3
  13.1 0.0 copy-start.5
  13.2 0.8 %collective-permute-start.4 = (f32[5,16,128]{2,1,0:T(8,128)S(1)}, f32[5,16,128]{2,1,0:T(8,128)S(1)}, u32[]{:S(2)}, u32[]{:S(2)}) collective-permute-start(f32[5,16,128]{2,1,0:T(8,128)S(1)} %get-tuple-element.22), channel_id=1, source_target_pairs={{8,16},{16,8},{9,17},{17,9},{10,18},{18,10},{11,19},{19,11},{12,20... | collective-permute-start | bytes 122888 | tf_op jit(solution)/shard_map/ppermute | solution.py:523
  14.0 1.3 %collective-permute-start.5 = (f32[5,16,128]{2,1,0:T(8,128)S(1)}, f32[5,16,128]{2,1,0:T(8,128)S(1)}, u32[]{:S(2)}, u32[]{:S(2)}) collective-permute-start(f32[5,16,128]{2,1,0:T(8,128)S(1)} %get-tuple-element.21), channel_id=1, source_target_pairs={{0,8},{16,24},{8,0},{24,16},{1,9},{17,25},{9,1},{25,17},{2,10},{18... | collective-permute-start | bytes 122888 | tf_op jit(solution)/shard_map/ppermute | solution.py:526
  15.3 0.0 collective-permute-done.odd_ref
  15.3 0.0 collective-permute-done.1.even_ref
  15.3 0.0 copy-done.1
  15.4 2.6 %render_inner.1 = (s16[4,2,128,128]{3,2,1,0:T(8,128)(2,1)S(1)}, f32[10,144,128]{2,1,0:T(8,128)S(1)}, bf16[8,128,256]{2,1,0:T(8,128)(2,1)S(1)}, bf16[128,256]{1,0:T(8,128)(2,1)S(1)}) custom-call(s32[4,8]{1,0:T(4,128)S(1)} %copy-done.2, f32[2]{0:T(128)S(1)} %copy-done.6, f32[3]{0:T(128)S(1)} %copy-done.5, s32[2,4]{1,0:T(2,128)S(1)} %copy-done.3, ...), custom_call_target="tpu_custom_call" | custom-call | flops 13107200 | bytes 8388608 | tf_op jit(solution)/shard_map/render_inner/pallas_call | solution.py:278
  18.0 0.0 collective-permute-done.4.corner_odd_ref
  18.0 0.0 collective-permute-done.5.corner_even_ref
  18.0 0.9 %render_edges.1 = s16[4,2,128,128]{3,2,1,0:T(8,128)(2,1)S(1)} custom-call(s32[4,8]{1,0:T(4,128)S(1)} %copy-done.2, f32[3]{0:T(128)S(1)} %copy-done.5, s32[2,4]{1,0:T(2,128)S(1)} %copy-done.3, s16[4,2,128,128]{3,2,1,0:T(8,128)(2,1)S(1)} %get-tuple-element.15.inner_ref, f32[10,144,128]{2,1,0:T(8,128)S(1)} %get-tuple-element.16.deep_ref, ...), custom_call_target="tpu_custom_call" | custom-call | tf_op jit(solution)/shard_map/render_edges/pallas_call | solution.py:422
  18.9 0.0 copy-start.4
  18.9 8.4 %all_to_all.5.in_ref = s16[4,2,128,128]{3,2,1,0:T(8,128)(2,1)S(1)} all-to-all(s16[4,2,128,128]{3,2,1,0:T(8,128)(2,1)S(1)} %render_edges.1), channel_id=1, replica_groups=mesh['gz'=4,'xy'=8] {'gz'}, dimensions={0} | all-to-all | bytes 524288 | tf_op jit(solution)/shard_map/all_to_all | solution.py:536
  27.4 0.0 copy-done.4
  27.4 1.2 %composite.1 = f32[2,4,1,32,128]{4,3,2,1,0:T(8,128)} custom-call(s32[2,4]{1,0:T(2,128)S(1)} %copy-done.4, s16[4,2,128,128]{3,2,1,0:T(8,128)(2,1)S(1)} %all_to_all.5.in_ref), custom_call_target="tpu_custom_call" | custom-call | tf_op jit(solution)/shard_map/composite/pallas_call | solution.py:538
  (10 shorter events, 0.0 us)
Async XLA Ops:
  0.0 1.0 %copy-start = (f32[8,128,128]{2,1,0:T(8,128)S(1)}, f32[8,128,128]{2,1,0:T(8,128)}, u32[]{:S(2)}) copy-start(f32[8,128,128]{2,1,0:T(8,128)} %own_ref.1) | copy-start | bytes 1572868
  1.0 14.3 %copy-start.1 = (f32[8,128,128]{2,1,0:T(8,128)S(1)}, f32[8,128,128]{2,1,0:T(8,128)}, u32[]{:S(2)}) copy-start(f32[8,128,128]{2,1,0:T(8,128)} %own_ref.1) | copy-start | bytes 1572868
  1.2 7.5 %collective-permute-start.2 = (f32[8,8,128]{2,1,0:T(8,128)S(1)}, f32[8,8,128]{2,1,0:T(8,128)S(1)}, u32[]{:S(2)}, u32[]{:S(2)}) collective-permute-start(f32[8,8,128]{2,1,0:T(8,128)S(1)} %get-tuple-element.19), channel_id=1, source_target_pairs={{0,1},{2,3},{4,5},{6,7},{1,0},{3,2},{5,4},{7,6},{8,9},{10,11},{12,... | collective-permute-start | bytes 98312 | tf_op jit(solution)/shard_map/ppermute | solution.py:517
  2.8 12.5 %collective-permute-start = (s32[50,8,128]{2,1,0:T(8,128)S(1)}, s32[50,8,128]{2,1,0:T(8,128)S(1)}, u32[]{:S(2)}, u32[]{:S(2)}) collective-permute-start(s32[50,8,128]{2,1,0:T(8,128)S(1)} %get-tuple-element.13), channel_id=1, source_target_pairs={{8,16},{16,8},{9,17},{17,9},{10,18},{18,10},{11,19},{19,11},{12,20... | collective-permute-start | bytes 614408 | tf_op jit(solution)/shard_map/ppermute | solution.py:519
  3.5 11.8 %collective-permute-start.1 = (s32[50,8,128]{2,1,0:T(8,128)S(1)}, s32[50,8,128]{2,1,0:T(8,128)S(1)}, u32[]{:S(2)}, u32[]{:S(2)}) collective-permute-start(s32[50,8,128]{2,1,0:T(8,128)S(1)} %get-tuple-element.14), channel_id=1, source_target_pairs={{0,8},{16,24},{8,0},{24,16},{1,9},{17,25},{9,1},{25,17},{2,10},{18... | collective-permute-start | bytes 614408 | tf_op jit(solution)/shard_map/ppermute | solution.py:520
  6.4 6.7 %collective-permute-start.3 = (f32[8,8,128]{2,1,0:T(8,128)S(1)}, f32[8,8,128]{2,1,0:T(8,128)S(1)}, u32[]{:S(2)}, u32[]{:S(2)}) collective-permute-start(f32[8,8,128]{2,1,0:T(8,128)S(1)} %get-tuple-element.20), channel_id=1, source_target_pairs={{1,2},{3,4},{5,6},{2,1},{4,3},{6,5},{9,10},{11,12},{13,14},{10,9},... | collective-permute-start | bytes 98312 | tf_op jit(solution)/shard_map/ppermute | solution.py:518
  13.1 2.2 %copy-start.6 = (f32[2]{0:T(128)S(1)}, f32[2]{0:T(128)}, u32[]{:S(2)}) copy-start(f32[2]{0:T(128)} %slopes_in.1) | copy-start | bytes 28
  13.1 2.2 %copy-start.2 = (s32[4,8]{1,0:T(4,128)S(1)}, s32[4,8]{1,0:T(4,128)}, u32[]{:S(2)}) copy-start(s32[4,8]{1,0:T(4,128)} %live_in.3) | copy-start | bytes 388
  13.1 2.2 %copy-start.3 = (s32[2,4]{1,0:T(2,128)S(1)}, s32[2,4]{1,0:T(2,128)}, u32[]{:S(2)}) copy-start(s32[2,4]{1,0:T(2,128)} %owner_in.3) | copy-start | bytes 100
  13.1 2.2 %copy-start.5 = (f32[3]{0:T(128)S(1)}, f32[3]{0:T(128)}, u32[]{:S(2)}) copy-start(f32[3]{0:T(128)} %palette_in.3) | copy-start | bytes 40
  13.2 4.8 %collective-permute-start.4 = (f32[5,16,128]{2,1,0:T(8,128)S(1)}, f32[5,16,128]{2,1,0:T(8,128)S(1)}, u32[]{:S(2)}, u32[]{:S(2)}) collective-permute-start(f32[5,16,128]{2,1,0:T(8,128)S(1)} %get-tuple-element.22), channel_id=1, source_target_pairs={{8,16},{16,8},{9,17},{17,9},{10,18},{18,10},{11,19},{19,11},{12,20... | collective-permute-start | bytes 122888 | tf_op jit(solution)/shard_map/ppermute | solution.py:523
  14.0 4.0 %collective-permute-start.5 = (f32[5,16,128]{2,1,0:T(8,128)S(1)}, f32[5,16,128]{2,1,0:T(8,128)S(1)}, u32[]{:S(2)}, u32[]{:S(2)}) collective-permute-start(f32[5,16,128]{2,1,0:T(8,128)S(1)} %get-tuple-element.21), channel_id=1, source_target_pairs={{0,8},{16,24},{8,0},{24,16},{1,9},{17,25},{9,1},{25,17},{2,10},{18... | collective-permute-start | bytes 122888 | tf_op jit(solution)/shard_map/ppermute | solution.py:526
  18.9 8.4 %copy-start.4 = (s32[2,4]{1,0:T(2,128)S(1)}, s32[2,4]{1,0:T(2,128)}, u32[]{:S(2)}) copy-start(s32[2,4]{1,0:T(2,128)} %order_in.1) | copy-start | bytes 100

commit v22 on v21

--- a/solution.py
+++ b/solution.py
@@ -308,7 +308,7 @@
 
 def render_edges(
     live_slices, palette, owner, inner, deep, shear, band_weights,
-    corner_odd, corner_even, row_even, row_odd, n_depth,
+    corner_odd, corner_even, row_odd, row_even, n_depth,
 ):
     layers, padded_rows, columns = deep.shape
     row_cells = padded_rows - 2 * ROW_TILE
@@ -322,7 +322,7 @@
 
     def kernel(
         live_in, palette_in, owner_in, inner_ref, deep_ref, shear_ref, band_ref,
-        corner_odd_ref, corner_even_ref, row_even_ref, row_odd_ref,
+        corner_odd_ref, corner_even_ref, row_odd_ref, row_even_ref,
         out_ref, halo, triple, split_sums, smooth, across, sheared,
         live_ref, palette_ref, owner_ref, sems,
     ):
@@ -334,7 +334,7 @@
         odd_depth = depth_index % 2 == 1
 
         odd_row = row_index % 2 == 1
-        from_even, from_odd = pl.ds(0, ROW_TILE), pl.ds(ROW_TILE, ROW_TILE)
+        from_odd, from_even = pl.ds(0, ROW_TILE), pl.ds(ROW_TILE, ROW_TILE)
         for side in range(2):
             take_even = odd_row if side == 0 else jnp.logical_not(odd_row)
 
@@ -440,7 +440,7 @@
         name="render_edges",
     )(
         live_slices, palette, owner, inner, deep, shear, band_weights,
-        corner_odd, corner_even, row_even, row_odd,
+        corner_odd, corner_even, row_odd, row_even,
     )
 
 
@@ -514,11 +514,11 @@
         return [(i, i + 1) for i in lower] + [(i + 1, i) for i in lower]
 
     row_even, row_odd, deep_even, deep_odd = cut_edges(density)
+    row_odd = lax.ppermute(row_odd, "xy", pairs("xy", 1))
     row_even = lax.ppermute(row_even, "xy", pairs("xy", 0))
-    row_odd = lax.ppermute(row_odd, "xy", pairs("xy", 1))
     deep_odd = lax.ppermute(deep_odd, "gz", pairs("gz", 1))
     deep_even = lax.ppermute(deep_even, "gz", pairs("gz", 0))
-    rows = jnp.concatenate([row_even, row_odd], axis=1)
+    rows = jnp.concatenate([row_odd, row_even], axis=1)
     facing = jnp.where(odd_depth, edge, 0)
     corner_odd = lax.ppermute(
         lax.dynamic_slice_in_dim(rows, facing, HALO), "gz", pairs("gz", 1)
@@ -531,7 +531,7 @@
     )
     outgoing = render_edges(
         live_slices, palette, tile_owner, inner, deep, shear, band_weights,
-        corner_odd, corner_even, row_even, row_odd, n_depth,
+        corner_odd, corner_even, row_odd, row_even, n_depth,
     )
     incoming = lax.all_to_all(outgoing, "gz", split_axis=0, concat_axis=0, tiled=True)
     tile_rows = row_cells // n_depth

time: 28.9 us -> 29.1 us (level)
  the two profiles are of different devices: /device:TPU:24 before, /device:TPU:0 now
where the time goes in v22:
time: 29.1 us; the launch traced here: 28.8 us
  starting transfers between devices  12.3 us (42%)
  blocking collectives  8.42 us (29%)
  Pallas kernels  4.99 us (17%)
  waiting for transfers between devices  1.9 us (7%)
  local copies, waits for them, and re-layouts  1.09 us (4%)
    all_to_all x1, blocking collectives, body(): lax.all_to_all(outgoing, 'gz', split_axis=0, concat_axis=0, tiled=True)  8.42 us
    ppermute x1, starting transfers between devices, body(): deep_even = lax.ppermute(deep_even, 'gz', pairs('gz', 0))  4.38 us
    ppermute x1, starting transfers between devices, body(): row_even = lax.ppermute(row_even, 'xy', pairs('xy', 0))  4.28 us
    pallas_call x1, Pallas kernels, render_inner(): pl.pallas_call(kernel, out_shape=(jax.ShapeDtypeStruct((n_depth, VIEWS, 4...  2.6 us
    ppermute x1, waiting for transfers between devices, body(): row_even = lax.ppermute(row_even, 'xy', pairs('xy', 0))  1.88 us
    ppermute x1, starting transfers between devices, body(): lax.ppermute(lax.dynamic_slice_in_dim(rows, edge - facing, HALO), 'gz', p...  1.49 us
    pallas_call x1, Pallas kernels, body(): pl.pallas_call(composite_kernel, out_shape=jax.ShapeDtypeStruct((VIEWS, 4...  1.25 us
    unnamed x15, local copies, waits for them, and re-layouts  1.08 us
  transfers between devices with their start and end apart: 6, of which 1 were waited for; matrix products, arithmetic and copies ran while one was open for 0% of the time, Pallas kernels for 9%

profile of v22, /device:TPU:0, one launch (start us, length us, event | category | flops | bytes accessed | tf_op | source)
XLA Modules:
  0.0 28.8 jit_solution(6568283660234220876)
XLA Ops:
  0.0 1.0 %copy-done = f32[8,128,128]{2,1,0:T(8,128)S(1)} copy-done((f32[8,128,128]{2,1,0:T(8,128)S(1)}, f32[8,128,128]{2,1,0:T(8,128)}, u32[]{:S(2)}) %copy-start) | copy-done | bytes 524312
  1.0 0.2 cut_edges.1
  1.2 0.7 %collective-permute-start.2 = (f32[8,8,128]{2,1,0:T(8,128)S(1)}, f32[8,8,128]{2,1,0:T(8,128)S(1)}, u32[]{:S(2)}, u32[]{:S(2)}) collective-permute-start(f32[8,8,128]{2,1,0:T(8,128)S(1)} %get-tuple-element.19), channel_id=1, source_target_pairs={{1,2},{3,4},{5,6},{2,1},{4,3},{6,5},{9,10},{11,12},{13,14},{10,9},... | collective-permute-start | bytes 98312 | tf_op jit(solution)/shard_map/ppermute | solution.py:517
  1.9 0.7 %collective-permute-start = (s32[50,8,128]{2,1,0:T(8,128)S(1)}, s32[50,8,128]{2,1,0:T(8,128)S(1)}, u32[]{:S(2)}, u32[]{:S(2)}) collective-permute-start(s32[50,8,128]{2,1,0:T(8,128)S(1)} %get-tuple-element.13), channel_id=1, source_target_pairs={{8,16},{16,8},{9,17},{17,9},{10,18},{18,10},{11,19},{19,11},{12,20... | collective-permute-start | bytes 614408 | tf_op jit(solution)/shard_map/ppermute | solution.py:519
  2.6 4.4 %collective-permute-start.1 = (s32[50,8,128]{2,1,0:T(8,128)S(1)}, s32[50,8,128]{2,1,0:T(8,128)S(1)}, u32[]{:S(2)}, u32[]{:S(2)}) collective-permute-start(s32[50,8,128]{2,1,0:T(8,128)S(1)} %get-tuple-element.14), channel_id=1, source_target_pairs={{0,8},{16,24},{8,0},{24,16},{1,9},{17,25},{9,1},{25,17},{2,10},{18... | collective-permute-start | bytes 614408 | tf_op jit(solution)/shard_map/ppermute | solution.py:520
  7.0 4.3 %collective-permute-start.3 = (f32[8,8,128]{2,1,0:T(8,128)S(1)}, f32[8,8,128]{2,1,0:T(8,128)S(1)}, u32[]{:S(2)}, u32[]{:S(2)}) collective-permute-start(f32[8,8,128]{2,1,0:T(8,128)S(1)} %get-tuple-element.20), channel_id=1, source_target_pairs={{0,1},{2,3},{4,5},{6,7},{1,0},{3,2},{5,4},{7,6},{8,9},{10,11},{12,... | collective-permute-start | bytes 98312 | tf_op jit(solution)/shard_map/ppermute | solution.py:518
  11.3 0.0 collective-permute-done.2.row_odd_ref
  11.3 1.9 %collective-permute-done.3.row_even_ref = f32[8,8,128]{2,1,0:T(8,128)S(1)} collective-permute-done((f32[8,8,128]{2,1,0:T(8,128)S(1)}, f32[8,8,128]{2,1,0:T(8,128)S(1)}, u32[]{:S(2)}, u32[]{:S(2)}) %collective-permute-start.3) | collective-permute-done | bytes 32800 | tf_op jit(solution)/shard_map/ppermute | solution.py:518
  13.2 0.0 copy-start.2
  13.2 0.0 copy-start.3
  13.2 0.0 copy-start.5
  13.2 0.8 %collective-permute-start.4 = (f32[5,16,128]{2,1,0:T(8,128)S(1)}, f32[5,16,128]{2,1,0:T(8,128)S(1)}, u32[]{:S(2)}, u32[]{:S(2)}) collective-permute-start(f32[5,16,128]{2,1,0:T(8,128)S(1)} %get-tuple-element.22), channel_id=1, source_target_pairs={{8,16},{16,8},{9,17},{17,9},{10,18},{18,10},{11,19},{19,11},{12,20... | collective-permute-start | bytes 122888 | tf_op jit(solution)/shard_map/ppermute | solution.py:523
  14.0 1.5 %collective-permute-start.5 = (f32[5,16,128]{2,1,0:T(8,128)S(1)}, f32[5,16,128]{2,1,0:T(8,128)S(1)}, u32[]{:S(2)}, u32[]{:S(2)}) collective-permute-start(f32[5,16,128]{2,1,0:T(8,128)S(1)} %get-tuple-element.21), channel_id=1, source_target_pairs={{0,8},{16,24},{8,0},{24,16},{1,9},{17,25},{9,1},{25,17},{2,10},{18... | collective-permute-start | bytes 122888 | tf_op jit(solution)/shard_map/ppermute | solution.py:526
  15.5 0.0 collective-permute-done.odd_ref
  15.5 0.0 collective-permute-done.1.even_ref
  15.5 0.0 copy-done.6
  15.5 0.0 copy-done.2
  15.6 2.6 %render_inner.1 = (s16[4,2,128,128]{3,2,1,0:T(8,128)(2,1)S(1)}, f32[10,144,128]{2,1,0:T(8,128)S(1)}, bf16[8,128,256]{2,1,0:T(8,128)(2,1)S(1)}, bf16[128,256]{1,0:T(8,128)(2,1)S(1)}) custom-call(s32[4,8]{1,0:T(4,128)S(1)} %copy-done.2, f32[2]{0:T(128)S(1)} %copy-done.6, f32[3]{0:T(128)S(1)} %copy-done.5, s32[2,4]{1,0:T(2,128)S(1)} %copy-done.3, ...), custom_call_target="tpu_custom_call" | custom-call | flops 13107200 | bytes 8388608 | tf_op jit(solution)/shard_map/render_inner/pallas_call | solution.py:278
  18.2 0.0 collective-permute-done.4.corner_odd_ref
  18.2 0.0 collective-permute-done.5.corner_even_ref
  18.2 0.9 %render_edges.1 = s16[4,2,128,128]{3,2,1,0:T(8,128)(2,1)S(1)} custom-call(s32[4,8]{1,0:T(4,128)S(1)} %copy-done.2, f32[3]{0:T(128)S(1)} %copy-done.5, s32[2,4]{1,0:T(2,128)S(1)} %copy-done.3, s16[4,2,128,128]{3,2,1,0:T(8,128)(2,1)S(1)} %get-tuple-element.15.inner_ref, f32[10,144,128]{2,1,0:T(8,128)S(1)} %get-tuple-element.16.deep_ref, ...), custom_call_target="tpu_custom_call" | custom-call | tf_op jit(solution)/shard_map/render_edges/pallas_call | solution.py:422
  19.1 0.0 copy-start.4
  19.1 8.4 %all_to_all.5.in_ref = s16[4,2,128,128]{3,2,1,0:T(8,128)(2,1)S(1)} all-to-all(s16[4,2,128,128]{3,2,1,0:T(8,128)(2,1)S(1)} %render_edges.1), channel_id=1, replica_groups=mesh['gz'=4,'xy'=8] {'gz'}, dimensions={0} | all-to-all | bytes 524288 | tf_op jit(solution)/shard_map/all_to_all | solution.py:536
  27.6 1.2 %composite.1 = f32[2,4,1,32,128]{4,3,2,1,0:T(8,128)} custom-call(s32[2,4]{1,0:T(2,128)S(1)} %copy-done.4, s16[4,2,128,128]{3,2,1,0:T(8,128)(2,1)S(1)} %all_to_all.5.in_ref), custom_call_target="tpu_custom_call" | custom-call | tf_op jit(solution)/shard_map/composite/pallas_call | solution.py:538
  (10 shorter events, 0.0 us)
Async XLA Ops:
  0.0 1.0 %copy-start = (f32[8,128,128]{2,1,0:T(8,128)S(1)}, f32[8,128,128]{2,1,0:T(8,128)}, u32[]{:S(2)}) copy-start(f32[8,128,128]{2,1,0:T(8,128)} %own_ref.1) | copy-start | bytes 1572868
  1.0 14.5 %copy-start.1 = (f32[8,128,128]{2,1,0:T(8,128)S(1)}, f32[8,128,128]{2,1,0:T(8,128)}, u32[]{:S(2)}) copy-start(f32[8,128,128]{2,1,0:T(8,128)} %own_ref.1) | copy-start | bytes 1572868
  1.2 10.0 %collective-permute-start.2 = (f32[8,8,128]{2,1,0:T(8,128)S(1)}, f32[8,8,128]{2,1,0:T(8,128)S(1)}, u32[]{:S(2)}, u32[]{:S(2)}) collective-permute-start(f32[8,8,128]{2,1,0:T(8,128)S(1)} %get-tuple-element.19), channel_id=1, source_target_pairs={{1,2},{3,4},{5,6},{2,1},{4,3},{6,5},{9,10},{11,12},{13,14},{10,9},... | collective-permute-start | bytes 98312 | tf_op jit(solution)/shard_map/ppermute | solution.py:517
  1.9 13.6 %collective-permute-start = (s32[50,8,128]{2,1,0:T(8,128)S(1)}, s32[50,8,128]{2,1,0:T(8,128)S(1)}, u32[]{:S(2)}, u32[]{:S(2)}) collective-permute-start(s32[50,8,128]{2,1,0:T(8,128)S(1)} %get-tuple-element.13), channel_id=1, source_target_pairs={{8,16},{16,8},{9,17},{17,9},{10,18},{18,10},{11,19},{19,11},{12,20... | collective-permute-start | bytes 614408 | tf_op jit(solution)/shard_map/ppermute | solution.py:519
  2.6 12.9 %collective-permute-start.1 = (s32[50,8,128]{2,1,0:T(8,128)S(1)}, s32[50,8,128]{2,1,0:T(8,128)S(1)}, u32[]{:S(2)}, u32[]{:S(2)}) collective-permute-start(s32[50,8,128]{2,1,0:T(8,128)S(1)} %get-tuple-element.14), channel_id=1, source_target_pairs={{0,8},{16,24},{8,0},{24,16},{1,9},{17,25},{9,1},{25,17},{2,10},{18... | collective-permute-start | bytes 614408 | tf_op jit(solution)/shard_map/ppermute | solution.py:520
  7.0 6.2 %collective-permute-start.3 = (f32[8,8,128]{2,1,0:T(8,128)S(1)}, f32[8,8,128]{2,1,0:T(8,128)S(1)}, u32[]{:S(2)}, u32[]{:S(2)}) collective-permute-start(f32[8,8,128]{2,1,0:T(8,128)S(1)} %get-tuple-element.20), channel_id=1, source_target_pairs={{0,1},{2,3},{4,5},{6,7},{1,0},{3,2},{5,4},{7,6},{8,9},{10,11},{12,... | collective-permute-start | bytes 98312 | tf_op jit(solution)/shard_map/ppermute | solution.py:518
  13.2 2.4 %copy-start.6 = (f32[2]{0:T(128)S(1)}, f32[2]{0:T(128)}, u32[]{:S(2)}) copy-start(f32[2]{0:T(128)} %slopes_in.1) | copy-start | bytes 28
  13.2 2.4 %copy-start.2 = (s32[4,8]{1,0:T(4,128)S(1)}, s32[4,8]{1,0:T(4,128)}, u32[]{:S(2)}) copy-start(s32[4,8]{1,0:T(4,128)} %live_in.3) | copy-start | bytes 388
  13.2 2.4 %copy-start.3 = (s32[2,4]{1,0:T(2,128)S(1)}, s32[2,4]{1,0:T(2,128)}, u32[]{:S(2)}) copy-start(s32[2,4]{1,0:T(2,128)} %owner_in.3) | copy-start | bytes 100
  13.2 2.4 %copy-start.5 = (f32[3]{0:T(128)S(1)}, f32[3]{0:T(128)}, u32[]{:S(2)}) copy-start(f32[3]{0:T(128)} %palette_in.3) | copy-start | bytes 40
  13.2 5.0 %collective-permute-start.4 = (f32[5,16,128]{2,1,0:T(8,128)S(1)}, f32[5,16,128]{2,1,0:T(8,128)S(1)}, u32[]{:S(2)}, u32[]{:S(2)}) collective-permute-start(f32[5,16,128]{2,1,0:T(8,128)S(1)} %get-tuple-element.22), channel_id=1, source_target_pairs={{8,16},{16,8},{9,17},{17,9},{10,18},{18,10},{11,19},{19,11},{12,20... | collective-permute-start | bytes 122888 | tf_op jit(solution)/shard_map/ppermute | solution.py:523
  14.0 4.2 %collective-permute-start.5 = (f32[5,16,128]{2,1,0:T(8,128)S(1)}, f32[5,16,128]{2,1,0:T(8,128)S(1)}, u32[]{:S(2)}, u32[]{:S(2)}) collective-permute-start(f32[5,16,128]{2,1,0:T(8,128)S(1)} %get-tuple-element.21), channel_id=1, source_target_pairs={{0,8},{16,24},{8,0},{24,16},{1,9},{17,25},{9,1},{25,17},{2,10},{18... | collective-permute-start | bytes 122888 | tf_op jit(solution)/shard_map/ppermute | solution.py:526
  19.1 8.4 %copy-start.4 = (s32[2,4]{1,0:T(2,128)S(1)}, s32[2,4]{1,0:T(2,128)}, u32[]{:S(2)}) copy-start(s32[2,4]{1,0:T(2,128)} %order_in.1) | copy-start | bytes 100

commit v23 on v21

--- a/solution.py
+++ b/solution.py
@@ -307,8 +307,8 @@
 
 
 def render_edges(
-    live_slices, palette, owner, inner, deep, shear, band_weights,
-    corner_odd, corner_even, row_even, row_odd, n_depth,
+    live_slices, palette, owner, corner_odd, corner_even, row_even, row_odd,
+    inner, deep, shear, band_weights, n_depth,
 ):
     layers, padded_rows, columns = deep.shape
     row_cells = padded_rows - 2 * ROW_TILE
@@ -321,8 +321,8 @@
     height = 2 * EDGE
 
     def kernel(
-        live_in, palette_in, owner_in, inner_ref, deep_ref, shear_ref, band_ref,
-        corner_odd_ref, corner_even_ref, row_even_ref, row_odd_ref,
+        live_in, palette_in, owner_in, corner_odd_ref, corner_even_ref, row_even_ref, row_odd_ref,
+        inner_ref, deep_ref, shear_ref, band_ref,
         out_ref, halo, triple, split_sums, smooth, across, sheared,
         live_ref, palette_ref, owner_ref, sems,
     ):
@@ -439,8 +439,8 @@
         compiler_params=pltpu.CompilerParams(vmem_limit_bytes=VMEM_BYTES),
         name="render_edges",
     )(
-        live_slices, palette, owner, inner, deep, shear, band_weights,
-        corner_odd, corner_even, row_even, row_odd,
+        live_slices, palette, owner, corner_odd, corner_even, row_even, row_odd,
+        inner, deep, shear, band_weights,
     )
 
 
@@ -530,8 +530,8 @@
         live_slices, shear_slopes, palette, tile_owner, density, deep_odd, deep_even, n_depth
     )
     outgoing = render_edges(
-        live_slices, palette, tile_owner, inner, deep, shear, band_weights,
-        corner_odd, corner_even, row_even, row_odd, n_depth,
+        live_slices, palette, tile_owner, corner_odd, corner_even, row_even, row_odd,
+        inner, deep, shear, band_weights, n_depth,
     )
     incoming = lax.all_to_all(outgoing, "gz", split_axis=0, concat_axis=0, tiled=True)
     tile_rows = row_cells // n_depth

time: 28.9 us -> 27.1 us (0.938)
  the two profiles are of different devices: /device:TPU:24 before, /device:TPU:2 now
where the time goes in v23:
time: 27.1 us; the launch traced here: 26.9 us
  blocking collectives  11 us (41%)
  starting transfers between devices  9.37 us (35%)
  Pallas kernels  5 us (18%)
  local copies, waits for them, and re-layouts  1.1 us (4%)
    all_to_all x1, blocking collectives, body(): lax.all_to_all(outgoing, 'gz', split_axis=0, concat_axis=0, tiled=True)  11 us
    ppermute x1, starting transfers between devices, body(): row_odd = lax.ppermute(row_odd, 'xy', pairs('xy', 1))  4.92 us
    ppermute x1, starting transfers between devices, body(): deep_even = lax.ppermute(deep_even, 'gz', pairs('gz', 0))  2.93 us
    pallas_call x1, Pallas kernels, render_inner(): pl.pallas_call(kernel, out_shape=(jax.ShapeDtypeStruct((n_depth, VIEWS, 4...  2.62 us
    pallas_call x1, Pallas kernels, body(): pl.pallas_call(composite_kernel, out_shape=jax.ShapeDtypeStruct((VIEWS, 4...  1.25 us
    unnamed x15, local copies, waits for them, and re-layouts  1.08 us
    pallas_call x1, Pallas kernels, render_edges(): pl.pallas_call(kernel, out_shape=jax.ShapeDtypeStruct(inner.shape, inner....  0.95 us
    ppermute x1, starting transfers between devices, body(): deep_odd = lax.ppermute(deep_odd, 'gz', pairs('gz', 1))  0.67 us
  transfers between devices with their start and end apart: 6, of which 1 were waited for; matrix products, arithmetic and copies ran while one was open for 0% of the time, Pallas kernels for 10%

profile of v23, /device:TPU:2, one launch (start us, length us, event | category | flops | bytes accessed | tf_op | source)
XLA Modules:
  0.0 26.9 jit_solution(6415344421404640072)
XLA Ops:
  0.0 1.0 %copy-done = f32[8,128,128]{2,1,0:T(8,128)S(1)} copy-done((f32[8,128,128]{2,1,0:T(8,128)S(1)}, f32[8,128,128]{2,1,0:T(8,128)}, u32[]{:S(2)}) %copy-start) | copy-done | bytes 524312
  1.0 0.2 cut_edges.1
  1.2 0.1 collective-permute-start
  1.3 4.9 %collective-permute-start.1 = (f32[8,8,128]{2,1,0:T(8,128)S(1)}, f32[8,8,128]{2,1,0:T(8,128)S(1)}, u32[]{:S(2)}, u32[]{:S(2)}) collective-permute-start(f32[8,8,128]{2,1,0:T(8,128)S(1)} %get-tuple-element.14), channel_id=1, source_target_pairs={{1,2},{3,4},{5,6},{2,1},{4,3},{6,5},{9,10},{11,12},{13,14},{10,9},... | collective-permute-start | bytes 98312 | tf_op jit(solution)/shard_map/ppermute | solution.py:518
  6.2 0.7 %collective-permute-start.4 = (s32[50,8,128]{2,1,0:T(8,128)S(1)}, s32[50,8,128]{2,1,0:T(8,128)S(1)}, u32[]{:S(2)}, u32[]{:S(2)}) collective-permute-start(s32[50,8,128]{2,1,0:T(8,128)S(1)} %get-tuple-element.15), channel_id=1, source_target_pairs={{8,16},{16,8},{9,17},{17,9},{10,18},{18,10},{11,19},{19,11},{12,20... | collective-permute-start | bytes 614408 | tf_op jit(solution)/shard_map/ppermute | solution.py:519
  6.9 2.9 %collective-permute-start.5 = (s32[50,8,128]{2,1,0:T(8,128)S(1)}, s32[50,8,128]{2,1,0:T(8,128)S(1)}, u32[]{:S(2)}, u32[]{:S(2)}) collective-permute-start(s32[50,8,128]{2,1,0:T(8,128)S(1)} %get-tuple-element.16), channel_id=1, source_target_pairs={{0,8},{16,24},{8,0},{24,16},{1,9},{17,25},{9,1},{25,17},{2,10},{18... | collective-permute-start | bytes 614408 | tf_op jit(solution)/shard_map/ppermute | solution.py:520
  9.9 0.0 collective-permute-done.row_even_ref
  9.9 0.0 collective-permute-done.1.row_odd_ref
  9.9 0.0 copy-start.6
  9.9 0.0 copy-start.2
  9.9 0.0 copy-start.3
  10.0 0.0 copy-start.5
  10.0 0.1 collective-permute-start.3
  10.1 0.7 %collective-permute-start.2 = (f32[5,16,128]{2,1,0:T(8,128)S(1)}, f32[5,16,128]{2,1,0:T(8,128)S(1)}, u32[]{:S(2)}, u32[]{:S(2)}) collective-permute-start(f32[5,16,128]{2,1,0:T(8,128)S(1)} %get-tuple-element.22), channel_id=1, source_target_pairs={{8,16},{16,8},{9,17},{17,9},{10,18},{18,10},{11,19},{19,11},{12,20... | collective-permute-start | bytes 122888 | tf_op jit(solution)/shard_map/ppermute | solution.py:523
  10.7 0.0 collective-permute-done.4.odd_ref
  10.7 0.2 collective-permute-done.5.even_ref
  11.0 0.0 copy-done.6
  11.0 2.6 %render_inner.1 = (s16[4,2,128,128]{3,2,1,0:T(8,128)(2,1)S(1)}, f32[10,144,128]{2,1,0:T(8,128)S(1)}, bf16[8,128,256]{2,1,0:T(8,128)(2,1)S(1)}, bf16[128,256]{1,0:T(8,128)(2,1)S(1)}) custom-call(s32[4,8]{1,0:T(4,128)S(1)} %copy-done.2, f32[2]{0:T(128)S(1)} %copy-done.6, f32[3]{0:T(128)S(1)} %copy-done.5, s32[2,4]{1,0:T(2,128)S(1)} %copy-done.3, ...), custom_call_target="tpu_custom_call" | custom-call | flops 13107200 | bytes 8388608 | tf_op jit(solution)/shard_map/render_inner/pallas_call | solution.py:278
  13.6 0.0 collective-permute-done.3.corner_even_ref
  13.6 0.0 collective-permute-done.2.corner_odd_ref
  13.6 0.9 %render_edges.1 = s16[4,2,128,128]{3,2,1,0:T(8,128)(2,1)S(1)} custom-call(s32[4,8]{1,0:T(4,128)S(1)} %copy-done.2, f32[3]{0:T(128)S(1)} %copy-done.5, s32[2,4]{1,0:T(2,128)S(1)} %copy-done.3, f32[5,16,128]{2,1,0:T(8,128)S(1)} %collective-permute-done.2.corner_odd_ref, f32[5,16,128]{2,1,0:T(8,128)S(1)} %collective-permute-done.3.corner_even_ref, ...), custom_call_target="tpu_custom_call" | custom-call | tf_op jit(solution)/shard_map/render_edges/pallas_call | solution.py:422
  14.6 0.0 copy-start.4
  14.6 11.0 %all_to_all.5.in_ref = s16[4,2,128,128]{3,2,1,0:T(8,128)(2,1)S(1)} all-to-all(s16[4,2,128,128]{3,2,1,0:T(8,128)(2,1)S(1)} %render_edges.1), channel_id=1, replica_groups=mesh['gz'=4,'xy'=8] {'gz'}, dimensions={0} | all-to-all | bytes 524288 | tf_op jit(solution)/shard_map/all_to_all | solution.py:536
  25.6 1.2 %composite.1 = f32[2,4,1,32,128]{4,3,2,1,0:T(8,128)} custom-call(s32[2,4]{1,0:T(2,128)S(1)} %copy-done.4, s16[4,2,128,128]{3,2,1,0:T(8,128)(2,1)S(1)} %all_to_all.5.in_ref), custom_call_target="tpu_custom_call" | custom-call | tf_op jit(solution)/shard_map/composite/pallas_call | solution.py:538
  (10 shorter events, 0.0 us)
Async XLA Ops:
  0.0 1.0 %copy-start = (f32[8,128,128]{2,1,0:T(8,128)S(1)}, f32[8,128,128]{2,1,0:T(8,128)}, u32[]{:S(2)}) copy-start(f32[8,128,128]{2,1,0:T(8,128)} %own_ref.1) | copy-start | bytes 1572868
  1.0 9.9 %copy-start.1 = (f32[8,128,128]{2,1,0:T(8,128)S(1)}, f32[8,128,128]{2,1,0:T(8,128)}, u32[]{:S(2)}) copy-start(f32[8,128,128]{2,1,0:T(8,128)} %own_ref.1) | copy-start | bytes 1572868
  1.2 8.6 %collective-permute-start = (f32[8,8,128]{2,1,0:T(8,128)S(1)}, f32[8,8,128]{2,1,0:T(8,128)S(1)}, u32[]{:S(2)}, u32[]{:S(2)}) collective-permute-start(f32[8,8,128]{2,1,0:T(8,128)S(1)} %get-tuple-element.13), channel_id=1, source_target_pairs={{0,1},{2,3},{4,5},{6,7},{1,0},{3,2},{5,4},{7,6},{8,9},{10,11},{12,... | collective-permute-start | bytes 98312 | tf_op jit(solution)/shard_map/ppermute | solution.py:517
  1.3 8.6 %collective-permute-start.1 = (f32[8,8,128]{2,1,0:T(8,128)S(1)}, f32[8,8,128]{2,1,0:T(8,128)S(1)}, u32[]{:S(2)}, u32[]{:S(2)}) collective-permute-start(f32[8,8,128]{2,1,0:T(8,128)S(1)} %get-tuple-element.14), channel_id=1, source_target_pairs={{1,2},{3,4},{5,6},{2,1},{4,3},{6,5},{9,10},{11,12},{13,14},{10,9},... | collective-permute-start | bytes 98312 | tf_op jit(solution)/shard_map/ppermute | solution.py:518
  6.2 4.5 %collective-permute-start.4 = (s32[50,8,128]{2,1,0:T(8,128)S(1)}, s32[50,8,128]{2,1,0:T(8,128)S(1)}, u32[]{:S(2)}, u32[]{:S(2)}) collective-permute-start(s32[50,8,128]{2,1,0:T(8,128)S(1)} %get-tuple-element.15), channel_id=1, source_target_pairs={{8,16},{16,8},{9,17},{17,9},{10,18},{18,10},{11,19},{19,11},{12,20... | collective-permute-start | bytes 614408 | tf_op jit(solution)/shard_map/ppermute | solution.py:519
  6.9 4.0 %collective-permute-start.5 = (s32[50,8,128]{2,1,0:T(8,128)S(1)}, s32[50,8,128]{2,1,0:T(8,128)S(1)}, u32[]{:S(2)}, u32[]{:S(2)}) collective-permute-start(s32[50,8,128]{2,1,0:T(8,128)S(1)} %get-tuple-element.16), channel_id=1, source_target_pairs={{0,8},{16,24},{8,0},{24,16},{1,9},{17,25},{9,1},{25,17},{2,10},{18... | collective-permute-start | bytes 614408 | tf_op jit(solution)/shard_map/ppermute | solution.py:520
  9.9 1.1 %copy-start.6 = (f32[2]{0:T(128)S(1)}, f32[2]{0:T(128)}, u32[]{:S(2)}) copy-start(f32[2]{0:T(128)} %slopes_in.1) | copy-start | bytes 28
  9.9 1.0 %copy-start.2 = (s32[4,8]{1,0:T(4,128)S(1)}, s32[4,8]{1,0:T(4,128)}, u32[]{:S(2)}) copy-start(s32[4,8]{1,0:T(4,128)} %live_in.3) | copy-start | bytes 388
  9.9 1.0 %copy-start.3 = (s32[2,4]{1,0:T(2,128)S(1)}, s32[2,4]{1,0:T(2,128)}, u32[]{:S(2)}) copy-start(s32[2,4]{1,0:T(2,128)} %owner_in.3) | copy-start | bytes 100
  10.0 1.0 %copy-start.5 = (f32[3]{0:T(128)S(1)}, f32[3]{0:T(128)}, u32[]{:S(2)}) copy-start(f32[3]{0:T(128)} %palette_in.3) | copy-start | bytes 40
  10.0 3.6 %collective-permute-start.3 = (f32[5,16,128]{2,1,0:T(8,128)S(1)}, f32[5,16,128]{2,1,0:T(8,128)S(1)}, u32[]{:S(2)}, u32[]{:S(2)}) collective-permute-start(f32[5,16,128]{2,1,0:T(8,128)S(1)} %get-tuple-element.21), channel_id=1, source_target_pairs={{0,8},{16,24},{8,0},{24,16},{1,9},{17,25},{9,1},{25,17},{2,10},{18... | collective-permute-start | bytes 122888 | tf_op jit(solution)/shard_map/ppermute | solution.py:526
  10.1 3.5 %collective-permute-start.2 = (f32[5,16,128]{2,1,0:T(8,128)S(1)}, f32[5,16,128]{2,1,0:T(8,128)S(1)}, u32[]{:S(2)}, u32[]{:S(2)}) collective-permute-start(f32[5,16,128]{2,1,0:T(8,128)S(1)} %get-tuple-element.22), channel_id=1, source_target_pairs={{8,16},{16,8},{9,17},{17,9},{10,18},{18,10},{11,19},{19,11},{12,20... | collective-permute-start | bytes 122888 | tf_op jit(solution)/shard_map/ppermute | solution.py:523
  14.6 11.0 %copy-start.4 = (s32[2,4]{1,0:T(2,128)S(1)}, s32[2,4]{1,0:T(2,128)}, u32[]{:S(2)}) copy-start(s32[2,4]{1,0:T(2,128)} %order_in.1) | copy-start | bytes 100

commit v24 on v23

--- a/solution.py
+++ b/solution.py
@@ -406,7 +406,6 @@
             sheared[z] = jnp.dot(
                 jnp.concatenate(channels), shear_ref[z], preferred_element_type=jnp.float32
             )
-        out_ref[...] = inner_ref[...]
         for view in range(VIEWS):
             lanes = pl.ds(view * columns, columns)
             values = march(
@@ -416,12 +415,13 @@
             for side, row in enumerate((0, row_cells - EDGE)):
                 place = owner_ref[view, row // tile_rows]
                 part = [code[side * EDGE : (side + 1) * EDGE] for code in codes]
-                store_codes(out_ref, place, view, part, row % tile_rows, tile_rows, inner_ref)
+                store_codes(out_ref, place, view, part, row % tile_rows, tile_rows, out_ref)
 
     vmem = pl.BlockSpec(memory_space=pltpu.VMEM)
     return pl.pallas_call(
         kernel,
         out_shape=jax.ShapeDtypeStruct(inner.shape, inner.dtype),
+        input_output_aliases={7: 0},
         in_specs=[vmem] * 11,
         out_specs=vmem,
         scratch_shapes=[
@@ -479,15 +479,16 @@
     )(density)
 
 
-def composite_kernel(order_in, in_ref, out_ref, values, order_ref, sems):
+def composite_kernel(order_in, in_ref, out_ref, values, image, order_ref, sems):
     wait_scalars = fetch_scalars([(order_in, order_ref)], sems)
     count = in_ref.shape[0]
     rows = in_ref.shape[2] // 4
-    for source in range(count):
-        for view in range(VIEWS):
+    copies = []
+    for view in range(VIEWS):
+        for source in range(count):
             values[source, view] = decode(in_ref[source, view])
-    wait_scalars()
-    for view in range(VIEWS):
+        if view == 0:
+            wait_scalars()
         colour, transmit = None, None
         for k in range(count):
             source = order_ref[view, k]
@@ -499,7 +500,11 @@
                 colour = [colour[c] + transmit * part[c] for c in range(3)]
                 transmit = transmit * clear
         for c, value in enumerate(colour + [1.0 - transmit]):
-            out_ref[view, c, 0] = value
+            image[view, c, 0] = value
+        copies.append(pltpu.make_async_copy(image.at[view], out_ref.at[view], sems.at[1 + view]))
+        copies[-1].start()
+    for copy in copies:
+        copy.wait()
 
 
 def body(density, live_slices, shear_slopes, palette, depth_order, tile_owner):
@@ -539,11 +544,12 @@
         composite_kernel,
         out_shape=jax.ShapeDtypeStruct((VIEWS, 4, 1, tile_rows, columns), jnp.float32),
         in_specs=[pl.BlockSpec(memory_space=pltpu.VMEM)] * 2,
-        out_specs=pl.BlockSpec(memory_space=pltpu.VMEM),
+        out_specs=pl.BlockSpec(memory_space=pltpu.HBM),
         scratch_shapes=[
             pltpu.VMEM(incoming.shape, jnp.float32),
+            pltpu.VMEM((VIEWS, 4, 1, tile_rows, columns), jnp.float32),
             pltpu.SMEM(depth_order.shape, jnp.int32),
-            pltpu.SemaphoreType.DMA((1,)),
+            pltpu.SemaphoreType.DMA((1 + VIEWS,)),
         ],
         compiler_params=pltpu.CompilerParams(vmem_limit_bytes=VMEM_BYTES),
         name="composite",

time: 27.1 us -> 27.2 us (level)
  no operation moved by 1% of the time
where the time goes in v24:
time: 27.2 us; the launch traced here: 26.9 us
  blocking collectives  11 us (40%)
  starting transfers between devices  9.37 us (34%)
  Pallas kernels  5.06 us (19%)
  local copies, waits for them, and re-layouts  1.1 us (4%)
    all_to_all x1, blocking collectives, body(): lax.all_to_all(outgoing, 'gz', split_axis=0, concat_axis=0, tiled=True)  11 us
    ppermute x1, starting transfers between devices, body(): row_odd = lax.ppermute(row_odd, 'xy', pairs('xy', 1))  4.92 us
    ppermute x1, starting transfers between devices, body(): deep_even = lax.ppermute(deep_even, 'gz', pairs('gz', 0))  2.93 us
    pallas_call x1, Pallas kernels, render_inner(): pl.pallas_call(kernel, out_shape=(jax.ShapeDtypeStruct((n_depth, VIEWS, 4...  2.62 us
    pallas_call x1, Pallas kernels, body(): pl.pallas_call(composite_kernel, out_shape=jax.ShapeDtypeStruct((VIEWS, 4...  1.3 us
    unnamed x15, local copies, waits for them, and re-layouts  1.08 us
    pallas_call x1, Pallas kernels, render_edges(): pl.pallas_call(kernel, out_shape=jax.ShapeDtypeStruct(inner.shape, inner....  0.95 us
    ppermute x1, starting transfers between devices, body(): deep_odd = lax.ppermute(deep_odd, 'gz', pairs('gz', 1))  0.67 us
  transfers between devices with their start and end apart: 6, of which 1 were waited for; matrix products, arithmetic and copies ran while one was open for 0% of the time, Pallas kernels for 10%

profile of v24, /device:TPU:2, one launch (start us, length us, event | category | flops | bytes accessed | tf_op | source)
XLA Modules:
  0.0 26.9 jit_solution(16433777912881801257)
XLA Ops:
  0.0 1.0 %copy-done = f32[8,128,128]{2,1,0:T(8,128)S(1)} copy-done((f32[8,128,128]{2,1,0:T(8,128)S(1)}, f32[8,128,128]{2,1,0:T(8,128)}, u32[]{:S(2)}) %copy-start) | copy-done | bytes 524312
  1.0 0.2 cut_edges.1
  1.2 0.1 collective-permute-start
  1.3 4.9 %collective-permute-start.1 = (f32[8,8,128]{2,1,0:T(8,128)S(1)}, f32[8,8,128]{2,1,0:T(8,128)S(1)}, u32[]{:S(2)}, u32[]{:S(2)}) collective-permute-start(f32[8,8,128]{2,1,0:T(8,128)S(1)} %get-tuple-element.14), channel_id=1, source_target_pairs={{1,2},{3,4},{5,6},{2,1},{4,3},{6,5},{9,10},{11,12},{13,14},{10,9},... | collective-permute-start | bytes 98312 | tf_op jit(solution)/shard_map/ppermute | solution.py:523
  6.2 0.7 %collective-permute-start.4 = (s32[50,8,128]{2,1,0:T(8,128)S(1)}, s32[50,8,128]{2,1,0:T(8,128)S(1)}, u32[]{:S(2)}, u32[]{:S(2)}) collective-permute-start(s32[50,8,128]{2,1,0:T(8,128)S(1)} %get-tuple-element.15), channel_id=1, source_target_pairs={{8,16},{16,8},{9,17},{17,9},{10,18},{18,10},{11,19},{19,11},{12,20... | collective-permute-start | bytes 614408 | tf_op jit(solution)/shard_map/ppermute | solution.py:524
  6.9 2.9 %collective-permute-start.5 = (s32[50,8,128]{2,1,0:T(8,128)S(1)}, s32[50,8,128]{2,1,0:T(8,128)S(1)}, u32[]{:S(2)}, u32[]{:S(2)}) collective-permute-start(s32[50,8,128]{2,1,0:T(8,128)S(1)} %get-tuple-element.16), channel_id=1, source_target_pairs={{0,8},{16,24},{8,0},{24,16},{1,9},{17,25},{9,1},{25,17},{2,10},{18... | collective-permute-start | bytes 614408 | tf_op jit(solution)/shard_map/ppermute | solution.py:525
  9.9 0.0 collective-permute-done.row_even_ref
  9.9 0.0 collective-permute-done.1.row_odd_ref
  9.9 0.0 copy-start.6
  9.9 0.0 copy-start.2
  9.9 0.0 copy-start.3
  10.0 0.0 copy-start.5
  10.0 0.1 collective-permute-start.3
  10.1 0.7 %collective-permute-start.2 = (f32[5,16,128]{2,1,0:T(8,128)S(1)}, f32[5,16,128]{2,1,0:T(8,128)S(1)}, u32[]{:S(2)}, u32[]{:S(2)}) collective-permute-start(f32[5,16,128]{2,1,0:T(8,128)S(1)} %get-tuple-element.22), channel_id=1, source_target_pairs={{8,16},{16,8},{9,17},{17,9},{10,18},{18,10},{11,19},{19,11},{12,20... | collective-permute-start | bytes 122888 | tf_op jit(solution)/shard_map/ppermute | solution.py:528
  10.7 0.0 collective-permute-done.4.odd_ref
  10.7 0.2 collective-permute-done.5.even_ref
  11.0 0.0 copy-done.6
  11.0 2.6 %render_inner.1 = (s16[4,2,128,128]{3,2,1,0:T(8,128)(2,1)S(1)}, f32[10,144,128]{2,1,0:T(8,128)S(1)}, bf16[8,128,256]{2,1,0:T(8,128)(2,1)S(1)}, bf16[128,256]{1,0:T(8,128)(2,1)S(1)}) custom-call(s32[4,8]{1,0:T(4,128)S(1)} %copy-done.2, f32[2]{0:T(128)S(1)} %copy-done.6, f32[3]{0:T(128)S(1)} %copy-done.5, s32[2,4]{1,0:T(2,128)S(1)} %copy-done.3, ...), custom_call_target="tpu_custom_call" | custom-call | flops 13107200 | bytes 8388608 | tf_op jit(solution)/shard_map/render_inner/pallas_call | solution.py:278
  13.6 0.0 collective-permute-done.3.corner_even_ref
  13.6 0.0 collective-permute-done.2.corner_odd_ref
  13.6 0.9 %render_edges.1 = s16[4,2,128,128]{3,2,1,0:T(8,128)(2,1)S(1)} custom-call(s32[4,8]{1,0:T(4,128)S(1)} %copy-done.2, f32[3]{0:T(128)S(1)} %copy-done.5, s32[2,4]{1,0:T(2,128)S(1)} %copy-done.3, f32[5,16,128]{2,1,0:T(8,128)S(1)} %collective-permute-done.2.corner_odd_ref, ...), custom_call_target="tpu_custom_call", output_to_operand_aliasing={{}: (7, {})} | custom-call | tf_op jit(solution)/shard_map/render_edges/pallas_call | solution.py:421
  14.6 0.0 copy-start.4
  14.6 11.0 %all_to_all.5.in_ref = s16[4,2,128,128]{3,2,1,0:T(8,128)(2,1)S(1)} all-to-all(s16[4,2,128,128]{3,2,1,0:T(8,128)(2,1)S(1)} %render_edges.1), channel_id=1, replica_groups=mesh['gz'=4,'xy'=8] {'gz'}, dimensions={0} | all-to-all | bytes 524288 | tf_op jit(solution)/shard_map/all_to_all | solution.py:541
  25.6 1.3 %composite.1 = f32[2,4,1,32,128]{4,3,2,1,0:T(8,128)} custom-call(s32[2,4]{1,0:T(2,128)S(1)} %copy-done.4, s16[4,2,128,128]{3,2,1,0:T(8,128)(2,1)S(1)} %all_to_all.5.in_ref), custom_call_target="tpu_custom_call" | custom-call | tf_op jit(solution)/shard_map/composite/pallas_call | solution.py:543
  (10 shorter events, 0.0 us)
Async XLA Ops:
  0.0 1.0 %copy-start = (f32[8,128,128]{2,1,0:T(8,128)S(1)}, f32[8,128,128]{2,1,0:T(8,128)}, u32[]{:S(2)}) copy-start(f32[8,128,128]{2,1,0:T(8,128)} %own_ref.1) | copy-start | bytes 1572868
  1.0 9.9 %copy-start.1 = (f32[8,128,128]{2,1,0:T(8,128)S(1)}, f32[8,128,128]{2,1,0:T(8,128)}, u32[]{:S(2)}) copy-start(f32[8,128,128]{2,1,0:T(8,128)} %own_ref.1) | copy-start | bytes 1572868
  1.2 8.6 %collective-permute-start = (f32[8,8,128]{2,1,0:T(8,128)S(1)}, f32[8,8,128]{2,1,0:T(8,128)S(1)}, u32[]{:S(2)}, u32[]{:S(2)}) collective-permute-start(f32[8,8,128]{2,1,0:T(8,128)S(1)} %get-tuple-element.13), channel_id=1, source_target_pairs={{0,1},{2,3},{4,5},{6,7},{1,0},{3,2},{5,4},{7,6},{8,9},{10,11},{12,... | collective-permute-start | bytes 98312 | tf_op jit(solution)/shard_map/ppermute | solution.py:522
  1.3 8.6 %collective-permute-start.1 = (f32[8,8,128]{2,1,0:T(8,128)S(1)}, f32[8,8,128]{2,1,0:T(8,128)S(1)}, u32[]{:S(2)}, u32[]{:S(2)}) collective-permute-start(f32[8,8,128]{2,1,0:T(8,128)S(1)} %get-tuple-element.14), channel_id=1, source_target_pairs={{1,2},{3,4},{5,6},{2,1},{4,3},{6,5},{9,10},{11,12},{13,14},{10,9},... | collective-permute-start | bytes 98312 | tf_op jit(solution)/shard_map/ppermute | solution.py:523
  6.2 4.5 %collective-permute-start.4 = (s32[50,8,128]{2,1,0:T(8,128)S(1)}, s32[50,8,128]{2,1,0:T(8,128)S(1)}, u32[]{:S(2)}, u32[]{:S(2)}) collective-permute-start(s32[50,8,128]{2,1,0:T(8,128)S(1)} %get-tuple-element.15), channel_id=1, source_target_pairs={{8,16},{16,8},{9,17},{17,9},{10,18},{18,10},{11,19},{19,11},{12,20... | collective-permute-start | bytes 614408 | tf_op jit(solution)/shard_map/ppermute | solution.py:524
  6.9 4.0 %collective-permute-start.5 = (s32[50,8,128]{2,1,0:T(8,128)S(1)}, s32[50,8,128]{2,1,0:T(8,128)S(1)}, u32[]{:S(2)}, u32[]{:S(2)}) collective-permute-start(s32[50,8,128]{2,1,0:T(8,128)S(1)} %get-tuple-element.16), channel_id=1, source_target_pairs={{0,8},{16,24},{8,0},{24,16},{1,9},{17,25},{9,1},{25,17},{2,10},{18... | collective-permute-start | bytes 614408 | tf_op jit(solution)/shard_map/ppermute | solution.py:525
  9.9 1.1 %copy-start.6 = (f32[2]{0:T(128)S(1)}, f32[2]{0:T(128)}, u32[]{:S(2)}) copy-start(f32[2]{0:T(128)} %slopes_in.1) | copy-start | bytes 28
  9.9 1.0 %copy-start.2 = (s32[4,8]{1,0:T(4,128)S(1)}, s32[4,8]{1,0:T(4,128)}, u32[]{:S(2)}) copy-start(s32[4,8]{1,0:T(4,128)} %live_in.3) | copy-start | bytes 388
  9.9 1.0 %copy-start.3 = (s32[2,4]{1,0:T(2,128)S(1)}, s32[2,4]{1,0:T(2,128)}, u32[]{:S(2)}) copy-start(s32[2,4]{1,0:T(2,128)} %owner_in.3) | copy-start | bytes 100
  10.0 1.0 %copy-start.5 = (f32[3]{0:T(128)S(1)}, f32[3]{0:T(128)}, u32[]{:S(2)}) copy-start(f32[3]{0:T(128)} %palette_in.3) | copy-start | bytes 40
  10.0 3.6 %collective-permute-start.3 = (f32[5,16,128]{2,1,0:T(8,128)S(1)}, f32[5,16,128]{2,1,0:T(8,128)S(1)}, u32[]{:S(2)}, u32[]{:S(2)}) collective-permute-start(f32[5,16,128]{2,1,0:T(8,128)S(1)} %get-tuple-element.21), channel_id=1, source_target_pairs={{0,8},{16,24},{8,0},{24,16},{1,9},{17,25},{9,1},{25,17},{2,10},{18... | collective-permute-start | bytes 122888 | tf_op jit(solution)/shard_map/ppermute | solution.py:531
  10.1 3.5 %collective-permute-start.2 = (f32[5,16,128]{2,1,0:T(8,128)S(1)}, f32[5,16,128]{2,1,0:T(8,128)S(1)}, u32[]{:S(2)}, u32[]{:S(2)}) collective-permute-start(f32[5,16,128]{2,1,0:T(8,128)S(1)} %get-tuple-element.22), channel_id=1, source_target_pairs={{8,16},{16,8},{9,17},{17,9},{10,18},{18,10},{11,19},{19,11},{12,20... | collective-permute-start | bytes 122888 | tf_op jit(solution)/shard_map/ppermute | solution.py:528
  14.6 11.0 %copy-start.4 = (s32[2,4]{1,0:T(2,128)S(1)}, s32[2,4]{1,0:T(2,128)}, u32[]{:S(2)}) copy-start(s32[2,4]{1,0:T(2,128)} %order_in.1) | copy-start | bytes 100

commit v25 on v23

--- a/solution.py
+++ b/solution.py
@@ -18,9 +18,6 @@
 TOP = 2.2
 STEPS = 65535.0
 MIDDLE = 32768
-LEVELS_PER_UNIT = 5461.0
-ZERO_LEVEL = 1 << 19
-GROUP, WORDS = 8, 5
 VMEM_BYTES = 40 * 1024 * 1024
 
 
@@ -53,30 +50,6 @@
         sums = [sums[i] + sums[i + width] for i in range(len(sums) - width)]
         width *= 2
     return [sums[i] + layers[i + width] for i in range(len(layers) - width)]
-
-
-def pack(values):
-    v = [(x * LEVELS_PER_UNIT + (ZERO_LEVEL + 0.5)).astype(jnp.int32) for x in values]
-    v = [(x - ZERO_LEVEL) & 0xFFFFF for x in v]
-    upper = [
-        v[5] & 0xFFF,
-        (v[5] >> 12) | ((v[6] & 0xF) << 8),
-        (v[6] >> 4) & 0xFFF,
-        (v[6] >> 16) | ((v[7] & 0xFF) << 4),
-        v[7] >> 8,
-    ]
-    return [v[i] | (upper[i] << 20) for i in range(WORDS)]
-
-
-def unpack(words):
-    upper = [lax.shift_right_logical(w, jnp.full_like(w, 20)) for w in words]
-    levels = words + [
-        upper[0] | ((upper[1] & 0xFF) << 12),
-        (upper[1] >> 8) | (upper[2] << 4) | ((upper[3] & 0xF) << 16),
-        (upper[3] >> 4) | (upper[4] << 8),
-    ]
-    levels = [(x << 12) >> 12 for x in levels]
-    return [x.astype(jnp.float32) * (1.0 / LEVELS_PER_UNIT) for x in levels]
 
 
 def encode(value):
@@ -203,18 +176,15 @@
         row_index = lax.axis_index("xy")
         odd_depth = depth_index % 2 == 1
 
-        low, high, word = [], [], 0
         for start in range(0, row_cells, ROW_TILE):
-            while len(low) < HALO:
-                even = [even_ref[word + k] for k in range(WORDS)]
-                odd = [odd_ref[word + k] for k in range(WORDS)]
-                low += unpack([jnp.where(odd_depth, e, o) for e, o in zip(even, odd)])
-                high += unpack([jnp.where(odd_depth, o, e) for e, o in zip(even, odd)])
-                word += WORDS
-            own = [own_ref[i, pl.ds(start, ROW_TILE)] for i in range(depth_cells)]
-            for z, total in enumerate(window_sums(low[:HALO] + own + high[:HALO], TAPS)):
+            at = pl.ds(start, ROW_TILE)
+            even = [even_ref[i, at] for i in range(HALO)]
+            odd = [odd_ref[i, at] for i in range(HALO)]
+            low = [jnp.where(odd_depth, e, o) for e, o in zip(even, odd)]
+            high = [jnp.where(odd_depth, o, e) for e, o in zip(even, odd)]
+            own = [own_ref[i, at] for i in range(depth_cells)]
+            for z, total in enumerate(window_sums(low + own + high, TAPS)):
                 deep[z, pl.ds(ROW_TILE + start, ROW_TILE)] = total
-            low, high = low[HALO:], high[HALO:]
 
         band = column_matrix(columns)
         band_ref[...] = band
@@ -447,27 +417,19 @@
 def cut_edges(density):
     depth_cells, row_cells, columns = density.shape
 
-    places = [(i, start) for start in range(0, row_cells, ROW_TILE) for i in range(HALO)]
-    words = len(places) // GROUP * WORDS
-
     def kernel(density_ref, row_even_ref, row_odd_ref, deep_even_ref, deep_odd_ref):
         row_bit = lax.axis_index("xy") % 2
         depth_bit = lax.axis_index("gz") % 2
         last_rows, last_deep = row_cells - ROW_TILE, depth_cells - HALO
         for ref, bit in ((deep_odd_ref, depth_bit), (deep_even_ref, 1 - depth_bit)):
-            for group in range(len(places) // GROUP):
-                values = [
-                    density_ref[bit * last_deep + i, pl.ds(start, ROW_TILE)]
-                    for i, start in places[group * GROUP : (group + 1) * GROUP]
-                ]
-                for k, word in enumerate(pack(values)):
-                    ref[group * WORDS + k] = word
+            for i in range(HALO):
+                ref[i] = density_ref[bit * last_deep + i]
         for ref, bit in ((row_even_ref, 1 - row_bit), (row_odd_ref, row_bit)):
             start = pl.multiple_of(bit * last_rows, ROW_TILE)
             ref[...] = density_ref[:, pl.ds(start, ROW_TILE)]
 
     rows = jax.ShapeDtypeStruct((depth_cells, ROW_TILE, columns), jnp.float32)
-    deep = jax.ShapeDtypeStruct((words, ROW_TILE, columns), jnp.int32)
+    deep = jax.ShapeDtypeStruct((HALO, row_cells, columns), jnp.float32)
     vmem = pl.BlockSpec(memory_space=pltpu.VMEM)
     return pl.pallas_call(
         kernel,

time: 27.1 us -> 27.8 us (1.026)
  blocking collectives: 11 us -> 12.2 us
  Pallas kernels: 5 us -> 4.4 us
    all_to_all x1, blocking collectives: 11 us -> 12.2 us  [body(): lax.all_to_all(outgoing, 'gz', split_axis=0, concat_axis=0, tiled=True)]
    pallas_call x1, Pallas kernels: 2.62 us -> 2.16 us  [render_inner(): pl.pallas_call(kernel, out_shape=(jax.ShapeDtypeStruct((n_depth, VIEWS, 4...]
  transfers between devices with their start and end apart: 6 -> 6, of which waited for: 1 -> 1; matrix products, arithmetic and copies ran while one was open for 0% -> 0% of each run, Pallas kernels for 10% -> 8%
where the time goes in v25:
time: 27.8 us; the launch traced here: 27.6 us
  blocking collectives  12.2 us (44%)
  starting transfers between devices  9.37 us (34%)
  Pallas kernels  4.4 us (16%)
  local copies, waits for them, and re-layouts  1.1 us (4%)
  waiting for transfers between devices  0.39 us (1%)
    all_to_all x1, blocking collectives, body(): lax.all_to_all(outgoing, 'gz', split_axis=0, concat_axis=0, tiled=True)  12.2 us
    ppermute x1, starting transfers between devices, body(): row_odd = lax.ppermute(row_odd, 'xy', pairs('xy', 1))  4.92 us
    ppermute x1, starting transfers between devices, body(): deep_even = lax.ppermute(deep_even, 'gz', pairs('gz', 0))  2.93 us
    pallas_call x1, Pallas kernels, render_inner(): pl.pallas_call(kernel, out_shape=(jax.ShapeDtypeStruct((n_depth, VIEWS, 4...  2.16 us
    pallas_call x1, Pallas kernels, body(): pl.pallas_call(composite_kernel, out_shape=jax.ShapeDtypeStruct((VIEWS, 4...  1.25 us
    unnamed x15, local copies, waits for them, and re-layouts  1.08 us
    pallas_call x1, Pallas kernels, render_edges(): pl.pallas_call(kernel, out_shape=jax.ShapeDtypeStruct(inner.shape, inner....  0.95 us
    ppermute x1, starting transfers between devices, body(): deep_odd = lax.ppermute(deep_odd, 'gz', pairs('gz', 1))  0.68 us
  transfers between devices with their start and end apart: 6, of which 1 were waited for; matrix products, arithmetic and copies ran while one was open for 0% of the time, Pallas kernels for 8%

profile of v25, /device:TPU:2, one launch (start us, length us, event | category | flops | bytes accessed | tf_op | source)
XLA Modules:
  0.0 27.6 jit_solution(9097827755298398702)
XLA Ops:
  0.0 1.0 %copy-done = f32[8,128,128]{2,1,0:T(8,128)S(1)} copy-done((f32[8,128,128]{2,1,0:T(8,128)S(1)}, f32[8,128,128]{2,1,0:T(8,128)}, u32[]{:S(2)}) %copy-start) | copy-done | bytes 524312
  1.0 0.1 cut_edges.1
  1.1 0.1 collective-permute-start
  1.2 4.9 %collective-permute-start.1 = (f32[8,8,128]{2,1,0:T(8,128)S(1)}, f32[8,8,128]{2,1,0:T(8,128)S(1)}, u32[]{:S(2)}, u32[]{:S(2)}) collective-permute-start(f32[8,8,128]{2,1,0:T(8,128)S(1)} %get-tuple-element.14), channel_id=1, source_target_pairs={{1,2},{3,4},{5,6},{2,1},{4,3},{6,5},{9,10},{11,12},{13,14},{10,9},... | collective-permute-start | bytes 98312 | tf_op jit(solution)/shard_map/ppermute | solution.py:480
  6.1 0.7 %collective-permute-start.4 = (f32[5,128,128]{2,1,0:T(8,128)S(1)}, f32[5,128,128]{2,1,0:T(8,128)S(1)}, u32[]{:S(2)}, u32[]{:S(2)}) collective-permute-start(f32[5,128,128]{2,1,0:T(8,128)S(1)} %get-tuple-element.15), channel_id=1, source_target_pairs={{8,16},{16,8},{9,17},{17,9},{10,18},{18,10},{11,19},{19,11},{12,20... | collective-permute-start | bytes 983048 | tf_op jit(solution)/shard_map/ppermute | solution.py:481
  6.8 2.9 %collective-permute-start.5 = (f32[5,128,128]{2,1,0:T(8,128)S(1)}, f32[5,128,128]{2,1,0:T(8,128)S(1)}, u32[]{:S(2)}, u32[]{:S(2)}) collective-permute-start(f32[5,128,128]{2,1,0:T(8,128)S(1)} %get-tuple-element.16), channel_id=1, source_target_pairs={{0,8},{16,24},{8,0},{24,16},{1,9},{17,25},{9,1},{25,17},{2,10},{18... | collective-permute-start | bytes 983048 | tf_op jit(solution)/shard_map/ppermute | solution.py:482
  9.7 0.0 collective-permute-done.row_even_ref
  9.7 0.0 collective-permute-done.1.row_odd_ref
  9.8 0.0 copy-start.6
  9.8 0.0 copy-start.2
  9.8 0.0 copy-start.3
  9.8 0.0 copy-start.4
  9.8 0.1 collective-permute-start.3
  9.9 0.7 %collective-permute-start.2 = (f32[5,16,128]{2,1,0:T(8,128)S(1)}, f32[5,16,128]{2,1,0:T(8,128)S(1)}, u32[]{:S(2)}, u32[]{:S(2)}) collective-permute-start(f32[5,16,128]{2,1,0:T(8,128)S(1)} %get-tuple-element.22), channel_id=1, source_target_pairs={{8,16},{16,8},{9,17},{17,9},{10,18},{18,10},{11,19},{19,11},{12,20... | collective-permute-start | bytes 122888 | tf_op jit(solution)/shard_map/ppermute | solution.py:485
  10.6 0.0 collective-permute-done.4.odd_ref
  10.6 0.4 %collective-permute-done.5.even_ref = f32[5,128,128]{2,1,0:T(8,128)S(1)} collective-permute-done((f32[5,128,128]{2,1,0:T(8,128)S(1)}, f32[5,128,128]{2,1,0:T(8,128)S(1)}, u32[]{:S(2)}, u32[]{:S(2)}) %collective-permute-start.5) | collective-permute-done | bytes 327712 | tf_op jit(solution)/shard_map/ppermute | solution.py:482
  11.0 0.0 copy-done.1
  11.0 2.2 %render_inner.1 = (s16[4,2,128,128]{3,2,1,0:T(8,128)(2,1)S(1)}, f32[10,144,128]{2,1,0:T(8,128)S(1)}, bf16[8,128,256]{2,1,0:T(8,128)(2,1)S(1)}, bf16[128,256]{1,0:T(8,128)(2,1)S(1)}) custom-call(s32[4,8]{1,0:T(4,128)S(1)} %copy-done.2, f32[2]{0:T(128)S(1)} %copy-done.6, f32[3]{0:T(128)S(1)} %copy-done.4, s32[2,4]{1,0:T(2,128)S(1)} %copy-done.3, ...), custom_call_target="tpu_custom_call" | custom-call | flops 13107200 | bytes 8388608 | tf_op jit(solution)/shard_map/render_inner/pallas_call | solution.py:248
  13.2 0.0 collective-permute-done.3.corner_even_ref
  13.2 0.0 collective-permute-done.2.corner_odd_ref
  13.2 0.9 %render_edges.1 = s16[4,2,128,128]{3,2,1,0:T(8,128)(2,1)S(1)} custom-call(s32[4,8]{1,0:T(4,128)S(1)} %copy-done.2, f32[3]{0:T(128)S(1)} %copy-done.4, s32[2,4]{1,0:T(2,128)S(1)} %copy-done.3, f32[5,16,128]{2,1,0:T(8,128)S(1)} %collective-permute-done.2.corner_odd_ref, f32[5,16,128]{2,1,0:T(8,128)S(1)} %collective-permute-done.3.corner_even_ref, ...), custom_call_target="tpu_custom_call" | custom-call | tf_op jit(solution)/shard_map/render_edges/pallas_call | solution.py:392
  14.1 0.0 copy-start.5
  14.2 12.2 %all_to_all.5.in_ref = s16[4,2,128,128]{3,2,1,0:T(8,128)(2,1)S(1)} all-to-all(s16[4,2,128,128]{3,2,1,0:T(8,128)(2,1)S(1)} %render_edges.1), channel_id=1, replica_groups=mesh['gz'=4,'xy'=8] {'gz'}, dimensions={0} | all-to-all | bytes 524288 | tf_op jit(solution)/shard_map/all_to_all | solution.py:498
  26.3 1.2 %composite.1 = f32[2,4,1,32,128]{4,3,2,1,0:T(8,128)} custom-call(s32[2,4]{1,0:T(2,128)S(1)} %copy-done.5, s16[4,2,128,128]{3,2,1,0:T(8,128)(2,1)S(1)} %all_to_all.5.in_ref), custom_call_target="tpu_custom_call" | custom-call | tf_op jit(solution)/shard_map/composite/pallas_call | solution.py:500
  (10 shorter events, 0.0 us)
Async XLA Ops:
  0.0 1.0 %copy-start = (f32[8,128,128]{2,1,0:T(8,128)S(1)}, f32[8,128,128]{2,1,0:T(8,128)}, u32[]{:S(2)}) copy-start(f32[8,128,128]{2,1,0:T(8,128)} %own_ref.1) | copy-start | bytes 1572868
  1.0 9.9 %copy-start.1 = (f32[8,128,128]{2,1,0:T(8,128)S(1)}, f32[8,128,128]{2,1,0:T(8,128)}, u32[]{:S(2)}) copy-start(f32[8,128,128]{2,1,0:T(8,128)} %own_ref.1) | copy-start | bytes 1572868
  1.1 8.6 %collective-permute-start = (f32[8,8,128]{2,1,0:T(8,128)S(1)}, f32[8,8,128]{2,1,0:T(8,128)S(1)}, u32[]{:S(2)}, u32[]{:S(2)}) collective-permute-start(f32[8,8,128]{2,1,0:T(8,128)S(1)} %get-tuple-element.13), channel_id=1, source_target_pairs={{0,1},{2,3},{4,5},{6,7},{1,0},{3,2},{5,4},{7,6},{8,9},{10,11},{12,... | collective-permute-start | bytes 98312 | tf_op jit(solution)/shard_map/ppermute | solution.py:479
  1.2 8.6 %collective-permute-start.1 = (f32[8,8,128]{2,1,0:T(8,128)S(1)}, f32[8,8,128]{2,1,0:T(8,128)S(1)}, u32[]{:S(2)}, u32[]{:S(2)}) collective-permute-start(f32[8,8,128]{2,1,0:T(8,128)S(1)} %get-tuple-element.14), channel_id=1, source_target_pairs={{1,2},{3,4},{5,6},{2,1},{4,3},{6,5},{9,10},{11,12},{13,14},{10,9},... | collective-permute-start | bytes 98312 | tf_op jit(solution)/shard_map/ppermute | solution.py:480
  6.1 4.5 %collective-permute-start.4 = (f32[5,128,128]{2,1,0:T(8,128)S(1)}, f32[5,128,128]{2,1,0:T(8,128)S(1)}, u32[]{:S(2)}, u32[]{:S(2)}) collective-permute-start(f32[5,128,128]{2,1,0:T(8,128)S(1)} %get-tuple-element.15), channel_id=1, source_target_pairs={{8,16},{16,8},{9,17},{17,9},{10,18},{18,10},{11,19},{19,11},{12,20... | collective-permute-start | bytes 983048 | tf_op jit(solution)/shard_map/ppermute | solution.py:481
  6.8 4.2 %collective-permute-start.5 = (f32[5,128,128]{2,1,0:T(8,128)S(1)}, f32[5,128,128]{2,1,0:T(8,128)S(1)}, u32[]{:S(2)}, u32[]{:S(2)}) collective-permute-start(f32[5,128,128]{2,1,0:T(8,128)S(1)} %get-tuple-element.16), channel_id=1, source_target_pairs={{0,8},{16,24},{8,0},{24,16},{1,9},{17,25},{9,1},{25,17},{2,10},{18... | collective-permute-start | bytes 983048 | tf_op jit(solution)/shard_map/ppermute | solution.py:482
  9.8 1.2 %copy-start.6 = (f32[2]{0:T(128)S(1)}, f32[2]{0:T(128)}, u32[]{:S(2)}) copy-start(f32[2]{0:T(128)} %slopes_in.1) | copy-start | bytes 28
  9.8 1.2 %copy-start.2 = (s32[4,8]{1,0:T(4,128)S(1)}, s32[4,8]{1,0:T(4,128)}, u32[]{:S(2)}) copy-start(s32[4,8]{1,0:T(4,128)} %live_in.3) | copy-start | bytes 388
  9.8 1.2 %copy-start.3 = (s32[2,4]{1,0:T(2,128)S(1)}, s32[2,4]{1,0:T(2,128)}, u32[]{:S(2)}) copy-start(s32[2,4]{1,0:T(2,128)} %owner_in.3) | copy-start | bytes 100
  9.8 1.2 %copy-start.4 = (f32[3]{0:T(128)S(1)}, f32[3]{0:T(128)}, u32[]{:S(2)}) copy-start(f32[3]{0:T(128)} %palette_in.3) | copy-start | bytes 40
  9.8 3.3 %collective-permute-start.3 = (f32[5,16,128]{2,1,0:T(8,128)S(1)}, f32[5,16,128]{2,1,0:T(8,128)S(1)}, u32[]{:S(2)}, u32[]{:S(2)}) collective-permute-start(f32[5,16,128]{2,1,0:T(8,128)S(1)} %get-tuple-element.21), channel_id=1, source_target_pairs={{0,8},{16,24},{8,0},{24,16},{1,9},{17,25},{9,1},{25,17},{2,10},{18... | collective-permute-start | bytes 122888 | tf_op jit(solution)/shard_map/ppermute | solution.py:488
  9.9 3.2 %collective-permute-start.2 = (f32[5,16,128]{2,1,0:T(8,128)S(1)}, f32[5,16,128]{2,1,0:T(8,128)S(1)}, u32[]{:S(2)}, u32[]{:S(2)}) collective-permute-start(f32[5,16,128]{2,1,0:T(8,128)S(1)} %get-tuple-element.22), channel_id=1, source_target_pairs={{8,16},{16,8},{9,17},{17,9},{10,18},{18,10},{11,19},{19,11},{12,20... | collective-permute-start | bytes 122888 | tf_op jit(solution)/shard_map/ppermute | solution.py:485
  14.1 12.2 %copy-start.5 = (s32[2,4]{1,0:T(2,128)S(1)}, s32[2,4]{1,0:T(2,128)}, u32[]{:S(2)}) copy-start(s32[2,4]{1,0:T(2,128)} %order_in.1) | copy-start | bytes 100

commit v26 on v25

--- a/solution.py
+++ b/solution.py
@@ -18,6 +18,8 @@
 TOP = 2.2
 STEPS = 65535.0
 MIDDLE = 32768
+LEVELS_PER_UNIT = float(1 << 17)
+WORDS, SPARE = HALO - 1, 7
 VMEM_BYTES = 40 * 1024 * 1024
 
 
@@ -50,6 +52,21 @@
         sums = [sums[i] + sums[i + width] for i in range(len(sums) - width)]
         width *= 2
     return [sums[i] + layers[i + width] for i in range(len(layers) - width)]
+
+
+def pack(values):
+    levels = [jnp.floor(x * LEVELS_PER_UNIT + 0.5).astype(jnp.int32) for x in values]
+    return [
+        (levels[i] << SPARE) | ((levels[WORDS] >> (SPARE * i)) & 0x7F) for i in range(WORDS)
+    ]
+
+
+def unpack(words):
+    last = words[0] & 0x7F
+    for i in range(1, WORDS):
+        last = last | ((words[i] & 0x7F) << (SPARE * i))
+    levels = [word >> SPARE for word in words] + [(last << 4) >> 4]
+    return [x.astype(jnp.float32) * (1.0 / LEVELS_PER_UNIT) for x in levels]
 
 
 def encode(value):
@@ -178,10 +195,10 @@
 
         for start in range(0, row_cells, ROW_TILE):
             at = pl.ds(start, ROW_TILE)
-            even = [even_ref[i, at] for i in range(HALO)]
-            odd = [odd_ref[i, at] for i in range(HALO)]
-            low = [jnp.where(odd_depth, e, o) for e, o in zip(even, odd)]
-            high = [jnp.where(odd_depth, o, e) for e, o in zip(even, odd)]
+            even = [even_ref[i, at] for i in range(WORDS)]
+            odd = [odd_ref[i, at] for i in range(WORDS)]
+            low = unpack([jnp.where(odd_depth, e, o) for e, o in zip(even, odd)])
+            high = unpack([jnp.where(odd_depth, o, e) for e, o in zip(even, odd)])
             own = [own_ref[i, at] for i in range(depth_cells)]
             for z, total in enumerate(window_sums(low + own + high, TAPS)):
                 deep[z, pl.ds(ROW_TILE + start, ROW_TILE)] = total
@@ -422,14 +439,17 @@
         depth_bit = lax.axis_index("gz") % 2
         last_rows, last_deep = row_cells - ROW_TILE, depth_cells - HALO
         for ref, bit in ((deep_odd_ref, depth_bit), (deep_even_ref, 1 - depth_bit)):
-            for i in range(HALO):
-                ref[i] = density_ref[bit * last_deep + i]
+            for start in range(0, row_cells, ROW_TILE):
+                at = pl.ds(start, ROW_TILE)
+                layers = [density_ref[bit * last_deep + i, at] for i in range(HALO)]
+                for i, word in enumerate(pack(layers)):
+                    ref[i, at] = word
         for ref, bit in ((row_even_ref, 1 - row_bit), (row_odd_ref, row_bit)):
             start = pl.multiple_of(bit * last_rows, ROW_TILE)
             ref[...] = density_ref[:, pl.ds(start, ROW_TILE)]
 
     rows = jax.ShapeDtypeStruct((depth_cells, ROW_TILE, columns), jnp.float32)
-    deep = jax.ShapeDtypeStruct((HALO, row_cells, columns), jnp.float32)
+    deep = jax.ShapeDtypeStruct((WORDS, row_cells, columns), jnp.int32)
     vmem = pl.BlockSpec(memory_space=pltpu.VMEM)
     return pl.pallas_call(
         kernel,

time: 27.8 us -> 27.4 us (0.986)
  blocking collectives: 12.2 us -> 11.6 us
    all_to_all x1, blocking collectives: 12.2 us -> 11.6 us  [body(): lax.all_to_all(outgoing, 'gz', split_axis=0, concat_axis=0, tiled=True)]
where the time goes in v26:
time: 27.4 us; the launch traced here: 27.1 us
  blocking collectives  11.6 us (42%)
  starting transfers between devices  9.37 us (34%)
  Pallas kernels  4.67 us (17%)
  local copies, waits for them, and re-layouts  1.1 us (4%)
  waiting for transfers between devices  0.29 us (1%)
    all_to_all x1, blocking collectives, body(): lax.all_to_all(outgoing, 'gz', split_axis=0, concat_axis=0, tiled=True)  11.6 us
    ppermute x1, starting transfers between devices, body(): row_odd = lax.ppermute(row_odd, 'xy', pairs('xy', 1))  4.92 us
    ppermute x1, starting transfers between devices, body(): deep_even = lax.ppermute(deep_even, 'gz', pairs('gz', 0))  2.93 us
    pallas_call x1, Pallas kernels, render_inner(): pl.pallas_call(kernel, out_shape=(jax.ShapeDtypeStruct((n_depth, VIEWS, 4...  2.3 us
    pallas_call x1, Pallas kernels, body(): pl.pallas_call(composite_kernel, out_shape=jax.ShapeDtypeStruct((VIEWS, 4...  1.25 us
    unnamed x15, local copies, waits for them, and re-layouts  1.08 us
    pallas_call x1, Pallas kernels, render_edges(): pl.pallas_call(kernel, out_shape=jax.ShapeDtypeStruct(inner.shape, inner....  0.95 us
    ppermute x1, starting transfers between devices, body(): deep_odd = lax.ppermute(deep_odd, 'gz', pairs('gz', 1))  0.68 us
  transfers between devices with their start and end apart: 6, of which 1 were waited for; matrix products, arithmetic and copies ran while one was open for 0% of the time, Pallas kernels for 8%

profile of v26, /device:TPU:2, one launch (start us, length us, event | category | flops | bytes accessed | tf_op | source)
XLA Modules:
  0.0 27.1 jit_solution(1621544042030690421)
XLA Ops:
  0.0 1.0 %copy-done = f32[8,128,128]{2,1,0:T(8,128)S(1)} copy-done((f32[8,128,128]{2,1,0:T(8,128)S(1)}, f32[8,128,128]{2,1,0:T(8,128)}, u32[]{:S(2)}) %copy-start) | copy-done | bytes 524312
  1.0 0.2 cut_edges.1
  1.2 0.1 collective-permute-start
  1.3 4.9 %collective-permute-start.1 = (f32[8,8,128]{2,1,0:T(8,128)S(1)}, f32[8,8,128]{2,1,0:T(8,128)S(1)}, u32[]{:S(2)}, u32[]{:S(2)}) collective-permute-start(f32[8,8,128]{2,1,0:T(8,128)S(1)} %get-tuple-element.14), channel_id=1, source_target_pairs={{1,2},{3,4},{5,6},{2,1},{4,3},{6,5},{9,10},{11,12},{13,14},{10,9},... | collective-permute-start | bytes 98312 | tf_op jit(solution)/shard_map/ppermute | solution.py:500
  6.2 0.7 %collective-permute-start.4 = (s32[4,128,128]{2,1,0:T(8,128)S(1)}, s32[4,128,128]{2,1,0:T(8,128)S(1)}, u32[]{:S(2)}, u32[]{:S(2)}) collective-permute-start(s32[4,128,128]{2,1,0:T(8,128)S(1)} %get-tuple-element.15), channel_id=1, source_target_pairs={{8,16},{16,8},{9,17},{17,9},{10,18},{18,10},{11,19},{19,11},{12,20... | collective-permute-start | bytes 786440 | tf_op jit(solution)/shard_map/ppermute | solution.py:501
  6.9 2.9 %collective-permute-start.5 = (s32[4,128,128]{2,1,0:T(8,128)S(1)}, s32[4,128,128]{2,1,0:T(8,128)S(1)}, u32[]{:S(2)}, u32[]{:S(2)}) collective-permute-start(s32[4,128,128]{2,1,0:T(8,128)S(1)} %get-tuple-element.16), channel_id=1, source_target_pairs={{0,8},{16,24},{8,0},{24,16},{1,9},{17,25},{9,1},{25,17},{2,10},{18... | collective-permute-start | bytes 786440 | tf_op jit(solution)/shard_map/ppermute | solution.py:502
  9.8 0.0 collective-permute-done.row_even_ref
  9.9 0.0 collective-permute-done.1.row_odd_ref
  9.9 0.0 copy-start.6
  9.9 0.0 copy-start.2
  9.9 0.0 copy-start.3
  9.9 0.0 copy-start.4
  9.9 0.1 collective-permute-start.3
  10.1 0.7 %collective-permute-start.2 = (f32[5,16,128]{2,1,0:T(8,128)S(1)}, f32[5,16,128]{2,1,0:T(8,128)S(1)}, u32[]{:S(2)}, u32[]{:S(2)}) collective-permute-start(f32[5,16,128]{2,1,0:T(8,128)S(1)} %get-tuple-element.22), channel_id=1, source_target_pairs={{8,16},{16,8},{9,17},{17,9},{10,18},{18,10},{11,19},{19,11},{12,20... | collective-permute-start | bytes 122888 | tf_op jit(solution)/shard_map/ppermute | solution.py:505
  10.7 0.0 collective-permute-done.4.odd_ref
  10.7 0.3 %collective-permute-done.5.even_ref = s32[4,128,128]{2,1,0:T(8,128)S(1)} collective-permute-done((s32[4,128,128]{2,1,0:T(8,128)S(1)}, s32[4,128,128]{2,1,0:T(8,128)S(1)}, u32[]{:S(2)}, u32[]{:S(2)}) %collective-permute-start.5) | collective-permute-done | bytes 262176 | tf_op jit(solution)/shard_map/ppermute | solution.py:502
  11.0 0.0 copy-done.2
  11.0 2.3 %render_inner.1 = (s16[4,2,128,128]{3,2,1,0:T(8,128)(2,1)S(1)}, f32[10,144,128]{2,1,0:T(8,128)S(1)}, bf16[8,128,256]{2,1,0:T(8,128)(2,1)S(1)}, bf16[128,256]{1,0:T(8,128)(2,1)S(1)}) custom-call(s32[4,8]{1,0:T(4,128)S(1)} %copy-done.2, f32[2]{0:T(128)S(1)} %copy-done.6, f32[3]{0:T(128)S(1)} %copy-done.4, s32[2,4]{1,0:T(2,128)S(1)} %copy-done.3, ...), custom_call_target="tpu_custom_call" | custom-call | flops 13107200 | bytes 8388608 | tf_op jit(solution)/shard_map/render_inner/pallas_call | solution.py:265
  13.3 0.0 collective-permute-done.3.corner_even_ref
  13.4 0.0 collective-permute-done.2.corner_odd_ref
  13.4 0.9 %render_edges.1 = s16[4,2,128,128]{3,2,1,0:T(8,128)(2,1)S(1)} custom-call(s32[4,8]{1,0:T(4,128)S(1)} %copy-done.2, f32[3]{0:T(128)S(1)} %copy-done.4, s32[2,4]{1,0:T(2,128)S(1)} %copy-done.3, f32[5,16,128]{2,1,0:T(8,128)S(1)} %collective-permute-done.2.corner_odd_ref, f32[5,16,128]{2,1,0:T(8,128)S(1)} %collective-permute-done.3.corner_even_ref, ...), custom_call_target="tpu_custom_call" | custom-call | tf_op jit(solution)/shard_map/render_edges/pallas_call | solution.py:409
  14.3 0.0 copy-start.5
  14.3 11.6 %all_to_all.5.in_ref = s16[4,2,128,128]{3,2,1,0:T(8,128)(2,1)S(1)} all-to-all(s16[4,2,128,128]{3,2,1,0:T(8,128)(2,1)S(1)} %render_edges.1), channel_id=1, replica_groups=mesh['gz'=4,'xy'=8] {'gz'}, dimensions={0} | all-to-all | bytes 524288 | tf_op jit(solution)/shard_map/all_to_all | solution.py:518
  25.9 1.2 %composite.1 = f32[2,4,1,32,128]{4,3,2,1,0:T(8,128)} custom-call(s32[2,4]{1,0:T(2,128)S(1)} %copy-done.5, s16[4,2,128,128]{3,2,1,0:T(8,128)(2,1)S(1)} %all_to_all.5.in_ref), custom_call_target="tpu_custom_call" | custom-call | tf_op jit(solution)/shard_map/composite/pallas_call | solution.py:520
  (10 shorter events, 0.0 us)
Async XLA Ops:
  0.0 1.0 %copy-start = (f32[8,128,128]{2,1,0:T(8,128)S(1)}, f32[8,128,128]{2,1,0:T(8,128)}, u32[]{:S(2)}) copy-start(f32[8,128,128]{2,1,0:T(8,128)} %own_ref.1) | copy-start | bytes 1572868
  1.0 10.0 %copy-start.1 = (f32[8,128,128]{2,1,0:T(8,128)S(1)}, f32[8,128,128]{2,1,0:T(8,128)}, u32[]{:S(2)}) copy-start(f32[8,128,128]{2,1,0:T(8,128)} %own_ref.1) | copy-start | bytes 1572868
  1.2 8.6 %collective-permute-start = (f32[8,8,128]{2,1,0:T(8,128)S(1)}, f32[8,8,128]{2,1,0:T(8,128)S(1)}, u32[]{:S(2)}, u32[]{:S(2)}) collective-permute-start(f32[8,8,128]{2,1,0:T(8,128)S(1)} %get-tuple-element.13), channel_id=1, source_target_pairs={{0,1},{2,3},{4,5},{6,7},{1,0},{3,2},{5,4},{7,6},{8,9},{10,11},{12,... | collective-permute-start | bytes 98312 | tf_op jit(solution)/shard_map/ppermute | solution.py:499
  1.3 8.6 %collective-permute-start.1 = (f32[8,8,128]{2,1,0:T(8,128)S(1)}, f32[8,8,128]{2,1,0:T(8,128)S(1)}, u32[]{:S(2)}, u32[]{:S(2)}) collective-permute-start(f32[8,8,128]{2,1,0:T(8,128)S(1)} %get-tuple-element.14), channel_id=1, source_target_pairs={{1,2},{3,4},{5,6},{2,1},{4,3},{6,5},{9,10},{11,12},{13,14},{10,9},... | collective-permute-start | bytes 98312 | tf_op jit(solution)/shard_map/ppermute | solution.py:500
  6.2 4.5 %collective-permute-start.4 = (s32[4,128,128]{2,1,0:T(8,128)S(1)}, s32[4,128,128]{2,1,0:T(8,128)S(1)}, u32[]{:S(2)}, u32[]{:S(2)}) collective-permute-start(s32[4,128,128]{2,1,0:T(8,128)S(1)} %get-tuple-element.15), channel_id=1, source_target_pairs={{8,16},{16,8},{9,17},{17,9},{10,18},{18,10},{11,19},{19,11},{12,20... | collective-permute-start | bytes 786440 | tf_op jit(solution)/shard_map/ppermute | solution.py:501
  6.9 4.1 %collective-permute-start.5 = (s32[4,128,128]{2,1,0:T(8,128)S(1)}, s32[4,128,128]{2,1,0:T(8,128)S(1)}, u32[]{:S(2)}, u32[]{:S(2)}) collective-permute-start(s32[4,128,128]{2,1,0:T(8,128)S(1)} %get-tuple-element.16), channel_id=1, source_target_pairs={{0,8},{16,24},{8,0},{24,16},{1,9},{17,25},{9,1},{25,17},{2,10},{18... | collective-permute-start | bytes 786440 | tf_op jit(solution)/shard_map/ppermute | solution.py:502
  9.9 1.1 %copy-start.6 = (f32[2]{0:T(128)S(1)}, f32[2]{0:T(128)}, u32[]{:S(2)}) copy-start(f32[2]{0:T(128)} %slopes_in.1) | copy-start | bytes 28
  9.9 1.1 %copy-start.2 = (s32[4,8]{1,0:T(4,128)S(1)}, s32[4,8]{1,0:T(4,128)}, u32[]{:S(2)}) copy-start(s32[4,8]{1,0:T(4,128)} %live_in.3) | copy-start | bytes 388
  9.9 1.1 %copy-start.3 = (s32[2,4]{1,0:T(2,128)S(1)}, s32[2,4]{1,0:T(2,128)}, u32[]{:S(2)}) copy-start(s32[2,4]{1,0:T(2,128)} %owner_in.3) | copy-start | bytes 100
  9.9 1.1 %copy-start.4 = (f32[3]{0:T(128)S(1)}, f32[3]{0:T(128)}, u32[]{:S(2)}) copy-start(f32[3]{0:T(128)} %palette_in.3) | copy-start | bytes 40
  9.9 3.4 %collective-permute-start.3 = (f32[5,16,128]{2,1,0:T(8,128)S(1)}, f32[5,16,128]{2,1,0:T(8,128)S(1)}, u32[]{:S(2)}, u32[]{:S(2)}) collective-permute-start(f32[5,16,128]{2,1,0:T(8,128)S(1)} %get-tuple-element.21), channel_id=1, source_target_pairs={{0,8},{16,24},{8,0},{24,16},{1,9},{17,25},{9,1},{25,17},{2,10},{18... | collective-permute-start | bytes 122888 | tf_op jit(solution)/shard_map/ppermute | solution.py:508
  10.1 3.3 %collective-permute-start.2 = (f32[5,16,128]{2,1,0:T(8,128)S(1)}, f32[5,16,128]{2,1,0:T(8,128)S(1)}, u32[]{:S(2)}, u32[]{:S(2)}) collective-permute-start(f32[5,16,128]{2,1,0:T(8,128)S(1)} %get-tuple-element.22), channel_id=1, source_target_pairs={{8,16},{16,8},{9,17},{17,9},{10,18},{18,10},{11,19},{19,11},{12,20... | collective-permute-start | bytes 122888 | tf_op jit(solution)/shard_map/ppermute | solution.py:505
  14.3 11.6 %copy-start.5 = (s32[2,4]{1,0:T(2,128)S(1)}, s32[2,4]{1,0:T(2,128)}, u32[]{:S(2)}) copy-start(s32[2,4]{1,0:T(2,128)} %order_in.1) | copy-start | bytes 100

commit v27 on v26

--- a/solution.py
+++ b/solution.py
@@ -165,10 +165,40 @@
         smooth[layers - 1] = jnp.zeros_like(smooth[layers - 1])
 
 
-def render_inner(live_slices, slopes, palette, owner, density, deep_odd, deep_even, n_depth):
+def make_tables(slopes, depth_cells, columns, n_depth):
+    def kernel(slopes_in, shear_ref, band_ref, slopes_ref, sems):
+        wait_scalars = fetch_scalars([(slopes_in, slopes_ref)], sems)
+        band_ref[...] = column_matrix(columns)
+        slab_start = (lax.axis_index("gz") * depth_cells).astype(jnp.float32)
+        wait_scalars()
+        for z in range(depth_cells):
+            shear_ref[z] = shear_matrices(
+                slopes_ref, slab_start + float(z), columns, depth_cells * n_depth
+            )
+
+    vmem = pl.BlockSpec(memory_space=pltpu.VMEM)
+    return pl.pallas_call(
+        kernel,
+        out_shape=(
+            jax.ShapeDtypeStruct((depth_cells, columns, VIEWS * columns), jnp.bfloat16),
+            jax.ShapeDtypeStruct((columns, 2 * columns), jnp.bfloat16),
+        ),
+        in_specs=[vmem],
+        out_specs=(vmem,) * 2,
+        scratch_shapes=[
+            pltpu.SMEM(slopes.shape, jnp.float32),
+            pltpu.SemaphoreType.DMA((1,)),
+        ],
+        compiler_params=pltpu.CompilerParams(vmem_limit_bytes=VMEM_BYTES),
+        name="tables",
+    )(slopes)
+
+
+def render_inner(
+    live_slices, palette, owner, density, deep_odd, deep_even, shear, band_weights, n_depth
+):
     depth_cells, row_cells, columns = density.shape
-    total_depth = depth_cells * n_depth
-    extinct = 3.0 / total_depth
+    extinct = 3.0 / (depth_cells * n_depth)
     tile_rows = row_cells // n_depth
     layers = depth_cells + 2
     rows = range(EDGE, row_cells - EDGE)
@@ -176,18 +206,12 @@
     lead, span = EDGE, height + 2 * ROW_TILE
 
     def kernel(
-        live_in, slopes_in, palette_in, owner_in, own_ref, odd_ref, even_ref,
-        out_ref, deep, shear_ref, band_ref, triple, smooth, across, sheared,
-        live_ref, slopes_ref, palette_ref, owner_ref, sems,
+        live_in, palette_in, owner_in, own_ref, odd_ref, even_ref, shear_ref, band_ref,
+        out_ref, deep, triple, smooth, across, sheared,
+        live_ref, palette_ref, owner_ref, sems,
     ):
         wait_scalars = fetch_scalars(
-            [
-                (live_in, live_ref),
-                (slopes_in, slopes_ref),
-                (palette_in, palette_ref),
-                (owner_in, owner_ref),
-            ],
-            sems,
+            [(live_in, live_ref), (palette_in, palette_ref), (owner_in, owner_ref)], sems
         )
         depth_index = lax.axis_index("gz")
         row_index = lax.axis_index("xy")
@@ -203,9 +227,7 @@
             for z, total in enumerate(window_sums(low + own + high, TAPS)):
                 deep[z, pl.ds(ROW_TILE + start, ROW_TILE)] = total
 
-        band = column_matrix(columns)
-        band_ref[...] = band
-        weights = jnp.concatenate([band, band, band], axis=0)
+        weights = jnp.concatenate([band_ref[...]] * 3, axis=0)
         for z in range(layers):
             triple[z] = (
                 deep[z, pl.ds(lead - 4, span + ROW_TILE)]
@@ -224,10 +246,6 @@
         zero_outside(smooth, depth_index, n_depth, layers)
 
         wait_scalars()
-        slab_start = (depth_index * depth_cells).astype(jnp.float32)
-        for z in range(depth_cells):
-            shear_ref[z] = shear_matrices(slopes_ref, slab_start + float(z), columns, total_depth)
-
         own_live = live_ref[depth_index, row_index]
         middle = pl.ds(ROW_TILE, height)
         for z in range(depth_cells):
@@ -267,21 +285,18 @@
         out_shape=(
             jax.ShapeDtypeStruct((n_depth, VIEWS, 4 * tile_rows, columns), jnp.int16),
             jax.ShapeDtypeStruct((layers, row_cells + 2 * ROW_TILE, columns), jnp.float32),
-            jax.ShapeDtypeStruct((depth_cells, columns, VIEWS * columns), jnp.bfloat16),
-            jax.ShapeDtypeStruct((columns, 2 * columns), jnp.bfloat16),
         ),
-        in_specs=[vmem] * 7,
-        out_specs=(vmem,) * 4,
+        in_specs=[vmem] * 8,
+        out_specs=(vmem,) * 2,
         scratch_shapes=[
             pltpu.VMEM((layers, span + ROW_TILE, columns), jnp.float32),
             pltpu.VMEM((layers, span, columns), jnp.float32),
             pltpu.VMEM((depth_cells, height, columns), jnp.float32),
             pltpu.VMEM((depth_cells, 4 * height, VIEWS * columns), jnp.float32),
             pltpu.SMEM(live_slices.shape, jnp.int32),
-            pltpu.SMEM(slopes.shape, jnp.float32),
             pltpu.SMEM(palette.shape, jnp.float32),
             pltpu.SMEM(owner.shape, jnp.int32),
-            pltpu.SemaphoreType.DMA((4,)),
+            pltpu.SemaphoreType.DMA((3,)),
         ],
         compiler_params=pltpu.CompilerParams(vmem_limit_bytes=VMEM_BYTES),
         cost_estimate=pl.CostEstimate(
@@ -290,7 +305,7 @@
             transcendentals=4 * depth_cells * row_cells * columns,
         ),
         name="render_inner",
-    )(live_slices, slopes, palette, owner, density, deep_odd, deep_even)
+    )(live_slices, palette, owner, density, deep_odd, deep_even, shear, band_weights)
 
 
 def render_edges(
@@ -508,8 +523,9 @@
     corner_even = lax.ppermute(
         lax.dynamic_slice_in_dim(rows, edge - facing, HALO), "gz", pairs("gz", 0)
     )
-    inner, deep, shear, band_weights = render_inner(
-        live_slices, shear_slopes, palette, tile_owner, density, deep_odd, deep_even, n_depth
+    shear, band_weights = make_tables(shear_slopes, depth_cells, columns, n_depth)
+    inner, deep = render_inner(
+        live_slices, palette, tile_owner, density, deep_odd, deep_even, shear, band_weights, n_depth
     )
     outgoing = render_edges(
         live_slices, palette, tile_owner, corner_odd, corner_even, row_even, row_odd,

time: 27.4 us -> 28.2 us (1.029)
  Pallas kernels: 4.67 us -> 5.53 us
  local copies, waits for them, and re-layouts: 1.1 us -> 1.75 us
  blocking collectives: 11.6 us -> 11.1 us
    pallas_call x0 -> x1, Pallas kernels: none -> 0.71 us  [make_tables(): pl.pallas_call(kernel, out_shape=(jax.ShapeDtypeStruct((depth_cells, colu...]
    unnamed x15, local copies, waits for them, and re-layouts: 1.08 us -> 1.72 us
    all_to_all x1, blocking collectives: 11.6 us -> 11.1 us  [body(): lax.all_to_all(outgoing, 'gz', split_axis=0, concat_axis=0, tiled=True)]
  transfers between devices with their start and end apart: 6 -> 6, of which waited for: 1 -> 0; matrix products, arithmetic and copies ran while one was open for 0% -> 0% of each run, Pallas kernels for 8% -> 11%
where the time goes in v27:
time: 28.2 us; the launch traced here: 27.9 us
  blocking collectives  11.1 us (39%)
  starting transfers between devices  9.37 us (33%)
  Pallas kernels  5.53 us (20%)
  local copies, waits for them, and re-layouts  1.75 us (6%)
    all_to_all x1, blocking collectives, body(): lax.all_to_all(outgoing, 'gz', split_axis=0, concat_axis=0, tiled=True)  11.1 us
    ppermute x1, starting transfers between devices, body(): row_odd = lax.ppermute(row_odd, 'xy', pairs('xy', 1))  4.92 us
    ppermute x1, starting transfers between devices, body(): deep_even = lax.ppermute(deep_even, 'gz', pairs('gz', 0))  2.93 us
    pallas_call x1, Pallas kernels, render_inner(): pl.pallas_call(kernel, out_shape=(jax.ShapeDtypeStruct((n_depth, VIEWS, 4...  2.45 us
    unnamed x15, local copies, waits for them, and re-layouts  1.72 us
    pallas_call x1, Pallas kernels, body(): pl.pallas_call(composite_kernel, out_shape=jax.ShapeDtypeStruct((VIEWS, 4...  1.25 us
    pallas_call x1, Pallas kernels, render_edges(): pl.pallas_call(kernel, out_shape=jax.ShapeDtypeStruct(inner.shape, inner....  0.95 us
    pallas_call x1, Pallas kernels, make_tables(): pl.pallas_call(kernel, out_shape=(jax.ShapeDtypeStruct((depth_cells, colu...  0.71 us
  transfers between devices with their start and end apart: 6, of which 0 were waited for; matrix products, arithmetic and copies ran while one was open for 0% of the time, Pallas kernels for 11%

profile of v27, /device:TPU:2, one launch (start us, length us, event | category | flops | bytes accessed | tf_op | source)
XLA Modules:
  0.0 27.9 jit_solution(107561526762102560)
XLA Ops:
  0.0 1.0 %copy-done = f32[8,128,128]{2,1,0:T(8,128)S(1)} copy-done((f32[8,128,128]{2,1,0:T(8,128)S(1)}, f32[8,128,128]{2,1,0:T(8,128)}, u32[]{:S(2)}) %copy-start) | copy-done | bytes 524312
  1.0 0.2 cut_edges.1
  1.2 0.1 collective-permute-start
  1.3 4.9 %collective-permute-start.1 = (f32[8,8,128]{2,1,0:T(8,128)S(1)}, f32[8,8,128]{2,1,0:T(8,128)S(1)}, u32[]{:S(2)}, u32[]{:S(2)}) collective-permute-start(f32[8,8,128]{2,1,0:T(8,128)S(1)} %get-tuple-element.14), channel_id=1, source_target_pairs={{1,2},{3,4},{5,6},{2,1},{4,3},{6,5},{9,10},{11,12},{13,14},{10,9},... | collective-permute-start | bytes 98312 | tf_op jit(solution)/shard_map/ppermute | solution.py:515
  6.2 0.7 %collective-permute-start.4 = (s32[4,128,128]{2,1,0:T(8,128)S(1)}, s32[4,128,128]{2,1,0:T(8,128)S(1)}, u32[]{:S(2)}, u32[]{:S(2)}) collective-permute-start(s32[4,128,128]{2,1,0:T(8,128)S(1)} %get-tuple-element.15), channel_id=1, source_target_pairs={{8,16},{16,8},{9,17},{17,9},{10,18},{18,10},{11,19},{19,11},{12,20... | collective-permute-start | bytes 786440 | tf_op jit(solution)/shard_map/ppermute | solution.py:516
  6.9 2.9 %collective-permute-start.5 = (s32[4,128,128]{2,1,0:T(8,128)S(1)}, s32[4,128,128]{2,1,0:T(8,128)S(1)}, u32[]{:S(2)}, u32[]{:S(2)}) collective-permute-start(s32[4,128,128]{2,1,0:T(8,128)S(1)} %get-tuple-element.16), channel_id=1, source_target_pairs={{0,8},{16,24},{8,0},{24,16},{1,9},{17,25},{9,1},{25,17},{2,10},{18... | collective-permute-start | bytes 786440 | tf_op jit(solution)/shard_map/ppermute | solution.py:517
  9.8 0.0 collective-permute-done.row_even_ref
  9.9 0.0 copy-start.6
  9.9 0.1 collective-permute-start.3
  10.0 0.7 %collective-permute-start.2 = (f32[5,16,128]{2,1,0:T(8,128)S(1)}, f32[5,16,128]{2,1,0:T(8,128)S(1)}, u32[]{:S(2)}, u32[]{:S(2)}) collective-permute-start(f32[5,16,128]{2,1,0:T(8,128)S(1)} %get-tuple-element.22), channel_id=1, source_target_pairs={{8,16},{16,8},{9,17},{17,9},{10,18},{18,10},{11,19},{19,11},{12,20... | collective-permute-start | bytes 122888 | tf_op jit(solution)/shard_map/ppermute | solution.py:520
  10.7 0.7 %tables.1 = (bf16[8,128,256]{2,1,0:T(8,128)(2,1)S(1)}, bf16[128,256]{1,0:T(8,128)(2,1)S(1)}) custom-call(f32[2]{0:T(128)S(1)} %copy-done.6), custom_call_target="tpu_custom_call" | custom-call | tf_op jit(solution)/shard_map/tables/pallas_call | solution.py:180
  11.4 0.0 copy-start.2
  11.4 0.0 collective-permute-done.4.odd_ref
  11.4 0.0 collective-permute-done.5.even_ref
  11.4 0.0 copy-start.3
  11.5 0.0 copy-start.4
  11.5 0.6 %copy-done.2 = s32[4,8]{1,0:T(4,128)S(1)} copy-done((s32[4,8]{1,0:T(4,128)S(1)}, s32[4,8]{1,0:T(4,128)}, u32[]{:S(2)}) %copy-start.2) | copy-done | bytes 152
  12.1 0.0 copy-done.3
  12.1 2.5 %render_inner.1 = (s16[4,2,128,128]{3,2,1,0:T(8,128)(2,1)S(1)}, f32[10,144,128]{2,1,0:T(8,128)S(1)}) custom-call(s32[4,8]{1,0:T(4,128)S(1)} %copy-done.2, f32[3]{0:T(128)S(1)} %copy-done.4, s32[2,4]{1,0:T(2,128)S(1)} %copy-done.3, f32[8,128,128]{2,1,0:T(8,128)S(1)} %copy-done.1, s32[4,128,128]{2,1,0:T(8,128)S(1)} %collective-permute-done.4.odd_ref, ...), custom_call_target="tpu_custom_call" | custom-call | flops 13107200 | bytes 8388608 | tf_op jit(solution)/shard_map/render_inner/pallas_call | solution.py:283
  14.6 0.0 collective-permute-done.2.corner_odd_ref
  14.6 0.9 %render_edges.1 = s16[4,2,128,128]{3,2,1,0:T(8,128)(2,1)S(1)} custom-call(s32[4,8]{1,0:T(4,128)S(1)} %copy-done.2, f32[3]{0:T(128)S(1)} %copy-done.4, s32[2,4]{1,0:T(2,128)S(1)} %copy-done.3, f32[5,16,128]{2,1,0:T(8,128)S(1)} %collective-permute-done.2.corner_odd_ref, f32[5,16,128]{2,1,0:T(8,128)S(1)} %collective-permute-done.3.corner_even_ref, ...), custom_call_target="tpu_custom_call" | custom-call | tf_op jit(solution)/shard_map/render_edges/pallas_call | solution.py:424
  15.6 0.0 copy-start.5
  15.6 11.1 %all_to_all.5.in_ref = s16[4,2,128,128]{3,2,1,0:T(8,128)(2,1)S(1)} all-to-all(s16[4,2,128,128]{3,2,1,0:T(8,128)(2,1)S(1)} %render_edges.1), channel_id=1, replica_groups=mesh['gz'=4,'xy'=8] {'gz'}, dimensions={0} | all-to-all | bytes 524288 | tf_op jit(solution)/shard_map/all_to_all | solution.py:534
  26.7 1.2 %composite.1 = f32[2,4,1,32,128]{4,3,2,1,0:T(8,128)} custom-call(s32[2,4]{1,0:T(2,128)S(1)} %copy-done.5, s16[4,2,128,128]{3,2,1,0:T(8,128)(2,1)S(1)} %all_to_all.5.in_ref), custom_call_target="tpu_custom_call" | custom-call | tf_op jit(solution)/shard_map/composite/pallas_call | solution.py:536
  (11 shorter events, 0.0 us)
Async XLA Ops:
  0.0 1.0 %copy-start = (f32[8,128,128]{2,1,0:T(8,128)S(1)}, f32[8,128,128]{2,1,0:T(8,128)}, u32[]{:S(2)}) copy-start(f32[8,128,128]{2,1,0:T(8,128)} %own_ref.1) | copy-start | bytes 1572868
  1.0 10.4 %copy-start.1 = (f32[8,128,128]{2,1,0:T(8,128)S(1)}, f32[8,128,128]{2,1,0:T(8,128)}, u32[]{:S(2)}) copy-start(f32[8,128,128]{2,1,0:T(8,128)} %own_ref.1) | copy-start | bytes 1572868
  1.2 8.6 %collective-permute-start = (f32[8,8,128]{2,1,0:T(8,128)S(1)}, f32[8,8,128]{2,1,0:T(8,128)S(1)}, u32[]{:S(2)}, u32[]{:S(2)}) collective-permute-start(f32[8,8,128]{2,1,0:T(8,128)S(1)} %get-tuple-element.13), channel_id=1, source_target_pairs={{0,1},{2,3},{4,5},{6,7},{1,0},{3,2},{5,4},{7,6},{8,9},{10,11},{12,... | collective-permute-start | bytes 98312 | tf_op jit(solution)/shard_map/ppermute | solution.py:514
  1.3 8.6 %collective-permute-start.1 = (f32[8,8,128]{2,1,0:T(8,128)S(1)}, f32[8,8,128]{2,1,0:T(8,128)S(1)}, u32[]{:S(2)}, u32[]{:S(2)}) collective-permute-start(f32[8,8,128]{2,1,0:T(8,128)S(1)} %get-tuple-element.14), channel_id=1, source_target_pairs={{1,2},{3,4},{5,6},{2,1},{4,3},{6,5},{9,10},{11,12},{13,14},{10,9},... | collective-permute-start | bytes 98312 | tf_op jit(solution)/shard_map/ppermute | solution.py:515
  6.2 5.2 %collective-permute-start.4 = (s32[4,128,128]{2,1,0:T(8,128)S(1)}, s32[4,128,128]{2,1,0:T(8,128)S(1)}, u32[]{:S(2)}, u32[]{:S(2)}) collective-permute-start(s32[4,128,128]{2,1,0:T(8,128)S(1)} %get-tuple-element.15), channel_id=1, source_target_pairs={{8,16},{16,8},{9,17},{17,9},{10,18},{18,10},{11,19},{19,11},{12,20... | collective-permute-start | bytes 786440 | tf_op jit(solution)/shard_map/ppermute | solution.py:516
  6.9 4.5 %collective-permute-start.5 = (s32[4,128,128]{2,1,0:T(8,128)S(1)}, s32[4,128,128]{2,1,0:T(8,128)S(1)}, u32[]{:S(2)}, u32[]{:S(2)}) collective-permute-start(s32[4,128,128]{2,1,0:T(8,128)S(1)} %get-tuple-element.16), channel_id=1, source_target_pairs={{0,8},{16,24},{8,0},{24,16},{1,9},{17,25},{9,1},{25,17},{2,10},{18... | collective-permute-start | bytes 786440 | tf_op jit(solution)/shard_map/ppermute | solution.py:517
  9.9 0.8 %copy-start.6 = (f32[2]{0:T(128)S(1)}, f32[2]{0:T(128)}, u32[]{:S(2)}) copy-start(f32[2]{0:T(128)} %slopes_in.1) | copy-start | bytes 28
  9.9 4.7 %collective-permute-start.3 = (f32[5,16,128]{2,1,0:T(8,128)S(1)}, f32[5,16,128]{2,1,0:T(8,128)S(1)}, u32[]{:S(2)}, u32[]{:S(2)}) collective-permute-start(f32[5,16,128]{2,1,0:T(8,128)S(1)} %get-tuple-element.21), channel_id=1, source_target_pairs={{0,8},{16,24},{8,0},{24,16},{1,9},{17,25},{9,1},{25,17},{2,10},{18... | collective-permute-start | bytes 122888 | tf_op jit(solution)/shard_map/ppermute | solution.py:523
  10.0 4.6 %collective-permute-start.2 = (f32[5,16,128]{2,1,0:T(8,128)S(1)}, f32[5,16,128]{2,1,0:T(8,128)S(1)}, u32[]{:S(2)}, u32[]{:S(2)}) collective-permute-start(f32[5,16,128]{2,1,0:T(8,128)S(1)} %get-tuple-element.22), channel_id=1, source_target_pairs={{8,16},{16,8},{9,17},{17,9},{10,18},{18,10},{11,19},{19,11},{12,20... | collective-permute-start | bytes 122888 | tf_op jit(solution)/shard_map/ppermute | solution.py:520
  11.4 0.7 %copy-start.2 = (s32[4,8]{1,0:T(4,128)S(1)}, s32[4,8]{1,0:T(4,128)}, u32[]{:S(2)}) copy-start(s32[4,8]{1,0:T(4,128)} %live_in.3) | copy-start | bytes 388
  11.4 0.7 %copy-start.3 = (s32[2,4]{1,0:T(2,128)S(1)}, s32[2,4]{1,0:T(2,128)}, u32[]{:S(2)}) copy-start(s32[2,4]{1,0:T(2,128)} %owner_in.3) | copy-start | bytes 100
  11.5 0.7 %copy-start.4 = (f32[3]{0:T(128)S(1)}, f32[3]{0:T(128)}, u32[]{:S(2)}) copy-start(f32[3]{0:T(128)} %palette_in.3) | copy-start | bytes 40
  15.6 11.1 %copy-start.5 = (s32[2,4]{1,0:T(2,128)S(1)}, s32[2,4]{1,0:T(2,128)}, u32[]{:S(2)}) copy-start(s32[2,4]{1,0:T(2,128)} %order_in.1) | copy-start | bytes 100

commit v28 on v26

--- a/solution.py
+++ b/solution.py
@@ -294,7 +294,7 @@
 
 
 def render_edges(
-    live_slices, palette, owner, corner_odd, corner_even, row_even, row_odd,
+    live_slices, palette, owner, corner_even, corner_odd, row_even, row_odd,
     inner, deep, shear, band_weights, n_depth,
 ):
     layers, padded_rows, columns = deep.shape
@@ -308,7 +308,7 @@
     height = 2 * EDGE
 
     def kernel(
-        live_in, palette_in, owner_in, corner_odd_ref, corner_even_ref, row_even_ref, row_odd_ref,
+        live_in, palette_in, owner_in, corner_even_ref, corner_odd_ref, row_even_ref, row_odd_ref,
         inner_ref, deep_ref, shear_ref, band_ref,
         out_ref, halo, triple, split_sums, smooth, across, sheared,
         live_ref, palette_ref, owner_ref, sems,
@@ -426,7 +426,7 @@
         compiler_params=pltpu.CompilerParams(vmem_limit_bytes=VMEM_BYTES),
         name="render_edges",
     )(
-        live_slices, palette, owner, corner_odd, corner_even, row_even, row_odd,
+        live_slices, palette, owner, corner_even, corner_odd, row_even, row_odd,
         inner, deep, shear, band_weights,
     )
 
@@ -512,7 +512,7 @@
         live_slices, shear_slopes, palette, tile_owner, density, deep_odd, deep_even, n_depth
     )
     outgoing = render_edges(
-        live_slices, palette, tile_owner, corner_odd, corner_even, row_even, row_odd,
+        live_slices, palette, tile_owner, corner_even, corner_odd, row_even, row_odd,
         inner, deep, shear, band_weights, n_depth,
     )
     incoming = lax.all_to_all(outgoing, "gz", split_axis=0, concat_axis=0, tiled=True)

time: 27.4 us -> 27.4 us (level)
  starting transfers between devices: 9.37 us -> 11 us
  blocking collectives: 11.6 us -> 10.2 us
    ppermute x1, starting transfers between devices: 0.11 us -> 1.57 us  [body(): lax.ppermute(lax.dynamic_slice_in_dim(rows, edge - facing, HALO), 'gz', p...]
    all_to_all x1, blocking collectives: 11.6 us -> 10.2 us  [body(): lax.all_to_all(outgoing, 'gz', split_axis=0, concat_axis=0, tiled=True)]
    ppermute x1, waiting for transfers between devices: 0.28 us -> 0.01 us  [body(): deep_even = lax.ppermute(deep_even, 'gz', pairs('gz', 0))]
  transfers between devices with their start and end apart: 6 -> 6, of which waited for: 1 -> 0; matrix products, arithmetic and copies ran while one was open for 0% -> 0% of each run, Pallas kernels for 8% -> 9%
where the time goes in v28:
time: 27.4 us; the launch traced here: 27.1 us
  starting transfers between devices  11 us (40%)
  blocking collectives  10.2 us (37%)
  Pallas kernels  4.68 us (17%)
  local copies, waits for them, and re-layouts  1.1 us (4%)
    all_to_all x1, blocking collectives, body(): lax.all_to_all(outgoing, 'gz', split_axis=0, concat_axis=0, tiled=True)  10.2 us
    ppermute x1, starting transfers between devices, body(): row_odd = lax.ppermute(row_odd, 'xy', pairs('xy', 1))  4.92 us
    ppermute x1, starting transfers between devices, body(): deep_even = lax.ppermute(deep_even, 'gz', pairs('gz', 0))  2.93 us
    pallas_call x1, Pallas kernels, render_inner(): pl.pallas_call(kernel, out_shape=(jax.ShapeDtypeStruct((n_depth, VIEWS, 4...  2.31 us
    ppermute x1, starting transfers between devices, body(): lax.ppermute(lax.dynamic_slice_in_dim(rows, edge - facing, HALO), 'gz', p...  1.57 us
    pallas_call x1, Pallas kernels, body(): pl.pallas_call(composite_kernel, out_shape=jax.ShapeDtypeStruct((VIEWS, 4...  1.25 us
    unnamed x15, local copies, waits for them, and re-layouts  1.08 us
    pallas_call x1, Pallas kernels, render_edges(): pl.pallas_call(kernel, out_shape=jax.ShapeDtypeStruct(inner.shape, inner....  0.95 us
  transfers between devices with their start and end apart: 6, of which 0 were waited for; matrix products, arithmetic and copies ran while one was open for 0% of the time, Pallas kernels for 9%

profile of v28, /device:TPU:2, one launch (start us, length us, event | category | flops | bytes accessed | tf_op | source)
XLA Modules:
  0.0 27.1 jit_solution(8082713311077285187)
XLA Ops:
  0.0 1.0 %copy-done = f32[8,128,128]{2,1,0:T(8,128)S(1)} copy-done((f32[8,128,128]{2,1,0:T(8,128)S(1)}, f32[8,128,128]{2,1,0:T(8,128)}, u32[]{:S(2)}) %copy-start) | copy-done | bytes 524312
  1.0 0.2 cut_edges.1
  1.2 0.1 collective-permute-start
  1.3 4.9 %collective-permute-start.1 = (f32[8,8,128]{2,1,0:T(8,128)S(1)}, f32[8,8,128]{2,1,0:T(8,128)S(1)}, u32[]{:S(2)}, u32[]{:S(2)}) collective-permute-start(f32[8,8,128]{2,1,0:T(8,128)S(1)} %get-tuple-element.14), channel_id=1, source_target_pairs={{1,2},{3,4},{5,6},{2,1},{4,3},{6,5},{9,10},{11,12},{13,14},{10,9},... | collective-permute-start | bytes 98312 | tf_op jit(solution)/shard_map/ppermute | solution.py:500
  6.2 0.7 %collective-permute-start.4 = (s32[4,128,128]{2,1,0:T(8,128)S(1)}, s32[4,128,128]{2,1,0:T(8,128)S(1)}, u32[]{:S(2)}, u32[]{:S(2)}) collective-permute-start(s32[4,128,128]{2,1,0:T(8,128)S(1)} %get-tuple-element.15), channel_id=1, source_target_pairs={{8,16},{16,8},{9,17},{17,9},{10,18},{18,10},{11,19},{19,11},{12,20... | collective-permute-start | bytes 786440 | tf_op jit(solution)/shard_map/ppermute | solution.py:501
  6.9 2.9 %collective-permute-start.5 = (s32[4,128,128]{2,1,0:T(8,128)S(1)}, s32[4,128,128]{2,1,0:T(8,128)S(1)}, u32[]{:S(2)}, u32[]{:S(2)}) collective-permute-start(s32[4,128,128]{2,1,0:T(8,128)S(1)} %get-tuple-element.16), channel_id=1, source_target_pairs={{0,8},{16,24},{8,0},{24,16},{1,9},{17,25},{9,1},{25,17},{2,10},{18... | collective-permute-start | bytes 786440 | tf_op jit(solution)/shard_map/ppermute | solution.py:502
  9.8 0.0 collective-permute-done.row_even_ref
  9.9 0.0 collective-permute-done.1.row_odd_ref
  9.9 0.0 copy-start.6
  9.9 0.0 copy-start.2
  9.9 0.0 copy-start.3
  9.9 0.0 copy-start.4
  9.9 0.8 %collective-permute-start.3 = (f32[5,16,128]{2,1,0:T(8,128)S(1)}, f32[5,16,128]{2,1,0:T(8,128)S(1)}, u32[]{:S(2)}, u32[]{:S(2)}) collective-permute-start(f32[5,16,128]{2,1,0:T(8,128)S(1)} %get-tuple-element.21), channel_id=1, source_target_pairs={{8,16},{16,8},{9,17},{17,9},{10,18},{18,10},{11,19},{19,11},{12,20... | collective-permute-start | bytes 122888 | tf_op jit(solution)/shard_map/ppermute | solution.py:505
  10.7 1.6 %collective-permute-start.2 = (f32[5,16,128]{2,1,0:T(8,128)S(1)}, f32[5,16,128]{2,1,0:T(8,128)S(1)}, u32[]{:S(2)}, u32[]{:S(2)}) collective-permute-start(f32[5,16,128]{2,1,0:T(8,128)S(1)} %get-tuple-element.22), channel_id=1, source_target_pairs={{0,8},{16,24},{8,0},{24,16},{1,9},{17,25},{9,1},{25,17},{2,10},{18... | collective-permute-start | bytes 122888 | tf_op jit(solution)/shard_map/ppermute | solution.py:508
  12.3 0.0 collective-permute-done.4.odd_ref
  12.3 0.0 collective-permute-done.5.even_ref
  12.3 0.0 copy-done.1
  12.4 2.3 %render_inner.1 = (s16[4,2,128,128]{3,2,1,0:T(8,128)(2,1)S(1)}, f32[10,144,128]{2,1,0:T(8,128)S(1)}, bf16[8,128,256]{2,1,0:T(8,128)(2,1)S(1)}, bf16[128,256]{1,0:T(8,128)(2,1)S(1)}) custom-call(s32[4,8]{1,0:T(4,128)S(1)} %copy-done.2, f32[2]{0:T(128)S(1)} %copy-done.6, f32[3]{0:T(128)S(1)} %copy-done.4, s32[2,4]{1,0:T(2,128)S(1)} %copy-done.3, ...), custom_call_target="tpu_custom_call" | custom-call | flops 13107200 | bytes 8388608 | tf_op jit(solution)/shard_map/render_inner/pallas_call | solution.py:265
  14.7 0.0 collective-permute-done.3.corner_odd_ref
  14.7 0.0 collective-permute-done.2.corner_even_ref
  14.7 0.9 %render_edges.1 = s16[4,2,128,128]{3,2,1,0:T(8,128)(2,1)S(1)} custom-call(s32[4,8]{1,0:T(4,128)S(1)} %copy-done.2, f32[3]{0:T(128)S(1)} %copy-done.4, s32[2,4]{1,0:T(2,128)S(1)} %copy-done.3, f32[5,16,128]{2,1,0:T(8,128)S(1)} %collective-permute-done.2.corner_even_ref, f32[5,16,128]{2,1,0:T(8,128)S(1)} %collective-permute-done.3.corner_odd_ref, ...), custom_call_target="tpu_custom_call" | custom-call | tf_op jit(solution)/shard_map/render_edges/pallas_call | solution.py:409
  15.7 0.0 copy-start.5
  15.7 10.2 %all_to_all.5.in_ref = s16[4,2,128,128]{3,2,1,0:T(8,128)(2,1)S(1)} all-to-all(s16[4,2,128,128]{3,2,1,0:T(8,128)(2,1)S(1)} %render_edges.1), channel_id=1, replica_groups=mesh['gz'=4,'xy'=8] {'gz'}, dimensions={0} | all-to-all | bytes 524288 | tf_op jit(solution)/shard_map/all_to_all | solution.py:518
  25.9 1.2 %composite.1 = f32[2,4,1,32,128]{4,3,2,1,0:T(8,128)} custom-call(s32[2,4]{1,0:T(2,128)S(1)} %copy-done.5, s16[4,2,128,128]{3,2,1,0:T(8,128)(2,1)S(1)} %all_to_all.5.in_ref), custom_call_target="tpu_custom_call" | custom-call | tf_op jit(solution)/shard_map/composite/pallas_call | solution.py:520
  (10 shorter events, 0.0 us)
Async XLA Ops:
  0.0 1.0 %copy-start = (f32[8,128,128]{2,1,0:T(8,128)S(1)}, f32[8,128,128]{2,1,0:T(8,128)}, u32[]{:S(2)}) copy-start(f32[8,128,128]{2,1,0:T(8,128)} %own_ref.1) | copy-start | bytes 1572868
  1.0 11.3 %copy-start.1 = (f32[8,128,128]{2,1,0:T(8,128)S(1)}, f32[8,128,128]{2,1,0:T(8,128)}, u32[]{:S(2)}) copy-start(f32[8,128,128]{2,1,0:T(8,128)} %own_ref.1) | copy-start | bytes 1572868
  1.2 8.6 %collective-permute-start = (f32[8,8,128]{2,1,0:T(8,128)S(1)}, f32[8,8,128]{2,1,0:T(8,128)S(1)}, u32[]{:S(2)}, u32[]{:S(2)}) collective-permute-start(f32[8,8,128]{2,1,0:T(8,128)S(1)} %get-tuple-element.13), channel_id=1, source_target_pairs={{0,1},{2,3},{4,5},{6,7},{1,0},{3,2},{5,4},{7,6},{8,9},{10,11},{12,... | collective-permute-start | bytes 98312 | tf_op jit(solution)/shard_map/ppermute | solution.py:499
  1.3 8.6 %collective-permute-start.1 = (f32[8,8,128]{2,1,0:T(8,128)S(1)}, f32[8,8,128]{2,1,0:T(8,128)S(1)}, u32[]{:S(2)}, u32[]{:S(2)}) collective-permute-start(f32[8,8,128]{2,1,0:T(8,128)S(1)} %get-tuple-element.14), channel_id=1, source_target_pairs={{1,2},{3,4},{5,6},{2,1},{4,3},{6,5},{9,10},{11,12},{13,14},{10,9},... | collective-permute-start | bytes 98312 | tf_op jit(solution)/shard_map/ppermute | solution.py:500
  6.2 6.1 %collective-permute-start.4 = (s32[4,128,128]{2,1,0:T(8,128)S(1)}, s32[4,128,128]{2,1,0:T(8,128)S(1)}, u32[]{:S(2)}, u32[]{:S(2)}) collective-permute-start(s32[4,128,128]{2,1,0:T(8,128)S(1)} %get-tuple-element.15), channel_id=1, source_target_pairs={{8,16},{16,8},{9,17},{17,9},{10,18},{18,10},{11,19},{19,11},{12,20... | collective-permute-start | bytes 786440 | tf_op jit(solution)/shard_map/ppermute | solution.py:501
  6.9 5.4 %collective-permute-start.5 = (s32[4,128,128]{2,1,0:T(8,128)S(1)}, s32[4,128,128]{2,1,0:T(8,128)S(1)}, u32[]{:S(2)}, u32[]{:S(2)}) collective-permute-start(s32[4,128,128]{2,1,0:T(8,128)S(1)} %get-tuple-element.16), channel_id=1, source_target_pairs={{0,8},{16,24},{8,0},{24,16},{1,9},{17,25},{9,1},{25,17},{2,10},{18... | collective-permute-start | bytes 786440 | tf_op jit(solution)/shard_map/ppermute | solution.py:502
  9.9 2.5 %copy-start.6 = (f32[2]{0:T(128)S(1)}, f32[2]{0:T(128)}, u32[]{:S(2)}) copy-start(f32[2]{0:T(128)} %slopes_in.1) | copy-start | bytes 28
  9.9 2.4 %copy-start.2 = (s32[4,8]{1,0:T(4,128)S(1)}, s32[4,8]{1,0:T(4,128)}, u32[]{:S(2)}) copy-start(s32[4,8]{1,0:T(4,128)} %live_in.3) | copy-start | bytes 388
  9.9 2.4 %copy-start.3 = (s32[2,4]{1,0:T(2,128)S(1)}, s32[2,4]{1,0:T(2,128)}, u32[]{:S(2)}) copy-start(s32[2,4]{1,0:T(2,128)} %owner_in.3) | copy-start | bytes 100
  9.9 2.4 %copy-start.4 = (f32[3]{0:T(128)S(1)}, f32[3]{0:T(128)}, u32[]{:S(2)}) copy-start(f32[3]{0:T(128)} %palette_in.3) | copy-start | bytes 40
  9.9 4.7 %collective-permute-start.3 = (f32[5,16,128]{2,1,0:T(8,128)S(1)}, f32[5,16,128]{2,1,0:T(8,128)S(1)}, u32[]{:S(2)}, u32[]{:S(2)}) collective-permute-start(f32[5,16,128]{2,1,0:T(8,128)S(1)} %get-tuple-element.21), channel_id=1, source_target_pairs={{8,16},{16,8},{9,17},{17,9},{10,18},{18,10},{11,19},{19,11},{12,20... | collective-permute-start | bytes 122888 | tf_op jit(solution)/shard_map/ppermute | solution.py:505
  10.7 4.0 %collective-permute-start.2 = (f32[5,16,128]{2,1,0:T(8,128)S(1)}, f32[5,16,128]{2,1,0:T(8,128)S(1)}, u32[]{:S(2)}, u32[]{:S(2)}) collective-permute-start(f32[5,16,128]{2,1,0:T(8,128)S(1)} %get-tuple-element.22), channel_id=1, source_target_pairs={{0,8},{16,24},{8,0},{24,16},{1,9},{17,25},{9,1},{25,17},{2,10},{18... | collective-permute-start | bytes 122888 | tf_op jit(solution)/shard_map/ppermute | solution.py:508
  15.7 10.2 %copy-start.5 = (s32[2,4]{1,0:T(2,128)S(1)}, s32[2,4]{1,0:T(2,128)}, u32[]{:S(2)}) copy-start(s32[2,4]{1,0:T(2,128)} %order_in.1) | copy-start | bytes 100

commit v29 on v26

--- a/solution.py
+++ b/solution.py
@@ -393,7 +393,6 @@
             sheared[z] = jnp.dot(
                 jnp.concatenate(channels), shear_ref[z], preferred_element_type=jnp.float32
             )
-        out_ref[...] = inner_ref[...]
         for view in range(VIEWS):
             lanes = pl.ds(view * columns, columns)
             values = march(
@@ -403,12 +402,13 @@
             for side, row in enumerate((0, row_cells - EDGE)):
                 place = owner_ref[view, row // tile_rows]
                 part = [code[side * EDGE : (side + 1) * EDGE] for code in codes]
-                store_codes(out_ref, place, view, part, row % tile_rows, tile_rows, inner_ref)
+                store_codes(out_ref, place, view, part, row % tile_rows, tile_rows, out_ref)
 
     vmem = pl.BlockSpec(memory_space=pltpu.VMEM)
     return pl.pallas_call(
         kernel,
         out_shape=jax.ShapeDtypeStruct(inner.shape, inner.dtype),
+        input_output_aliases={7: 0},
         in_specs=[vmem] * 11,
         out_specs=vmem,
         scratch_shapes=[

time: 27.4 us -> 27.4 us (level)
  no operation moved by 1% of the time
where the time goes in v29:
time: 27.4 us; the launch traced here: 27.2 us
  blocking collectives  11.6 us (42%)
  starting transfers between devices  9.37 us (34%)
  Pallas kernels  4.68 us (17%)
  local copies, waits for them, and re-layouts  1.1 us (4%)
  waiting for transfers between devices  0.29 us (1%)
    all_to_all x1, blocking collectives, body(): lax.all_to_all(outgoing, 'gz', split_axis=0, concat_axis=0, tiled=True)  11.6 us
    ppermute x1, starting transfers between devices, body(): row_odd = lax.ppermute(row_odd, 'xy', pairs('xy', 1))  4.92 us
    ppermute x1, starting transfers between devices, body(): deep_even = lax.ppermute(deep_even, 'gz', pairs('gz', 0))  2.93 us
    pallas_call x1, Pallas kernels, render_inner(): pl.pallas_call(kernel, out_shape=(jax.ShapeDtypeStruct((n_depth, VIEWS, 4...  2.3 us
    pallas_call x1, Pallas kernels, body(): pl.pallas_call(composite_kernel, out_shape=jax.ShapeDtypeStruct((VIEWS, 4...  1.25 us
    unnamed x15, local copies, waits for them, and re-layouts  1.08 us
    pallas_call x1, Pallas kernels, render_edges(): pl.pallas_call(kernel, out_shape=jax.ShapeDtypeStruct(inner.shape, inner....  0.95 us
    ppermute x1, starting transfers between devices, body(): deep_odd = lax.ppermute(deep_odd, 'gz', pairs('gz', 1))  0.68 us
  transfers between devices with their start and end apart: 6, of which 1 were waited for; matrix products, arithmetic and copies ran while one was open for 0% of the time, Pallas kernels for 8%

profile of v29, /device:TPU:2, one launch (start us, length us, event | category | flops | bytes accessed | tf_op | source)
XLA Modules:
  0.0 27.2 jit_solution(15196591899713410333)
XLA Ops:
  0.0 1.0 %copy-done = f32[8,128,128]{2,1,0:T(8,128)S(1)} copy-done((f32[8,128,128]{2,1,0:T(8,128)S(1)}, f32[8,128,128]{2,1,0:T(8,128)}, u32[]{:S(2)}) %copy-start) | copy-done | bytes 524312
  1.0 0.2 cut_edges.1
  1.2 0.1 collective-permute-start
  1.3 4.9 %collective-permute-start.1 = (f32[8,8,128]{2,1,0:T(8,128)S(1)}, f32[8,8,128]{2,1,0:T(8,128)S(1)}, u32[]{:S(2)}, u32[]{:S(2)}) collective-permute-start(f32[8,8,128]{2,1,0:T(8,128)S(1)} %get-tuple-element.14), channel_id=1, source_target_pairs={{1,2},{3,4},{5,6},{2,1},{4,3},{6,5},{9,10},{11,12},{13,14},{10,9},... | collective-permute-start | bytes 98312 | tf_op jit(solution)/shard_map/ppermute | solution.py:500
  6.2 0.7 %collective-permute-start.4 = (s32[4,128,128]{2,1,0:T(8,128)S(1)}, s32[4,128,128]{2,1,0:T(8,128)S(1)}, u32[]{:S(2)}, u32[]{:S(2)}) collective-permute-start(s32[4,128,128]{2,1,0:T(8,128)S(1)} %get-tuple-element.15), channel_id=1, source_target_pairs={{8,16},{16,8},{9,17},{17,9},{10,18},{18,10},{11,19},{19,11},{12,20... | collective-permute-start | bytes 786440 | tf_op jit(solution)/shard_map/ppermute | solution.py:501
  6.9 2.9 %collective-permute-start.5 = (s32[4,128,128]{2,1,0:T(8,128)S(1)}, s32[4,128,128]{2,1,0:T(8,128)S(1)}, u32[]{:S(2)}, u32[]{:S(2)}) collective-permute-start(s32[4,128,128]{2,1,0:T(8,128)S(1)} %get-tuple-element.16), channel_id=1, source_target_pairs={{0,8},{16,24},{8,0},{24,16},{1,9},{17,25},{9,1},{25,17},{2,10},{18... | collective-permute-start | bytes 786440 | tf_op jit(solution)/shard_map/ppermute | solution.py:502
  9.8 0.0 collective-permute-done.row_even_ref
  9.9 0.0 collective-permute-done.1.row_odd_ref
  9.9 0.0 copy-start.6
  9.9 0.0 copy-start.2
  9.9 0.0 copy-start.3
  9.9 0.0 copy-start.4
  9.9 0.1 collective-permute-start.3
  10.1 0.7 %collective-permute-start.2 = (f32[5,16,128]{2,1,0:T(8,128)S(1)}, f32[5,16,128]{2,1,0:T(8,128)S(1)}, u32[]{:S(2)}, u32[]{:S(2)}) collective-permute-start(f32[5,16,128]{2,1,0:T(8,128)S(1)} %get-tuple-element.22), channel_id=1, source_target_pairs={{8,16},{16,8},{9,17},{17,9},{10,18},{18,10},{11,19},{19,11},{12,20... | collective-permute-start | bytes 122888 | tf_op jit(solution)/shard_map/ppermute | solution.py:505
  10.7 0.0 collective-permute-done.4.odd_ref
  10.7 0.3 %collective-permute-done.5.even_ref = s32[4,128,128]{2,1,0:T(8,128)S(1)} collective-permute-done((s32[4,128,128]{2,1,0:T(8,128)S(1)}, s32[4,128,128]{2,1,0:T(8,128)S(1)}, u32[]{:S(2)}, u32[]{:S(2)}) %collective-permute-start.5) | collective-permute-done | bytes 262176 | tf_op jit(solution)/shard_map/ppermute | solution.py:502
  11.0 0.0 copy-done.6
  11.0 2.3 %render_inner.1 = (s16[4,2,128,128]{3,2,1,0:T(8,128)(2,1)S(1)}, f32[10,144,128]{2,1,0:T(8,128)S(1)}, bf16[8,128,256]{2,1,0:T(8,128)(2,1)S(1)}, bf16[128,256]{1,0:T(8,128)(2,1)S(1)}) custom-call(s32[4,8]{1,0:T(4,128)S(1)} %copy-done.2, f32[2]{0:T(128)S(1)} %copy-done.6, f32[3]{0:T(128)S(1)} %copy-done.4, s32[2,4]{1,0:T(2,128)S(1)} %copy-done.3, ...), custom_call_target="tpu_custom_call" | custom-call | flops 13107200 | bytes 8388608 | tf_op jit(solution)/shard_map/render_inner/pallas_call | solution.py:265
  13.3 0.0 collective-permute-done.3.corner_even_ref
  13.4 0.0 collective-permute-done.2.corner_odd_ref
  13.4 1.0 %render_edges.1 = s16[4,2,128,128]{3,2,1,0:T(8,128)(2,1)S(1)} custom-call(s32[4,8]{1,0:T(4,128)S(1)} %copy-done.2, f32[3]{0:T(128)S(1)} %copy-done.4, s32[2,4]{1,0:T(2,128)S(1)} %copy-done.3, f32[5,16,128]{2,1,0:T(8,128)S(1)} %collective-permute-done.2.corner_odd_ref, ...), custom_call_target="tpu_custom_call", output_to_operand_aliasing={{}: (7, {})} | custom-call | tf_op jit(solution)/shard_map/render_edges/pallas_call | solution.py:408
  14.3 0.0 copy-start.5
  14.3 11.6 %all_to_all.5.in_ref = s16[4,2,128,128]{3,2,1,0:T(8,128)(2,1)S(1)} all-to-all(s16[4,2,128,128]{3,2,1,0:T(8,128)(2,1)S(1)} %render_edges.1), channel_id=1, replica_groups=mesh['gz'=4,'xy'=8] {'gz'}, dimensions={0} | all-to-all | bytes 524288 | tf_op jit(solution)/shard_map/all_to_all | solution.py:518
  25.9 1.2 %composite.1 = f32[2,4,1,32,128]{4,3,2,1,0:T(8,128)} custom-call(s32[2,4]{1,0:T(2,128)S(1)} %copy-done.5, s16[4,2,128,128]{3,2,1,0:T(8,128)(2,1)S(1)} %all_to_all.5.in_ref), custom_call_target="tpu_custom_call" | custom-call | tf_op jit(solution)/shard_map/composite/pallas_call | solution.py:520
  (10 shorter events, 0.0 us)
Async XLA Ops:
  0.0 1.0 %copy-start = (f32[8,128,128]{2,1,0:T(8,128)S(1)}, f32[8,128,128]{2,1,0:T(8,128)}, u32[]{:S(2)}) copy-start(f32[8,128,128]{2,1,0:T(8,128)} %own_ref.1) | copy-start | bytes 1572868
  1.0 10.0 %copy-start.1 = (f32[8,128,128]{2,1,0:T(8,128)S(1)}, f32[8,128,128]{2,1,0:T(8,128)}, u32[]{:S(2)}) copy-start(f32[8,128,128]{2,1,0:T(8,128)} %own_ref.1) | copy-start | bytes 1572868
  1.2 8.6 %collective-permute-start = (f32[8,8,128]{2,1,0:T(8,128)S(1)}, f32[8,8,128]{2,1,0:T(8,128)S(1)}, u32[]{:S(2)}, u32[]{:S(2)}) collective-permute-start(f32[8,8,128]{2,1,0:T(8,128)S(1)} %get-tuple-element.13), channel_id=1, source_target_pairs={{0,1},{2,3},{4,5},{6,7},{1,0},{3,2},{5,4},{7,6},{8,9},{10,11},{12,... | collective-permute-start | bytes 98312 | tf_op jit(solution)/shard_map/ppermute | solution.py:499
  1.3 8.6 %collective-permute-start.1 = (f32[8,8,128]{2,1,0:T(8,128)S(1)}, f32[8,8,128]{2,1,0:T(8,128)S(1)}, u32[]{:S(2)}, u32[]{:S(2)}) collective-permute-start(f32[8,8,128]{2,1,0:T(8,128)S(1)} %get-tuple-element.14), channel_id=1, source_target_pairs={{1,2},{3,4},{5,6},{2,1},{4,3},{6,5},{9,10},{11,12},{13,14},{10,9},... | collective-permute-start | bytes 98312 | tf_op jit(solution)/shard_map/ppermute | solution.py:500
  6.2 4.5 %collective-permute-start.4 = (s32[4,128,128]{2,1,0:T(8,128)S(1)}, s32[4,128,128]{2,1,0:T(8,128)S(1)}, u32[]{:S(2)}, u32[]{:S(2)}) collective-permute-start(s32[4,128,128]{2,1,0:T(8,128)S(1)} %get-tuple-element.15), channel_id=1, source_target_pairs={{8,16},{16,8},{9,17},{17,9},{10,18},{18,10},{11,19},{19,11},{12,20... | collective-permute-start | bytes 786440 | tf_op jit(solution)/shard_map/ppermute | solution.py:501
  6.9 4.1 %collective-permute-start.5 = (s32[4,128,128]{2,1,0:T(8,128)S(1)}, s32[4,128,128]{2,1,0:T(8,128)S(1)}, u32[]{:S(2)}, u32[]{:S(2)}) collective-permute-start(s32[4,128,128]{2,1,0:T(8,128)S(1)} %get-tuple-element.16), channel_id=1, source_target_pairs={{0,8},{16,24},{8,0},{24,16},{1,9},{17,25},{9,1},{25,17},{2,10},{18... | collective-permute-start | bytes 786440 | tf_op jit(solution)/shard_map/ppermute | solution.py:502
  9.9 1.1 %copy-start.6 = (f32[2]{0:T(128)S(1)}, f32[2]{0:T(128)}, u32[]{:S(2)}) copy-start(f32[2]{0:T(128)} %slopes_in.1) | copy-start | bytes 28
  9.9 1.1 %copy-start.2 = (s32[4,8]{1,0:T(4,128)S(1)}, s32[4,8]{1,0:T(4,128)}, u32[]{:S(2)}) copy-start(s32[4,8]{1,0:T(4,128)} %live_in.3) | copy-start | bytes 388
  9.9 1.1 %copy-start.3 = (s32[2,4]{1,0:T(2,128)S(1)}, s32[2,4]{1,0:T(2,128)}, u32[]{:S(2)}) copy-start(s32[2,4]{1,0:T(2,128)} %owner_in.3) | copy-start | bytes 100
  9.9 1.1 %copy-start.4 = (f32[3]{0:T(128)S(1)}, f32[3]{0:T(128)}, u32[]{:S(2)}) copy-start(f32[3]{0:T(128)} %palette_in.3) | copy-start | bytes 40
  9.9 3.4 %collective-permute-start.3 = (f32[5,16,128]{2,1,0:T(8,128)S(1)}, f32[5,16,128]{2,1,0:T(8,128)S(1)}, u32[]{:S(2)}, u32[]{:S(2)}) collective-permute-start(f32[5,16,128]{2,1,0:T(8,128)S(1)} %get-tuple-element.21), channel_id=1, source_target_pairs={{0,8},{16,24},{8,0},{24,16},{1,9},{17,25},{9,1},{25,17},{2,10},{18... | collective-permute-start | bytes 122888 | tf_op jit(solution)/shard_map/ppermute | solution.py:508
  10.1 3.3 %collective-permute-start.2 = (f32[5,16,128]{2,1,0:T(8,128)S(1)}, f32[5,16,128]{2,1,0:T(8,128)S(1)}, u32[]{:S(2)}, u32[]{:S(2)}) collective-permute-start(f32[5,16,128]{2,1,0:T(8,128)S(1)} %get-tuple-element.22), channel_id=1, source_target_pairs={{8,16},{16,8},{9,17},{17,9},{10,18},{18,10},{11,19},{19,11},{12,20... | collective-permute-start | bytes 122888 | tf_op jit(solution)/shard_map/ppermute | solution.py:505
  14.3 11.6 %copy-start.5 = (s32[2,4]{1,0:T(2,128)S(1)}, s32[2,4]{1,0:T(2,128)}, u32[]{:S(2)}) copy-start(s32[2,4]{1,0:T(2,128)} %order_in.1) | copy-start | bytes 100
